TPU v7x, 32 devices: a whole 2x2x4 slice. The times are simulated.
32 devices in a mesh: groups: 2 (over x), tp: 8 (over z, y), rep: 2 (over core).
Axes of the slice: x: 2, y: 2, z: 4, core: 2. Of those that a mesh axis runs over, the one named last changes fastest.
Arguments:
- queries: bfloat16 [512, 8192], P(('groups', 'rep'), 'tp'), parts along dimension 0
- key_cache: bfloat16 [8, 512, 32, 128], P('tp', ('groups', 'rep')), parts along dimension 1, as said below
- value_cache: bfloat16 [8, 512, 32, 128], P('tp', ('groups', 'rep')), parts along dimension 1, as said below
- new_keys: bfloat16 [8, 512, 128], P('tp', ('groups', 'rep')), parts along dimension 1, as said below
- new_values: bfloat16 [8, 512, 128], P('tp', ('groups', 'rep')), parts along dimension 1, as said below
- lengths: int32 [512], P(('groups', 'rep')), parts along dimension 0, may hold values from 2 to 32, as said below
- request_variant: int32 [512], P(('groups', 'rep')), parts along dimension 0, may hold values from 0 to 31
- holder_slot: int32 [32], replicated, may hold values from 0 to 31, each once
- out_weight: bfloat16 [8192, 8192], P('tp'), may hold values from -0.375 to 0.375
- factor_in: bfloat16 [32, 8192, 64], P('tp'), may hold values from -0.25 to 0.25
- second_factor: bfloat16 [32, 64, 8192], P('tp'), may hold values from -0.75 to 0.75
- block_values: bfloat16 [32, 16, 128, 128], P('tp'), may hold values from -0.5 to 0.5
- block_scale: float32 [32, 16], P('tp'), may hold values from 1 to 16
- block_owner: int32 [32, 16, 1], P('tp'), may hold values from 0 to 7; in each aligned block of 16 rows (0 to 15, 16 to 31, ..., all dimensions but the last counted through in order) at most 2 rows name the same one
- block_cell: int32 [32, 16], P('tp'), may hold values from 0 to 511
Outputs:
- mixed: bfloat16 [512, 8192], P(('groups', 'rep'), 'tp'), parts along dimension 0
There are 2 independent parts, one for each index of `groups`. A program takes and returns all parts, laid end to end along the dimension named above; an argument that names none is the same for every part. Nothing has to cross between parts.
Inputs may be any that keep to these rules, and one draw needn't show every extreme that they name: `lengths`: within the rows of each rep index some row has 32 live positions. `block_owner`: in each slot at most 2 blocks lie on one tensor shard's rows; some slot reaches 2. `key_cache`: entries s and s' along the first dimension are equal when floor(s * 8 / number of tensor shards) equals floor(s' * 8 / number of tensor shards). `value_cache`: equal along the first dimension within a key-value head, as key_cache. `new_keys`: equal along the first dimension within a key-value head, as key_cache. `new_values`: equal along the first dimension within a key-value head, as key_cache.
All inputs are finite; a program needn't handle non-finite values.
Results may differ from a plain program's by a relative error of at most 0.015.
Values may be sent and summed in bfloat16 or wider, within the bound.
No kernel may reach another device: no remote copies, remote signals or barrier semaphores. Data moves between devices by JAX's collectives and lax.ppermute only.
A program may use at most 128 MiB of HBM per device.

v0:
```python
import math

import jax
import jax.numpy as jnp
from jax import lax
from jax.sharding import PartitionSpec as P

CAP = 2


def attend_local(queries, key_cache, value_cache, new_keys, new_values, lengths):
    row_count = queries.shape[0]
    cache_len = key_cache.shape[2]
    head_dim = key_cache.shape[3]
    cached_keys = key_cache[0]
    cached_values = value_cache[0]
    query_heads = queries.reshape(row_count, -1, head_dim)
    inv_scale = 1.0 / math.sqrt(head_dim)
    scores = (
        jnp.einsum("rhd,rpd->rhp", query_heads, cached_keys, preferred_element_type=jnp.float32)
        * inv_scale
    )
    fresh_score = (
        jnp.einsum("rhd,rd->rh", query_heads, new_keys[0], preferred_element_type=jnp.float32)
        * inv_scale
    )
    in_cache = (jnp.arange(cache_len, dtype=jnp.int32)[None, :] < lengths[:, None])[:, None, :]
    masked = jnp.where(in_cache, scores, -1e30)
    top_score = jnp.maximum(jnp.max(masked, axis=-1), fresh_score)
    raw_weights = jnp.where(in_cache, jnp.exp(masked - top_score[..., None]), 0.0)
    fresh_raw = jnp.exp(fresh_score - top_score)
    denominator = jnp.sum(raw_weights, axis=-1) + fresh_raw
    weights = (raw_weights / denominator[..., None]).astype(jnp.bfloat16)
    fresh_weight = (fresh_raw / denominator).astype(jnp.bfloat16)
    attended_f = jnp.einsum(
        "rhp,rpd->rhd", weights, cached_values, preferred_element_type=jnp.float32
    )
    attended_f = (
        attended_f
        + fresh_weight.astype(jnp.float32)[..., None]
        * new_values[0].astype(jnp.float32)[:, None, :]
    )
    return attended_f.astype(jnp.bfloat16).reshape(row_count, -1)


def apply_blocks(features, slot_row, slot_of, row_block, col_block, rebuilt, complete_width):
    row_count = features.shape[0]
    block_size = rebuilt.shape[1]
    feature_tiles = features.reshape(row_count, -1, block_size)
    picked = jnp.take(feature_tiles, row_block, axis=1)
    row_match = slot_row[:, None] == slot_of[None, :]
    picked = jnp.where(row_match[:, :, None], picked, jnp.zeros((), features.dtype))
    contrib = jnp.einsum("reb,ebc->rec", picked, rebuilt, preferred_element_type=jnp.float32)
    placed = jnp.zeros((row_count, complete_width // block_size, block_size), jnp.float32)
    return placed.at[:, col_block].add(contrib).reshape(row_count, complete_width)


def pack_blocks(block_values, block_scale, block_owner, block_cell, shard_count, capacity):
    owner_ids = block_owner[:, :, 0]
    owner_hot = owner_ids[:, :, None] == jnp.arange(shard_count, dtype=jnp.int32)[None, None, :]
    position = jnp.cumsum(owner_hot.astype(jnp.int32), axis=1) - 1
    place_own = jnp.sum(jnp.where(owner_hot, position, 0), axis=2)
    slot_hits = (
        place_own[:, None, None, :] == jnp.arange(capacity, dtype=jnp.int32)[None, None, :, None]
    )
    select = jnp.transpose(owner_hot, (0, 2, 1))[:, :, None, :] & slot_hits
    packed_vals = jnp.einsum(
        "iocb,ibxy->iocxy",
        select.astype(jnp.bfloat16),
        block_values,
        preferred_element_type=jnp.float32,
    ).astype(jnp.bfloat16)
    scales = jnp.sum(jnp.where(select, block_scale[:, None, None, :], 0.0), axis=3)
    cell_ids = jnp.sum(jnp.where(select, block_cell[:, None, None, :], 0), axis=3)
    return (packed_vals, scales, cell_ids)


def body(
    queries,
    key_cache,
    value_cache,
    new_keys,
    new_values,
    lengths,
    request_variant,
    holder_slot,
    out_weight,
    factor_in,
    second_factor,
    block_values,
    block_scale,
    block_owner,
    block_cell,
):
    attended = attend_local(queries, key_cache, value_cache, new_keys, new_values, lengths)
    row_count, local_width = attended.shape
    complete_width = out_weight.shape[1]
    shard_count = lax.axis_size("tp")
    variants = holder_slot.shape[0]
    slots_here, block_count, block_size, _ = block_values.shape
    col_blocks = complete_width // block_size
    slot_row = jnp.sum(
        jnp.where(
            request_variant[:, None] == jnp.arange(variants, dtype=jnp.int32)[None, :],
            holder_slot[None, :],
            0,
        ),
        axis=1,
    )
    partial_sum = jnp.dot(attended, out_weight, preferred_element_type=jnp.float32)
    factor_rows = lax.all_to_all(factor_in, "tp", split_axis=1, concat_axis=0, tiled=True)
    slot_pick = slot_row[:, None] == jnp.arange(variants, dtype=jnp.int32)[None, :]
    low_all = jnp.einsum("rf,jfk->rjk", attended, factor_rows, preferred_element_type=jnp.float32)
    low_part = jnp.sum(jnp.where(slot_pick[:, :, None], low_all, 0.0), axis=1)
    low_rank = lax.psum(low_part.astype(jnp.bfloat16), "tp")
    factor_cols = lax.all_to_all(second_factor, "tp", split_axis=2, concat_axis=0, tiled=True)
    broadcast_rows = jnp.where(
        slot_pick[:, :, None], low_rank[:, None, :], jnp.zeros((), jnp.bfloat16)
    ).reshape(row_count, -1)
    adapter_columns = jnp.dot(
        broadcast_rows, factor_cols.reshape(-1, local_width), preferred_element_type=jnp.float32
    )
    packed = pack_blocks(block_values, block_scale, block_owner, block_cell, shard_count, CAP)
    recv_vals, recv_scale, recv_cell = (
        lax.all_to_all(packed[0], "tp", split_axis=1, concat_axis=0, tiled=True),
        lax.all_to_all(
            packed[1].astype(jnp.bfloat16), "tp", split_axis=1, concat_axis=0, tiled=True
        ).astype(jnp.float32),
        lax.all_to_all(packed[2], "tp", split_axis=1, concat_axis=0, tiled=True),
    )
    rebuilt = (
        (recv_vals.astype(jnp.float32) * recv_scale[..., None, None])
        .astype(jnp.bfloat16)
        .reshape(-1, block_size, block_size)
    )
    cell_ids = recv_cell.reshape(-1)
    slot_of = jnp.arange(cell_ids.shape[0], dtype=jnp.int32) // CAP
    partial_sum = partial_sum + apply_blocks(
        attended,
        slot_row,
        slot_of,
        cell_ids // col_blocks,
        cell_ids % col_blocks,
        rebuilt,
        complete_width,
    )
    combined_output = lax.psum_scatter(
        partial_sum.astype(jnp.bfloat16), "tp", scatter_dimension=1, tiled=True
    ).astype(jnp.float32)
    combined_output = combined_output + adapter_columns
    return combined_output.astype(jnp.bfloat16)


def solution(mesh):
    return jax.shard_map(
        body,
        mesh=mesh,
        in_specs=(
            P(("groups", "rep"), "tp"),
            P("tp", ("groups", "rep"), None, None),
            P("tp", ("groups", "rep"), None, None),
            P("tp", ("groups", "rep"), None),
            P("tp", ("groups", "rep"), None),
            P(("groups", "rep")),
            P(("groups", "rep")),
            P(),
            P("tp", None),
            P("tp", None, None),
            P("tp", None, None),
            P("tp", None, None, None),
            P("tp", None),
            P("tp", None, None),
            P("tp", None),
        ),
        out_specs=P(("groups", "rep"), "tp"),
        check_vma=False,
    )
```

profile of v0, /device:TPU:0, one launch (start us, length us, event | category | flops | bytes accessed | tf_op | source)
XLA Modules:
  0.0 367.2 jit_solution(3509944785082703527)
XLA Ops:
  10.6 7.3 %all-to-all-start.2 = ((bf16[4,8,2]{0,2,1:T(2,128)(2,1)}), bf16[4,8,2]{0,2,1:T(2,128)(2,1)S(1)}, u32[]{:S(2)}, u32[]{:S(2)}) async-start(bf16[4,8,2]{0,2,1:T(2,128)(2,1)} %copy.103), calls=%async_computation.2 | async-start | bytes 8192 | tf_op jit(solution)/shard_map/all_to_all | solution.py:126
  17.8 0.9 fusion.30
  19.4 4.9 %all-to-all-done.2 = bf16[4,8,2]{0,2,1:T(2,128)(2,1)S(1)} async-done(((bf16[4,8,2]{0,2,1:T(2,128)(2,1)}), bf16[4,8,2]{0,2,1:T(2,128)(2,1)S(1)}, u32[]{:S(2)}, u32[]{:S(2)}) %all-to-all-start.2) | async-done | bytes 160 | tf_op jit(solution)/shard_map/all_to_all | solution.py:126
  24.3 3.3 all-to-all-start
  27.7 1.3 fusion.8
  29.0 1.9 copy.102
  30.9 3.2 all-to-all-done
  34.1 3.6 all-to-all-start.1
  37.7 12.7 %copy.107 = bf16[4,8192,64]{2,0,1:T(4,128)(2,1)} copy(bf16[4,8192,64]{1,2,0:T(8,128)(2,1)} %param.24) | data formatting | bytes 8388608 | tf_op args[9]
  50.4 10.5 %reshape.322 = bf16[8,2,131072]{2,1,0:T(2,128)(2,1)} reshape(bf16[8192,4,64]{2,1,0:T(4,128)(2,1)} %bitcast.108) | data formatting | bytes 8388608
  60.9 22.9 %all-to-all-done.1 = bf16[4,8,2,128,128]{4,3,2,0,1:T(8,128)(2,1)S(1)} async-done(((bf16[4,8,2,128,128]{4,3,2,0,1:T(8,128)(2,1)}), bf16[4,8,2,128,128]{4,3,2,0,1:T(8,128)(2,1)S(1)}, u32[]{:S(2)}, u32[]{:S(2)}) %all-to-all-start.1) | async-done | bytes 2097184 | tf_op jit(solution)/shard_map/all_to_all | solution.py:125
  83.8 4.6 %all-to-all-start.3 = ((bf16[8,2,131072]{2,1,0:T(2,128)(2,1)}), bf16[8,2,131072]{2,1,0:T(2,128)(2,1)}, u32[]{:S(2)}, u32[]{:S(2)}) async-start(bf16[8,2,131072]{2,1,0:T(2,128)(2,1)} %reshape.322), calls=%async_computation.4 | async-start | bytes 8388608 | tf_op jit(solution)/shard_map/all_to_all | solution.py:111
  88.4 1.0 copy.121
  91.4 12.7 %copy.109 = bf16[4,64,8192]{1,0,2:T(4,128)(2,1)} copy(bf16[4,64,8192]{2,1,0:T(8,128)(2,1)} %param.25) | data formatting | bytes 8388608 | tf_op args[10]
  104.1 10.5 %reshape.324 = bf16[8,2,131072]{2,1,0:T(2,128)(2,1)} reshape(bf16[8192,4,64]{2,1,0:T(4,128)(2,1)} %bitcast.109) | data formatting | bytes 8388608
  114.6 66.0 %all-to-all-done.3 = bf16[8,2,131072]{2,1,0:T(2,128)(2,1)} async-done(((bf16[8,2,131072]{2,1,0:T(2,128)(2,1)}), bf16[8,2,131072]{2,1,0:T(2,128)(2,1)}, u32[]{:S(2)}, u32[]{:S(2)}) %all-to-all-start.3) | async-done | bytes 4194336 | tf_op jit(solution)/shard_map/all_to_all | solution.py:111
  180.6 4.5 %all-to-all-start.4 = ((bf16[8,2,131072]{2,1,0:T(2,128)(2,1)}), bf16[8,2,131072]{2,1,0:T(2,128)(2,1)}, u32[]{:S(2)}, u32[]{:S(2)}) async-start(bf16[8,2,131072]{2,1,0:T(2,128)(2,1)} %reshape.324), calls=%async_computation.5 | async-start | bytes 8388608 | tf_op jit(solution)/shard_map/all_to_all | solution.py:116
  187.0 2.2 gather_fusion
  189.2 2.1 bitcast_convert_fusion
  191.7 1.2 copy-done.3
  192.9 3.4 fusion.4
  196.3 2.4 broadcast_in_dim.142
  198.8 13.5 %scatter_fusion = f32[128,64,128]{2,0,1:T(8,128)} fusion(f32[128,64,128]{2,0,1:T(8,128)} %broadcast_in_dim.142, s32[64]{0:T(128)S(1)} %get-tuple-element.8, f32[64,128,128]{2,1,0:T(8,128)} %fusion.4), kind=kCustom, calls=%fused_computation.1 | custom fusion | flops 1048576 | bytes 12583168 | tf_op jit(solution)/shard_map/scatter-add | solution.py:55
  212.3 10.7 %fusion = bf16[128,8192]{1,0:T(8,128)(2,1)} fusion(bf16[1024,8192]{1,0:T(8,128)(2,1)} %param.23, bf16[16,8,8,128]{3,2,1,0:T(8,128)(2,1)S(1)} %bitcast.113, f32[128,64,128]{2,0,1:T(8,128)} %scatter_fusion), kind=kOutput, calls=%fused_computation.3 | convolution fusion | flops 2149580800 | bytes 23330816 | tf_op jit(solution)/shard_map/dot_general | solution.py:110
  223.0 10.3 %reshape.323 = bf16[8192,4,64]{2,1,0:T(4,128)(2,1)} reshape(bf16[8,2,131072]{2,1,0:T(2,128)(2,1)} %all-to-all-done.3) | data formatting | bytes 8388608
  233.3 12.8 %copy.108 = bf16[4,8,1024,64]{2,3,0,1:T(8,128)(2,1)} copy(bf16[4,8,1024,64]{3,0,2,1:T(4,128)(2,1)} %bitcast.106) | data formatting | bytes 8388608 | tf_op jit(solution)/shard_map/all_to_all | solution.py:111
  246.1 48.6 %all-to-all-done.4 = bf16[8,2,131072]{2,1,0:T(2,128)(2,1)} async-done(((bf16[8,2,131072]{2,1,0:T(2,128)(2,1)}), bf16[8,2,131072]{2,1,0:T(2,128)(2,1)}, u32[]{:S(2)}, u32[]{:S(2)}) %all-to-all-start.4) | async-done | bytes 4194336 | tf_op jit(solution)/shard_map/all_to_all | solution.py:116
  294.7 10.3 %reshape.325 = bf16[8192,4,64]{2,1,0:T(4,128)(2,1)} reshape(bf16[8,2,131072]{2,1,0:T(2,128)(2,1)} %all-to-all-done.4) | data formatting | bytes 8388608
  305.0 12.8 %copy.119 = bf16[4,64,8,1024]{3,1,0,2:T(8,128)(2,1)} copy(bf16[4,64,8,1024]{1,0,3,2:T(4,128)(2,1)} %bitcast.107) | data formatting | bytes 8388608 | tf_op jit(solution)/shard_map/all_to_all | solution.py:116
  317.8 3.6 fusion.19
  321.5 35.1 %psum.7 = bf16[128,64]{0,1:T(8,128)(2,1)S(1)} all-reduce(bf16[128,64]{0,1:T(8,128)(2,1)S(1)} %select_reduce_fusion), channel_id=1, replica_groups=mesh['groups'=2,'tp'=8,'rep'=2] {'tp'}, use_global_device_ids=true, to_apply=%region_10.11 | all-reduce | flops 8192 | bytes 32768 | tf_op jit(solution)/shard_map/psum | solution.py:115
  356.7 3.7 fusion.13
  (65 shorter events, 9.1 us)
Async XLA Ops:
  6.5 21.1 %copy-start = (bf16[4,16,128,128]{3,2,1,0:T(8,128)(2,1)S(1)}, bf16[4,16,128,128]{3,2,1,0:T(8,128)(2,1)}, u32[]{:S(2)}) copy-start(bf16[4,16,128,128]{3,2,1,0:T(8,128)(2,1)} %param.26) | copy-start | bytes 6291460
  10.6 13.7 %all-to-all-start.2 = ((bf16[4,8,2]{0,2,1:T(2,128)(2,1)}), bf16[4,8,2]{0,2,1:T(2,128)(2,1)S(1)}, u32[]{:S(2)}, u32[]{:S(2)}) async-start(bf16[4,8,2]{0,2,1:T(2,128)(2,1)} %copy.103), calls=%async_computation.2 | async-start | bytes 8192 | tf_op jit(solution)/shard_map/all_to_all | solution.py:126
  24.3 9.8 %all-to-all-start = ((s32[4,8,2]{0,2,1:T(2,128)}), s32[4,8,2]{0,2,1:T(2,128)S(1)}, u32[]{:S(2)}, u32[]{:S(2)}) async-start(s32[4,8,2]{0,2,1:T(2,128)} %copy.96), calls=%async_computation | async-start | bytes 16384 | tf_op jit(solution)/shard_map/all_to_all | solution.py:129
  34.1 49.7 %all-to-all-start.1 = ((bf16[4,8,2,128,128]{4,3,2,0,1:T(8,128)(2,1)}), bf16[4,8,2,128,128]{4,3,2,0,1:T(8,128)(2,1)S(1)}, u32[]{:S(2)}, u32[]{:S(2)}) async-start(bf16[4,8,2,128,128]{4,3,2,0,1:T(8,128)(2,1)} %copy.102), calls=%async_computation.1 | async-start | bytes 4194304 | tf_op jit(solution)/shard_map/all_to_all | solution.py:125
  60.9 28.5 %copy-start.8 = (bf16[1,128,128]{2,1,0:T(8,128)(2,1)S(1)}, bf16[1,128,128]{2,1,0:T(8,128)(2,1)}, u32[]{:S(2)}) copy-start(bf16[1,128,128]{2,1,0:T(8,128)(2,1)} %param.18) | copy-start | bytes 98308
  60.9 28.8 %copy-start.6 = (s32[128]{0:T(128)S(1)}, s32[128]{0:T(128)}, u32[]{:S(2)}) copy-start(s32[128]{0:T(128)} %param.20) | copy-start | bytes 1540
  60.9 29.0 %copy-start.4 = (bf16[1,128,32,128]{3,2,1,0:T(8,128)(2,1)S(1)}, bf16[1,128,32,128]{3,2,1,0:T(8,128)(2,1)}, u32[]{:S(2)}) copy-start(bf16[1,128,32,128]{3,2,1,0:T(8,128)(2,1)} %param.16) | copy-start | bytes 3145732
  83.8 4.6 %copy-start.2 = (bf16[4,8,2,128,128]{4,3,2,0,1:T(8,128)(2,1)}, bf16[4,8,2,128,128]{4,3,2,0,1:T(8,128)(2,1)S(1)}, u32[]{:S(2)}) copy-start(bf16[4,8,2,128,128]{4,3,2,0,1:T(8,128)(2,1)S(1)} %all-to-all-done.1) | copy-start | bytes 6291460
  83.8 96.9 %all-to-all-start.3 = ((bf16[8,2,131072]{2,1,0:T(2,128)(2,1)}), bf16[8,2,131072]{2,1,0:T(2,128)(2,1)}, u32[]{:S(2)}, u32[]{:S(2)}) async-start(bf16[8,2,131072]{2,1,0:T(2,128)(2,1)} %reshape.322), calls=%async_computation.4 | async-start | bytes 8388608 | tf_op jit(solution)/shard_map/all_to_all | solution.py:111
  114.6 70.9 %copy-start.5 = (bf16[1,128,128]{2,1,0:T(8,128)(2,1)S(1)}, bf16[1,128,128]{2,1,0:T(8,128)(2,1)}, u32[]{:S(2)}) copy-start(bf16[1,128,128]{2,1,0:T(8,128)(2,1)} %param.19) | copy-start | bytes 98308
  114.6 70.9 %copy-start.7 = (bf16[1,128,32,128]{3,2,1,0:T(8,128)(2,1)S(1)}, bf16[1,128,32,128]{3,2,1,0:T(8,128)(2,1)}, u32[]{:S(2)}) copy-start(bf16[1,128,32,128]{3,2,1,0:T(8,128)(2,1)} %param.17) | copy-start | bytes 3145732
  180.6 114.1 %all-to-all-start.4 = ((bf16[8,2,131072]{2,1,0:T(2,128)(2,1)}), bf16[8,2,131072]{2,1,0:T(2,128)(2,1)}, u32[]{:S(2)}, u32[]{:S(2)}) async-start(bf16[8,2,131072]{2,1,0:T(2,128)(2,1)} %reshape.324), calls=%async_computation.5 | async-start | bytes 8388608 | tf_op jit(solution)/shard_map/all_to_all | solution.py:116
  185.2 0.8 copy-start.9
  185.2 0.8 copy-start.10
  185.2 171.5 %reduce-scatter.2.cloned.1.call-start = ((), (), s32[]{:S(2)}) async-start(), calls=%async_computation.6 | async-start | bytes 2359296 | tf_op jit(solution)/shard_map/reduce_scatter | solution.py:147
  191.3 1.6 copy-start.3
  317.8 42.6 %copy-start.1 = (bf16[4,16,128,128]{3,2,1,0:T(8,128)(2,1)S(1)}, bf16[4,16,128,128]{3,2,1,0:T(8,128)(2,1)}, u32[]{:S(2)}) copy-start(bf16[4,16,128,128]{3,2,1,0:T(8,128)(2,1)} %param.26) | copy-start | bytes 6291460
Sparse Core Ops, SparseCore 0:
  223.1 107.1 reduce-scatter.1
where the time goes:
time: 370 us; the launch traced here: 367 us
  waiting for transfers between devices  146 us (39%)
  local copies, waits for them, and re-layouts  104 us (28%)
  blocking collectives  35.1 us (9%)
  matrix products  24.2 us (7%)
  starting transfers between devices  23.6 us (6%)
  other arithmetic  21.1 us (6%)
  between operations  13.7 us (4%)
    unnamed x29, local copies, waits for them, and re-layouts  69.1 us
    all_to_all x1, waiting for transfers between devices, body(): lax.all_to_all(factor_in, 'tp', split_axis=1, concat_axis=0, tiled=True)  66 us
    all_to_all x1, waiting for transfers between devices, body(): lax.all_to_all(second_factor, 'tp', split_axis=2, concat_axis=0, tiled=True)  48.6 us
    psum x1, blocking collectives, body(): low_rank = lax.psum(low_part.astype(jnp.bfloat16), 'tp')  35.1 us
    all_to_all x1, waiting for transfers between devices, body(): lax.all_to_all(packed[0], 'tp', split_axis=1, concat_axis=0, tiled=True)  22.9 us
    scatter-add x1, other arithmetic, apply_blocks(): placed.at[:, col_block].add(contrib).reshape(row_count, complete_width)  13.5 us
    all_to_all x1, local copies, waits for them, and re-layouts, body(): lax.all_to_all(second_factor, 'tp', split_axis=2, concat_axis=0, tiled=True)  12.8 us
    all_to_all x1, local copies, waits for them, and re-layouts, body(): lax.all_to_all(factor_in, 'tp', split_axis=1, concat_axis=0, tiled=True)  12.8 us
  transfers between devices with their start and end apart: 6, of which 5 were waited for; matrix products, arithmetic and copies ran while one was open for 38% of the time, Pallas kernels for 0%

commit v1 on v0

v1 whole, which is shorter than its diff:
```python
import functools
import math

import jax
import jax.numpy as jnp
from jax import lax
from jax.experimental import pallas as pl
from jax.experimental.pallas import tpu as pltpu
from jax.sharding import PartitionSpec as P

BF16 = jnp.bfloat16
F32 = jnp.float32


def attend_local(queries, key_cache, value_cache, new_keys, new_values, lengths):
    row_count = queries.shape[0]
    cache_len = key_cache.shape[2]
    head_dim = key_cache.shape[3]
    query_heads = queries.reshape(row_count, -1, head_dim)
    inv_scale = 1.0 / math.sqrt(head_dim)
    scores = (
        jnp.einsum("rhd,rpd->rhp", query_heads, key_cache[0], preferred_element_type=F32) * inv_scale
    )
    fresh_score = (
        jnp.einsum("rhd,rd->rh", query_heads, new_keys[0], preferred_element_type=F32) * inv_scale
    )
    in_cache = (jnp.arange(cache_len, dtype=jnp.int32)[None, :] < lengths[:, None])[:, None, :]
    masked = jnp.where(in_cache, scores, -1e30)
    top_score = jnp.maximum(jnp.max(masked, axis=-1), fresh_score)
    raw_weights = jnp.where(in_cache, jnp.exp(masked - top_score[..., None]), 0.0)
    fresh_raw = jnp.exp(fresh_score - top_score)
    denominator = jnp.sum(raw_weights, axis=-1) + fresh_raw
    weights = (raw_weights / denominator[..., None]).astype(BF16)
    fresh_weight = (fresh_raw / denominator).astype(BF16)
    attended = jnp.einsum("rhp,rpd->rhd", weights, value_cache[0], preferred_element_type=F32)
    attended = (
        attended + fresh_weight.astype(F32)[..., None] * new_values[0].astype(F32)[:, None, :]
    )
    return jnp.transpose(attended.astype(BF16), (1, 0, 2))


def delta_kernel(
    per_owner, tiles_ref, slot_ref, factor_ref, second_ref, base_ref, values_ref,
    scale_ref, owner_ref, cell_ref, out_ref, total,
):
    tiles, rows, side = tiles_ref.shape
    slots, block_count = values_ref.shape[:2]
    rank = factor_ref.shape[0] // slots
    low = jnp.zeros((rows, slots * rank), F32)
    for t in range(0, tiles, 2):
        pair = jnp.concatenate([tiles_ref[t], tiles_ref[t + 1]], axis=1)
        low = low + lax.dot_general(
            pair,
            factor_ref[:, t * side : (t + 2) * side],
            (((1,), (1,)), ((), ())),
            preferred_element_type=F32,
        )
    slot_row = slot_ref[...]
    held = lax.broadcasted_iota(jnp.int32, (rows, slots * rank), 1) // rank
    low = jnp.where(slot_row == held, low, 0.0).astype(BF16)
    for c in range(0, tiles, 2):
        part = base_ref[:, c * side : (c + 2) * side] + jnp.dot(
            low, second_ref[:, c * side : (c + 2) * side], preferred_element_type=F32
        )
        total[c] = part[:, :side]
        total[c + 1] = part[:, side:]
    group = 4
    for j in range(slots):
        mine = jnp.broadcast_to(slot_row == j, (rows, side))

        def step(i, carry, j=j, mine=mine):
            added = []
            for k in range(group):
                b = i * group + k
                cell = cell_ref[j, b]
                row_block = owner_ref[j, b] * per_owner + lax.div(cell, tiles)
                rebuilt = (values_ref[j, b].astype(F32) * scale_ref[j, b]).astype(BF16)
                product = jnp.dot(tiles_ref[row_block], rebuilt, preferred_element_type=F32)
                added.append((lax.rem(cell, tiles), jnp.where(mine, product, 0.0)))
            for column, product in added:
                total[column] += product
            return carry

        lax.fori_loop(0, block_count // group, step, 0)
    for c in range(tiles):
        out_ref[:, c * side : (c + 1) * side] = total[c].astype(BF16)


def add_delta(tiles, slot_local, factor_t, second, base, block_values, scale, owner, cell, per_owner):
    count, rows, side = tiles.shape
    vmem = pl.BlockSpec(memory_space=pltpu.VMEM)
    smem = pl.BlockSpec(memory_space=pltpu.SMEM)
    return pl.pallas_call(
        functools.partial(delta_kernel, per_owner),
        out_shape=jax.ShapeDtypeStruct((rows, count * side), BF16),
        in_specs=[vmem] * 6 + [smem] * 3,
        out_specs=vmem,
        scratch_shapes=[pltpu.VMEM((count, rows, side), F32)],
        compiler_params=pltpu.CompilerParams(vmem_limit_bytes=40 * 1024 * 1024),
        name="delta",
    )(tiles, slot_local, factor_t, second, base, block_values, scale, owner, cell)


def body(
    queries, key_cache, value_cache, new_keys, new_values, lengths, request_variant, holder_slot,
    out_weight, factor_in, second_factor, block_values, block_scale, block_owner, block_cell,
):
    attended = attend_local(queries, key_cache, value_cache, new_keys, new_values, lengths)
    heads, rows, side = attended.shape
    variants = holder_slot.shape[0]
    slots_here = block_values.shape[0]
    width = out_weight.shape[1]
    slot_row = jnp.sum(
        jnp.where(
            request_variant[:, None] == jnp.arange(variants, dtype=jnp.int32)[None, :],
            holder_slot[None, :],
            0,
        ),
        axis=1,
    )
    slot_local = (slot_row - lax.axis_index("tp") * slots_here)[:, None]
    tiles = lax.all_gather(attended, "tp", axis=0, tiled=True)
    base = lax.dot_general(
        attended,
        out_weight.reshape(heads, side, width),
        (((0, 2), (0, 1)), ((), ())),
        preferred_element_type=F32,
    )
    factor_t = jnp.swapaxes(factor_in, 1, 2).reshape(-1, factor_in.shape[1])
    partial = add_delta(
        tiles,
        slot_local,
        factor_t,
        second_factor.reshape(-1, width),
        base,
        block_values,
        block_scale,
        block_owner[:, :, 0],
        block_cell,
        heads,
    )
    return lax.psum_scatter(partial, "tp", scatter_dimension=1, tiled=True)


def solution(mesh):
    return jax.shard_map(
        body,
        mesh=mesh,
        in_specs=(
            P(("groups", "rep"), "tp"),
            P("tp", ("groups", "rep"), None, None),
            P("tp", ("groups", "rep"), None, None),
            P("tp", ("groups", "rep"), None),
            P("tp", ("groups", "rep"), None),
            P(("groups", "rep")),
            P(("groups", "rep")),
            P(),
            P("tp", None),
            P("tp", None, None),
            P("tp", None, None),
            P("tp", None, None, None),
            P("tp", None),
            P("tp", None, None),
            P("tp", None),
        ),
        out_specs=P(("groups", "rep"), "tp"),
        check_vma=False,
    )
```

time: 370 us -> 156 us (0.42)
  local copies, waits for them, and re-layouts: 104 us -> 6.13 us
  waiting for transfers between devices: 146 us -> 109 us
  blocking collectives: 35.1 us -> 0 us
  starting transfers between devices: 23.6 us -> 0.04 us
  other arithmetic: 21.1 us -> 2.12 us
  Pallas kernels: 0 us -> 11.6 us
  matrix products: 24.2 us -> 12.7 us
    all_to_all x5 -> x0, waiting for transfers between devices: 146 us -> none  [the longest x1 66 us: body(): lax.all_to_all(factor_in, 'tp', split_axis=1, concat_axis=0, tiled=True)]
    reduce_scatter x1, waiting for transfers between devices: 0.02 us -> 66.7 us  [body(): return lax.psum_scatter(partial, 'tp', scatter_dimension=1, tiled=True)]
    unnamed x29 -> x19, local copies, waits for them, and re-layouts: 69.1 us -> 4.81 us
    all_gather x0 -> x1, waiting for transfers between devices: none -> 42.6 us  [body(): tiles = lax.all_gather(attended, 'tp', axis=0, tiled=True)]
    psum x1 -> x0, blocking collectives: 35.1 us -> none  [body(): low_rank = lax.psum(low_part.astype(jnp.bfloat16), 'tp')]
    all_to_all x5 -> x0, local copies, waits for them, and re-layouts: 25.8 us -> none  [the longest x1 12.8 us: body(): lax.all_to_all(second_factor, 'tp', split_axis=2, concat_axis=0, tiled=True)]
    all_to_all x5 -> x0, starting transfers between devices: 23.3 us -> none  [the longest x1 7.28 us: body(): lax.all_to_all(packed[1].astype(jnp.bfloat16), 'tp', split_axis=1, concat...]
    scatter-add x1 -> x0, other arithmetic: 13.5 us -> none  [apply_blocks(): placed.at[:, col_block].add(contrib).reshape(row_count, complete_width)]
  transfers between devices with their start and end apart: 6 -> 2, of which waited for: 5 -> 2; matrix products, arithmetic and copies ran while one was open for 38% -> 6% of each run, Pallas kernels for 0% -> 0%
where the time goes in v1:
time: 156 us; the launch traced here: 155 us
  waiting for transfers between devices  109 us (70%)
  between operations  13.5 us (9%)
  matrix products  12.7 us (8%)
  Pallas kernels  11.6 us (7%)
  local copies, waits for them, and re-layouts  6.13 us (4%)
  other arithmetic  2.12 us (1%)
    reduce_scatter x1, waiting for transfers between devices, body(): return lax.psum_scatter(partial, 'tp', scatter_dimension=1, tiled=True)  66.7 us
    all_gather x1, waiting for transfers between devices, body(): tiles = lax.all_gather(attended, 'tp', axis=0, tiled=True)  42.6 us
    pallas_call x1, Pallas kernels, add_delta(): pl.pallas_call(functools.partial(delta_kernel, per_owner), out_shape=jax....  11.6 us
    dot_general x1, matrix products, body(): lax.dot_general(attended, out_weight.reshape(heads, side, width), (((0, 2...  9.18 us
    unnamed x19, local copies, waits for them, and re-layouts  4.81 us
  transfers between devices with their start and end apart: 2, of which 2 were waited for; matrix products, arithmetic and copies ran while one was open for 6% of the time, Pallas kernels for 0%

profile of v1, /device:TPU:0, one launch (start us, length us, event | category | flops | bytes accessed | tf_op | source)
XLA Modules:
  0.0 155.4 jit_solution(723581125629661503)
XLA Ops:
  6.5 0.0 copy-start
  6.5 0.0 all-gather.2.cloned.1.call-start
  6.5 0.8 iota_compare_fusion
  7.4 1.0 copy.38
  8.4 0.0 copy-start.7
  8.4 0.0 copy-start.8
  8.4 1.0 fusion.10
  9.5 2.0 %fusion.18 = (f32[128,8]{1,0:T(8,128)S(1)}, f32[128,8,32]{2,1,0:T(8,128)S(1)}) fusion(bf16[128,8,128]{2,1,0:T(8,128)(2,1)S(1)} %bitcast.69, bf16[1,128,32,128]{3,2,1,0:T(8,128)(2,1)} %param.16, pred[128,32]{1,0:T(8,128)(4,1)S(1)} %iota_compare_fusion), kind=kOutput, calls=%fused_computation.32 | convolution fusion | flops 8485888 | bytes 1449984 | tf_op jit(solution)/shard_map/rhd,rpd->rhp/dot_general | solution.py:22
  11.5 0.1 copy.27
  11.7 0.4 fusion.5
  12.1 0.8 bitcast_convert_fusion
  12.9 0.1 copy.29
  13.0 0.1 copy.32
  13.1 0.5 fusion.2
  13.6 0.7 copy.33
  14.4 0.0 all-gather.2.cloned.1.call-update
  14.4 0.0 reduce-scatter.2.cloned.1.call-start
  14.5 0.1 select_reduce_fusion
  14.5 0.1 copy.35.slot_ref
  14.7 0.0 copy-start.4
  14.7 0.0 copy-start.5
  14.7 0.0 copy-start.6
  14.7 9.2 %convolution_bitcast_fusion.base_ref = f32[128,8192]{1,0:T(8,128)} fusion(bf16[8,128,8192]{2,1,0:T(8,128)(2,1)} %bitcast.66, bf16[8,128,128]{2,0,1:T(8,128)(2,1)S(1)} %fusion.2), kind=kOutput, calls=%fused_computation | convolution fusion | flops 2147483648 | bytes 21233664 | tf_op jit(solution)/shard_map/dot_general | solution.py:123
  23.9 42.6 %all-gather.2.cloned.1.call-done.tiles_ref = bf16[64,128,128]{2,1,0:T(8,128)(2,1)} async-done(((bf16[8,128,128]{2,1,0:T(8,128)(2,1)}), bf16[64,128,128]{2,1,0:T(8,128)(2,1)}) %all-gather.2.cloned.1.call-update) | async-done | bytes 2097168 | tf_op jit(solution)/shard_map/all_gather | solution.py:122
  66.5 0.0 copy-done.4
  66.5 0.0 copy-done.6
  66.5 0.0 copy-start.1
  66.5 2.2 %copy-done.1 = bf16[4,8192,64]{1,2,0:T(8,128)(2,1)S(1)} copy-done((bf16[4,8192,64]{1,2,0:T(8,128)(2,1)S(1)}, bf16[4,8192,64]{1,2,0:T(8,128)(2,1)}, u32[]{:S(2)}) %copy-start.1) | copy-done | bytes 4194328
  68.7 1.6 %copy-done.3 = bf16[64,128,128]{2,1,0:T(8,128)(2,1)S(1)} copy-done((bf16[64,128,128]{2,1,0:T(8,128)(2,1)S(1)}, bf16[64,128,128]{2,1,0:T(8,128)(2,1)}, u32[]{:S(2)}) %copy-start.3) | copy-done | bytes 2097176
  70.3 11.6 %delta.1 = bf16[128,8192]{1,0:T(8,128)(2,1)} custom-call(bf16[64,128,128]{2,1,0:T(8,128)(2,1)S(1)} %copy-done.3, s32[128,1]{1,0:T(8,128)S(1)} %copy.35.slot_ref, bf16[256,8192]{1,0:T(8,128)(2,1)S(1)} %bitcast.64, bf16[256,8192]{1,0:T(8,128)(2,1)} %bitcast.67, f32[128,8192]{1,0:T(8,128)} %convolution_bitcast_fusion.base_ref, ...), custom_call_target="tpu_custom_call" | custom-call | tf_op jit(solution)/shard_map/delta/pallas_call | solution.py:93
  81.9 0.0 reduce-scatter.2.cloned.1.call-update
  81.9 66.7 %reduce-scatter.2.cloned.1.call-done = bf16[128,1024]{1,0:T(8,128)(2,1)} async-done(((bf16[128,8192]{1,0:T(8,128)(2,1)}), bf16[128,1024]{1,0:T(8,128)(2,1)}) %reduce-scatter.2.cloned.1.call-update) | async-done | bytes 262160 | tf_op jit(solution)/shard_map/reduce_scatter | solution.py:142
  (14 shorter events, 0.2 us)
Async XLA Ops:
  6.5 6.6 %copy-start = (bf16[1,128,32,128]{3,2,1,0:T(8,128)(2,1)S(1)}, bf16[1,128,32,128]{3,2,1,0:T(8,128)(2,1)}, u32[]{:S(2)}) copy-start(bf16[1,128,32,128]{3,2,1,0:T(8,128)(2,1)} %param.17) | copy-start | bytes 3145732
  6.5 60.0 %all-gather.2.cloned.1.call-start = ((), (), s32[]{:S(2)}) async-start(), calls=%async_computation.1 | async-start | bytes 2359296 | tf_op jit(solution)/shard_map/all_gather | solution.py:122
  8.4 6.1 %copy-start.7 = (s32[32]{0:T(128)S(1)}, s32[32]{0:T(128)}, u32[]{:S(2)}) copy-start(s32[32]{0:T(128)} %param.22) | copy-start | bytes 388
  8.4 6.1 %copy-start.8 = (s32[128]{0:T(128)S(1)}, s32[128]{0:T(128)}, u32[]{:S(2)}) copy-start(s32[128]{0:T(128)} %param.21) | copy-start | bytes 1540
  14.4 134.2 %reduce-scatter.2.cloned.1.call-start = ((), (), s32[]{:S(2)}) async-start(), calls=%async_computation.2 | async-start | bytes 2359296 | tf_op jit(solution)/shard_map/reduce_scatter | solution.py:142
  14.7 51.9 %copy-start.2 = (bf16[4,16,128,128]{3,2,1,0:T(8,128)(2,1)S(1)}, bf16[4,16,128,128]{3,2,1,0:T(8,128)(2,1)}, u32[]{:S(2)}) copy-start(bf16[4,16,128,128]{3,2,1,0:T(8,128)(2,1)} %values_ref.1) | copy-start | bytes 6291460
  14.7 51.9 %copy-start.4 = (f32[4,16]{1,0:T(4,128)S(1)}, f32[4,16]{1,0:T(4,128)}, u32[]{:S(2)}) copy-start(f32[4,16]{1,0:T(4,128)} %scale_ref.1) | copy-start | bytes 772
  14.7 51.8 %copy-start.5 = (s32[4,16,1]{1,2,0:T(1,128)S(1)}, s32[4,16,1]{1,2,0:T(1,128)}, u32[]{:S(2)}) copy-start(s32[4,16,1]{1,2,0:T(1,128)} %param.28) | copy-start | bytes 772
  14.7 51.8 %copy-start.6 = (s32[4,16]{1,0:T(4,128)S(1)}, s32[4,16]{1,0:T(4,128)}, u32[]{:S(2)}) copy-start(s32[4,16]{1,0:T(4,128)} %cell_ref.1) | copy-start | bytes 772
  66.5 2.2 %copy-start.1 = (bf16[4,8192,64]{1,2,0:T(8,128)(2,1)S(1)}, bf16[4,8192,64]{1,2,0:T(8,128)(2,1)}, u32[]{:S(2)}) copy-start(bf16[4,8192,64]{1,2,0:T(8,128)(2,1)} %param.24) | copy-start | bytes 12582916
  68.7 1.6 %copy-start.3 = (bf16[64,128,128]{2,1,0:T(8,128)(2,1)S(1)}, bf16[64,128,128]{2,1,0:T(8,128)(2,1)}, u32[]{:S(2)}) copy-start(bf16[64,128,128]{2,1,0:T(8,128)(2,1)} %all-gather.2.cloned.1.call-done.tiles_ref) | copy-start | bytes 6291460
Sparse Core Ops, SparseCore 0:
  14.5 51.9 all-gather.1
  82.0 66.5 reduce-scatter.1

commit v2 on v1

--- a/solution.py
+++ b/solution.py
@@ -39,72 +39,153 @@
     return jnp.transpose(attended.astype(BF16), (1, 0, 2))
 
 
-def delta_kernel(
-    per_owner, tiles_ref, slot_ref, factor_ref, second_ref, base_ref, values_ref,
-    scale_ref, owner_ref, cell_ref, out_ref, total,
-):
-    tiles, rows, side = tiles_ref.shape
+def ring_order(count):
+    if count == 8:
+        return [0, 2, 4, 6, 7, 5, 3, 1]
+    return list(range(count))
+
+
+def gather_ring(first, second, to_left, to_right, count):
+    got = [[None, None] for _ in range(count)]
+    got[0] = [first, second]
+    half = count // 2
+    right, left = [first, second], [first, second]
+    for step in range(1, half + 1):
+        for part in (0, 1):
+            if step < half or part == 0:
+                right[part] = lax.ppermute(right[part], "tp", to_left)
+                got[step][part] = right[part]
+            if step < half or part == 1:
+                left[part] = lax.ppermute(left[part], "tp", to_right)
+                got[count - step][part] = left[part]
+    return got
+
+
+def scatter_ring(parts, to_left, to_right, count):
+    half = count // 2
+    sums = [None, None]
+    for part in (0, 1):
+        reach_left, reach_right = (half, half - 1) if part == 0 else (half - 1, half)
+        left = right = None
+        for distance in range(reach_left, 0, -1):
+            mine = parts[count - distance][part]
+            left = mine if left is None else (mine.astype(F32) + left.astype(F32)).astype(BF16)
+            left = lax.ppermute(left, "tp", to_left)
+        for distance in range(reach_right, 0, -1):
+            mine = parts[distance][part]
+            right = mine if right is None else (mine.astype(F32) + right.astype(F32)).astype(BF16)
+            right = lax.ppermute(right, "tp", to_right)
+        sums[part] = parts[0][part] + left.astype(F32) + right.astype(F32)
+    return jnp.concatenate(sums, axis=0).astype(BF16)
+
+
+def delta_kernel(count, *refs):
+    chunk_refs, refs = refs[: 2 * count], refs[2 * count :]
+    slot_ref, factor_ref, second_ref, base_ref, values_ref = refs[:5]
+    scale_ref, owner_ref, cell_ref, order_ref, place_ref = refs[5:10]
+    out_refs, (tiles, total) = refs[10:-2], refs[-2:]
+    half, rows, side = chunk_refs[0].shape
+    heads = 2 * half
+    width = heads * side
     slots, block_count = values_ref.shape[:2]
     rank = factor_ref.shape[0] // slots
     low = jnp.zeros((rows, slots * rank), F32)
-    for t in range(0, tiles, 2):
-        pair = jnp.concatenate([tiles_ref[t], tiles_ref[t + 1]], axis=1)
-        low = low + lax.dot_general(
-            pair,
-            factor_ref[:, t * side : (t + 2) * side],
-            (((1,), (1,)), ((), ())),
-            preferred_element_type=F32,
-        )
+    for k in range(count):
+        for i in range(0, heads, 2):
+            one = chunk_refs[2 * k + i // half][i % half]
+            two = chunk_refs[2 * k + (i + 1) // half][(i + 1) % half]
+            tiles[k * heads + i] = one
+            tiles[k * heads + i + 1] = two
+            start = pl.multiple_of(order_ref[k] * width + i * side, 2 * side)
+            low = low + lax.dot_general(
+                jnp.concatenate([one, two], axis=1),
+                factor_ref[:, pl.ds(start, 2 * side)],
+                (((1,), (1,)), ((), ())),
+                preferred_element_type=F32,
+            )
     slot_row = slot_ref[...]
     held = lax.broadcasted_iota(jnp.int32, (rows, slots * rank), 1) // rank
     low = jnp.where(slot_row == held, low, 0.0).astype(BF16)
-    for c in range(0, tiles, 2):
-        part = base_ref[:, c * side : (c + 2) * side] + jnp.dot(
-            low, second_ref[:, c * side : (c + 2) * side], preferred_element_type=F32
-        )
-        total[c] = part[:, :side]
-        total[c + 1] = part[:, side:]
+    for k in range(count):
+        for i in range(0, heads, 2):
+            start = pl.multiple_of(order_ref[k] * width + i * side, 2 * side)
+            part = base_ref[:, pl.ds(start, 2 * side)] + jnp.dot(
+                low, second_ref[:, pl.ds(start, 2 * side)], preferred_element_type=F32
+            )
+            total[k * heads + i] = part[:, :side]
+            total[k * heads + i + 1] = part[:, side:]
     group = 4
     for j in range(slots):
         mine = jnp.broadcast_to(slot_row == j, (rows, side))
 
         def step(i, carry, j=j, mine=mine):
             added = []
-            for k in range(group):
-                b = i * group + k
+            for g in range(group):
+                b = i * group + g
                 cell = cell_ref[j, b]
-                row_block = owner_ref[j, b] * per_owner + lax.div(cell, tiles)
+                row_cell, column = lax.div(cell, count * heads), lax.rem(cell, count * heads)
+                source = place_ref[owner_ref[j, b]] * heads + row_cell
+                target = place_ref[lax.div(column, heads)] * heads + lax.rem(column, heads)
                 rebuilt = (values_ref[j, b].astype(F32) * scale_ref[j, b]).astype(BF16)
-                product = jnp.dot(tiles_ref[row_block], rebuilt, preferred_element_type=F32)
-                added.append((lax.rem(cell, tiles), jnp.where(mine, product, 0.0)))
-            for column, product in added:
-                total[column] += product
+                product = jnp.dot(tiles[source], rebuilt, preferred_element_type=F32)
+                added.append((target, jnp.where(mine, product, 0.0)))
+            for target, product in added:
+                total[target] += product
             return carry
 
         lax.fori_loop(0, block_count // group, step, 0)
-    for c in range(tiles):
-        out_ref[:, c * side : (c + 1) * side] = total[c].astype(BF16)
-
-
-def add_delta(tiles, slot_local, factor_t, second, base, block_values, scale, owner, cell, per_owner):
-    count, rows, side = tiles.shape
+    for i in range(heads):
+        out_refs[0][:, i * side : (i + 1) * side] = total[i]
+    for k in range(1, count):
+        for part in (0, 1):
+            out = out_refs[2 * k - 1 + part]
+            for i in range(heads):
+                out[:, i * side : (i + 1) * side] = total[
+                    k * heads + i, part * (rows // 2) : (part + 1) * (rows // 2)
+                ].astype(BF16)
+
+
+def add_delta(chunks, slot_local, factor_t, second, base, block_values, scale, owner, cell, order, place):
+    count = len(chunks)
+    half, rows, side = chunks[0][0].shape
+    heads = 2 * half
+    width = heads * side
     vmem = pl.BlockSpec(memory_space=pltpu.VMEM)
     smem = pl.BlockSpec(memory_space=pltpu.SMEM)
-    return pl.pallas_call(
-        functools.partial(delta_kernel, per_owner),
-        out_shape=jax.ShapeDtypeStruct((rows, count * side), BF16),
-        in_specs=[vmem] * 6 + [smem] * 3,
-        out_specs=vmem,
-        scratch_shapes=[pltpu.VMEM((count, rows, side), F32)],
+    outs = [jax.ShapeDtypeStruct((rows, width), F32)]
+    outs += [jax.ShapeDtypeStruct((rows // 2, width), BF16)] * (2 * (count - 1))
+    got = pl.pallas_call(
+        functools.partial(delta_kernel, count),
+        out_shape=outs,
+        in_specs=[vmem] * (2 * count + 5) + [smem] * 5,
+        out_specs=[vmem] * len(outs),
+        scratch_shapes=[
+            pltpu.VMEM((count * heads, rows, side), BF16),
+            pltpu.VMEM((count * heads, rows, side), F32),
+        ],
         compiler_params=pltpu.CompilerParams(vmem_limit_bytes=40 * 1024 * 1024),
         name="delta",
-    )(tiles, slot_local, factor_t, second, base, block_values, scale, owner, cell)
+    )(
+        *[part for chunk in chunks for part in chunk],
+        slot_local, factor_t, second, base, block_values, scale, owner, cell, order, place,
+    )
+    own = [got[0][: rows // 2], got[0][rows // 2 :]]
+    return [own] + [[got[2 * k - 1], got[2 * k]] for k in range(1, count)]
 
 
 def body(
     queries, key_cache, value_cache, new_keys, new_values, lengths, request_variant, holder_slot,
     out_weight, factor_in, second_factor, block_values, block_scale, block_owner, block_cell,
 ):
+    count = lax.axis_size("tp")
+    ring = ring_order(count)
+    to_right = [(ring[i], ring[(i + 1) % count]) for i in range(count)]
+    to_left = [(ring[(i + 1) % count], ring[i]) for i in range(count)]
+    spots = jnp.asarray([ring.index(i) for i in range(count)], jnp.int32)
+    spot = spots[lax.axis_index("tp")]
+    order = jnp.asarray(ring, jnp.int32)[(spot + jnp.arange(count, dtype=jnp.int32)) % count]
+    place = (spots - spot) % count
+
     attended = attend_local(queries, key_cache, value_cache, new_keys, new_values, lengths)
     heads, rows, side = attended.shape
     variants = holder_slot.shape[0]
@@ -119,7 +200,7 @@
         axis=1,
     )
     slot_local = (slot_row - lax.axis_index("tp") * slots_here)[:, None]
-    tiles = lax.all_gather(attended, "tp", axis=0, tiled=True)
+    chunks = gather_ring(attended[: heads // 2], attended[heads // 2 :], to_left, to_right, count)
     base = lax.dot_general(
         attended,
         out_weight.reshape(heads, side, width),
@@ -127,8 +208,8 @@
         preferred_element_type=F32,
     )
     factor_t = jnp.swapaxes(factor_in, 1, 2).reshape(-1, factor_in.shape[1])
-    partial = add_delta(
-        tiles,
+    parts = add_delta(
+        chunks,
         slot_local,
         factor_t,
         second_factor.reshape(-1, width),
@@ -137,9 +218,10 @@
         block_scale,
         block_owner[:, :, 0],
         block_cell,
-        heads,
-    )
-    return lax.psum_scatter(partial, "tp", scatter_dimension=1, tiled=True)
+        order,
+        place,
+    )
+    return scatter_ring(parts, to_left, to_right, count)
 
 
 def solution(mesh):

time: 156 us -> 85 us (0.54)
  waiting for transfers between devices: 109 us -> 15.1 us
  starting transfers between devices: 0.04 us -> 31.6 us
  between operations: 13.5 us -> 0.23 us
  other arithmetic: 2.12 us -> 6.53 us
  local copies, waits for them, and re-layouts: 6.13 us -> 7.75 us
    reduce_scatter x1 -> x0, waiting for transfers between devices: 66.7 us -> none  [body(): return lax.psum_scatter(partial, 'tp', scatter_dimension=1, tiled=True)]
    all_gather x1 -> x0, waiting for transfers between devices: 42.6 us -> none  [body(): tiles = lax.all_gather(attended, 'tp', axis=0, tiled=True)]
    ppermute x0 -> x28, starting transfers between devices: none -> 31.6 us  [the longest x7 11.4 us: gather_ring(): left[part] = lax.ppermute(left[part], 'tp', to_right)]
    ppermute x0 -> x28, waiting for transfers between devices: none -> 15.1 us  [the longest x7 7.24 us: scatter_ring(): right = lax.ppermute(right, 'tp', to_right)]
    select_n x0 -> x2, other arithmetic: none -> 1.82 us  [the longest x1 1.24 us: body(): place = (spots - spot) % count]
  transfers between devices with their start and end apart: 2 -> 28, of which waited for: 2 -> 13; matrix products, arithmetic and copies ran while one was open for 6% -> 18% of each run, Pallas kernels for 0% -> 0%
where the time goes in v2:
time: 85 us; the launch traced here: 84.6 us
  starting transfers between devices  31.6 us (37%)
  waiting for transfers between devices  15.1 us (18%)
  matrix products  12.8 us (15%)
  Pallas kernels  10.6 us (12%)
  local copies, waits for them, and re-layouts  7.75 us (9%)
  other arithmetic  6.53 us (8%)
    ppermute x7, starting transfers between devices, gather_ring(): left[part] = lax.ppermute(left[part], 'tp', to_right)  11.4 us
    pallas_call x1, Pallas kernels, add_delta(): pl.pallas_call(functools.partial(delta_kernel, count), out_shape=outs, in...  10.6 us
    ppermute x7, starting transfers between devices, scatter_ring(): left = lax.ppermute(left, 'tp', to_left)  9.35 us
    dot_general x1, matrix products, body(): lax.dot_general(attended, out_weight.reshape(heads, side, width), (((0, 2...  9.29 us
    ppermute x7, waiting for transfers between devices, scatter_ring(): right = lax.ppermute(right, 'tp', to_right)  7.24 us
    ppermute x7, starting transfers between devices, gather_ring(): right[part] = lax.ppermute(right[part], 'tp', to_left)  5.54 us
    ppermute x7, starting transfers between devices, scatter_ring(): right = lax.ppermute(right, 'tp', to_right)  5.29 us
    unnamed x19, local copies, waits for them, and re-layouts  4.76 us
  transfers between devices with their start and end apart: 28, of which 13 were waited for; matrix products, arithmetic and copies ran while one was open for 18% of the time, Pallas kernels for 0%

profile of v2, /device:TPU:0, one launch (start us, length us, event | category | flops | bytes accessed | tf_op | source)
XLA Modules:
  0.0 84.6 jit_solution(10551890666156387757)
XLA Ops:
  0.8 1.0 %copy.42 = bf16[16,8,8,128]{3,2,1,0:T(8,128)(2,1)S(1)} copy(bf16[16,8,8,128]{3,1,2,0:T(8,128)(2,1)} %bitcast.72) | data formatting | bytes 524288
  1.8 1.0 %fusion.10 = f32[128,1,8]{2,1,0:T(1,128)S(1)} fusion(bf16[128,8,128]{2,1,0:T(8,128)(2,1)S(1)} %bitcast.70, bf16[128,128,1]{1,0,2:T(8,128)(2,1)} %bitcast.73), kind=kOutput, calls=%fused_computation.30 | convolution fusion | flops 262144 | bytes 299008 | tf_op jit(solution)/shard_map/rhd,rd->rh/dot_general | solution.py:25
  2.9 2.0 %fusion.21 = (f32[128,8]{1,0:T(8,128)S(1)}, f32[128,8,32]{2,1,0:T(8,128)S(1)}) fusion(bf16[128,8,128]{2,1,0:T(8,128)(2,1)S(1)} %bitcast.71, bf16[1,128,32,128]{3,2,1,0:T(8,128)(2,1)} %param.18, pred[128,32]{1,0:T(8,128)(4,1)S(1)} %iota_compare_fusion), kind=kOutput, calls=%fused_computation.57 | convolution fusion | flops 8485888 | bytes 1449984 | tf_op jit(solution)/shard_map/rhd,rpd->rhp/dot_general | solution.py:22
  7.2 3.1 %collective-permute-start.7 = (bf16[4,128,128]{2,1,0:T(8,128)(2,1)S(1)}, bf16[4,128,128]{2,1,0:T(8,128)(2,1)S(1)}, u32[]{:S(2)}, u32[]{:S(2)}) collective-permute-start(bf16[4,128,128]{2,1,0:T(8,128)(2,1)S(1)} %get-tuple-element.37.refs_1_), channel_id=1, source_target_pairs={{0,4},{4,8},{8,12},{12,14},{14,10},{10,6},{6,2},{2,0},{1,5},{5,9},... | collective-permute-start | bytes 393224 | tf_op jit(solution)/shard_map/ppermute | solution.py:59
  10.3 2.0 %collective-permute-start.11 = (bf16[4,128,128]{2,1,0:T(8,128)(2,1)S(1)}, bf16[4,128,128]{2,1,0:T(8,128)(2,1)}, u32[]{:S(2)}, u32[]{:S(2)}) collective-permute-start(bf16[4,128,128]{2,1,0:T(8,128)(2,1)S(1)} %get-tuple-element.38.refs_0_), channel_id=1, source_target_pairs={{0,4},{4,8},{8,12},{12,14},{14,10},{10,6},{6,2},{2,0},{1,5},{5,9},... | collective-permute-start | bytes 393224 | tf_op jit(solution)/shard_map/ppermute | solution.py:59
  12.3 9.3 %convolution_bitcast_fusion.refs_19_ = f32[128,8192]{1,0:T(8,128)} fusion(bf16[8,128,128]{2,1,0:T(8,128)(2,1)S(1)} %fusion.4, bf16[8,128,8192]{2,1,0:T(8,128)(2,1)} %bitcast.68), kind=kOutput, calls=%fused_computation.1 | convolution fusion | flops 2147483648 | bytes 21233664 | tf_op jit(solution)/shard_map/dot_general | solution.py:204
  21.6 1.2 %dynamic_slice.3 = s32[1]{0:T(128)} dynamic-slice(s32[8]{0:T(128)} %constant.44.clone, s32[]{:T(128)S(6)} %select_n.45), dynamic_slice_sizes={1} | dynamic-slice | bytes 12 | tf_op jit(solution)/shard_map/dynamic_slice | solution.py:185
  23.6 2.1 %collective-permute-start.8 = (bf16[4,128,128]{2,1,0:T(8,128)(2,1)S(1)}, bf16[4,128,128]{2,1,0:T(8,128)(2,1)}, u32[]{:S(2)}, u32[]{:S(2)}) collective-permute-start(bf16[4,128,128]{2,1,0:T(8,128)(2,1)S(1)} %collective-permute-done.7.refs_15_), channel_id=1, source_target_pairs={{0,4},{4,8},{8,12},{12,14},{14,10},{10,6},{6,2},{2,0},{1,5},{5,9},... | collective-permute-start | bytes 393224 | tf_op jit(solution)/shard_map/ppermute | solution.py:59
  26.9 2.0 %collective-permute-start.3 = (bf16[4,128,128]{2,1,0:T(8,128)(2,1)}, bf16[4,128,128]{2,1,0:T(8,128)(2,1)}, u32[]{:S(2)}, u32[]{:S(2)}) collective-permute-start(bf16[4,128,128]{2,1,0:T(8,128)(2,1)} %collective-permute-done.1.refs_3_), channel_id=1, source_target_pairs={{4,0},{8,4},{12,8},{14,12},{10,14},{6,10},{2,6},{0,2},{5,1},{9,5},... | collective-permute-start | bytes 393224 | tf_op jit(solution)/shard_map/ppermute | solution.py:56
  28.9 2.6 %collective-permute-start.9 = (bf16[4,128,128]{2,1,0:T(8,128)(2,1)}, bf16[4,128,128]{2,1,0:T(8,128)(2,1)}, u32[]{:S(2)}, u32[]{:S(2)}) collective-permute-start(bf16[4,128,128]{2,1,0:T(8,128)(2,1)} %collective-permute-done.8.refs_13_), channel_id=1, source_target_pairs={{0,4},{4,8},{8,12},{12,14},{14,10},{10,6},{6,2},{2,0},{1,5},{5,9},... | collective-permute-start | bytes 393224 | tf_op jit(solution)/shard_map/ppermute | solution.py:59
  31.9 1.0 %collective-permute-start.4 = (bf16[4,128,128]{2,1,0:T(8,128)(2,1)}, bf16[4,128,128]{2,1,0:T(8,128)(2,1)}, u32[]{:S(2)}, u32[]{:S(2)}) collective-permute-start(bf16[4,128,128]{2,1,0:T(8,128)(2,1)} %collective-permute-done.2.refs_4_), channel_id=1, source_target_pairs={{4,0},{8,4},{12,8},{14,12},{10,14},{6,10},{2,6},{0,2},{5,1},{9,5},... | collective-permute-start | bytes 393224 | tf_op jit(solution)/shard_map/ppermute | solution.py:56
  34.9 1.5 %collective-permute-start.5 = (bf16[4,128,128]{2,1,0:T(8,128)(2,1)}, bf16[4,128,128]{2,1,0:T(8,128)(2,1)S(1)}, u32[]{:S(2)}, u32[]{:S(2)}) collective-permute-start(bf16[4,128,128]{2,1,0:T(8,128)(2,1)} %collective-permute-done.3.refs_5_), channel_id=1, source_target_pairs={{4,0},{8,4},{12,8},{14,12},{10,14},{6,10},{2,6},{0,2},{5,1},{9,5},... | collective-permute-start | bytes 393224 | tf_op jit(solution)/shard_map/ppermute | solution.py:56
  37.0 1.0 %collective-permute-start.10 = (bf16[4,128,128]{2,1,0:T(8,128)(2,1)}, bf16[4,128,128]{2,1,0:T(8,128)(2,1)S(1)}, u32[]{:S(2)}, u32[]{:S(2)}) collective-permute-start(bf16[4,128,128]{2,1,0:T(8,128)(2,1)} %collective-permute-done.9.refs_11_), channel_id=1, source_target_pairs={{0,4},{4,8},{8,12},{12,14},{14,10},{10,6},{6,2},{2,0},{1,5},{5,9},... | collective-permute-start | bytes 393224 | tf_op jit(solution)/shard_map/ppermute | solution.py:59
  38.0 1.0 %collective-permute-start.6 = (bf16[4,128,128]{2,1,0:T(8,128)(2,1)}, bf16[4,128,128]{2,1,0:T(8,128)(2,1)S(1)}, u32[]{:S(2)}, u32[]{:S(2)}) collective-permute-start(bf16[4,128,128]{2,1,0:T(8,128)(2,1)} %collective-permute-done.4.refs_6_), channel_id=1, source_target_pairs={{4,0},{8,4},{12,8},{14,12},{10,14},{6,10},{2,6},{0,2},{5,1},{9,5},... | collective-permute-start | bytes 393224 | tf_op jit(solution)/shard_map/ppermute | solution.py:56
  39.0 1.2 %and_select_fusion.refs_25_ = s32[8]{0:T(128)S(1)} fusion(s32[8]{0:T(128)} %constant.44.clone, s32[]{:T(128)} %bitcast.17), kind=kLoop, calls=%fused_computation.49 | loop fusion | flops 96 | bytes 68 | tf_op jit(solution)/shard_map/jit(remainder)/select_n | solution.py:187
  40.4 1.2 %collective-permute-done.13.refs_10_ = bf16[4,128,128]{2,1,0:T(8,128)(2,1)S(1)} collective-permute-done((bf16[4,128,128]{2,1,0:T(8,128)(2,1)}, bf16[4,128,128]{2,1,0:T(8,128)(2,1)S(1)}, u32[]{:S(2)}, u32[]{:S(2)}) %collective-permute-start.13) | collective-permute-done | bytes 131104 | tf_op jit(solution)/shard_map/ppermute | solution.py:59
  41.6 1.4 %collective-permute-done.10.refs_9_ = bf16[4,128,128]{2,1,0:T(8,128)(2,1)S(1)} collective-permute-done((bf16[4,128,128]{2,1,0:T(8,128)(2,1)}, bf16[4,128,128]{2,1,0:T(8,128)(2,1)S(1)}, u32[]{:S(2)}, u32[]{:S(2)}) %collective-permute-start.10) | collective-permute-done | bytes 131104 | tf_op jit(solution)/shard_map/ppermute | solution.py:59
  43.2 2.2 %copy-done.1 = bf16[4,8192,64]{1,2,0:T(8,128)(2,1)S(1)} copy-done((bf16[4,8192,64]{1,2,0:T(8,128)(2,1)S(1)}, bf16[4,8192,64]{1,2,0:T(8,128)(2,1)}, u32[]{:S(2)}) %copy-start.1) | copy-done | bytes 4194328
  46.3 10.6 %delta.1 = (f32[128,1024]{1,0:T(8,128)S(1)}, bf16[64,1024]{1,0:T(8,128)(2,1)S(1)}, bf16[64,1024]{1,0:T(8,128)(2,1)S(1)}, bf16[64,1024]{1,0:T(8,128)(2,1)S(1)}, b...) custom-call(bf16[4,128,128]{2,1,0:T(8,128)(2,1)S(1)} %get-tuple-elem, ...), custom_call_target="tpu_custom_call" | custom-call | tf_op jit(solution)/shard_map/delta/pallas_call | solution.py:157
  56.9 1.5 %collective-permute-start.14 = (bf16[64,1024]{1,0:T(8,128)(2,1)S(1)}, bf16[64,1024]{1,0:T(8,128)(2,1)S(1)}, u32[]{:S(2)}, u32[]{:S(2)}) collective-permute-start(bf16[64,1024]{1,0:T(8,128)(2,1)S(1)} %get-tuple-element.24), channel_id=1, source_target_pairs={{4,0},{8,4},{12,8},{14,12},{10,14},{6,10},{2,6},{0,2},{5,1},{9,5},... | collective-permute-start | bytes 393224 | tf_op jit(solution)/shard_map/ppermute | solution.py:73
  59.0 1.4 %collective-permute-start.21 = (bf16[64,1024]{1,0:T(8,128)(2,1)S(1)}, bf16[64,1024]{1,0:T(8,128)(2,1)S(1)}, u32[]{:S(2)}, u32[]{:S(2)}) collective-permute-start(bf16[64,1024]{1,0:T(8,128)(2,1)S(1)} %get-tuple-element.30), channel_id=1, source_target_pairs={{4,0},{8,4},{12,8},{14,12},{10,14},{6,10},{2,6},{0,2},{5,1},{9,5},... | collective-permute-start | bytes 393224 | tf_op jit(solution)/shard_map/ppermute | solution.py:73
  61.0 2.3 %collective-permute-done.14 = bf16[64,1024]{1,0:T(8,128)(2,1)S(1)} collective-permute-done((bf16[64,1024]{1,0:T(8,128)(2,1)S(1)}, bf16[64,1024]{1,0:T(8,128)(2,1)S(1)}, u32[]{:S(2)}, u32[]{:S(2)}) %collective-permute-start.14) | collective-permute-done | bytes 131104 | tf_op jit(solution)/shard_map/ppermute | solution.py:73
  63.4 1.2 %collective-permute-start.15 = (bf16[64,1024]{1,0:T(8,128)(2,1)S(1)}, bf16[64,1024]{1,0:T(8,128)(2,1)S(1)}, u32[]{:S(2)}, u32[]{:S(2)}) collective-permute-start(bf16[64,1024]{1,0:T(8,128)(2,1)S(1)} %add_convert_fusion.11), channel_id=1, source_target_pairs={{4,0},{8,4},{12,8},{14,12},{10,14},{6,10},{2,6},{0,2},{5,1},{9,5},... | collective-permute-start | bytes 393224 | tf_op jit(solution)/shard_map/ppermute | solution.py:73
  67.0 1.2 %collective-permute-start.25 = (bf16[64,1024]{1,0:T(8,128)(2,1)S(1)}, bf16[64,1024]{1,0:T(8,128)(2,1)S(1)}, u32[]{:S(2)}, u32[]{:S(2)}) collective-permute-start(bf16[64,1024]{1,0:T(8,128)(2,1)S(1)} %add_convert_fusion.3), channel_id=1, source_target_pairs={{0,4},{4,8},{8,12},{12,14},{14,10},{10,6},{6,2},{2,0},{1,5},{5,9},... | collective-permute-start | bytes 393224 | tf_op jit(solution)/shard_map/ppermute | solution.py:77
  68.8 2.0 %collective-permute-start.16 = (bf16[64,1024]{1,0:T(8,128)(2,1)S(1)}, bf16[64,1024]{1,0:T(8,128)(2,1)S(1)}, u32[]{:S(2)}, u32[]{:S(2)}) collective-permute-start(bf16[64,1024]{1,0:T(8,128)(2,1)S(1)} %add_convert_fusion.10), channel_id=1, source_target_pairs={{4,0},{8,4},{12,8},{14,12},{10,14},{6,10},{2,6},{0,2},{5,1},{9,5},... | collective-permute-start | bytes 393224 | tf_op jit(solution)/shard_map/ppermute | solution.py:73
  71.2 1.2 %collective-permute-done.22 = bf16[64,1024]{1,0:T(8,128)(2,1)S(1)} collective-permute-done((bf16[64,1024]{1,0:T(8,128)(2,1)S(1)}, bf16[64,1024]{1,0:T(8,128)(2,1)S(1)}, u32[]{:S(2)}, u32[]{:S(2)}) %collective-permute-start.22) | collective-permute-done | bytes 131104 | tf_op jit(solution)/shard_map/ppermute | solution.py:73
  72.5 1.1 %collective-permute-start.23 = (bf16[64,1024]{1,0:T(8,128)(2,1)S(1)}, bf16[64,1024]{1,0:T(8,128)(2,1)S(1)}, u32[]{:S(2)}, u32[]{:S(2)}) collective-permute-start(bf16[64,1024]{1,0:T(8,128)(2,1)S(1)} %add_convert_fusion.4), channel_id=1, source_target_pairs={{4,0},{8,4},{12,8},{14,12},{10,14},{6,10},{2,6},{0,2},{5,1},{9,5},... | collective-permute-start | bytes 393224 | tf_op jit(solution)/shard_map/ppermute | solution.py:73
  73.7 1.0 %collective-permute-start.26 = (bf16[64,1024]{1,0:T(8,128)(2,1)S(1)}, bf16[64,1024]{1,0:T(8,128)(2,1)S(1)}, u32[]{:S(2)}, u32[]{:S(2)}) collective-permute-start(bf16[64,1024]{1,0:T(8,128)(2,1)S(1)} %add_convert_fusion.2), channel_id=1, source_target_pairs={{0,4},{4,8},{8,12},{12,14},{14,10},{10,6},{6,2},{2,0},{1,5},{5,9},... | collective-permute-start | bytes 393224 | tf_op jit(solution)/shard_map/ppermute | solution.py:77
  74.7 1.2 %collective-permute-start.17 = (bf16[64,1024]{1,0:T(8,128)(2,1)S(1)}, bf16[64,1024]{1,0:T(8,128)(2,1)S(1)}, u32[]{:S(2)}, u32[]{:S(2)}) collective-permute-start(bf16[64,1024]{1,0:T(8,128)(2,1)S(1)} %add_convert_fusion.9), channel_id=1, source_target_pairs={{4,0},{8,4},{12,8},{14,12},{10,14},{6,10},{2,6},{0,2},{5,1},{9,5},... | collective-permute-start | bytes 393224 | tf_op jit(solution)/shard_map/ppermute | solution.py:73
  75.9 2.8 %collective-permute-done.26 = bf16[64,1024]{1,0:T(8,128)(2,1)S(1)} collective-permute-done((bf16[64,1024]{1,0:T(8,128)(2,1)S(1)}, bf16[64,1024]{1,0:T(8,128)(2,1)S(1)}, u32[]{:S(2)}, u32[]{:S(2)}) %collective-permute-start.26) | collective-permute-done | bytes 131104 | tf_op jit(solution)/shard_map/ppermute | solution.py:77
  78.7 1.0 %collective-permute-start.27 = (bf16[64,1024]{1,0:T(8,128)(2,1)S(1)}, bf16[64,1024]{1,0:T(8,128)(2,1)S(1)}, u32[]{:S(2)}, u32[]{:S(2)}) collective-permute-start(bf16[64,1024]{1,0:T(8,128)(2,1)S(1)} %add_convert_fusion.1), channel_id=1, source_target_pairs={{0,4},{4,8},{8,12},{12,14},{14,10},{10,6},{6,2},{2,0},{1,5},{5,9},... | collective-permute-start | bytes 393224 | tf_op jit(solution)/shard_map/ppermute | solution.py:77
  79.7 4.0 %collective-permute-done.27 = bf16[64,1024]{1,0:T(8,128)(2,1)S(1)} collective-permute-done((bf16[64,1024]{1,0:T(8,128)(2,1)S(1)}, bf16[64,1024]{1,0:T(8,128)(2,1)S(1)}, u32[]{:S(2)}, u32[]{:S(2)}) %collective-permute-start.27) | collective-permute-done | bytes 131104 | tf_op jit(solution)/shard_map/ppermute | solution.py:77
  (81 shorter events, 15.0 us)
Async XLA Ops:
  7.2 16.4 %collective-permute-start.7 = (bf16[4,128,128]{2,1,0:T(8,128)(2,1)S(1)}, bf16[4,128,128]{2,1,0:T(8,128)(2,1)S(1)}, u32[]{:S(2)}, u32[]{:S(2)}) collective-permute-start(bf16[4,128,128]{2,1,0:T(8,128)(2,1)S(1)} %get-tuple-element.37.refs_1_), channel_id=1, source_target_pairs={{0,4},{4,8},{8,12},{12,14},{14,10},{10,6},{6,2},{2,0},{1,5},{5,9},... | collective-permute-start | bytes 393224 | tf_op jit(solution)/shard_map/ppermute | solution.py:59
  10.2 16.6 %collective-permute-start.1 = (bf16[4,128,128]{2,1,0:T(8,128)(2,1)S(1)}, bf16[4,128,128]{2,1,0:T(8,128)(2,1)}, u32[]{:S(2)}, u32[]{:S(2)}) collective-permute-start(bf16[4,128,128]{2,1,0:T(8,128)(2,1)S(1)} %get-tuple-element.37.refs_1_), channel_id=1, source_target_pairs={{4,0},{8,4},{12,8},{14,12},{10,14},{6,10},{2,6},{0,2},{5,1},{9,5},... | collective-permute-start | bytes 393224 | tf_op jit(solution)/shard_map/ppermute | solution.py:56
  10.3 18.6 %collective-permute-start.11 = (bf16[4,128,128]{2,1,0:T(8,128)(2,1)S(1)}, bf16[4,128,128]{2,1,0:T(8,128)(2,1)}, u32[]{:S(2)}, u32[]{:S(2)}) collective-permute-start(bf16[4,128,128]{2,1,0:T(8,128)(2,1)S(1)} %get-tuple-element.38.refs_0_), channel_id=1, source_target_pairs={{0,4},{4,8},{8,12},{12,14},{14,10},{10,6},{6,2},{2,0},{1,5},{5,9},... | collective-permute-start | bytes 393224 | tf_op jit(solution)/shard_map/ppermute | solution.py:59
  12.3 14.1 %collective-permute-start = (bf16[4,128,128]{2,1,0:T(8,128)(2,1)S(1)}, bf16[4,128,128]{2,1,0:T(8,128)(2,1)}, u32[]{:S(2)}, u32[]{:S(2)}) collective-permute-start(bf16[4,128,128]{2,1,0:T(8,128)(2,1)S(1)} %get-tuple-element.38.refs_0_), channel_id=1, source_target_pairs={{4,0},{8,4},{12,8},{14,12},{10,14},{6,10},{2,6},{0,2},{5,1},{9,5},... | collective-permute-start | bytes 393224 | tf_op jit(solution)/shard_map/ppermute | solution.py:56
  12.3 30.9 %copy-start.2 = (bf16[4,16,128,128]{3,2,1,0:T(8,128)(2,1)S(1)}, bf16[4,16,128,128]{3,2,1,0:T(8,128)(2,1)}, u32[]{:S(2)}) copy-start(bf16[4,16,128,128]{3,2,1,0:T(8,128)(2,1)} %refs_20_.1) | copy-start | bytes 6291460
  12.3 30.9 %copy-start.5 = (f32[4,16]{1,0:T(4,128)S(1)}, f32[4,16]{1,0:T(4,128)}, u32[]{:S(2)}) copy-start(f32[4,16]{1,0:T(4,128)} %refs_21_.1) | copy-start | bytes 772
  12.3 30.9 %copy-start.6 = (s32[4,16,1]{1,2,0:T(1,128)S(1)}, s32[4,16,1]{1,2,0:T(1,128)}, u32[]{:S(2)}) copy-start(s32[4,16,1]{1,2,0:T(1,128)} %param.30) | copy-start | bytes 772
  12.3 30.9 %copy-start.7 = (s32[4,16]{1,0:T(4,128)S(1)}, s32[4,16]{1,0:T(4,128)}, u32[]{:S(2)}) copy-start(s32[4,16]{1,0:T(4,128)} %refs_23_.1) | copy-start | bytes 772
  23.6 5.3 %collective-permute-start.8 = (bf16[4,128,128]{2,1,0:T(8,128)(2,1)S(1)}, bf16[4,128,128]{2,1,0:T(8,128)(2,1)}, u32[]{:S(2)}, u32[]{:S(2)}) collective-permute-start(bf16[4,128,128]{2,1,0:T(8,128)(2,1)S(1)} %collective-permute-done.7.refs_15_), channel_id=1, source_target_pairs={{0,4},{4,8},{8,12},{12,14},{14,10},{10,6},{6,2},{2,0},{1,5},{5,9},... | collective-permute-start | bytes 393224 | tf_op jit(solution)/shard_map/ppermute | solution.py:59
  26.3 5.6 %collective-permute-start.2 = (bf16[4,128,128]{2,1,0:T(8,128)(2,1)}, bf16[4,128,128]{2,1,0:T(8,128)(2,1)}, u32[]{:S(2)}, u32[]{:S(2)}) collective-permute-start(bf16[4,128,128]{2,1,0:T(8,128)(2,1)} %collective-permute-done.refs_2_), channel_id=1, source_target_pairs={{4,0},{8,4},{12,8},{14,12},{10,14},{6,10},{2,6},{0,2},{5,1},{9,5},... | collective-permute-start | bytes 393224 | tf_op jit(solution)/shard_map/ppermute | solution.py:56
  26.9 8.0 %collective-permute-start.3 = (bf16[4,128,128]{2,1,0:T(8,128)(2,1)}, bf16[4,128,128]{2,1,0:T(8,128)(2,1)}, u32[]{:S(2)}, u32[]{:S(2)}) collective-permute-start(bf16[4,128,128]{2,1,0:T(8,128)(2,1)} %collective-permute-done.1.refs_3_), channel_id=1, source_target_pairs={{4,0},{8,4},{12,8},{14,12},{10,14},{6,10},{2,6},{0,2},{5,1},{9,5},... | collective-permute-start | bytes 393224 | tf_op jit(solution)/shard_map/ppermute | solution.py:56
  28.8 7.6 %collective-permute-start.12 = (bf16[4,128,128]{2,1,0:T(8,128)(2,1)}, bf16[4,128,128]{2,1,0:T(8,128)(2,1)}, u32[]{:S(2)}, u32[]{:S(2)}) collective-permute-start(bf16[4,128,128]{2,1,0:T(8,128)(2,1)} %collective-permute-done.11.refs_14_), channel_id=1, source_target_pairs={{0,4},{4,8},{8,12},{12,14},{14,10},{10,6},{6,2},{2,0},{1,5},{5,9},... | collective-permute-start | bytes 393224 | tf_op jit(solution)/shard_map/ppermute | solution.py:59
  28.9 8.0 %collective-permute-start.9 = (bf16[4,128,128]{2,1,0:T(8,128)(2,1)}, bf16[4,128,128]{2,1,0:T(8,128)(2,1)}, u32[]{:S(2)}, u32[]{:S(2)}) collective-permute-start(bf16[4,128,128]{2,1,0:T(8,128)(2,1)} %collective-permute-done.8.refs_13_), channel_id=1, source_target_pairs={{0,4},{4,8},{8,12},{12,14},{14,10},{10,6},{6,2},{2,0},{1,5},{5,9},... | collective-permute-start | bytes 393224 | tf_op jit(solution)/shard_map/ppermute | solution.py:59
  31.9 6.1 %collective-permute-start.4 = (bf16[4,128,128]{2,1,0:T(8,128)(2,1)}, bf16[4,128,128]{2,1,0:T(8,128)(2,1)}, u32[]{:S(2)}, u32[]{:S(2)}) collective-permute-start(bf16[4,128,128]{2,1,0:T(8,128)(2,1)} %collective-permute-done.2.refs_4_), channel_id=1, source_target_pairs={{4,0},{8,4},{12,8},{14,12},{10,14},{6,10},{2,6},{0,2},{5,1},{9,5},... | collective-permute-start | bytes 393224 | tf_op jit(solution)/shard_map/ppermute | solution.py:56
  34.9 5.5 %collective-permute-start.5 = (bf16[4,128,128]{2,1,0:T(8,128)(2,1)}, bf16[4,128,128]{2,1,0:T(8,128)(2,1)S(1)}, u32[]{:S(2)}, u32[]{:S(2)}) collective-permute-start(bf16[4,128,128]{2,1,0:T(8,128)(2,1)} %collective-permute-done.3.refs_5_), channel_id=1, source_target_pairs={{4,0},{8,4},{12,8},{14,12},{10,14},{6,10},{2,6},{0,2},{5,1},{9,5},... | collective-permute-start | bytes 393224 | tf_op jit(solution)/shard_map/ppermute | solution.py:56
  36.4 5.2 %collective-permute-start.13 = (bf16[4,128,128]{2,1,0:T(8,128)(2,1)}, bf16[4,128,128]{2,1,0:T(8,128)(2,1)S(1)}, u32[]{:S(2)}, u32[]{:S(2)}) collective-permute-start(bf16[4,128,128]{2,1,0:T(8,128)(2,1)} %collective-permute-done.12.refs_12_), channel_id=1, source_target_pairs={{0,4},{4,8},{8,12},{12,14},{14,10},{10,6},{6,2},{2,0},{1,5},{5,9},... | collective-permute-start | bytes 393224 | tf_op jit(solution)/shard_map/ppermute | solution.py:59
  37.0 6.0 %collective-permute-start.10 = (bf16[4,128,128]{2,1,0:T(8,128)(2,1)}, bf16[4,128,128]{2,1,0:T(8,128)(2,1)S(1)}, u32[]{:S(2)}, u32[]{:S(2)}) collective-permute-start(bf16[4,128,128]{2,1,0:T(8,128)(2,1)} %collective-permute-done.9.refs_11_), channel_id=1, source_target_pairs={{0,4},{4,8},{8,12},{12,14},{14,10},{10,6},{6,2},{2,0},{1,5},{5,9},... | collective-permute-start | bytes 393224 | tf_op jit(solution)/shard_map/ppermute | solution.py:59
  38.0 5.2 %collective-permute-start.6 = (bf16[4,128,128]{2,1,0:T(8,128)(2,1)}, bf16[4,128,128]{2,1,0:T(8,128)(2,1)S(1)}, u32[]{:S(2)}, u32[]{:S(2)}) collective-permute-start(bf16[4,128,128]{2,1,0:T(8,128)(2,1)} %collective-permute-done.4.refs_6_), channel_id=1, source_target_pairs={{4,0},{8,4},{12,8},{14,12},{10,14},{6,10},{2,6},{0,2},{5,1},{9,5},... | collective-permute-start | bytes 393224 | tf_op jit(solution)/shard_map/ppermute | solution.py:56
  56.9 6.4 %collective-permute-start.14 = (bf16[64,1024]{1,0:T(8,128)(2,1)S(1)}, bf16[64,1024]{1,0:T(8,128)(2,1)S(1)}, u32[]{:S(2)}, u32[]{:S(2)}) collective-permute-start(bf16[64,1024]{1,0:T(8,128)(2,1)S(1)} %get-tuple-element.24), channel_id=1, source_target_pairs={{4,0},{8,4},{12,8},{14,12},{10,14},{6,10},{2,6},{0,2},{5,1},{9,5},... | collective-permute-start | bytes 393224 | tf_op jit(solution)/shard_map/ppermute | solution.py:73
  58.4 6.3 %collective-permute-start.18 = (bf16[64,1024]{1,0:T(8,128)(2,1)S(1)}, bf16[64,1024]{1,0:T(8,128)(2,1)S(1)}, u32[]{:S(2)}, u32[]{:S(2)}) collective-permute-start(bf16[64,1024]{1,0:T(8,128)(2,1)S(1)} %get-tuple-element.27), channel_id=1, source_target_pairs={{0,4},{4,8},{8,12},{12,14},{14,10},{10,6},{6,2},{2,0},{1,5},{5,9},... | collective-permute-start | bytes 393224 | tf_op jit(solution)/shard_map/ppermute | solution.py:77
  59.0 6.9 %collective-permute-start.21 = (bf16[64,1024]{1,0:T(8,128)(2,1)S(1)}, bf16[64,1024]{1,0:T(8,128)(2,1)S(1)}, u32[]{:S(2)}, u32[]{:S(2)}) collective-permute-start(bf16[64,1024]{1,0:T(8,128)(2,1)S(1)} %get-tuple-element.30), channel_id=1, source_target_pairs={{4,0},{8,4},{12,8},{14,12},{10,14},{6,10},{2,6},{0,2},{5,1},{9,5},... | collective-permute-start | bytes 393224 | tf_op jit(solution)/shard_map/ppermute | solution.py:73
  60.4 6.5 %collective-permute-start.24 = (bf16[64,1024]{1,0:T(8,128)(2,1)S(1)}, bf16[64,1024]{1,0:T(8,128)(2,1)S(1)}, u32[]{:S(2)}, u32[]{:S(2)}) collective-permute-start(bf16[64,1024]{1,0:T(8,128)(2,1)S(1)} %get-tuple-element.34), channel_id=1, source_target_pairs={{0,4},{4,8},{8,12},{12,14},{14,10},{10,6},{6,2},{2,0},{1,5},{5,9},... | collective-permute-start | bytes 393224 | tf_op jit(solution)/shard_map/ppermute | solution.py:77
  63.4 5.4 %collective-permute-start.15 = (bf16[64,1024]{1,0:T(8,128)(2,1)S(1)}, bf16[64,1024]{1,0:T(8,128)(2,1)S(1)}, u32[]{:S(2)}, u32[]{:S(2)}) collective-permute-start(bf16[64,1024]{1,0:T(8,128)(2,1)S(1)} %add_convert_fusion.11), channel_id=1, source_target_pairs={{4,0},{8,4},{12,8},{14,12},{10,14},{6,10},{2,6},{0,2},{5,1},{9,5},... | collective-permute-start | bytes 393224 | tf_op jit(solution)/shard_map/ppermute | solution.py:73
  64.8 6.4 %collective-permute-start.19 = (bf16[64,1024]{1,0:T(8,128)(2,1)S(1)}, bf16[64,1024]{1,0:T(8,128)(2,1)S(1)}, u32[]{:S(2)}, u32[]{:S(2)}) collective-permute-start(bf16[64,1024]{1,0:T(8,128)(2,1)S(1)} %add_convert_fusion.8), channel_id=1, source_target_pairs={{0,4},{4,8},{8,12},{12,14},{14,10},{10,6},{6,2},{2,0},{1,5},{5,9},... | collective-permute-start | bytes 393224 | tf_op jit(solution)/shard_map/ppermute | solution.py:77
  66.0 6.4 %collective-permute-start.22 = (bf16[64,1024]{1,0:T(8,128)(2,1)S(1)}, bf16[64,1024]{1,0:T(8,128)(2,1)S(1)}, u32[]{:S(2)}, u32[]{:S(2)}) collective-permute-start(bf16[64,1024]{1,0:T(8,128)(2,1)S(1)} %add_convert_fusion.5), channel_id=1, source_target_pairs={{4,0},{8,4},{12,8},{14,12},{10,14},{6,10},{2,6},{0,2},{5,1},{9,5},... | collective-permute-start | bytes 393224 | tf_op jit(solution)/shard_map/ppermute | solution.py:73
  67.0 6.6 %collective-permute-start.25 = (bf16[64,1024]{1,0:T(8,128)(2,1)S(1)}, bf16[64,1024]{1,0:T(8,128)(2,1)S(1)}, u32[]{:S(2)}, u32[]{:S(2)}) collective-permute-start(bf16[64,1024]{1,0:T(8,128)(2,1)S(1)} %add_convert_fusion.3), channel_id=1, source_target_pairs={{0,4},{4,8},{8,12},{12,14},{14,10},{10,6},{6,2},{2,0},{1,5},{5,9},... | collective-permute-start | bytes 393224 | tf_op jit(solution)/shard_map/ppermute | solution.py:77
  68.8 5.8 %collective-permute-start.16 = (bf16[64,1024]{1,0:T(8,128)(2,1)S(1)}, bf16[64,1024]{1,0:T(8,128)(2,1)S(1)}, u32[]{:S(2)}, u32[]{:S(2)}) collective-permute-start(bf16[64,1024]{1,0:T(8,128)(2,1)S(1)} %add_convert_fusion.10), channel_id=1, source_target_pairs={{4,0},{8,4},{12,8},{14,12},{10,14},{6,10},{2,6},{0,2},{5,1},{9,5},... | collective-permute-start | bytes 393224 | tf_op jit(solution)/shard_map/ppermute | solution.py:73
  71.2 8.5 %collective-permute-start.20 = (bf16[64,1024]{1,0:T(8,128)(2,1)S(1)}, bf16[64,1024]{1,0:T(8,128)(2,1)S(1)}, u32[]{:S(2)}, u32[]{:S(2)}) collective-permute-start(bf16[64,1024]{1,0:T(8,128)(2,1)S(1)} %add_convert_fusion.7), channel_id=1, source_target_pairs={{0,4},{4,8},{8,12},{12,14},{14,10},{10,6},{6,2},{2,0},{1,5},{5,9},... | collective-permute-start | bytes 393224 | tf_op jit(solution)/shard_map/ppermute | solution.py:77
  72.5 7.2 %collective-permute-start.23 = (bf16[64,1024]{1,0:T(8,128)(2,1)S(1)}, bf16[64,1024]{1,0:T(8,128)(2,1)S(1)}, u32[]{:S(2)}, u32[]{:S(2)}) collective-permute-start(bf16[64,1024]{1,0:T(8,128)(2,1)S(1)} %add_convert_fusion.4), channel_id=1, source_target_pairs={{4,0},{8,4},{12,8},{14,12},{10,14},{6,10},{2,6},{0,2},{5,1},{9,5},... | collective-permute-start | bytes 393224 | tf_op jit(solution)/shard_map/ppermute | solution.py:73
  73.7 5.0 %collective-permute-start.26 = (bf16[64,1024]{1,0:T(8,128)(2,1)S(1)}, bf16[64,1024]{1,0:T(8,128)(2,1)S(1)}, u32[]{:S(2)}, u32[]{:S(2)}) collective-permute-start(bf16[64,1024]{1,0:T(8,128)(2,1)S(1)} %add_convert_fusion.2), channel_id=1, source_target_pairs={{0,4},{4,8},{8,12},{12,14},{14,10},{10,6},{6,2},{2,0},{1,5},{5,9},... | collective-permute-start | bytes 393224 | tf_op jit(solution)/shard_map/ppermute | solution.py:77
  74.7 5.0 %collective-permute-start.17 = (bf16[64,1024]{1,0:T(8,128)(2,1)S(1)}, bf16[64,1024]{1,0:T(8,128)(2,1)S(1)}, u32[]{:S(2)}, u32[]{:S(2)}) collective-permute-start(bf16[64,1024]{1,0:T(8,128)(2,1)S(1)} %add_convert_fusion.9), channel_id=1, source_target_pairs={{4,0},{8,4},{12,8},{14,12},{10,14},{6,10},{2,6},{0,2},{5,1},{9,5},... | collective-permute-start | bytes 393224 | tf_op jit(solution)/shard_map/ppermute | solution.py:73
  78.7 5.0 %collective-permute-start.27 = (bf16[64,1024]{1,0:T(8,128)(2,1)S(1)}, bf16[64,1024]{1,0:T(8,128)(2,1)S(1)}, u32[]{:S(2)}, u32[]{:S(2)}) collective-permute-start(bf16[64,1024]{1,0:T(8,128)(2,1)S(1)} %add_convert_fusion.1), channel_id=1, source_target_pairs={{0,4},{4,8},{8,12},{12,14},{14,10},{10,6},{6,2},{2,0},{1,5},{5,9},... | collective-permute-start | bytes 393224 | tf_op jit(solution)/shard_map/ppermute | solution.py:77
  (5 other events, 32.2 us)

commit v3 on v1

v3 whole, which is shorter than its diff:
```python
import functools
import math

import jax
import jax.numpy as jnp
from jax import lax
from jax.experimental import pallas as pl
from jax.experimental.pallas import tpu as pltpu
from jax.sharding import PartitionSpec as P

BF16 = jnp.bfloat16
F32 = jnp.float32
CAP = 2
ROW_BLOCK = 16
MIB = 1024 * 1024
NT = (((1,), (1,)), ((), ()))
VMEM = pl.BlockSpec(memory_space=pltpu.VMEM)
SMEM = pl.BlockSpec(memory_space=pltpu.SMEM)
ANY = pl.BlockSpec(memory_space=pl.ANY)


def ring_order(count):
    if count == 8:
        return [0, 2, 4, 6, 7, 5, 3, 1]
    return list(range(count))


def owner_at(distance, count):
    me = lax.axis_index("tp")
    if count != 8:
        return lax.rem(me + distance, count)
    spot = jnp.where((me & 1) == 0, me >> 1, count - 1 - (me >> 1))
    spot = lax.rem(spot + distance, count)
    return jnp.where(spot < count // 2, 2 * spot, 2 * (count - 1 - spot) + 1)


def call(kernel, name, outs, ins, specs, out_specs, scratch=(), limit=16, flops=0, moved=0):
    return pl.pallas_call(
        kernel,
        out_shape=outs,
        in_specs=specs,
        out_specs=out_specs,
        scratch_shapes=list(scratch),
        compiler_params=pltpu.CompilerParams(vmem_limit_bytes=limit * MIB),
        cost_estimate=pl.CostEstimate(flops=flops, bytes_accessed=moved, transcendentals=0),
        name=name,
    )(*ins)


def attend_kernel(q_ref, key_ref, value_ref, new_key_ref, new_value_ref, length_ref, out_ref):
    heads, rows, side = out_ref.shape
    cache = key_ref.shape[0] // rows
    tall, wide = heads * ROW_BLOCK, cache * ROW_BLOCK
    scale = 1.0 / math.sqrt(side)
    lengths = jnp.transpose(jnp.broadcast_to(length_ref[...].astype(F32), (rows, rows)))[:, :1]
    row_in = lax.broadcasted_iota(jnp.int32, (tall, wide), 0) % ROW_BLOCK
    place = (lax.broadcasted_iota(jnp.int32, (tall, wide), 1) - cache * row_in).astype(F32)
    place = jnp.where(place < 0, 1e9, place)
    for r in range(0, rows, ROW_BLOCK):
        here = slice(r, r + ROW_BLOCK)
        cached = slice(r * cache, (r + ROW_BLOCK) * cache)
        query = jnp.concatenate(
            [q_ref[here, h * side : (h + 1) * side] for h in range(heads)], axis=0
        )
        new_key = jnp.concatenate([new_key_ref[here].astype(F32)] * heads, axis=0)
        new_value = jnp.concatenate([new_value_ref[here].astype(F32)] * heads, axis=0)
        live = place < jnp.concatenate([lengths[here]] * heads, axis=0)
        scores = lax.dot_general(query, key_ref[cached], NT, preferred_element_type=F32) * scale
        fresh = jnp.sum(query.astype(F32) * new_key, axis=1, keepdims=True) * scale
        scores = jnp.where(live, scores, -1e30)
        top = jnp.maximum(jnp.max(scores, axis=1, keepdims=True), fresh)
        raw = jnp.where(live, jnp.exp(scores - top), 0.0)
        fresh_raw = jnp.exp(fresh - top)
        inverse = 1.0 / (jnp.sum(raw, axis=1, keepdims=True) + fresh_raw)
        weights = (raw * inverse).astype(BF16)
        fresh_weight = (fresh_raw * inverse).astype(BF16).astype(F32)
        attended = jnp.dot(weights, value_ref[cached], preferred_element_type=F32)
        attended = (attended + fresh_weight * new_value).astype(BF16)
        for h in range(heads):
            out_ref[h, here, :] = attended[h * ROW_BLOCK : (h + 1) * ROW_BLOCK]


def dense_kernel(distances, count, first, *refs):
    x_ref, weight_ref = refs[:2]
    if first:
        variant_ref, holder_ref, owner_ref = refs[2:5]
        outs, slot_ref, table_ref = refs[5 : 5 + len(distances)], refs[-4], refs[-3]
    else:
        outs = refs[3 : 3 + len(distances)]
    buffers, sems = refs[-2:]
    heads, rows, side = x_ref.shape
    width = heads * side
    depth = buffers.shape[0]
    cuts = 2 if width >= 512 else 1
    piece = width // cuts

    def fetch(i):
        start = pl.multiple_of(owner_at(distances[i // cuts], count) * width, width) + i % cuts * piece
        return pltpu.make_async_copy(
            weight_ref.at[:, pl.ds(pl.multiple_of(start, piece), piece)],
            buffers.at[i % depth],
            sems.at[i % depth],
        )

    total = len(distances) * cuts
    for i in range(min(depth, total)):
        fetch(i).start()
    if first:
        slots = owner_ref.shape[0]
        variant = variant_ref[...]
        slot_row = jnp.zeros(variant.shape, jnp.int32)
        for v in range(holder_ref.shape[0]):
            slot_row = jnp.where(variant == v, holder_ref[v], slot_row)
        slot_row = (slot_row - lax.axis_index("tp") * slots).astype(F32)
        slot_ref[...] = jnp.transpose(jnp.broadcast_to(slot_row, (rows, rows))).astype(jnp.int32)
        for e in range(table_ref.shape[0]):
            table_ref[e] = -1
        for j in range(slots):

            def note(b, carry, j=j):
                e = (owner_ref[j, b] * slots + j) * CAP
                table_ref[e + jnp.where(table_ref[e] >= 0, 1, 0)] = b
                return carry

            lax.fori_loop(0, owner_ref.shape[1], note, 0)
    x = jnp.concatenate([x_ref[h] for h in range(heads)], axis=1)
    for i in range(total):
        fetch(i).wait()
        outs[i // cuts][:, i % cuts * piece : (i % cuts + 1) * piece] = jnp.dot(
            x, buffers[i % depth], preferred_element_type=F32
        )
        if i + depth < total:
            fetch(i + depth).start()


def held_blocks(distance, count, slots, heads, scale_ref, cell_ref, table_ref):
    tiles = count * heads
    owner = owner_at(distance, count)
    listed = []
    for j in range(slots):
        for c in range(CAP):
            b = table_ref[(owner * slots + j) * CAP + c]
            found = jnp.maximum(b, 0)
            cell = cell_ref[j, found]
            scale = jnp.where(b >= 0, scale_ref[j, found], 0.0)
            listed.append((j, found, scale, lax.div(cell, tiles), lax.rem(cell, tiles)))
    return listed


def fold_chunk(distance, count, chunk_ref, slot, factor_ref, values_ref, scale_ref, cell_ref,
               table_ref, low_ref):
    heads, rows, side = chunk_ref.shape
    width = heads * side
    features = jnp.concatenate([chunk_ref[h] for h in range(heads)], axis=1)
    start = pl.multiple_of(owner_at(distance, count) * width, width)
    low_ref[...] += lax.dot_general(
        features, factor_ref[:, pl.ds(start, width)], NT, preferred_element_type=F32
    )
    added = []
    for j, b, scale, row_block, column in held_blocks(
        distance, count, values_ref.shape[0], heads, scale_ref, cell_ref, table_ref
    ):
        mine = jnp.where(slot == j, 1.0, 0.0)
        product = jnp.dot(chunk_ref[row_block], values_ref[j, b], preferred_element_type=F32)
        added.append((column, product * (mine * scale)))
    return added


def fold_kernel(distances, count, first, *refs):
    chunks, refs = refs[: len(distances)], refs[len(distances) :]
    slot_ref, factor_ref, values_ref, scale_ref, cell_ref, table_ref = refs[:6]
    low_ref, block_ref = refs[-2:]
    if first:
        low_ref[...] = jnp.zeros_like(low_ref)
        block_ref[...] = jnp.zeros_like(block_ref)
    else:
        low_ref[...] = refs[6][...]
        block_ref[...] = refs[7][...]
    slot = slot_ref[...]
    for distance, chunk in zip(distances, chunks):
        for column, product in fold_chunk(distance, count, chunk, slot, factor_ref, values_ref,
                                          scale_ref, cell_ref, table_ref, low_ref):
            block_ref[column] += product


def part_for(distance, count, low, second_ref, dense_ref, block_ref, extra_ref, columns, out_ref):
    rows, width = dense_ref.shape
    side = block_ref.shape[2]
    heads = width // side
    owner = owner_at(distance, count)
    start = pl.multiple_of(owner * width, width)
    blocks = jnp.concatenate([block_ref[owner * heads + i] for i in range(heads)], axis=1)
    out_ref[...] = (
        jnp.dot(low, second_ref[:, pl.ds(start, width)], preferred_element_type=F32)
        + dense_ref[...]
        + blocks
    )
    for e, column in enumerate(columns):

        @pl.when(lax.div(column, heads) == owner)
        def _(e=e, column=column):
            place = pl.ds(pl.multiple_of(lax.rem(column, heads) * side, side), side)
            out_ref[:, place] += extra_ref[e]


def finish_kernel(distances, count, *refs):
    front_ref, back_ref, slot_ref, factor_ref, values_ref, scale_ref, cell_ref, table_ref = refs[:8]
    second_ref, low_in, block_ref = refs[8:11]
    dense_refs = refs[11 : 11 + len(distances)]
    low_out, extra_out, top_out, bottom_out = refs[11 + len(distances) : 15 + len(distances)]
    outs = refs[15 + len(distances) : -3]
    chunk, low_sum, farthest = refs[-3:]
    half, rows, side = front_ref.shape
    chunk[:half] = front_ref[...]
    chunk[half:] = back_ref[...]
    low_sum[...] = low_in[...]
    slot = slot_ref[...]
    added = fold_chunk(distances[0], count, chunk, slot, factor_ref, values_ref, scale_ref, cell_ref,
                       table_ref, low_sum)
    for e, (_, product) in enumerate(added):
        extra_out[e] = product
    columns = [column for column, _ in added]
    low_width = low_sum.shape[1]
    rank = low_width // values_ref.shape[0]
    held = lax.broadcasted_iota(jnp.int32, (rows, low_width), 1) // rank
    slots_wide = jnp.concatenate([slot] * -(-low_width // side), axis=1)[:, :low_width]
    low = jnp.where(slots_wide == held, low_sum[...], 0.0).astype(BF16)
    low_out[...] = low
    for distance, dense_ref, out in zip(distances, dense_refs, (farthest, *outs)):
        part_for(distance, count, low, second_ref, dense_ref, block_ref, extra_out, columns, out)
    top_out[...] = farthest[: rows // 2].astype(BF16)
    bottom_out[...] = farthest[rows // 2 :].astype(BF16)


def part_kernel(distances, count, slots, *refs):
    low_ref, second_ref, block_ref, extra_ref, scale_ref, cell_ref, table_ref = refs[:7]
    dense_refs = refs[7 : 7 + len(distances)]
    outs = refs[7 + len(distances) :]
    heads = dense_refs[0].shape[1] // block_ref.shape[2]
    listed = held_blocks(count // 2, count, slots, heads, scale_ref, cell_ref, table_ref)
    columns = [entry[-1] for entry in listed]
    for distance, dense_ref, out in zip(distances, dense_refs, outs):
        part_for(distance, count, low_ref[...], second_ref, dense_ref, block_ref, extra_ref, columns, out)


def after(value, *others):
    return lax.optimization_barrier((value, *others))[0]


def body(
    queries, key_cache, value_cache, new_keys, new_values, lengths, request_variant, holder_slot,
    out_weight, factor_in, second_factor, block_values, block_scale, block_owner, block_cell,
):
    count = lax.axis_size("tp")
    half = count // 2
    ring = ring_order(count)
    to_right = [(ring[i], ring[(i + 1) % count]) for i in range(count)]
    to_left = [(ring[(i + 1) % count], ring[i]) for i in range(count)]
    rows, width = queries.shape
    side = key_cache.shape[3]
    cache = key_cache.shape[2]
    heads = width // side
    slots = block_values.shape[0]
    complete = out_weight.shape[1]
    low_width = slots * factor_in.shape[2]
    shape = jax.ShapeDtypeStruct

    attended = call(
        attend_kernel,
        "attend",
        shape((heads, rows, side), BF16),
        (queries, key_cache.reshape(-1, side), value_cache.reshape(-1, side), new_keys[0],
         new_values[0], lengths[None, :]),
        [VMEM] * 6,
        VMEM,
    )

    chunks = {0: attended}
    right = left = attended
    for step in range(1, half):
        right = chunks[step] = lax.ppermute(right, "tp", to_left)
        left = chunks[count - step] = lax.ppermute(left, "tp", to_right)
    front = lax.ppermute(right[: heads // 2], "tp", to_left)
    back = lax.ppermute(left[heads // 2 :], "tp", to_right)

    wanted = [half]
    for distance in range(half - 1, 0, -1):
        wanted += [distance, count - distance]
    wanted += [0]
    piece = width // 2 if width >= 512 else width
    streams = [pltpu.VMEM((4, width, piece), BF16), pltpu.SemaphoreType.DMA((4,))]
    dense_cost = dict(flops=rows * width * complete, moved=width * complete)
    dense = {}
    *sums, slot, table = call(
        functools.partial(dense_kernel, wanted[:half], count, True),
        "dense_first",
        [shape((rows, width), F32)] * half
        + [shape((rows, rows), jnp.int32), shape((count * slots * CAP,), jnp.int32)],
        (attended, out_weight, request_variant[None, :], holder_slot, block_owner[:, :, 0]),
        [VMEM, ANY, VMEM, SMEM, SMEM],
        [VMEM] * half + [VMEM, SMEM],
        streams,
        **dense_cost,
    )
    dense.update(zip(wanted[:half], sums))
    sums = call(
        functools.partial(dense_kernel, wanted[half:], count, False),
        "dense_second",
        [shape((rows, width), F32)] * half,
        (attended, out_weight, chunks[1]),
        [VMEM, ANY, ANY],
        [VMEM] * half,
        streams,
        **dense_cost,
    )
    dense.update(zip(wanted[half:], sums))

    factor_t = jnp.swapaxes(factor_in, 1, 2).reshape(low_width, -1)
    second = second_factor.reshape(low_width, complete)
    state = [shape((rows, low_width), F32), shape((complete // side, rows, side), F32)]
    early = [0]
    for distance in range(1, half - 1):
        early += [distance, count - distance]
    late = [half - 1, count - half + 1]
    tables = (slot, factor_t, block_values, block_scale, block_cell, table)
    table_specs = [VMEM, VMEM, VMEM, SMEM, SMEM, SMEM]
    low, blocks = call(
        functools.partial(fold_kernel, early, count, True),
        "fold_early",
        state,
        (*[chunks[d] for d in early], *tables),
        [VMEM] * len(early) + table_specs,
        [VMEM] * 2,
        flops=rows * low_width * complete,
        moved=4 * MIB,
    )
    low, blocks = call(
        functools.partial(fold_kernel, late, count, False),
        "fold_late",
        state,
        (*[chunks[d] for d in late], *tables, low, blocks),
        [VMEM] * len(late) + table_specs + [VMEM] * 2,
        [VMEM] * 2,
        flops=rows * low_width * width * 4,
        moved=MIB,
    )
    first = wanted[:3]
    extras = shape((slots * CAP, rows, side), F32)
    low, extra, top, bottom, one, two = call(
        functools.partial(finish_kernel, first, count),
        "finish",
        [shape((rows, low_width), BF16), extras]
        + [shape((rows // 2, width), BF16)] * 2
        + [shape((rows, width), F32)] * 2,
        (front, back, *tables, second, low, blocks, *[dense[d] for d in first]),
        [VMEM] * 2 + table_specs + [VMEM] * (3 + len(first)),
        [VMEM] * 6,
        [pltpu.VMEM((heads, rows, side), BF16), pltpu.VMEM((rows, low_width), F32),
         pltpu.VMEM((rows, width), F32)],
        flops=rows * low_width * width * 8,
        moved=2 * MIB,
    )
    parts = {first[1]: one, first[2]: two}
    for distance in range(half - 2, -1, -1):
        pair = [distance, count - distance] if distance else [0]
        sums = call(
            functools.partial(part_kernel, pair, count, slots),
            "part",
            [shape((rows, width), F32)] * len(pair),
            (low, second, blocks, extra, block_scale, block_cell, table, *[dense[d] for d in pair]),
            [VMEM] * 4 + [SMEM] * 3 + [VMEM] * len(pair),
            [VMEM] * len(pair),
            flops=rows * low_width * width * 4,
            moved=2 * MIB,
        )
        parts.update(zip(pair, sums))

    left = lax.ppermute(top, "tp", to_left)
    right = lax.ppermute(bottom, "tp", to_right)
    for distance in range(half - 1, 0, -1):
        mine, other = parts[count - distance], parts[distance]
        if distance == half - 1:
            none = jnp.zeros_like(left)
            left = jnp.concatenate([left, none], axis=0)
            right = jnp.concatenate([none, right], axis=0)
        left = lax.ppermute((mine + left.astype(F32)).astype(BF16), "tp", to_left)
        right = lax.ppermute((other + right.astype(F32)).astype(BF16), "tp", to_right)
    return (parts[0] + left.astype(F32) + right.astype(F32)).astype(BF16)


def solution(mesh):
    return jax.shard_map(
        body,
        mesh=mesh,
        in_specs=(
            P(("groups", "rep"), "tp"),
            P("tp", ("groups", "rep"), None, None),
            P("tp", ("groups", "rep"), None, None),
            P("tp", ("groups", "rep"), None),
            P("tp", ("groups", "rep"), None),
            P(("groups", "rep")),
            P(("groups", "rep")),
            P(),
            P("tp", None),
            P("tp", None, None),
            P("tp", None, None),
            P("tp", None, None, None),
            P("tp", None),
            P("tp", None, None),
            P("tp", None),
        ),
        out_specs=P(("groups", "rep"), "tp"),
        check_vma=False,
    )
```

time: 156 us -> 87.2 us (0.56)
  waiting for transfers between devices: 109 us -> 31.4 us
  starting transfers between devices: 0.04 us -> 18.6 us
  between operations: 13.5 us -> 0.26 us
  matrix products: 12.7 us -> 0 us
  Pallas kernels: 11.6 us -> 21.9 us
  local copies, waits for them, and re-layouts: 6.13 us -> 13.4 us
    reduce_scatter x1 -> x0, waiting for transfers between devices: 66.7 us -> none  [body(): return lax.psum_scatter(partial, 'tp', scatter_dimension=1, tiled=True)]
    all_gather x1 -> x0, waiting for transfers between devices: 42.6 us -> none  [body(): tiles = lax.all_gather(attended, 'tp', axis=0, tiled=True)]
    ppermute x0 -> x16, waiting for transfers between devices: none -> 31.4 us  [the longest x3 16.2 us: body(): right = chunks[step] = lax.ppermute(right, 'tp', to_left)]
    ppermute x0 -> x16, starting transfers between devices: none -> 18.6 us  [the longest x3 6.09 us: body(): right = chunks[step] = lax.ppermute(right, 'tp', to_left)]
    dot_general x4 -> x0, matrix products: 12.7 us -> none  [the longest x1 9.18 us: body(): lax.dot_general(attended, out_weight.reshape(heads, side, width), (((0, 2...]
    pallas_call x1 -> x9, Pallas kernels: 11.6 us -> 21.9 us  [call(): pl.pallas_call(kernel, out_shape=outs, in_specs=specs, out_specs=out_spec...]
    unnamed x19 -> x38, local copies, waits for them, and re-layouts: 4.81 us -> 13.4 us
  transfers between devices with their start and end apart: 2 -> 16, of which waited for: 2 -> 10; matrix products, arithmetic and copies ran while one was open for 6% -> 0% of each run, Pallas kernels for 0% -> 19%
where the time goes in v3:
time: 87.2 us; the launch traced here: 86.7 us
  waiting for transfers between devices  31.4 us (36%)
  Pallas kernels  21.9 us (25%)
  starting transfers between devices  18.6 us (21%)
  local copies, waits for them, and re-layouts  13.4 us (15%)
  other arithmetic  1.09 us (1%)
    pallas_call x9, Pallas kernels, call(): pl.pallas_call(kernel, out_shape=outs, in_specs=specs, out_specs=out_spec...  21.9 us
    ppermute x3, waiting for transfers between devices, body(): right = chunks[step] = lax.ppermute(right, 'tp', to_left)  16.2 us
    unnamed x38, local copies, waits for them, and re-layouts  13.4 us
    ppermute x3, starting transfers between devices, body(): right = chunks[step] = lax.ppermute(right, 'tp', to_left)  6.09 us
    ppermute x3, waiting for transfers between devices, body(): left = lax.ppermute((mine + left.astype(F32)).astype(BF16), 'tp', to_left)  6.03 us
    ppermute x3, waiting for transfers between devices, body(): lax.ppermute((other + right.astype(F32)).astype(BF16), 'tp', to_right)  4.81 us
    ppermute x1, waiting for transfers between devices, body(): left = lax.ppermute(top, 'tp', to_left)  4.34 us
    ppermute x3, starting transfers between devices, body(): left = lax.ppermute((mine + left.astype(F32)).astype(BF16), 'tp', to_left)  3.64 us
  transfers between devices with their start and end apart: 16, of which 10 were waited for; matrix products, arithmetic and copies ran while one was open for 0% of the time, Pallas kernels for 19%

profile of v3, /device:TPU:0, one launch (start us, length us, event | category | flops | bytes accessed | tf_op | source)
XLA Modules:
  0.0 86.7 jit_solution(16125607828171042122)
XLA Ops:
  0.0 1.2 %copy-done.4 = bf16[1,128,32,128]{3,2,1,0:T(8,128)(2,1)S(1)} copy-done((bf16[1,128,32,128]{3,2,1,0:T(8,128)(2,1)S(1)}, bf16[1,128,32,128]{3,2,1,0:T(8,128)(2,1)}, u32[]{:S(2)}) %copy-start.4) | copy-done | bytes 1048600
  1.2 1.2 %copy-done.5 = bf16[1,128,32,128]{3,2,1,0:T(8,128)(2,1)S(1)} copy-done((bf16[1,128,32,128]{3,2,1,0:T(8,128)(2,1)S(1)}, bf16[1,128,32,128]{3,2,1,0:T(8,128)(2,1)}, u32[]{:S(2)}) %copy-start.5) | copy-done | bytes 1048600
  2.5 0.9 %copy-done.6 = bf16[128,1024]{1,0:T(8,128)(2,1)S(1)} copy-done((bf16[128,1024]{1,0:T(8,128)(2,1)S(1)}, bf16[128,1024]{1,0:T(8,128)(2,1)}, u32[]{:S(2)}) %copy-start.6) | copy-done | bytes 262168
  5.6 3.0 %attend.1.refs_0_ = bf16[8,128,128]{2,1,0:T(8,128)(2,1)S(1)} custom-call(bf16[128,1024]{1,0:T(8,128)(2,1)S(1)} %copy-done.6, bf16[4096,128]{1,0:T(8,128)(2,1)S(1)} %bitcast.20, bf16[4096,128]{1,0:T(8,128)(2,1)S(1)} %bitcast.21, bf16[128,128]{1,0:T(8,128)(2,1)S(1)} %bitcast.22, bf16[128,128]{1,0:T(8,128)(2,1)S(1)} %bitcast.23, s32[1,128]{1,0:T(1,128)S(1)} %bitcast.26), custom_call_target="tpu_custom_call" | custom-call | tf_op jit(solution)/shard_map/attend/pallas_call | solution.py:38
  8.6 3.0 %collective-permute-start = (bf16[8,128,128]{2,1,0:T(8,128)(2,1)S(1)}, bf16[8,128,128]{2,1,0:T(8,128)(2,1)S(1)}, u32[]{:S(2)}, u32[]{:S(2)}) collective-permute-start(bf16[8,128,128]{2,1,0:T(8,128)(2,1)S(1)} %attend.1.refs_0_), channel_id=1, source_target_pairs={{4,0},{8,4},{12,8},{14,12},{10,14},{6,10},{2,6},{0,2},{5,1},{9,5},... | collective-permute-start | bytes 786440 | tf_op jit(solution)/shard_map/ppermute | solution.py:281
  11.8 6.2 %collective-permute-done.refs_1_.refs_2_ = bf16[8,128,128]{2,1,0:T(8,128)(2,1)S(1)} collective-permute-done((bf16[8,128,128]{2,1,0:T(8,128)(2,1)S(1)}, bf16[8,128,128]{2,1,0:T(8,128)(2,1)S(1)}, u32[]{:S(2)}, u32[]{:S(2)}) %collective-permute-start) | collective-permute-done | bytes 262176 | tf_op jit(solution)/shard_map/ppermute | solution.py:281
  18.0 1.7 %collective-permute-start.1 = (bf16[8,128,128]{2,1,0:T(8,128)(2,1)S(1)}, bf16[8,128,128]{2,1,0:T(8,128)(2,1)S(1)}, u32[]{:S(2)}, u32[]{:S(2)}) collective-permute-start(bf16[8,128,128]{2,1,0:T(8,128)(2,1)S(1)} %collective-permute-done.refs_1_.refs_2_), channel_id=1, source_target_pairs={{4,0},{8,4},{12,8},{14,12},{10,14},{6,10},{2,6},{0,2},{5,1},{9,5},... | collective-permute-start | bytes 786440 | tf_op jit(solution)/shard_map/ppermute | solution.py:281
  20.0 5.5 %collective-permute-done.1.refs_3_ = bf16[8,128,128]{2,1,0:T(8,128)(2,1)S(1)} collective-permute-done((bf16[8,128,128]{2,1,0:T(8,128)(2,1)S(1)}, bf16[8,128,128]{2,1,0:T(8,128)(2,1)S(1)}, u32[]{:S(2)}, u32[]{:S(2)}) %collective-permute-start.1) | collective-permute-done | bytes 262176 | tf_op jit(solution)/shard_map/ppermute | solution.py:281
  25.5 1.4 %collective-permute-start.2 = (bf16[8,128,128]{2,1,0:T(8,128)(2,1)S(1)}, bf16[8,128,128]{2,1,0:T(8,128)(2,1)S(1)}, u32[]{:S(2)}, u32[]{:S(2)}) collective-permute-start(bf16[8,128,128]{2,1,0:T(8,128)(2,1)S(1)} %collective-permute-done.1.refs_3_), channel_id=1, source_target_pairs={{4,0},{8,4},{12,8},{14,12},{10,14},{6,10},{2,6},{0,2},{5,1},{9,5},... | collective-permute-start | bytes 786440 | tf_op jit(solution)/shard_map/ppermute | solution.py:281
  27.5 4.5 %collective-permute-done.2.refs_0_ = bf16[8,128,128]{2,1,0:T(8,128)(2,1)S(1)} collective-permute-done((bf16[8,128,128]{2,1,0:T(8,128)(2,1)S(1)}, bf16[8,128,128]{2,1,0:T(8,128)(2,1)S(1)}, u32[]{:S(2)}, u32[]{:S(2)}) %collective-permute-start.2) | collective-permute-done | bytes 262176 | tf_op jit(solution)/shard_map/ppermute | solution.py:281
  32.1 1.6 %collective-permute-start.3 = (bf16[4,128,128]{2,1,0:T(8,128)(2,1)S(1)}, bf16[4,128,128]{2,1,0:T(8,128)(2,1)S(1)}, u32[]{:S(2)}, u32[]{:S(2)}) collective-permute-start(bf16[4,128,128]{2,1,0:T(8,128)(2,1)S(1)} %slice.8), channel_id=1, source_target_pairs={{4,0},{8,4},{12,8},{14,12},{10,14},{6,10},{2,6},{0,2},{5,1},{9,5},... | collective-permute-start | bytes 393224 | tf_op jit(solution)/shard_map/ppermute | solution.py:283
  34.2 5.8 %copy-done = bf16[1024,8192]{1,0:T(8,128)(2,1)S(1)} copy-done((bf16[1024,8192]{1,0:T(8,128)(2,1)S(1)}, bf16[1024,8192]{1,0:T(8,128)(2,1)}, u32[]{:S(2)}) %copy-start) | copy-done | bytes 16777240
  42.0 6.0 %dense_first.1 = (f32[128,1024]{1,0:T(8,128)S(1)}, f32[128,1024]{1,0:T(8,128)S(1)}, f32[128,1024]{1,0:T(8,128)S(1)}, f32[128,1024]{1,0:T(8,128)S(1)}, s32[128,128]{1,0:T(8,128)S(1)}, /*index=5*/s32[64]{0:T(128)S(1)}) custom-call(bf16[8,128,128]{2,1,0:T(8,128)(2,1)S(1)} %attend.1.refs_0_, bf16[1024,8192]{1,0:T(8,128)(2,1)S(1)} %copy-done, ...), custom_call_target="tpu_custom_call" | custom-call | flops 1073741824 | bytes 8388608 | tf_op jit(solution)/shard_map/dense_first/pallas_call | solution.py:38
  48.0 2.2 %fold_early.1 = (f32[128,256]{1,0:T(8,128)S(1)}, f32[64,128,128]{2,1,0:T(8,128)S(1)}) custom-call(bf16[8,128,128]{2,1,0:T(8,128)(2,1)S(1)} %attend.1.refs_0_, bf16[8,128,128]{2,1,0:T(8,128)(2,1)S(1)} %collective-permute-done.refs_1_.refs_2_, bf16[8,128,128]{2,1,0:T(8,128)(2,1)S(1)} %collective-permute-done.4.refs_2_, ...), custom_call_target="tpu_custom_call" | custom-call | flops 268435456 | bytes 4194304 | tf_op jit(solution)/shard_map/fold_early/pallas_call | solution.py:38
  50.2 1.4 %fold_late.1 = (f32[128,256]{1,0:T(8,128)S(1)}, f32[64,128,128]{2,1,0:T(8,128)S(1)}) custom-call(bf16[8,128,128]{2,1,0:T(8,128)(2,1)S(1)} %collective-permute-done.2.refs_0_, bf16[8,128,128]{2,1,0:T(8,128)(2,1)S(1)} %collective-permute-done.6.refs_1_, s32[128,128]{1,0:T(8,128)S(1)} %get-tuple-element.29.refs_5_.refs_2_, bf16[256,8192]{1,0:T(8,128)(2,1)S(1)} %bitcast.18, ...), custom_call_target="tpu_custom_call" | custom-call | flops 134217728 | bytes 1048576 | tf_op jit(solution)/shard_map/fold_late/pallas_call | solution.py:38
  51.7 2.0 %finish.1 = (bf16[128,256]{1,0:T(8,128)(2,1)S(1)}, f32[8,128,128]{2,1,0:T(8,128)S(1)}, bf16[64,1024]{1,0:T(8,128)(2,1)S(1)}, bf16[64,1024]{1,0:T(8,128)(2,1)S(1)...) custom-call(bf16[4,128,128]{2,1,0:T(8,128)(2,1)S(1)} %collective-permute-done.3.refs_0_, ...), custom_call_target="tpu_custom_call" | custom-call | flops 268435456 | bytes 2097152 | tf_op jit(solution)/shard_map/finish/pallas_call | solution.py:38
  53.7 1.6 %collective-permute-start.8 = (bf16[64,1024]{1,0:T(8,128)(2,1)S(1)}, bf16[64,1024]{1,0:T(8,128)(2,1)S(1)}, u32[]{:S(2)}, u32[]{:S(2)}) collective-permute-start(bf16[64,1024]{1,0:T(8,128)(2,1)S(1)} %get-tuple-element.48), channel_id=1, source_target_pairs={{4,0},{8,4},{12,8},{14,12},{10,14},{6,10},{2,6},{0,2},{5,1},{9,5},... | collective-permute-start | bytes 393224 | tf_op jit(solution)/shard_map/ppermute | solution.py:378
  55.8 4.3 %collective-permute-done.8 = bf16[64,1024]{1,0:T(8,128)(2,1)S(1)} collective-permute-done((bf16[64,1024]{1,0:T(8,128)(2,1)S(1)}, bf16[64,1024]{1,0:T(8,128)(2,1)S(1)}, u32[]{:S(2)}, u32[]{:S(2)}) %collective-permute-start.8) | collective-permute-done | bytes 131104 | tf_op jit(solution)/shard_map/ppermute | solution.py:378
  60.2 1.6 %collective-permute-start.9 = (bf16[128,1024]{1,0:T(8,128)(2,1)S(1)}, bf16[128,1024]{1,0:T(8,128)(2,1)S(1)}, u32[]{:S(2)}, u32[]{:S(2)}) collective-permute-start(bf16[128,1024]{1,0:T(8,128)(2,1)S(1)} %add_convert_fusion.6), channel_id=1, source_target_pairs={{4,0},{8,4},{12,8},{14,12},{10,14},{6,10},{2,6},{0,2},{5,1},{9,5},... | collective-permute-start | bytes 786440 | tf_op jit(solution)/shard_map/ppermute | solution.py:386
  61.8 3.9 %dense_second.1 = (f32[128,1024]{1,0:T(8,128)S(1)}, f32[128,1024]{1,0:T(8,128)S(1)}, f32[128,1024]{1,0:T(8,128)S(1)}, f32[128,1024]{1,0:T(8,128)S(1)}) custom-call(bf16[8,128,128]{2,1,0:T(8,128)(2,1)S(1)} %attend.1.refs_0_, bf16[1024,8192]{1,0:T(8,128)(2,1)S(1)} %bitcast.12, bf16[8,128,128]{2,1,0:T(8,128)(2,1)S(1)} %collective-permute-done.refs_1_.refs_2_), custom_call_target="tpu_custom_call" | custom-call | flops 1073741824 | bytes 8388608 | tf_op jit(solution)/shard_map/dense_second/pallas_call | solution.py:38
  66.3 1.3 %part.5 = (f32[128,1024]{1,0:T(8,128)S(1)}, f32[128,1024]{1,0:T(8,128)S(1)}) custom-call(bf16[128,256]{1,0:T(8,128)(2,1)S(1)} %get-tuple-element.38.refs_0_, bf16[256,8192]{1,0:T(8,128)(2,1)S(1)} %bitcast.14, f32[64,128,128]{2,1,0:T(8,128)S(1)} %get-tuple-element.34.refs_10_.refs_2_, f32[8,128,128]{2,1,0:T(8,128)S(1)} %get-tuple-element.39.refs_3_, ...), custom_call_target="tpu_custom_call" | custom-call | flops 134217728 | bytes 2097152 | tf_op jit(solution)/shard_map/part/pallas_call | solution.py:38
  67.5 1.7 %collective-permute-done.9 = bf16[128,1024]{1,0:T(8,128)(2,1)S(1)} collective-permute-done((bf16[128,1024]{1,0:T(8,128)(2,1)S(1)}, bf16[128,1024]{1,0:T(8,128)(2,1)S(1)}, u32[]{:S(2)}, u32[]{:S(2)}) %collective-permute-start.9) | collective-permute-done | bytes 262176 | tf_op jit(solution)/shard_map/ppermute | solution.py:386
  69.3 1.3 %collective-permute-start.10 = (bf16[128,1024]{1,0:T(8,128)(2,1)S(1)}, bf16[128,1024]{1,0:T(8,128)(2,1)S(1)}, u32[]{:S(2)}, u32[]{:S(2)}) collective-permute-start(bf16[128,1024]{1,0:T(8,128)(2,1)S(1)} %add_convert_fusion.5), channel_id=1, source_target_pairs={{4,0},{8,4},{12,8},{14,12},{10,14},{6,10},{2,6},{0,2},{5,1},{9,5},... | collective-permute-start | bytes 786440 | tf_op jit(solution)/shard_map/ppermute | solution.py:386
  70.6 2.4 %collective-permute-done.13 = bf16[128,1024]{1,0:T(8,128)(2,1)S(1)} collective-permute-done((bf16[128,1024]{1,0:T(8,128)(2,1)S(1)}, bf16[128,1024]{1,0:T(8,128)(2,1)S(1)}, u32[]{:S(2)}, u32[]{:S(2)}) %collective-permute-start.13) | collective-permute-done | bytes 262176 | tf_op jit(solution)/shard_map/ppermute | solution.py:387
  73.0 1.2 %collective-permute-start.14 = (bf16[128,1024]{1,0:T(8,128)(2,1)S(1)}, bf16[128,1024]{1,0:T(8,128)(2,1)S(1)}, u32[]{:S(2)}, u32[]{:S(2)}) collective-permute-start(bf16[128,1024]{1,0:T(8,128)(2,1)S(1)} %add_convert_fusion.2), channel_id=1, source_target_pairs={{0,4},{4,8},{8,12},{12,14},{14,10},{10,6},{6,2},{2,0},{1,5},{5,9},... | collective-permute-start | bytes 786440 | tf_op jit(solution)/shard_map/ppermute | solution.py:387
  74.3 1.3 %part.4 = (f32[128,1024]{1,0:T(8,128)S(1)}, f32[128,1024]{1,0:T(8,128)S(1)}) custom-call(bf16[128,256]{1,0:T(8,128)(2,1)S(1)} %get-tuple-element.38.refs_0_, bf16[256,8192]{1,0:T(8,128)(2,1)S(1)} %bitcast.15, f32[64,128,128]{2,1,0:T(8,128)S(1)} %get-tuple-element.34.refs_10_.refs_2_, f32[8,128,128]{2,1,0:T(8,128)S(1)} %get-tuple-element.39.refs_3_, ...), custom_call_target="tpu_custom_call" | custom-call | flops 134217728 | bytes 2097152 | tf_op jit(solution)/shard_map/part/pallas_call | solution.py:38
  75.5 2.3 %collective-permute-done.10 = bf16[128,1024]{1,0:T(8,128)(2,1)S(1)} collective-permute-done((bf16[128,1024]{1,0:T(8,128)(2,1)S(1)}, bf16[128,1024]{1,0:T(8,128)(2,1)S(1)}, u32[]{:S(2)}, u32[]{:S(2)}) %collective-permute-start.10) | collective-permute-done | bytes 262176 | tf_op jit(solution)/shard_map/ppermute | solution.py:386
  78.6 0.8 collective-permute-done.14
  79.5 1.8 %collective-permute-start.15 = (bf16[128,1024]{1,0:T(8,128)(2,1)S(1)}, bf16[128,1024]{1,0:T(8,128)(2,1)S(1)}, u32[]{:S(2)}, u32[]{:S(2)}) collective-permute-start(bf16[128,1024]{1,0:T(8,128)(2,1)S(1)} %add_convert_fusion.1), channel_id=1, source_target_pairs={{0,4},{4,8},{8,12},{12,14},{14,10},{10,6},{6,2},{2,0},{1,5},{5,9},... | collective-permute-start | bytes 786440 | tf_op jit(solution)/shard_map/ppermute | solution.py:387
  81.3 0.9 %part.3 = f32[128,1024]{1,0:T(8,128)S(1)} custom-call(bf16[128,256]{1,0:T(8,128)(2,1)S(1)} %get-tuple-element.38.refs_0_, bf16[256,8192]{1,0:T(8,128)(2,1)S(1)} %bitcast.16, f32[64,128,128]{2,1,0:T(8,128)S(1)} %get-tuple-element.34.refs_10_.refs_2_, f32[8,128,128]{2,1,0:T(8,128)S(1)} %get-tuple-element.39.refs_3_, f32[4,16]{1,0:T(4,128)S(1)} %copy-done.7, ...), custom_call_target="tpu_custom_call" | custom-call | flops 134217728 | bytes 2097152 | tf_op jit(solution)/shard_map/part/pallas_call | solution.py:38
  82.3 2.0 %collective-permute-done.11 = bf16[128,1024]{1,0:T(8,128)(2,1)S(1)} collective-permute-done((bf16[128,1024]{1,0:T(8,128)(2,1)S(1)}, bf16[128,1024]{1,0:T(8,128)(2,1)S(1)}, u32[]{:S(2)}, u32[]{:S(2)}) %collective-permute-start.11) | collective-permute-done | bytes 262176 | tf_op jit(solution)/shard_map/ppermute | solution.py:386
  84.3 1.6 %collective-permute-done.15 = bf16[128,1024]{1,0:T(8,128)(2,1)S(1)} collective-permute-done((bf16[128,1024]{1,0:T(8,128)(2,1)S(1)}, bf16[128,1024]{1,0:T(8,128)(2,1)S(1)}, u32[]{:S(2)}, u32[]{:S(2)}) %collective-permute-start.15) | collective-permute-done | bytes 262176 | tf_op jit(solution)/shard_map/ppermute | solution.py:387
  (57 shorter events, 8.7 us)
Async XLA Ops:
  0.0 1.2 %copy-start.4 = (bf16[1,128,32,128]{3,2,1,0:T(8,128)(2,1)S(1)}, bf16[1,128,32,128]{3,2,1,0:T(8,128)(2,1)}, u32[]{:S(2)}) copy-start(bf16[1,128,32,128]{3,2,1,0:T(8,128)(2,1)} %param.16) | copy-start | bytes 3145732
  1.2 1.2 %copy-start.5 = (bf16[1,128,32,128]{3,2,1,0:T(8,128)(2,1)S(1)}, bf16[1,128,32,128]{3,2,1,0:T(8,128)(2,1)}, u32[]{:S(2)}) copy-start(bf16[1,128,32,128]{3,2,1,0:T(8,128)(2,1)} %param.17) | copy-start | bytes 3145732
  2.5 0.9 %copy-start.6 = (bf16[128,1024]{1,0:T(8,128)(2,1)S(1)}, bf16[128,1024]{1,0:T(8,128)(2,1)}, u32[]{:S(2)}) copy-start(bf16[128,1024]{1,0:T(8,128)(2,1)} %q_ref.1) | copy-start | bytes 786436
  3.4 0.8 copy-start.9
  4.2 0.8 copy-start.10
  8.6 9.4 %collective-permute-start = (bf16[8,128,128]{2,1,0:T(8,128)(2,1)S(1)}, bf16[8,128,128]{2,1,0:T(8,128)(2,1)S(1)}, u32[]{:S(2)}, u32[]{:S(2)}) collective-permute-start(bf16[8,128,128]{2,1,0:T(8,128)(2,1)S(1)} %attend.1.refs_0_), channel_id=1, source_target_pairs={{4,0},{8,4},{12,8},{14,12},{10,14},{6,10},{2,6},{0,2},{5,1},{9,5},... | collective-permute-start | bytes 786440 | tf_op jit(solution)/shard_map/ppermute | solution.py:281
  11.6 8.1 %collective-permute-start.4 = (bf16[8,128,128]{2,1,0:T(8,128)(2,1)S(1)}, bf16[8,128,128]{2,1,0:T(8,128)(2,1)S(1)}, u32[]{:S(2)}, u32[]{:S(2)}) collective-permute-start(bf16[8,128,128]{2,1,0:T(8,128)(2,1)S(1)} %attend.1.refs_0_), channel_id=1, source_target_pairs={{0,4},{4,8},{8,12},{12,14},{14,10},{10,6},{6,2},{2,0},{1,5},{5,9},... | collective-permute-start | bytes 786440 | tf_op jit(solution)/shard_map/ppermute | solution.py:282
  18.0 7.5 %collective-permute-start.1 = (bf16[8,128,128]{2,1,0:T(8,128)(2,1)S(1)}, bf16[8,128,128]{2,1,0:T(8,128)(2,1)S(1)}, u32[]{:S(2)}, u32[]{:S(2)}) collective-permute-start(bf16[8,128,128]{2,1,0:T(8,128)(2,1)S(1)} %collective-permute-done.refs_1_.refs_2_), channel_id=1, source_target_pairs={{4,0},{8,4},{12,8},{14,12},{10,14},{6,10},{2,6},{0,2},{5,1},{9,5},... | collective-permute-start | bytes 786440 | tf_op jit(solution)/shard_map/ppermute | solution.py:281
  19.7 7.2 %collective-permute-start.5 = (bf16[8,128,128]{2,1,0:T(8,128)(2,1)S(1)}, bf16[8,128,128]{2,1,0:T(8,128)(2,1)S(1)}, u32[]{:S(2)}, u32[]{:S(2)}) collective-permute-start(bf16[8,128,128]{2,1,0:T(8,128)(2,1)S(1)} %collective-permute-done.4.refs_2_), channel_id=1, source_target_pairs={{0,4},{4,8},{8,12},{12,14},{14,10},{10,6},{6,2},{2,0},{1,5},{5,9},... | collective-permute-start | bytes 786440 | tf_op jit(solution)/shard_map/ppermute | solution.py:282
  25.5 6.6 %collective-permute-start.2 = (bf16[8,128,128]{2,1,0:T(8,128)(2,1)S(1)}, bf16[8,128,128]{2,1,0:T(8,128)(2,1)S(1)}, u32[]{:S(2)}, u32[]{:S(2)}) collective-permute-start(bf16[8,128,128]{2,1,0:T(8,128)(2,1)S(1)} %collective-permute-done.1.refs_3_), channel_id=1, source_target_pairs={{4,0},{8,4},{12,8},{14,12},{10,14},{6,10},{2,6},{0,2},{5,1},{9,5},... | collective-permute-start | bytes 786440 | tf_op jit(solution)/shard_map/ppermute | solution.py:281
  26.9 6.8 %collective-permute-start.6 = (bf16[8,128,128]{2,1,0:T(8,128)(2,1)S(1)}, bf16[8,128,128]{2,1,0:T(8,128)(2,1)S(1)}, u32[]{:S(2)}, u32[]{:S(2)}) collective-permute-start(bf16[8,128,128]{2,1,0:T(8,128)(2,1)S(1)} %collective-permute-done.5.refs_4_), channel_id=1, source_target_pairs={{0,4},{4,8},{8,12},{12,14},{14,10},{10,6},{6,2},{2,0},{1,5},{5,9},... | collective-permute-start | bytes 786440 | tf_op jit(solution)/shard_map/ppermute | solution.py:282
  32.1 19.6 %collective-permute-start.3 = (bf16[4,128,128]{2,1,0:T(8,128)(2,1)S(1)}, bf16[4,128,128]{2,1,0:T(8,128)(2,1)S(1)}, u32[]{:S(2)}, u32[]{:S(2)}) collective-permute-start(bf16[4,128,128]{2,1,0:T(8,128)(2,1)S(1)} %slice.8), channel_id=1, source_target_pairs={{4,0},{8,4},{12,8},{14,12},{10,14},{6,10},{2,6},{0,2},{5,1},{9,5},... | collective-permute-start | bytes 393224 | tf_op jit(solution)/shard_map/ppermute | solution.py:283
  33.7 18.0 %collective-permute-start.7 = (bf16[4,128,128]{2,1,0:T(8,128)(2,1)S(1)}, bf16[4,128,128]{2,1,0:T(8,128)(2,1)S(1)}, u32[]{:S(2)}, u32[]{:S(2)}) collective-permute-start(bf16[4,128,128]{2,1,0:T(8,128)(2,1)S(1)} %slice.9), channel_id=1, source_target_pairs={{0,4},{4,8},{8,12},{12,14},{14,10},{10,6},{6,2},{2,0},{1,5},{5,9},... | collective-permute-start | bytes 393224 | tf_op jit(solution)/shard_map/ppermute | solution.py:284
  34.2 5.8 %copy-start = (bf16[1024,8192]{1,0:T(8,128)(2,1)S(1)}, bf16[1024,8192]{1,0:T(8,128)(2,1)}, u32[]{:S(2)}) copy-start(bf16[1024,8192]{1,0:T(8,128)(2,1)} %refs_1_.3) | copy-start | bytes 50331652
  40.0 0.7 copy-start.11
  42.0 6.0 %copy-start.2 = (bf16[4,8192,64]{1,2,0:T(8,128)(2,1)S(1)}, bf16[4,8192,64]{1,2,0:T(8,128)(2,1)}, u32[]{:S(2)}) copy-start(bf16[4,8192,64]{1,2,0:T(8,128)(2,1)} %param.24) | copy-start | bytes 12582916
  42.0 6.0 %copy-start.3 = (bf16[4,16,128,128]{3,2,1,0:T(8,128)(2,1)S(1)}, bf16[4,16,128,128]{3,2,1,0:T(8,128)(2,1)}, u32[]{:S(2)}) copy-start(bf16[4,16,128,128]{3,2,1,0:T(8,128)(2,1)} %refs_4_.6) | copy-start | bytes 6291460
  42.0 6.0 %copy-start.7 = (f32[4,16]{1,0:T(4,128)S(1)}, f32[4,16]{1,0:T(4,128)}, u32[]{:S(2)}) copy-start(f32[4,16]{1,0:T(4,128)} %refs_4_.9) | copy-start | bytes 772
  42.0 6.0 %copy-start.8 = (s32[4,16]{1,0:T(4,128)S(1)}, s32[4,16]{1,0:T(4,128)}, u32[]{:S(2)}) copy-start(s32[4,16]{1,0:T(4,128)} %refs_5_.9) | copy-start | bytes 772
  48.0 3.7 %copy-start.1 = (bf16[4,64,8192]{2,1,0:T(8,128)(2,1)S(1)}, bf16[4,64,8192]{2,1,0:T(8,128)(2,1)}, u32[]{:S(2)}) copy-start(bf16[4,64,8192]{2,1,0:T(8,128)(2,1)} %param.25) | copy-start | bytes 12582916
  48.0 13.8 %slice-start = ((s8[16777216]{0:T(1024)(128)(4,1)}), s8[4194304]{0:T(1024)(128)(4,1)S(1)}, s32[]{:S(2)}) async-start(s8[16777216]{0:T(1024)(128)(4,1)} %bitcast.11), calls=%async_computation | async-start | bytes 8388608
  50.2 11.6 %slice-start.1 = ((s8[16777216]{0:T(1024)(128)(4,1)}), s8[4194304]{0:T(1024)(128)(4,1)S(1)}, s32[]{:S(2)}) async-start(s8[16777216]{0:T(1024)(128)(4,1)} %bitcast.11), calls=%async_computation.1 | async-start | bytes 8388608
  50.2 11.6 %slice-start.2 = ((s8[16777216]{0:T(1024)(128)(4,1)}), s8[4194304]{0:T(1024)(128)(4,1)S(1)}, s32[]{:S(2)}) async-start(s8[16777216]{0:T(1024)(128)(4,1)} %bitcast.11), calls=%async_computation.2 | async-start | bytes 8388608
  51.7 10.1 %slice-start.3 = ((s8[16777216]{0:T(1024)(128)(4,1)}), s8[4194304]{0:T(1024)(128)(4,1)S(1)}, s32[]{:S(2)}) async-start(s8[16777216]{0:T(1024)(128)(4,1)} %bitcast.11), calls=%async_computation.3 | async-start | bytes 8388608
  53.7 6.4 %collective-permute-start.8 = (bf16[64,1024]{1,0:T(8,128)(2,1)S(1)}, bf16[64,1024]{1,0:T(8,128)(2,1)S(1)}, u32[]{:S(2)}, u32[]{:S(2)}) collective-permute-start(bf16[64,1024]{1,0:T(8,128)(2,1)S(1)} %get-tuple-element.48), channel_id=1, source_target_pairs={{4,0},{8,4},{12,8},{14,12},{10,14},{6,10},{2,6},{0,2},{5,1},{9,5},... | collective-permute-start | bytes 393224 | tf_op jit(solution)/shard_map/ppermute | solution.py:378
  55.3 10.3 %collective-permute-start.12 = (bf16[64,1024]{1,0:T(8,128)(2,1)S(1)}, bf16[64,1024]{1,0:T(8,128)(2,1)S(1)}, u32[]{:S(2)}, u32[]{:S(2)}) collective-permute-start(bf16[64,1024]{1,0:T(8,128)(2,1)S(1)} %get-tuple-element.52), channel_id=1, source_target_pairs={{0,4},{4,8},{8,12},{12,14},{14,10},{10,6},{6,2},{2,0},{1,5},{5,9},... | collective-permute-start | bytes 393224 | tf_op jit(solution)/shard_map/ppermute | solution.py:379
  60.2 9.0 %collective-permute-start.9 = (bf16[128,1024]{1,0:T(8,128)(2,1)S(1)}, bf16[128,1024]{1,0:T(8,128)(2,1)S(1)}, u32[]{:S(2)}, u32[]{:S(2)}) collective-permute-start(bf16[128,1024]{1,0:T(8,128)(2,1)S(1)} %add_convert_fusion.6), channel_id=1, source_target_pairs={{4,0},{8,4},{12,8},{14,12},{10,14},{6,10},{2,6},{0,2},{5,1},{9,5},... | collective-permute-start | bytes 786440 | tf_op jit(solution)/shard_map/ppermute | solution.py:386
  65.7 7.3 %collective-permute-start.13 = (bf16[128,1024]{1,0:T(8,128)(2,1)S(1)}, bf16[128,1024]{1,0:T(8,128)(2,1)S(1)}, u32[]{:S(2)}, u32[]{:S(2)}) collective-permute-start(bf16[128,1024]{1,0:T(8,128)(2,1)S(1)} %add_convert_fusion.3), channel_id=1, source_target_pairs={{0,4},{4,8},{8,12},{12,14},{14,10},{10,6},{6,2},{2,0},{1,5},{5,9},... | collective-permute-start | bytes 786440 | tf_op jit(solution)/shard_map/ppermute | solution.py:387
  69.3 8.6 %collective-permute-start.10 = (bf16[128,1024]{1,0:T(8,128)(2,1)S(1)}, bf16[128,1024]{1,0:T(8,128)(2,1)S(1)}, u32[]{:S(2)}, u32[]{:S(2)}) collective-permute-start(bf16[128,1024]{1,0:T(8,128)(2,1)S(1)} %add_convert_fusion.5), channel_id=1, source_target_pairs={{4,0},{8,4},{12,8},{14,12},{10,14},{6,10},{2,6},{0,2},{5,1},{9,5},... | collective-permute-start | bytes 786440 | tf_op jit(solution)/shard_map/ppermute | solution.py:386
  73.0 6.4 %collective-permute-start.14 = (bf16[128,1024]{1,0:T(8,128)(2,1)S(1)}, bf16[128,1024]{1,0:T(8,128)(2,1)S(1)}, u32[]{:S(2)}, u32[]{:S(2)}) collective-permute-start(bf16[128,1024]{1,0:T(8,128)(2,1)S(1)} %add_convert_fusion.2), channel_id=1, source_target_pairs={{0,4},{4,8},{8,12},{12,14},{14,10},{10,6},{6,2},{2,0},{1,5},{5,9},... | collective-permute-start | bytes 786440 | tf_op jit(solution)/shard_map/ppermute | solution.py:387
  77.9 6.4 %collective-permute-start.11 = (bf16[128,1024]{1,0:T(8,128)(2,1)S(1)}, bf16[128,1024]{1,0:T(8,128)(2,1)S(1)}, u32[]{:S(2)}, u32[]{:S(2)}) collective-permute-start(bf16[128,1024]{1,0:T(8,128)(2,1)S(1)} %add_convert_fusion.4), channel_id=1, source_target_pairs={{4,0},{8,4},{12,8},{14,12},{10,14},{6,10},{2,6},{0,2},{5,1},{9,5},... | collective-permute-start | bytes 786440 | tf_op jit(solution)/shard_map/ppermute | solution.py:386
  79.5 6.4 %collective-permute-start.15 = (bf16[128,1024]{1,0:T(8,128)(2,1)S(1)}, bf16[128,1024]{1,0:T(8,128)(2,1)S(1)}, u32[]{:S(2)}, u32[]{:S(2)}) collective-permute-start(bf16[128,1024]{1,0:T(8,128)(2,1)S(1)} %add_convert_fusion.1), channel_id=1, source_target_pairs={{0,4},{4,8},{8,12},{12,14},{14,10},{10,6},{6,2},{2,0},{1,5},{5,9},... | collective-permute-start | bytes 786440 | tf_op jit(solution)/shard_map/ppermute | solution.py:387
  (3 other events, 2.0 us)

commit v4 on v3

--- a/solution.py
+++ b/solution.py
@@ -12,6 +12,7 @@
 F32 = jnp.float32
 CAP = 2
 ROW_BLOCK = 16
+PIECES = 4
 MIB = 1024 * 1024
 NT = (((1,), (1,)), ((), ()))
 VMEM = pl.BlockSpec(memory_space=pltpu.VMEM)
@@ -47,9 +48,31 @@
     )(*ins)
 
 
-def attend_kernel(q_ref, key_ref, value_ref, new_key_ref, new_value_ref, length_ref, out_ref):
+def attend_kernel(
+    query_hbm, key_hbm, value_hbm, new_key_hbm, new_value_hbm, length_hbm, out_ref,
+    q_ref, key_ref, value_ref, new_key_ref, new_value_ref, length_ref, sems,
+):
     heads, rows, side = out_ref.shape
     cache = key_ref.shape[0] // rows
+    small = [
+        pltpu.make_async_copy(source, target, sems.at[i])
+        for i, (source, target) in enumerate(
+            ((length_hbm, length_ref), (query_hbm, q_ref), (new_key_hbm, new_key_ref),
+             (new_value_hbm, new_value_ref))
+        )
+    ]
+    tall_piece = key_ref.shape[0] // PIECES
+    pieces = []
+    for i in range(PIECES):
+        for n, (source, target) in enumerate(((key_hbm, key_ref), (value_hbm, value_ref))):
+            part = pl.ds(i * tall_piece, tall_piece)
+            pieces.append(
+                pltpu.make_async_copy(source.at[part], target.at[part], sems.at[4 + 2 * i + n])
+            )
+    for copy in small + pieces:
+        copy.start()
+    for copy in small:
+        copy.wait()
     tall, wide = heads * ROW_BLOCK, cache * ROW_BLOCK
     scale = 1.0 / math.sqrt(side)
     lengths = jnp.transpose(jnp.broadcast_to(length_ref[...].astype(F32), (rows, rows)))[:, :1]
@@ -57,6 +80,9 @@
     place = (lax.broadcasted_iota(jnp.int32, (tall, wide), 1) - cache * row_in).astype(F32)
     place = jnp.where(place < 0, 1e9, place)
     for r in range(0, rows, ROW_BLOCK):
+        if r % (rows // PIECES) == 0:
+            for copy in pieces[2 * (r * PIECES // rows) :][:2]:
+                copy.wait()
         here = slice(r, r + ROW_BLOCK)
         cached = slice(r * cache, (r + ROW_BLOCK) * cache)
         query = jnp.concatenate(
@@ -86,7 +112,7 @@
         variant_ref, holder_ref, owner_ref = refs[2:5]
         outs, slot_ref, table_ref = refs[5 : 5 + len(distances)], refs[-4], refs[-3]
     else:
-        outs = refs[3 : 3 + len(distances)]
+        outs = refs[2 : 2 + len(distances)]
     buffers, sems = refs[-2:]
     heads, rows, side = x_ref.shape
     width = heads * side
@@ -203,19 +229,17 @@
             out_ref[:, place] += extra_ref[e]
 
 
-def finish_kernel(distances, count, *refs):
+def finish_kernel(distance, count, *refs):
     front_ref, back_ref, slot_ref, factor_ref, values_ref, scale_ref, cell_ref, table_ref = refs[:8]
     second_ref, low_in, block_ref = refs[8:11]
-    dense_refs = refs[11 : 11 + len(distances)]
-    low_out, extra_out, top_out, bottom_out = refs[11 + len(distances) : 15 + len(distances)]
-    outs = refs[15 + len(distances) : -3]
+    dense_ref, low_out, extra_out, top_out, bottom_out = refs[11:16]
     chunk, low_sum, farthest = refs[-3:]
     half, rows, side = front_ref.shape
     chunk[:half] = front_ref[...]
     chunk[half:] = back_ref[...]
     low_sum[...] = low_in[...]
     slot = slot_ref[...]
-    added = fold_chunk(distances[0], count, chunk, slot, factor_ref, values_ref, scale_ref, cell_ref,
+    added = fold_chunk(distance, count, chunk, slot, factor_ref, values_ref, scale_ref, cell_ref,
                        table_ref, low_sum)
     for e, (_, product) in enumerate(added):
         extra_out[e] = product
@@ -226,8 +250,7 @@
     slots_wide = jnp.concatenate([slot] * -(-low_width // side), axis=1)[:, :low_width]
     low = jnp.where(slots_wide == held, low_sum[...], 0.0).astype(BF16)
     low_out[...] = low
-    for distance, dense_ref, out in zip(distances, dense_refs, (farthest, *outs)):
-        part_for(distance, count, low, second_ref, dense_ref, block_ref, extra_out, columns, out)
+    part_for(distance, count, low, second_ref, dense_ref, block_ref, extra_out, columns, farthest)
     top_out[...] = farthest[: rows // 2].astype(BF16)
     bottom_out[...] = farthest[rows // 2 :].astype(BF16)
 
@@ -271,49 +294,62 @@
         shape((heads, rows, side), BF16),
         (queries, key_cache.reshape(-1, side), value_cache.reshape(-1, side), new_keys[0],
          new_values[0], lengths[None, :]),
-        [VMEM] * 6,
+        [ANY] * 6,
         VMEM,
-    )
-
-    chunks = {0: attended}
-    right = left = attended
-    for step in range(1, half):
-        right = chunks[step] = lax.ppermute(right, "tp", to_left)
-        left = chunks[count - step] = lax.ppermute(left, "tp", to_right)
-    front = lax.ppermute(right[: heads // 2], "tp", to_left)
-    back = lax.ppermute(left[heads // 2 :], "tp", to_right)
+        [pltpu.VMEM((rows, width), BF16), pltpu.VMEM((rows * cache, side), BF16),
+         pltpu.VMEM((rows * cache, side), BF16), pltpu.VMEM((rows, side), BF16),
+         pltpu.VMEM((rows, side), BF16), pltpu.VMEM((1, rows), jnp.int32),
+         pltpu.SemaphoreType.DMA((4 + 2 * PIECES,))],
+        limit=60,
+    )
 
     wanted = [half]
     for distance in range(half - 1, 0, -1):
         wanted += [distance, count - distance]
     wanted += [0]
+    cut = max(half - 1, 1)
     piece = width // 2 if width >= 512 else width
     streams = [pltpu.VMEM((4, width, piece), BF16), pltpu.SemaphoreType.DMA((4,))]
     dense_cost = dict(flops=rows * width * complete, moved=width * complete)
     dense = {}
+    chunks = {0: attended}
+
+    def pass_on(step, *done):
+        right, left = chunks[step - 1], chunks[(count - step + 1) % count]
+        if done:
+            right, left = after(right, *done), after(left, *done)
+        chunks[step] = lax.ppermute(right, "tp", to_left)
+        chunks[count - step] = lax.ppermute(left, "tp", to_right)
+
+    pass_on(1)
     *sums, slot, table = call(
-        functools.partial(dense_kernel, wanted[:half], count, True),
+        functools.partial(dense_kernel, wanted[:cut], count, True),
         "dense_first",
-        [shape((rows, width), F32)] * half
+        [shape((rows, width), F32)] * cut
         + [shape((rows, rows), jnp.int32), shape((count * slots * CAP,), jnp.int32)],
         (attended, out_weight, request_variant[None, :], holder_slot, block_owner[:, :, 0]),
         [VMEM, ANY, VMEM, SMEM, SMEM],
-        [VMEM] * half + [VMEM, SMEM],
+        [VMEM] * cut + [VMEM, SMEM],
         streams,
+        limit=40,
         **dense_cost,
     )
-    dense.update(zip(wanted[:half], sums))
+    dense.update(zip(wanted[:cut], sums))
+    pass_on(2, slot)
     sums = call(
-        functools.partial(dense_kernel, wanted[half:], count, False),
+        functools.partial(dense_kernel, wanted[cut:], count, False),
         "dense_second",
-        [shape((rows, width), F32)] * half,
-        (attended, out_weight, chunks[1]),
-        [VMEM, ANY, ANY],
-        [VMEM] * half,
+        [shape((rows, width), F32)] * (count - cut),
+        (after(attended, slot), out_weight),
+        [VMEM, ANY],
+        [VMEM] * (count - cut),
         streams,
+        limit=40,
         **dense_cost,
     )
-    dense.update(zip(wanted[half:], sums))
+    dense.update(zip(wanted[cut:], sums))
+    for step in range(3, half):
+        pass_on(step, sums[0])
 
     factor_t = jnp.swapaxes(factor_in, 1, 2).reshape(low_width, -1)
     second = second_factor.reshape(low_width, complete)
@@ -334,6 +370,8 @@
         flops=rows * low_width * complete,
         moved=4 * MIB,
     )
+    front = lax.ppermute(after(chunks[half - 1], low)[: heads // 2], "tp", to_left)
+    back = lax.ppermute(after(chunks[count - half + 1], low)[heads // 2 :], "tp", to_right)
     low, blocks = call(
         functools.partial(fold_kernel, late, count, False),
         "fold_late",
@@ -344,25 +382,22 @@
         flops=rows * low_width * width * 4,
         moved=MIB,
     )
-    first = wanted[:3]
     extras = shape((slots * CAP, rows, side), F32)
-    low, extra, top, bottom, one, two = call(
-        functools.partial(finish_kernel, first, count),
+    low, extra, top, bottom = call(
+        functools.partial(finish_kernel, half, count),
         "finish",
         [shape((rows, low_width), BF16), extras]
-        + [shape((rows // 2, width), BF16)] * 2
-        + [shape((rows, width), F32)] * 2,
-        (front, back, *tables, second, low, blocks, *[dense[d] for d in first]),
-        [VMEM] * 2 + table_specs + [VMEM] * (3 + len(first)),
-        [VMEM] * 6,
+        + [shape((rows // 2, width), BF16)] * 2,
+        (front, back, *tables, second, low, blocks, dense[half]),
+        [VMEM] * 2 + table_specs + [VMEM] * 4,
+        [VMEM] * 4,
         [pltpu.VMEM((heads, rows, side), BF16), pltpu.VMEM((rows, low_width), F32),
          pltpu.VMEM((rows, width), F32)],
         flops=rows * low_width * width * 8,
         moved=2 * MIB,
     )
-    parts = {first[1]: one, first[2]: two}
-    for distance in range(half - 2, -1, -1):
-        pair = [distance, count - distance] if distance else [0]
+
+    def parts_for(pair, low):
         sums = call(
             functools.partial(part_kernel, pair, count, slots),
             "part",
@@ -373,19 +408,26 @@
             flops=rows * low_width * width * 4,
             moved=2 * MIB,
         )
-        parts.update(zip(pair, sums))
+        return sums
 
     left = lax.ppermute(top, "tp", to_left)
     right = lax.ppermute(bottom, "tp", to_right)
+    if half > 1:
+        other, mine = parts_for([half - 1, count - half + 1], low)
     for distance in range(half - 1, 0, -1):
-        mine, other = parts[count - distance], parts[distance]
         if distance == half - 1:
             none = jnp.zeros_like(left)
             left = jnp.concatenate([left, none], axis=0)
             right = jnp.concatenate([none, right], axis=0)
-        left = lax.ppermute((mine + left.astype(F32)).astype(BF16), "tp", to_left)
-        right = lax.ppermute((other + right.astype(F32)).astype(BF16), "tp", to_right)
-    return (parts[0] + left.astype(F32) + right.astype(F32)).astype(BF16)
+        sent_left = (mine + left.astype(F32)).astype(BF16)
+        sent_right = (other + right.astype(F32)).astype(BF16)
+        if distance > 1:
+            other, mine = parts_for([distance - 1, count - distance + 1], after(low, sent_right))
+        else:
+            (own,) = parts_for([0], after(low, sent_right))
+        left = lax.ppermute(sent_left, "tp", to_left)
+        right = lax.ppermute(sent_right, "tp", to_right)
+    return (own + left.astype(F32) + right.astype(F32)).astype(BF16)
 
 
 def solution(mesh):

time: 87.2 us -> 70.8 us (0.81)
  local copies, waits for them, and re-layouts: 13.4 us -> 3.05 us
  waiting for transfers between devices: 31.4 us -> 23.8 us
  Pallas kernels: 21.9 us -> 24.6 us
    unnamed x38 -> x20, local copies, waits for them, and re-layouts: 13.4 us -> 3.03 us
    ppermute x14, waiting for transfers between devices: 27.1 us -> 20.8 us  [the longest x3 13.2 us: body(): left = lax.ppermute(sent_left, 'tp', to_left)]
    pallas_call x9 -> x10, Pallas kernels: 21.9 us -> 24.6 us  [call(): pl.pallas_call(kernel, out_shape=outs, in_specs=specs, out_specs=out_spec...]
    ppermute x1, waiting for transfers between devices: 4.34 us -> 3.01 us  [body(): left = lax.ppermute(top, 'tp', to_left)]
    ppermute x1, starting transfers between devices: 0.48 us -> 1.7 us  [body(): right = lax.ppermute(bottom, 'tp', to_right)]
    ppermute x1, starting transfers between devices: 1.6 us -> 0.38 us  [body(): left = lax.ppermute(top, 'tp', to_left)]
  transfers between devices with their start and end apart: 16 -> 16, of which waited for: 10 -> 9; matrix products, arithmetic and copies ran while one was open for 0% -> 0% of each run, Pallas kernels for 19% -> 25%
where the time goes in v4:
time: 70.8 us; the launch traced here: 70.5 us
  Pallas kernels  24.6 us (35%)
  waiting for transfers between devices  23.8 us (34%)
  starting transfers between devices  17.8 us (25%)
  local copies, waits for them, and re-layouts  3.05 us (4%)
  other arithmetic  1.09 us (2%)
    pallas_call x10, Pallas kernels, call(): pl.pallas_call(kernel, out_shape=outs, in_specs=specs, out_specs=out_spec...  24.6 us
    ppermute x3, waiting for transfers between devices, body(): left = lax.ppermute(sent_left, 'tp', to_left)  13.2 us
    ppermute x3, starting transfers between devices, pass_on(): chunks[count - step] = lax.ppermute(left, 'tp', to_right)  6.83 us
    ppermute x3, starting transfers between devices, body(): right = lax.ppermute(sent_right, 'tp', to_right)  4.43 us
    ppermute x3, waiting for transfers between devices, pass_on(): chunks[count - step] = lax.ppermute(left, 'tp', to_right)  3.39 us
    unnamed x20, local copies, waits for them, and re-layouts  3.03 us
    ppermute x1, waiting for transfers between devices, body(): left = lax.ppermute(top, 'tp', to_left)  3.01 us
    ppermute x3, starting transfers between devices, body(): left = lax.ppermute(sent_left, 'tp', to_left)  1.96 us
  transfers between devices with their start and end apart: 16, of which 9 were waited for; matrix products, arithmetic and copies ran while one was open for 0% of the time, Pallas kernels for 25%

profile of v4, /device:TPU:0, one launch (start us, length us, event | category | flops | bytes accessed | tf_op | source)
XLA Modules:
  0.0 70.5 jit_solution(16728702664745819438)
XLA Ops:
  0.0 5.5 %attend.1.refs_0_ = bf16[8,128,128]{2,1,0:T(8,128)(2,1)} custom-call(bf16[128,1024]{1,0:T(8,128)(2,1)} %query_hbm.1, bf16[4096,128]{1,0:T(8,128)(2,1)} %bitcast.21, bf16[4096,128]{1,0:T(8,128)(2,1)} %bitcast.22, bf16[128,128]{1,0:T(8,128)(2,1)} %bitcast.23, bf16[128,128]{1,0:T(8,128)(2,1)} %bitcast.24, s32[1,128]{1,0:T(1,128)} %bitcast.25), custom_call_target="tpu_custom_call" | custom-call | tf_op jit(solution)/shard_map/attend/pallas_call | solution.py:39
  5.6 3.1 %collective-permute-start.3 = (bf16[8,128,128]{2,1,0:T(8,128)(2,1)}, bf16[8,128,128]{2,1,0:T(8,128)(2,1)S(1)}, u32[]{:S(2)}, u32[]{:S(2)}) collective-permute-start(bf16[8,128,128]{2,1,0:T(8,128)(2,1)} %attend.1.refs_0_), channel_id=1, source_target_pairs={{0,4},{4,8},{8,12},{12,14},{14,10},{10,6},{6,2},{2,0},{1,5},{5,9},... | collective-permute-start | bytes 786440 | tf_op jit(solution)/shard_map/ppermute | solution.py:322
  8.6 1.0 %copy-done.3 = bf16[8,128,128]{2,1,0:T(8,128)(2,1)S(1)} copy-done((bf16[8,128,128]{2,1,0:T(8,128)(2,1)S(1)}, bf16[8,128,128]{2,1,0:T(8,128)(2,1)}, u32[]{:S(2)}) %copy-start.3) | copy-done | bytes 262168
  9.6 0.7 copy-done.7
  11.6 4.3 %dense_first.1 = (f32[128,1024]{1,0:T(8,128)S(1)}, f32[128,1024]{1,0:T(8,128)S(1)}, f32[128,1024]{1,0:T(8,128)S(1)}, s32[128,128]{1,0:T(8,128)S(1)}, s32[64]{0:T(128)S(1)}) custom-call(bf16[8,128,128]{2,1,0:T(8,128)(2,1)S(1)} %copy-done.3, bf16[1024,8192]{1,0:T(8,128)(2,1)} %refs_1_.3, s32[1,128]{1,0:T(1,128)S(1)} %bitcast.20, s32[32]{0:T(128)S(1)} %copy-done.9, ...), custom_call_target="tpu_custom_call" | custom-call | flops 1073741824 | bytes 8388608 | tf_op jit(solution)/shard_map/dense_first/pallas_call | solution.py:39
  16.0 2.0 %collective-permute-start.4 = (bf16[8,128,128]{2,1,0:T(8,128)(2,1)S(1)}, bf16[8,128,128]{2,1,0:T(8,128)(2,1)S(1)}, u32[]{:S(2)}, u32[]{:S(2)}) collective-permute-start(bf16[8,128,128]{2,1,0:T(8,128)(2,1)S(1)} %collective-permute-done.3.refs_2_), channel_id=1, source_target_pairs={{0,4},{4,8},{8,12},{12,14},{14,10},{10,6},{6,2},{2,0},{1,5},{5,9},... | collective-permute-start | bytes 786440 | tf_op jit(solution)/shard_map/ppermute | solution.py:322
  18.1 5.0 %dense_second.1 = (f32[128,1024]{1,0:T(8,128)S(1)}, f32[128,1024]{1,0:T(8,128)S(1)}, f32[128,1024]{1,0:T(8,128)S(1)}, f32[128,1024]{1,0:T(8,128)S(1)}, f32[128,1024]{1,0:T(8,128)S(1)}) custom-call(bf16[8,128,128]{2,1,0:T(8,128)(2,1)S(1)} %copy-done.4, bf16[1024,8192]{1,0:T(8,128)(2,1)} %refs_1_.3), custom_call_target="tpu_custom_call" | custom-call | flops 1073741824 | bytes 8388608 | tf_op jit(solution)/shard_map/dense_second/pallas_call | solution.py:39
  23.2 0.7 collective-permute-done.4.refs_4_
  23.9 1.7 %collective-permute-start.6 = (bf16[8,128,128]{2,1,0:T(8,128)(2,1)S(1)}, bf16[8,128,128]{2,1,0:T(8,128)(2,1)S(1)}, u32[]{:S(2)}, u32[]{:S(2)}) collective-permute-start(bf16[8,128,128]{2,1,0:T(8,128)(2,1)S(1)} %collective-permute-done.4.refs_4_), channel_id=1, source_target_pairs={{0,4},{4,8},{8,12},{12,14},{14,10},{10,6},{6,2},{2,0},{1,5},{5,9},... | collective-permute-start | bytes 786440 | tf_op jit(solution)/shard_map/ppermute | solution.py:322
  25.9 2.1 %fold_early.1 = (f32[128,256]{1,0:T(8,128)S(1)}, f32[64,128,128]{2,1,0:T(8,128)S(1)}) custom-call(bf16[8,128,128]{2,1,0:T(8,128)(2,1)S(1)} %copy-done.4, bf16[8,128,128]{2,1,0:T(8,128)(2,1)S(1)} %collective-permute-done.refs_1_, bf16[8,128,128]{2,1,0:T(8,128)(2,1)S(1)} %collective-permute-done.3.refs_2_, ...), custom_call_target="tpu_custom_call" | custom-call | flops 268435456 | bytes 4194304 | tf_op jit(solution)/shard_map/fold_early/pallas_call | solution.py:39
  28.0 2.7 %collective-permute-done.6.refs_1_ = bf16[8,128,128]{2,1,0:T(8,128)(2,1)S(1)} collective-permute-done((bf16[8,128,128]{2,1,0:T(8,128)(2,1)S(1)}, bf16[8,128,128]{2,1,0:T(8,128)(2,1)S(1)}, u32[]{:S(2)}, u32[]{:S(2)}) %collective-permute-start.6) | collective-permute-done | bytes 262176 | tf_op jit(solution)/shard_map/ppermute | solution.py:322
  30.8 1.8 %collective-permute-start.7 = (bf16[4,128,128]{2,1,0:T(8,128)(2,1)S(1)}, bf16[4,128,128]{2,1,0:T(8,128)(2,1)S(1)}, u32[]{:S(2)}, u32[]{:S(2)}) collective-permute-start(bf16[4,128,128]{2,1,0:T(8,128)(2,1)S(1)} %slice.7), channel_id=1, source_target_pairs={{0,4},{4,8},{8,12},{12,14},{14,10},{10,6},{6,2},{2,0},{1,5},{5,9},... | collective-permute-start | bytes 393224 | tf_op jit(solution)/shard_map/ppermute | solution.py:374
  32.9 1.4 %fold_late.1 = (f32[128,256]{1,0:T(8,128)S(1)}, f32[64,128,128]{2,1,0:T(8,128)S(1)}) custom-call(bf16[8,128,128]{2,1,0:T(8,128)(2,1)S(1)} %collective-permute-done.2.refs_0_, bf16[8,128,128]{2,1,0:T(8,128)(2,1)S(1)} %collective-permute-done.6.refs_1_, s32[128,128]{1,0:T(8,128)S(1)} %get-tuple-element.39.refs_5_.refs_2_, bf16[256,8192]{1,0:T(8,128)(2,1)S(1)} %bitcast.17, ...), custom_call_target="tpu_custom_call" | custom-call | flops 134217728 | bytes 1048576 | tf_op jit(solution)/shard_map/fold_late/pallas_call | solution.py:39
  34.3 1.4 %collective-permute-done.7.refs_1_ = bf16[4,128,128]{2,1,0:T(8,128)(2,1)S(1)} collective-permute-done((bf16[4,128,128]{2,1,0:T(8,128)(2,1)S(1)}, bf16[4,128,128]{2,1,0:T(8,128)(2,1)S(1)}, u32[]{:S(2)}, u32[]{:S(2)}) %collective-permute-start.7) | collective-permute-done | bytes 131104 | tf_op jit(solution)/shard_map/ppermute | solution.py:374
  35.8 1.8 %collective-permute-done.5.refs_0_ = bf16[4,128,128]{2,1,0:T(8,128)(2,1)S(1)} collective-permute-done((bf16[4,128,128]{2,1,0:T(8,128)(2,1)S(1)}, bf16[4,128,128]{2,1,0:T(8,128)(2,1)S(1)}, u32[]{:S(2)}, u32[]{:S(2)}) %collective-permute-start.5) | collective-permute-done | bytes 131104 | tf_op jit(solution)/shard_map/ppermute | solution.py:373
  37.6 1.4 %finish.1 = (bf16[128,256]{1,0:T(8,128)(2,1)S(1)}, f32[8,128,128]{2,1,0:T(8,128)S(1)}, bf16[64,1024]{1,0:T(8,128)(2,1)S(1)}, bf16[64,1024]{1,0:T(8,128)(2,1)S(1)}) custom-call(bf16[4,128,128]{2,1,0:T(8,128)(2,1)S(1)} %collective-permute-done.5.refs_0_, bf16[4,128,128]{2,1,0:T(8,128)(2,1)S(1)} %collective-permute-done.7.refs_1_, ...), custom_call_target="tpu_custom_call" | custom-call | flops 268435456 | bytes 2097152 | tf_op jit(solution)/shard_map/finish/pallas_call | solution.py:39
  39.3 1.7 %collective-permute-start.8 = (bf16[64,1024]{1,0:T(8,128)(2,1)S(1)}, bf16[64,1024]{1,0:T(8,128)(2,1)S(1)}, u32[]{:S(2)}, u32[]{:S(2)}) collective-permute-start(bf16[64,1024]{1,0:T(8,128)(2,1)S(1)} %get-tuple-element.59), channel_id=1, source_target_pairs={{0,4},{4,8},{8,12},{12,14},{14,10},{10,6},{6,2},{2,0},{1,5},{5,9},... | collective-permute-start | bytes 393224 | tf_op jit(solution)/shard_map/ppermute | solution.py:414
  41.0 1.3 %part.4 = (f32[128,1024]{1,0:T(8,128)S(1)}, f32[128,1024]{1,0:T(8,128)S(1)}) custom-call(bf16[128,256]{1,0:T(8,128)(2,1)S(1)} %get-tuple-element.67.refs_0_, bf16[256,8192]{1,0:T(8,128)(2,1)S(1)} %bitcast.12, f32[64,128,128]{2,1,0:T(8,128)S(1)} %get-tuple-element.52.refs_10_.refs_2_, f32[8,128,128]{2,1,0:T(8,128)S(1)} %get-tuple-element.55.refs_3_, ...), custom_call_target="tpu_custom_call" | custom-call | flops 134217728 | bytes 2097152 | tf_op jit(solution)/shard_map/part/pallas_call | solution.py:39
  42.3 3.0 %collective-permute-done.11 = bf16[64,1024]{1,0:T(8,128)(2,1)S(1)} collective-permute-done((bf16[64,1024]{1,0:T(8,128)(2,1)S(1)}, bf16[64,1024]{1,0:T(8,128)(2,1)S(1)}, u32[]{:S(2)}, u32[]{:S(2)}) %collective-permute-start.11) | collective-permute-done | bytes 131104 | tf_op jit(solution)/shard_map/ppermute | solution.py:413
  45.8 1.7 %collective-permute-start.9 = (bf16[128,1024]{1,0:T(8,128)(2,1)S(1)}, bf16[128,1024]{1,0:T(8,128)(2,1)S(1)}, u32[]{:S(2)}, u32[]{:S(2)}) collective-permute-start(bf16[128,1024]{1,0:T(8,128)(2,1)S(1)} %add_convert_fusion.6), channel_id=1, source_target_pairs={{0,4},{4,8},{8,12},{12,14},{14,10},{10,6},{6,2},{2,0},{1,5},{5,9},... | collective-permute-start | bytes 786440 | tf_op jit(solution)/shard_map/ppermute | solution.py:429
  47.5 1.3 %part.5 = (f32[128,1024]{1,0:T(8,128)S(1)}, f32[128,1024]{1,0:T(8,128)S(1)}) custom-call(bf16[128,256]{1,0:T(8,128)(2,1)S(1)} %get-tuple-element.67.refs_0_, bf16[256,8192]{1,0:T(8,128)(2,1)S(1)} %bitcast.13, f32[64,128,128]{2,1,0:T(8,128)S(1)} %get-tuple-element.52.refs_10_.refs_2_, f32[8,128,128]{2,1,0:T(8,128)S(1)} %get-tuple-element.55.refs_3_, ...), custom_call_target="tpu_custom_call" | custom-call | flops 134217728 | bytes 2097152 | tf_op jit(solution)/shard_map/part/pallas_call | solution.py:39
  48.8 5.4 %collective-permute-done.12 = bf16[128,1024]{1,0:T(8,128)(2,1)S(1)} collective-permute-done((bf16[128,1024]{1,0:T(8,128)(2,1)S(1)}, bf16[128,1024]{1,0:T(8,128)(2,1)S(1)}, u32[]{:S(2)}, u32[]{:S(2)}) %collective-permute-start.12) | collective-permute-done | bytes 262176 | tf_op jit(solution)/shard_map/ppermute | solution.py:428
  54.2 0.7 collective-permute-start.13
  55.0 1.4 %collective-permute-start.10 = (bf16[128,1024]{1,0:T(8,128)(2,1)S(1)}, bf16[128,1024]{1,0:T(8,128)(2,1)S(1)}, u32[]{:S(2)}, u32[]{:S(2)}) collective-permute-start(bf16[128,1024]{1,0:T(8,128)(2,1)S(1)} %add_convert_fusion.5), channel_id=1, source_target_pairs={{0,4},{4,8},{8,12},{12,14},{14,10},{10,6},{6,2},{2,0},{1,5},{5,9},... | collective-permute-start | bytes 786440 | tf_op jit(solution)/shard_map/ppermute | solution.py:429
  56.4 1.3 %part.6 = (f32[128,1024]{1,0:T(8,128)S(1)}, f32[128,1024]{1,0:T(8,128)S(1)}) custom-call(bf16[128,256]{1,0:T(8,128)(2,1)S(1)} %get-tuple-element.67.refs_0_, bf16[256,8192]{1,0:T(8,128)(2,1)S(1)} %bitcast.14, f32[64,128,128]{2,1,0:T(8,128)S(1)} %get-tuple-element.52.refs_10_.refs_2_, f32[8,128,128]{2,1,0:T(8,128)S(1)} %get-tuple-element.55.refs_3_, ...), custom_call_target="tpu_custom_call" | custom-call | flops 134217728 | bytes 2097152 | tf_op jit(solution)/shard_map/part/pallas_call | solution.py:39
  57.7 4.6 %collective-permute-done.13 = bf16[128,1024]{1,0:T(8,128)(2,1)S(1)} collective-permute-done((bf16[128,1024]{1,0:T(8,128)(2,1)S(1)}, bf16[128,1024]{1,0:T(8,128)(2,1)S(1)}, u32[]{:S(2)}, u32[]{:S(2)}) %collective-permute-start.13) | collective-permute-done | bytes 262176 | tf_op jit(solution)/shard_map/ppermute | solution.py:428
  62.3 0.9 %collective-permute-start.14 = (bf16[128,1024]{1,0:T(8,128)(2,1)S(1)}, bf16[128,1024]{1,0:T(8,128)(2,1)S(1)}, u32[]{:S(2)}, u32[]{:S(2)}) collective-permute-start(bf16[128,1024]{1,0:T(8,128)(2,1)S(1)} %add_convert_fusion.1), channel_id=1, source_target_pairs={{4,0},{8,4},{12,8},{14,12},{10,14},{6,10},{2,6},{0,2},{5,1},{9,5},... | collective-permute-start | bytes 786440 | tf_op jit(solution)/shard_map/ppermute | solution.py:428
  63.3 1.2 %collective-permute-start.15 = (bf16[128,1024]{1,0:T(8,128)(2,1)S(1)}, bf16[128,1024]{1,0:T(8,128)(2,1)S(1)}, u32[]{:S(2)}, u32[]{:S(2)}) collective-permute-start(bf16[128,1024]{1,0:T(8,128)(2,1)S(1)} %add_convert_fusion.4), channel_id=1, source_target_pairs={{0,4},{4,8},{8,12},{12,14},{14,10},{10,6},{6,2},{2,0},{1,5},{5,9},... | collective-permute-start | bytes 786440 | tf_op jit(solution)/shard_map/ppermute | solution.py:429
  64.5 0.9 %part.7 = f32[128,1024]{1,0:T(8,128)S(1)} custom-call(bf16[128,256]{1,0:T(8,128)(2,1)S(1)} %get-tuple-element.67.refs_0_, bf16[256,8192]{1,0:T(8,128)(2,1)S(1)} %bitcast.15, f32[64,128,128]{2,1,0:T(8,128)S(1)} %get-tuple-element.52.refs_10_.refs_2_, f32[8,128,128]{2,1,0:T(8,128)S(1)} %get-tuple-element.55.refs_3_, f32[4,16]{1,0:T(4,128)S(1)} %copy-done.5, ...), custom_call_target="tpu_custom_call" | custom-call | flops 134217728 | bytes 2097152 | tf_op jit(solution)/shard_map/part/pallas_call | solution.py:39
  65.5 3.3 %collective-permute-done.14 = bf16[128,1024]{1,0:T(8,128)(2,1)S(1)} collective-permute-done((bf16[128,1024]{1,0:T(8,128)(2,1)S(1)}, bf16[128,1024]{1,0:T(8,128)(2,1)S(1)}, u32[]{:S(2)}, u32[]{:S(2)}) %collective-permute-start.14) | collective-permute-done | bytes 262176 | tf_op jit(solution)/shard_map/ppermute | solution.py:428
  68.8 1.0 %collective-permute-done.15 = bf16[128,1024]{1,0:T(8,128)(2,1)S(1)} collective-permute-done((bf16[128,1024]{1,0:T(8,128)(2,1)S(1)}, bf16[128,1024]{1,0:T(8,128)(2,1)S(1)}, u32[]{:S(2)}, u32[]{:S(2)}) %collective-permute-start.15) | collective-permute-done | bytes 262176 | tf_op jit(solution)/shard_map/ppermute | solution.py:429
  69.7 0.8 %add_convert_fusion = bf16[128,1024]{1,0:T(8,128)(2,1)} fusion(bf16[128,1024]{1,0:T(8,128)(2,1)S(1)} %collective-permute-done.15, f32[128,1024]{1,0:T(8,128)S(1)} %part.7, bf16[128,1024]{1,0:T(8,128)(2,1)S(1)} %collective-permute-done.14), kind=kLoop, calls=%fused_computation | loop fusion | flops 655360 | bytes 1310720 | tf_op jit(solution)/shard_map/convert_element_type | solution.py:430
  (39 shorter events, 3.2 us)
Async XLA Ops:
  5.6 10.4 %collective-permute-start.3 = (bf16[8,128,128]{2,1,0:T(8,128)(2,1)}, bf16[8,128,128]{2,1,0:T(8,128)(2,1)S(1)}, u32[]{:S(2)}, u32[]{:S(2)}) collective-permute-start(bf16[8,128,128]{2,1,0:T(8,128)(2,1)} %attend.1.refs_0_), channel_id=1, source_target_pairs={{0,4},{4,8},{8,12},{12,14},{14,10},{10,6},{6,2},{2,0},{1,5},{5,9},... | collective-permute-start | bytes 786440 | tf_op jit(solution)/shard_map/ppermute | solution.py:322
  8.6 9.5 %collective-permute-start = (bf16[8,128,128]{2,1,0:T(8,128)(2,1)}, bf16[8,128,128]{2,1,0:T(8,128)(2,1)S(1)}, u32[]{:S(2)}, u32[]{:S(2)}) collective-permute-start(bf16[8,128,128]{2,1,0:T(8,128)(2,1)} %attend.1.refs_0_), channel_id=1, source_target_pairs={{4,0},{8,4},{12,8},{14,12},{10,14},{6,10},{2,6},{0,2},{5,1},{9,5},... | collective-permute-start | bytes 786440 | tf_op jit(solution)/shard_map/ppermute | solution.py:321
  8.6 1.0 %copy-start.3 = (bf16[8,128,128]{2,1,0:T(8,128)(2,1)S(1)}, bf16[8,128,128]{2,1,0:T(8,128)(2,1)}, u32[]{:S(2)}) copy-start(bf16[8,128,128]{2,1,0:T(8,128)(2,1)} %attend.1.refs_0_) | copy-start | bytes 786436
  9.6 0.7 copy-start.7
  10.3 0.7 copy-start.8
  11.0 0.7 copy-start.9
  11.6 6.5 %copy-start.4 = (bf16[8,128,128]{2,1,0:T(8,128)(2,1)S(1)}, bf16[8,128,128]{2,1,0:T(8,128)(2,1)}, u32[]{:S(2)}) copy-start(bf16[8,128,128]{2,1,0:T(8,128)(2,1)} %attend.1.refs_0_) | copy-start | bytes 786436
  16.0 9.9 %copy-start.1 = (bf16[4,8192,64]{1,2,0:T(8,128)(2,1)S(1)}, bf16[4,8192,64]{1,2,0:T(8,128)(2,1)}, u32[]{:S(2)}) copy-start(bf16[4,8192,64]{1,2,0:T(8,128)(2,1)} %param.24) | copy-start | bytes 12582916
  16.0 9.9 %copy-start.2 = (bf16[4,16,128,128]{3,2,1,0:T(8,128)(2,1)S(1)}, bf16[4,16,128,128]{3,2,1,0:T(8,128)(2,1)}, u32[]{:S(2)}) copy-start(bf16[4,16,128,128]{3,2,1,0:T(8,128)(2,1)} %refs_4_.7) | copy-start | bytes 6291460
  16.0 9.9 %copy-start.5 = (f32[4,16]{1,0:T(4,128)S(1)}, f32[4,16]{1,0:T(4,128)}, u32[]{:S(2)}) copy-start(f32[4,16]{1,0:T(4,128)} %refs_4_.11) | copy-start | bytes 772
  16.0 9.9 %copy-start.6 = (s32[4,16]{1,0:T(4,128)S(1)}, s32[4,16]{1,0:T(4,128)}, u32[]{:S(2)}) copy-start(s32[4,16]{1,0:T(4,128)} %refs_5_.11) | copy-start | bytes 772
  16.0 7.8 %collective-permute-start.4 = (bf16[8,128,128]{2,1,0:T(8,128)(2,1)S(1)}, bf16[8,128,128]{2,1,0:T(8,128)(2,1)S(1)}, u32[]{:S(2)}, u32[]{:S(2)}) collective-permute-start(bf16[8,128,128]{2,1,0:T(8,128)(2,1)S(1)} %collective-permute-done.3.refs_2_), channel_id=1, source_target_pairs={{0,4},{4,8},{8,12},{12,14},{14,10},{10,6},{6,2},{2,0},{1,5},{5,9},... | collective-permute-start | bytes 786440 | tf_op jit(solution)/shard_map/ppermute | solution.py:322
  18.1 7.5 %collective-permute-start.1 = (bf16[8,128,128]{2,1,0:T(8,128)(2,1)S(1)}, bf16[8,128,128]{2,1,0:T(8,128)(2,1)S(1)}, u32[]{:S(2)}, u32[]{:S(2)}) collective-permute-start(bf16[8,128,128]{2,1,0:T(8,128)(2,1)S(1)} %collective-permute-done.refs_1_), channel_id=1, source_target_pairs={{4,0},{8,4},{12,8},{14,12},{10,14},{6,10},{2,6},{0,2},{5,1},{9,5},... | collective-permute-start | bytes 786440 | tf_op jit(solution)/shard_map/ppermute | solution.py:321
  23.9 6.9 %collective-permute-start.6 = (bf16[8,128,128]{2,1,0:T(8,128)(2,1)S(1)}, bf16[8,128,128]{2,1,0:T(8,128)(2,1)S(1)}, u32[]{:S(2)}, u32[]{:S(2)}) collective-permute-start(bf16[8,128,128]{2,1,0:T(8,128)(2,1)S(1)} %collective-permute-done.4.refs_4_), channel_id=1, source_target_pairs={{0,4},{4,8},{8,12},{12,14},{14,10},{10,6},{6,2},{2,0},{1,5},{5,9},... | collective-permute-start | bytes 786440 | tf_op jit(solution)/shard_map/ppermute | solution.py:322
  25.6 7.0 %collective-permute-start.2 = (bf16[8,128,128]{2,1,0:T(8,128)(2,1)S(1)}, bf16[8,128,128]{2,1,0:T(8,128)(2,1)S(1)}, u32[]{:S(2)}, u32[]{:S(2)}) collective-permute-start(bf16[8,128,128]{2,1,0:T(8,128)(2,1)S(1)} %collective-permute-done.1.refs_3_), channel_id=1, source_target_pairs={{4,0},{8,4},{12,8},{14,12},{10,14},{6,10},{2,6},{0,2},{5,1},{9,5},... | collective-permute-start | bytes 786440 | tf_op jit(solution)/shard_map/ppermute | solution.py:321
  30.8 5.0 %collective-permute-start.7 = (bf16[4,128,128]{2,1,0:T(8,128)(2,1)S(1)}, bf16[4,128,128]{2,1,0:T(8,128)(2,1)S(1)}, u32[]{:S(2)}, u32[]{:S(2)}) collective-permute-start(bf16[4,128,128]{2,1,0:T(8,128)(2,1)S(1)} %slice.7), channel_id=1, source_target_pairs={{0,4},{4,8},{8,12},{12,14},{14,10},{10,6},{6,2},{2,0},{1,5},{5,9},... | collective-permute-start | bytes 393224 | tf_op jit(solution)/shard_map/ppermute | solution.py:374
  32.5 5.0 %collective-permute-start.5 = (bf16[4,128,128]{2,1,0:T(8,128)(2,1)S(1)}, bf16[4,128,128]{2,1,0:T(8,128)(2,1)S(1)}, u32[]{:S(2)}, u32[]{:S(2)}) collective-permute-start(bf16[4,128,128]{2,1,0:T(8,128)(2,1)S(1)} %slice.6), channel_id=1, source_target_pairs={{4,0},{8,4},{12,8},{14,12},{10,14},{6,10},{2,6},{0,2},{5,1},{9,5},... | collective-permute-start | bytes 393224 | tf_op jit(solution)/shard_map/ppermute | solution.py:373
  32.9 4.7 %copy-start = (bf16[4,64,8192]{2,1,0:T(8,128)(2,1)S(1)}, bf16[4,64,8192]{2,1,0:T(8,128)(2,1)}, u32[]{:S(2)}) copy-start(bf16[4,64,8192]{2,1,0:T(8,128)(2,1)} %param.25) | copy-start | bytes 12582916
  38.9 6.4 %collective-permute-start.11 = (bf16[64,1024]{1,0:T(8,128)(2,1)S(1)}, bf16[64,1024]{1,0:T(8,128)(2,1)S(1)}, u32[]{:S(2)}, u32[]{:S(2)}) collective-permute-start(bf16[64,1024]{1,0:T(8,128)(2,1)S(1)} %get-tuple-element.72), channel_id=1, source_target_pairs={{4,0},{8,4},{12,8},{14,12},{10,14},{6,10},{2,6},{0,2},{5,1},{9,5},... | collective-permute-start | bytes 393224 | tf_op jit(solution)/shard_map/ppermute | solution.py:413
  39.3 6.4 %collective-permute-start.8 = (bf16[64,1024]{1,0:T(8,128)(2,1)S(1)}, bf16[64,1024]{1,0:T(8,128)(2,1)S(1)}, u32[]{:S(2)}, u32[]{:S(2)}) collective-permute-start(bf16[64,1024]{1,0:T(8,128)(2,1)S(1)} %get-tuple-element.59), channel_id=1, source_target_pairs={{0,4},{4,8},{8,12},{12,14},{14,10},{10,6},{6,2},{2,0},{1,5},{5,9},... | collective-permute-start | bytes 393224 | tf_op jit(solution)/shard_map/ppermute | solution.py:414
  45.4 8.8 %collective-permute-start.12 = (bf16[128,1024]{1,0:T(8,128)(2,1)S(1)}, bf16[128,1024]{1,0:T(8,128)(2,1)S(1)}, u32[]{:S(2)}, u32[]{:S(2)}) collective-permute-start(bf16[128,1024]{1,0:T(8,128)(2,1)S(1)} %add_convert_fusion.3), channel_id=1, source_target_pairs={{4,0},{8,4},{12,8},{14,12},{10,14},{6,10},{2,6},{0,2},{5,1},{9,5},... | collective-permute-start | bytes 786440 | tf_op jit(solution)/shard_map/ppermute | solution.py:428
  45.8 9.1 %collective-permute-start.9 = (bf16[128,1024]{1,0:T(8,128)(2,1)S(1)}, bf16[128,1024]{1,0:T(8,128)(2,1)S(1)}, u32[]{:S(2)}, u32[]{:S(2)}) collective-permute-start(bf16[128,1024]{1,0:T(8,128)(2,1)S(1)} %add_convert_fusion.6), channel_id=1, source_target_pairs={{0,4},{4,8},{8,12},{12,14},{14,10},{10,6},{6,2},{2,0},{1,5},{5,9},... | collective-permute-start | bytes 786440 | tf_op jit(solution)/shard_map/ppermute | solution.py:429
  54.2 8.0 %collective-permute-start.13 = (bf16[128,1024]{1,0:T(8,128)(2,1)S(1)}, bf16[128,1024]{1,0:T(8,128)(2,1)S(1)}, u32[]{:S(2)}, u32[]{:S(2)}) collective-permute-start(bf16[128,1024]{1,0:T(8,128)(2,1)S(1)} %add_convert_fusion.2), channel_id=1, source_target_pairs={{4,0},{8,4},{12,8},{14,12},{10,14},{6,10},{2,6},{0,2},{5,1},{9,5},... | collective-permute-start | bytes 786440 | tf_op jit(solution)/shard_map/ppermute | solution.py:428
  55.0 8.3 %collective-permute-start.10 = (bf16[128,1024]{1,0:T(8,128)(2,1)S(1)}, bf16[128,1024]{1,0:T(8,128)(2,1)S(1)}, u32[]{:S(2)}, u32[]{:S(2)}) collective-permute-start(bf16[128,1024]{1,0:T(8,128)(2,1)S(1)} %add_convert_fusion.5), channel_id=1, source_target_pairs={{0,4},{4,8},{8,12},{12,14},{14,10},{10,6},{6,2},{2,0},{1,5},{5,9},... | collective-permute-start | bytes 786440 | tf_op jit(solution)/shard_map/ppermute | solution.py:429
  62.3 6.4 %collective-permute-start.14 = (bf16[128,1024]{1,0:T(8,128)(2,1)S(1)}, bf16[128,1024]{1,0:T(8,128)(2,1)S(1)}, u32[]{:S(2)}, u32[]{:S(2)}) collective-permute-start(bf16[128,1024]{1,0:T(8,128)(2,1)S(1)} %add_convert_fusion.1), channel_id=1, source_target_pairs={{4,0},{8,4},{12,8},{14,12},{10,14},{6,10},{2,6},{0,2},{5,1},{9,5},... | collective-permute-start | bytes 786440 | tf_op jit(solution)/shard_map/ppermute | solution.py:428
  63.3 6.4 %collective-permute-start.15 = (bf16[128,1024]{1,0:T(8,128)(2,1)S(1)}, bf16[128,1024]{1,0:T(8,128)(2,1)S(1)}, u32[]{:S(2)}, u32[]{:S(2)}) collective-permute-start(bf16[128,1024]{1,0:T(8,128)(2,1)S(1)} %add_convert_fusion.4), channel_id=1, source_target_pairs={{0,4},{4,8},{8,12},{12,14},{14,10},{10,6},{6,2},{2,0},{1,5},{5,9},... | collective-permute-start | bytes 786440 | tf_op jit(solution)/shard_map/ppermute | solution.py:429

commit v5 on v4

--- a/solution.py
+++ b/solution.py
@@ -74,7 +74,7 @@
     for copy in small:
         copy.wait()
     tall, wide = heads * ROW_BLOCK, cache * ROW_BLOCK
-    scale = 1.0 / math.sqrt(side)
+    scale = math.log2(math.e) / math.sqrt(side)
     lengths = jnp.transpose(jnp.broadcast_to(length_ref[...].astype(F32), (rows, rows)))[:, :1]
     row_in = lax.broadcasted_iota(jnp.int32, (tall, wide), 0) % ROW_BLOCK
     place = (lax.broadcasted_iota(jnp.int32, (tall, wide), 1) - cache * row_in).astype(F32)
@@ -91,34 +91,32 @@
         new_key = jnp.concatenate([new_key_ref[here].astype(F32)] * heads, axis=0)
         new_value = jnp.concatenate([new_value_ref[here].astype(F32)] * heads, axis=0)
         live = place < jnp.concatenate([lengths[here]] * heads, axis=0)
-        scores = lax.dot_general(query, key_ref[cached], NT, preferred_element_type=F32) * scale
-        fresh = jnp.sum(query.astype(F32) * new_key, axis=1, keepdims=True) * scale
-        scores = jnp.where(live, scores, -1e30)
+        scores = lax.dot_general(query, key_ref[cached], NT, preferred_element_type=F32)
+        fresh = jnp.sum(query.astype(F32) * new_key, axis=1, keepdims=True)
+        scores = jnp.where(live, scores, -jnp.inf)
         top = jnp.maximum(jnp.max(scores, axis=1, keepdims=True), fresh)
-        raw = jnp.where(live, jnp.exp(scores - top), 0.0)
-        fresh_raw = jnp.exp(fresh - top)
+        raw = jnp.exp2((scores - top) * scale)
+        fresh_raw = jnp.exp2((fresh - top) * scale)
         inverse = 1.0 / (jnp.sum(raw, axis=1, keepdims=True) + fresh_raw)
-        weights = (raw * inverse).astype(BF16)
-        fresh_weight = (fresh_raw * inverse).astype(BF16).astype(F32)
-        attended = jnp.dot(weights, value_ref[cached], preferred_element_type=F32)
-        attended = (attended + fresh_weight * new_value).astype(BF16)
+        attended = jnp.dot(raw.astype(BF16), value_ref[cached], preferred_element_type=F32)
+        attended = ((attended + fresh_raw * new_value) * inverse).astype(BF16)
         for h in range(heads):
             out_ref[h, here, :] = attended[h * ROW_BLOCK : (h + 1) * ROW_BLOCK]
 
 
-def dense_kernel(distances, count, first, *refs):
-    x_ref, weight_ref = refs[:2]
-    if first:
+def dense_kernel(distances, count, listing, *refs):
+    x_hbm, weight_ref = refs[:2]
+    if listing:
         variant_ref, holder_ref, owner_ref = refs[2:5]
-        outs, slot_ref, table_ref = refs[5 : 5 + len(distances)], refs[-4], refs[-3]
+        outs, slot_ref, table_ref = refs[5 : 5 + len(distances)], refs[-6], refs[-5]
     else:
         outs = refs[2 : 2 + len(distances)]
-    buffers, sems = refs[-2:]
-    heads, rows, side = x_ref.shape
+    x_ref, buffers, sems, x_sem = refs[-4:]
+    heads, rows, side = x_hbm.shape
     width = heads * side
     depth = buffers.shape[0]
-    cuts = 2 if width >= 512 else 1
-    piece = width // cuts
+    piece = buffers.shape[2]
+    cuts = width // piece
 
     def fetch(i):
         start = pl.multiple_of(owner_at(distances[i // cuts], count) * width, width) + i % cuts * piece
@@ -128,10 +126,12 @@
             sems.at[i % depth],
         )
 
+    own = pltpu.make_async_copy(x_hbm, x_ref, x_sem)
+    own.start()
     total = len(distances) * cuts
     for i in range(min(depth, total)):
         fetch(i).start()
-    if first:
+    if listing:
         slots = owner_ref.shape[0]
         variant = variant_ref[...]
         slot_row = jnp.zeros(variant.shape, jnp.int32)
@@ -149,6 +149,7 @@
                 return carry
 
             lax.fori_loop(0, owner_ref.shape[1], note, 0)
+    own.wait()
     x = jnp.concatenate([x_ref[h] for h in range(heads)], axis=1)
     for i in range(total):
         fetch(i).wait()
@@ -209,16 +210,17 @@
             block_ref[column] += product
 
 
-def part_for(distance, count, low, second_ref, dense_ref, block_ref, extra_ref, columns, out_ref):
-    rows, width = dense_ref.shape
+def part_for(distance, count, low_ref, second_ref, dense_ref, block_ref, extra_ref, columns, rows,
+             out_ref):
+    width = dense_ref.shape[1]
     side = block_ref.shape[2]
     heads = width // side
     owner = owner_at(distance, count)
     start = pl.multiple_of(owner * width, width)
-    blocks = jnp.concatenate([block_ref[owner * heads + i] for i in range(heads)], axis=1)
+    blocks = jnp.concatenate([block_ref[owner * heads + i, rows] for i in range(heads)], axis=1)
     out_ref[...] = (
-        jnp.dot(low, second_ref[:, pl.ds(start, width)], preferred_element_type=F32)
-        + dense_ref[...]
+        jnp.dot(low_ref[rows], second_ref[:, pl.ds(start, width)], preferred_element_type=F32)
+        + dense_ref[rows]
         + blocks
     )
     for e, column in enumerate(columns):
@@ -226,7 +228,7 @@
         @pl.when(lax.div(column, heads) == owner)
         def _(e=e, column=column):
             place = pl.ds(pl.multiple_of(lax.rem(column, heads) * side, side), side)
-            out_ref[:, place] += extra_ref[e]
+            out_ref[:, place] += extra_ref[e, rows]
 
 
 def finish_kernel(distance, count, *refs):
@@ -250,20 +252,41 @@
     slots_wide = jnp.concatenate([slot] * -(-low_width // side), axis=1)[:, :low_width]
     low = jnp.where(slots_wide == held, low_sum[...], 0.0).astype(BF16)
     low_out[...] = low
-    part_for(distance, count, low, second_ref, dense_ref, block_ref, extra_out, columns, farthest)
+    part_for(distance, count, low_out, second_ref, dense_ref, block_ref, extra_out, columns,
+             slice(0, rows), farthest)
     top_out[...] = farthest[: rows // 2].astype(BF16)
     bottom_out[...] = farthest[rows // 2 :].astype(BF16)
 
 
-def part_kernel(distances, count, slots, *refs):
+def join_kernel(jobs, count, slots, *refs):
     low_ref, second_ref, block_ref, extra_ref, scale_ref, cell_ref, table_ref = refs[:7]
-    dense_refs = refs[7 : 7 + len(distances)]
-    outs = refs[7 + len(distances) :]
-    heads = dense_refs[0].shape[1] // block_ref.shape[2]
+    dense_refs, refs = refs[7 : 7 + len(jobs)], refs[7 + len(jobs) :]
+    came, outs, totals = refs[: -2 * len(jobs)], refs[-2 * len(jobs) : -len(jobs)], refs[-len(jobs) :]
+    rows, width = dense_refs[0].shape
+    heads = width // block_ref.shape[2]
     listed = held_blocks(count // 2, count, slots, heads, scale_ref, cell_ref, table_ref)
     columns = [entry[-1] for entry in listed]
-    for distance, dense_ref, out in zip(distances, dense_refs, outs):
-        part_for(distance, count, low_ref[...], second_ref, dense_ref, block_ref, extra_ref, columns, out)
+    for n, (distance, half) in enumerate(jobs):
+        here = slice(half * rows // 2, (half + 1) * rows // 2)
+        part_for(distance, count, low_ref, second_ref, dense_refs[n], block_ref, extra_ref, columns,
+                 here, totals[n])
+        total = totals[n][...]
+        if came:
+            total = total + came[n][...].astype(F32)
+        outs[n][...] = total.astype(outs[n].dtype)
+
+
+def sum_kernel(upper_ref, lower_ref, *refs):
+    out_ref = refs[-1]
+    cut = upper_ref.shape[0]
+    upper, lower = upper_ref[...], lower_ref[...]
+    for n, ref in enumerate(refs[:-1]):
+        if n in (0, 2):
+            upper = upper + ref[...].astype(F32)
+        else:
+            lower = lower + ref[...].astype(F32)
+    out_ref[:cut] = upper.astype(BF16)
+    out_ref[cut:] = lower.astype(BF16)
 
 
 def after(value, *others):
@@ -307,11 +330,28 @@
     for distance in range(half - 1, 0, -1):
         wanted += [distance, count - distance]
     wanted += [0]
-    cut = max(half - 1, 1)
     piece = width // 2 if width >= 512 else width
-    streams = [pltpu.VMEM((4, width, piece), BF16), pltpu.SemaphoreType.DMA((4,))]
-    dense_cost = dict(flops=rows * width * complete, moved=width * complete)
     dense = {}
+
+    def dense_for(distances, x, listing=False):
+        extra_shapes = [shape((rows, rows), jnp.int32), shape((count * slots * CAP,), jnp.int32)]
+        extra_ins = (request_variant[None, :], holder_slot, block_owner[:, :, 0])
+        got = call(
+            functools.partial(dense_kernel, distances, count, listing),
+            "dense",
+            [shape((rows, width), F32)] * len(distances) + extra_shapes * listing,
+            (x, out_weight) + extra_ins * listing,
+            [ANY, ANY] + [VMEM, SMEM, SMEM] * listing,
+            [VMEM] * len(distances) + [VMEM, SMEM] * listing,
+            [pltpu.VMEM((heads, rows, side), BF16), pltpu.VMEM((4, width, piece), BF16),
+             pltpu.SemaphoreType.DMA((4,)), pltpu.SemaphoreType.DMA],
+            limit=40,
+            flops=2 * rows * width * width * len(distances),
+            moved=2 * width * width * len(distances),
+        )
+        dense.update(zip(distances, got))
+        return got[len(distances) :] if listing else got[0]
+
     chunks = {0: attended}
 
     def pass_on(step, *done):
@@ -321,35 +361,14 @@
         chunks[step] = lax.ppermute(right, "tp", to_left)
         chunks[count - step] = lax.ppermute(left, "tp", to_right)
 
+    third = -(-3 * count // 8)
     pass_on(1)
-    *sums, slot, table = call(
-        functools.partial(dense_kernel, wanted[:cut], count, True),
-        "dense_first",
-        [shape((rows, width), F32)] * cut
-        + [shape((rows, rows), jnp.int32), shape((count * slots * CAP,), jnp.int32)],
-        (attended, out_weight, request_variant[None, :], holder_slot, block_owner[:, :, 0]),
-        [VMEM, ANY, VMEM, SMEM, SMEM],
-        [VMEM] * cut + [VMEM, SMEM],
-        streams,
-        limit=40,
-        **dense_cost,
-    )
-    dense.update(zip(wanted[:cut], sums))
-    pass_on(2, slot)
-    sums = call(
-        functools.partial(dense_kernel, wanted[cut:], count, False),
-        "dense_second",
-        [shape((rows, width), F32)] * (count - cut),
-        (after(attended, slot), out_weight),
-        [VMEM, ANY],
-        [VMEM] * (count - cut),
-        streams,
-        limit=40,
-        **dense_cost,
-    )
-    dense.update(zip(wanted[cut:], sums))
+    token = dense_for(wanted[:third], attended)
+    pass_on(2, token)
+    slot, table = dense_for(wanted[third : 2 * third], after(attended, token), True)
     for step in range(3, half):
-        pass_on(step, sums[0])
+        pass_on(step, slot)
+    token = dense_for(wanted[2 * third :], after(attended, slot))
 
     factor_t = jnp.swapaxes(factor_in, 1, 2).reshape(low_width, -1)
     second = second_factor.reshape(low_width, complete)
@@ -370,8 +389,8 @@
         flops=rows * low_width * complete,
         moved=4 * MIB,
     )
-    front = lax.ppermute(after(chunks[half - 1], low)[: heads // 2], "tp", to_left)
-    back = lax.ppermute(after(chunks[count - half + 1], low)[heads // 2 :], "tp", to_right)
+    front = lax.ppermute(after(chunks[half - 1], low, token)[: heads // 2], "tp", to_left)
+    back = lax.ppermute(after(chunks[count - half + 1], low, token)[heads // 2 :], "tp", to_right)
     low, blocks = call(
         functools.partial(fold_kernel, late, count, False),
         "fold_late",
@@ -397,37 +416,44 @@
         moved=2 * MIB,
     )
 
-    def parts_for(pair, low):
-        sums = call(
-            functools.partial(part_kernel, pair, count, slots),
-            "part",
-            [shape((rows, width), F32)] * len(pair),
-            (low, second, blocks, extra, block_scale, block_cell, table, *[dense[d] for d in pair]),
-            [VMEM] * 4 + [SMEM] * 3 + [VMEM] * len(pair),
-            [VMEM] * len(pair),
-            flops=rows * low_width * width * 4,
-            moved=2 * MIB,
-        )
-        return sums
-
-    left = lax.ppermute(top, "tp", to_left)
-    right = lax.ppermute(bottom, "tp", to_right)
+    def join(jobs, came, low, kind=BF16):
+        return call(
+            functools.partial(join_kernel, jobs, count, slots),
+            "join",
+            [shape((rows // 2, width), kind)] * len(jobs),
+            (low, second, blocks, extra, block_scale, block_cell, table,
+             *[dense[distance] for distance, _ in jobs], *came),
+            [VMEM] * 4 + [SMEM] * 3 + [VMEM] * (len(jobs) + len(came)),
+            [VMEM] * len(jobs),
+            [pltpu.VMEM((rows // 2, width), F32)] * len(jobs),
+            flops=rows * low_width * width * 2,
+            moved=MIB,
+        )
+
+    far, near = (top, bottom), ()
+    for distance in range(half, 0, -1):
+        if distance < half:
+            far = join([(count - distance, 0), (distance, 1)], far, low)
+        ready = far
+        far = [lax.ppermute(far[0], "tp", to_left), lax.ppermute(far[1], "tp", to_right)]
+        if distance > 1:
+            near = join([(count - distance + 1, 1), (distance - 1, 0)], near, low)
+            near = [lax.ppermute(near[0], "tp", to_left), lax.ppermute(near[1], "tp", to_right)]
+    own = join([(0, 0), (0, 1)], (), after(low, *ready), F32)
+    up_left, low_right = far
     if half > 1:
-        other, mine = parts_for([half - 1, count - half + 1], low)
-    for distance in range(half - 1, 0, -1):
-        if distance == half - 1:
-            none = jnp.zeros_like(left)
-            left = jnp.concatenate([left, none], axis=0)
-            right = jnp.concatenate([none, right], axis=0)
-        sent_left = (mine + left.astype(F32)).astype(BF16)
-        sent_right = (other + right.astype(F32)).astype(BF16)
-        if distance > 1:
-            other, mine = parts_for([distance - 1, count - distance + 1], after(low, sent_right))
-        else:
-            (own,) = parts_for([0], after(low, sent_right))
-        left = lax.ppermute(sent_left, "tp", to_left)
-        right = lax.ppermute(sent_right, "tp", to_right)
-    return (own + left.astype(F32) + right.astype(F32)).astype(BF16)
+        low_left, up_right = near
+    came = [up_left, low_right] if half == 1 else [up_left, low_right, up_right, low_left]
+    return call(
+        sum_kernel,
+        "sum_up",
+        shape((rows, width), BF16),
+        (*own, *came),
+        [VMEM] * (2 + len(came)),
+        VMEM,
+        flops=1,
+        moved=1,
+    )
 
 
 def solution(mesh):

time: 70.8 us -> 68.7 us (0.970)
  waiting for transfers between devices: 23.8 us -> 13.6 us
  starting transfers between devices: 17.8 us -> 24 us
  Pallas kernels: 24.6 us -> 29.7 us
  local copies, waits for them, and re-layouts: 3.05 us -> 1.05 us
  other arithmetic: 1.09 us -> 0 us
    ppermute x10 -> x16, waiting for transfers between devices: 20.4 us -> 10.5 us  [the longest x4 5.03 us: body(): lax.ppermute(far[1], 'tp', to_right)]
    ppermute x10 -> x16, starting transfers between devices: 10.6 us -> 16.8 us  [the longest x4 5.44 us: body(): lax.ppermute(far[0], 'tp', to_left)]
    pallas_call x10 -> x15, Pallas kernels: 24.6 us -> 29.7 us  [call(): pl.pallas_call(kernel, out_shape=outs, in_specs=specs, out_specs=out_spec...]
    unnamed x20 -> x18, local copies, waits for them, and re-layouts: 3.03 us -> 1.03 us
    convert_element_type x7 -> x0, other arithmetic: 1.09 us -> none  [the longest x1 0.8 us: body(): return (own + left.astype(F32) + right.astype(F32)).astype(BF16)]
  transfers between devices with their start and end apart: 16 -> 22, of which waited for: 9 -> 12; matrix products, arithmetic and copies ran while one was open for 0% -> 0% of each run, Pallas kernels for 25% -> 33%
where the time goes in v5:
time: 68.7 us; the launch traced here: 68.5 us
  Pallas kernels  29.7 us (43%)
  starting transfers between devices  24 us (35%)
  waiting for transfers between devices  13.6 us (20%)
  local copies, waits for them, and re-layouts  1.05 us (2%)
    pallas_call x15, Pallas kernels, call(): pl.pallas_call(kernel, out_shape=outs, in_specs=specs, out_specs=out_spec...  29.7 us
    ppermute x3, starting transfers between devices, pass_on(): chunks[count - step] = lax.ppermute(left, 'tp', to_right)  6.39 us
    ppermute x4, starting transfers between devices, body(): lax.ppermute(far[0], 'tp', to_left)  5.44 us
    ppermute x4, waiting for transfers between devices, body(): lax.ppermute(far[1], 'tp', to_right)  5.03 us
    ppermute x3, starting transfers between devices, body(): lax.ppermute(near[0], 'tp', to_left)  3.19 us
    ppermute x3, starting transfers between devices, body(): lax.ppermute(near[1], 'tp', to_right)  3.11 us
    ppermute x3, waiting for transfers between devices, pass_on(): chunks[count - step] = lax.ppermute(left, 'tp', to_right)  3.04 us
    ppermute x4, starting transfers between devices, body(): lax.ppermute(far[1], 'tp', to_right)  2.96 us
  transfers between devices with their start and end apart: 22, of which 12 were waited for; matrix products, arithmetic and copies ran while one was open for 0% of the time, Pallas kernels for 33%

profile of v5, /device:TPU:0, one launch (start us, length us, event | category | flops | bytes accessed | tf_op | source)
XLA Modules:
  0.0 68.5 jit_solution(2971462624561473480)
XLA Ops:
  0.0 4.8 %attend.1.refs_0_ = bf16[8,128,128]{2,1,0:T(8,128)(2,1)} custom-call(bf16[128,1024]{1,0:T(8,128)(2,1)} %query_hbm.1, bf16[4096,128]{1,0:T(8,128)(2,1)} %bitcast.24, bf16[4096,128]{1,0:T(8,128)(2,1)} %bitcast.25, bf16[128,128]{1,0:T(8,128)(2,1)} %bitcast.26, bf16[128,128]{1,0:T(8,128)(2,1)} %bitcast.27, s32[1,128]{1,0:T(1,128)} %bitcast.28), custom_call_target="tpu_custom_call" | custom-call | tf_op jit(solution)/shard_map/attend/pallas_call | solution.py:39
  4.8 3.1 %collective-permute-start.3 = (bf16[8,128,128]{2,1,0:T(8,128)(2,1)}, bf16[8,128,128]{2,1,0:T(8,128)(2,1)S(1)}, u32[]{:S(2)}, u32[]{:S(2)}) collective-permute-start(bf16[8,128,128]{2,1,0:T(8,128)(2,1)} %attend.1.refs_0_), channel_id=1, source_target_pairs={{0,4},{4,8},{8,12},{12,14},{14,10},{10,6},{6,2},{2,0},{1,5},{5,9},... | collective-permute-start | bytes 786440 | tf_op jit(solution)/shard_map/ppermute | solution.py:362
  8.9 3.5 %dense.3 = (f32[128,1024]{1,0:T(8,128)S(1)}, f32[128,1024]{1,0:T(8,128)S(1)}, f32[128,1024]{1,0:T(8,128)S(1)}) custom-call(bf16[8,128,128]{2,1,0:T(8,128)(2,1)S(1)} %copy-done.3, bf16[1024,8192]{1,0:T(8,128)(2,1)} %refs_1_.5), custom_call_target="tpu_custom_call" | custom-call | flops 805306368 | bytes 6291456 | tf_op jit(solution)/shard_map/dense/pallas_call | solution.py:39
  12.4 1.9 %collective-permute-done.3.refs_2_ = bf16[8,128,128]{2,1,0:T(8,128)(2,1)S(1)} collective-permute-done((bf16[8,128,128]{2,1,0:T(8,128)(2,1)}, bf16[8,128,128]{2,1,0:T(8,128)(2,1)S(1)}, u32[]{:S(2)}, u32[]{:S(2)}) %collective-permute-start.3) | collective-permute-done | bytes 262176 | tf_op jit(solution)/shard_map/ppermute | solution.py:362
  14.3 1.8 %collective-permute-start.4 = (bf16[8,128,128]{2,1,0:T(8,128)(2,1)S(1)}, bf16[8,128,128]{2,1,0:T(8,128)(2,1)S(1)}, u32[]{:S(2)}, u32[]{:S(2)}) collective-permute-start(bf16[8,128,128]{2,1,0:T(8,128)(2,1)S(1)} %collective-permute-done.3.refs_2_), channel_id=1, source_target_pairs={{0,4},{4,8},{8,12},{12,14},{14,10},{10,6},{6,2},{2,0},{1,5},{5,9},... | collective-permute-start | bytes 786440 | tf_op jit(solution)/shard_map/ppermute | solution.py:362
  16.3 4.4 %dense.4 = (f32[128,1024]{1,0:T(8,128)S(1)}, f32[128,1024]{1,0:T(8,128)S(1)}, f32[128,1024]{1,0:T(8,128)S(1)}, s32[128,128]{1,0:T(8,128)S(1)}, s32[64]{0:T(128)S(1)}) custom-call(bf16[8,128,128]{2,1,0:T(8,128)(2,1)S(1)} %copy-done.3, bf16[1024,8192]{1,0:T(8,128)(2,1)} %refs_1_.5, s32[1,128]{1,0:T(1,128)S(1)} %bitcast.23, s32[32]{0:T(128)S(1)} %copy-done.8, ...), custom_call_target="tpu_custom_call" | custom-call | flops 805306368 | bytes 6291456 | tf_op jit(solution)/shard_map/dense/pallas_call | solution.py:39
  21.8 1.5 %collective-permute-start.6 = (bf16[8,128,128]{2,1,0:T(8,128)(2,1)S(1)}, bf16[8,128,128]{2,1,0:T(8,128)(2,1)S(1)}, u32[]{:S(2)}, u32[]{:S(2)}) collective-permute-start(bf16[8,128,128]{2,1,0:T(8,128)(2,1)S(1)} %collective-permute-done.4.refs_4_), channel_id=1, source_target_pairs={{0,4},{4,8},{8,12},{12,14},{14,10},{10,6},{6,2},{2,0},{1,5},{5,9},... | collective-permute-start | bytes 786440 | tf_op jit(solution)/shard_map/ppermute | solution.py:362
  23.9 2.6 %dense.5 = (f32[128,1024]{1,0:T(8,128)S(1)}, f32[128,1024]{1,0:T(8,128)S(1)}) custom-call(bf16[8,128,128]{2,1,0:T(8,128)(2,1)S(1)} %copy-done.3, bf16[1024,8192]{1,0:T(8,128)(2,1)} %refs_1_.5), custom_call_target="tpu_custom_call" | custom-call | flops 536870912 | bytes 4194304 | tf_op jit(solution)/shard_map/dense/pallas_call | solution.py:39
  26.5 2.2 %fold_early.1 = (f32[128,256]{1,0:T(8,128)S(1)}, f32[64,128,128]{2,1,0:T(8,128)S(1)}) custom-call(bf16[8,128,128]{2,1,0:T(8,128)(2,1)S(1)} %copy-done.3, bf16[8,128,128]{2,1,0:T(8,128)(2,1)S(1)} %collective-permute-done.refs_1_, bf16[8,128,128]{2,1,0:T(8,128)(2,1)S(1)} %collective-permute-done.3.refs_2_, ...), custom_call_target="tpu_custom_call" | custom-call | flops 268435456 | bytes 4194304 | tf_op jit(solution)/shard_map/fold_early/pallas_call | solution.py:39
  28.7 1.5 %collective-permute-start.7 = (bf16[4,128,128]{2,1,0:T(8,128)(2,1)S(1)}, bf16[4,128,128]{2,1,0:T(8,128)(2,1)S(1)}, u32[]{:S(2)}, u32[]{:S(2)}) collective-permute-start(bf16[4,128,128]{2,1,0:T(8,128)(2,1)S(1)} %slice.7), channel_id=1, source_target_pairs={{0,4},{4,8},{8,12},{12,14},{14,10},{10,6},{6,2},{2,0},{1,5},{5,9},... | collective-permute-start | bytes 393224 | tf_op jit(solution)/shard_map/ppermute | solution.py:393
  30.9 1.4 %fold_late.1 = (f32[128,256]{1,0:T(8,128)S(1)}, f32[64,128,128]{2,1,0:T(8,128)S(1)}) custom-call(bf16[8,128,128]{2,1,0:T(8,128)(2,1)S(1)} %collective-permute-done.2.refs_0_, bf16[8,128,128]{2,1,0:T(8,128)(2,1)S(1)} %collective-permute-done.6.refs_1_, s32[128,128]{1,0:T(8,128)S(1)} %get-tuple-element.49.refs_5_.refs_2_, bf16[256,8192]{1,0:T(8,128)(2,1)S(1)} %bitcast.20, ...), custom_call_target="tpu_custom_call" | custom-call | flops 134217728 | bytes 1048576 | tf_op jit(solution)/shard_map/fold_late/pallas_call | solution.py:39
  32.3 1.4 %collective-permute-done.7.refs_1_ = bf16[4,128,128]{2,1,0:T(8,128)(2,1)S(1)} collective-permute-done((bf16[4,128,128]{2,1,0:T(8,128)(2,1)S(1)}, bf16[4,128,128]{2,1,0:T(8,128)(2,1)S(1)}, u32[]{:S(2)}, u32[]{:S(2)}) %collective-permute-start.7) | collective-permute-done | bytes 131104 | tf_op jit(solution)/shard_map/ppermute | solution.py:393
  33.8 1.5 %collective-permute-done.5.refs_0_ = bf16[4,128,128]{2,1,0:T(8,128)(2,1)S(1)} collective-permute-done((bf16[4,128,128]{2,1,0:T(8,128)(2,1)S(1)}, bf16[4,128,128]{2,1,0:T(8,128)(2,1)S(1)}, u32[]{:S(2)}, u32[]{:S(2)}) %collective-permute-start.5) | collective-permute-done | bytes 131104 | tf_op jit(solution)/shard_map/ppermute | solution.py:392
  35.3 1.4 %finish.1 = (bf16[128,256]{1,0:T(8,128)(2,1)S(1)}, f32[8,128,128]{2,1,0:T(8,128)S(1)}, bf16[64,1024]{1,0:T(8,128)(2,1)S(1)}, bf16[64,1024]{1,0:T(8,128)(2,1)S(1)}) custom-call(bf16[4,128,128]{2,1,0:T(8,128)(2,1)S(1)} %collective-permute-done.5.refs_0_, bf16[4,128,128]{2,1,0:T(8,128)(2,1)S(1)} %collective-permute-done.7.refs_1_, ...), custom_call_target="tpu_custom_call" | custom-call | flops 268435456 | bytes 2097152 | tf_op jit(solution)/shard_map/finish/pallas_call | solution.py:39
  37.3 1.5 %collective-permute-start.9 = (bf16[64,1024]{1,0:T(8,128)(2,1)S(1)}, bf16[64,1024]{1,0:T(8,128)(2,1)S(1)}, u32[]{:S(2)}, u32[]{:S(2)}) collective-permute-start(bf16[64,1024]{1,0:T(8,128)(2,1)S(1)} %get-tuple-element.70), channel_id=1, source_target_pairs={{0,4},{4,8},{8,12},{12,14},{14,10},{10,6},{6,2},{2,0},{1,5},{5,9},... | collective-permute-start | bytes 393224 | tf_op jit(solution)/shard_map/ppermute | solution.py:438
  38.8 1.2 %join.11 = (bf16[64,1024]{1,0:T(8,128)(2,1)S(1)}, bf16[64,1024]{1,0:T(8,128)(2,1)S(1)}) custom-call(bf16[128,256]{1,0:T(8,128)(2,1)S(1)} %get-tuple-element.77.refs_0_, bf16[256,8192]{1,0:T(8,128)(2,1)S(1)} %bitcast.12, f32[64,128,128]{2,1,0:T(8,128)S(1)} %get-tuple-element.61.refs_10_.refs_2_, f32[8,128,128]{2,1,0:T(8,128)S(1)} %get-tuple-element.63.refs_3_, ...), custom_call_target="tpu_custom_call" | custom-call | flops 67108864 | bytes 1048576 | tf_op jit(solution)/shard_map/join/pallas_call | solution.py:39
  40.6 1.4 %collective-permute-start.17 = (bf16[64,1024]{1,0:T(8,128)(2,1)S(1)}, bf16[64,1024]{1,0:T(8,128)(2,1)S(1)}, u32[]{:S(2)}, u32[]{:S(2)}) collective-permute-start(bf16[64,1024]{1,0:T(8,128)(2,1)S(1)} %get-tuple-element.82), channel_id=1, source_target_pairs={{0,4},{4,8},{8,12},{12,14},{14,10},{10,6},{6,2},{2,0},{1,5},{5,9},... | collective-permute-start | bytes 393224 | tf_op jit(solution)/shard_map/ppermute | solution.py:441
  42.3 1.2 %join.7 = (bf16[64,1024]{1,0:T(8,128)(2,1)S(1)}, bf16[64,1024]{1,0:T(8,128)(2,1)S(1)}) custom-call(bf16[128,256]{1,0:T(8,128)(2,1)S(1)} %get-tuple-element.77.refs_0_, bf16[256,8192]{1,0:T(8,128)(2,1)S(1)} %bitcast.13, f32[64,128,128]{2,1,0:T(8,128)S(1)} %get-tuple-element.61.refs_10_.refs_2_, f32[8,128,128]{2,1,0:T(8,128)S(1)} %get-tuple-element.63.refs_3_, ...), custom_call_target="tpu_custom_call" | custom-call | flops 67108864 | bytes 1048576 | tf_op jit(solution)/shard_map/join/pallas_call | solution.py:39
  43.5 1.5 %collective-permute-start.10 = (bf16[64,1024]{1,0:T(8,128)(2,1)S(1)}, bf16[64,1024]{1,0:T(8,128)(2,1)S(1)}, u32[]{:S(2)}, u32[]{:S(2)}) collective-permute-start(bf16[64,1024]{1,0:T(8,128)(2,1)S(1)} %get-tuple-element.71), channel_id=1, source_target_pairs={{4,0},{8,4},{12,8},{14,12},{10,14},{6,10},{2,6},{0,2},{5,1},{9,5},... | collective-permute-start | bytes 393224 | tf_op jit(solution)/shard_map/ppermute | solution.py:438
  45.9 1.2 %join.12 = (bf16[64,1024]{1,0:T(8,128)(2,1)S(1)}, bf16[64,1024]{1,0:T(8,128)(2,1)S(1)}) custom-call(bf16[128,256]{1,0:T(8,128)(2,1)S(1)} %get-tuple-element.77.refs_0_, bf16[256,8192]{1,0:T(8,128)(2,1)S(1)} %bitcast.14, f32[64,128,128]{2,1,0:T(8,128)S(1)} %get-tuple-element.61.refs_10_.refs_2_, f32[8,128,128]{2,1,0:T(8,128)S(1)} %get-tuple-element.63.refs_3_, ...), custom_call_target="tpu_custom_call" | custom-call | flops 67108864 | bytes 1048576 | tf_op jit(solution)/shard_map/join/pallas_call | solution.py:39
  47.1 1.3 %collective-permute-start.18 = (bf16[64,1024]{1,0:T(8,128)(2,1)S(1)}, bf16[64,1024]{1,0:T(8,128)(2,1)S(1)}, u32[]{:S(2)}, u32[]{:S(2)}) collective-permute-start(bf16[64,1024]{1,0:T(8,128)(2,1)S(1)} %get-tuple-element.83), channel_id=1, source_target_pairs={{4,0},{8,4},{12,8},{14,12},{10,14},{6,10},{2,6},{0,2},{5,1},{9,5},... | collective-permute-start | bytes 393224 | tf_op jit(solution)/shard_map/ppermute | solution.py:441
  49.5 1.6 %collective-permute-done.11.refs_10_ = bf16[64,1024]{1,0:T(8,128)(2,1)S(1)} collective-permute-done((bf16[64,1024]{1,0:T(8,128)(2,1)S(1)}, bf16[64,1024]{1,0:T(8,128)(2,1)S(1)}, u32[]{:S(2)}, u32[]{:S(2)}) %collective-permute-start.11) | collective-permute-done | bytes 131104 | tf_op jit(solution)/shard_map/ppermute | solution.py:438
  51.1 1.2 %join.8 = (bf16[64,1024]{1,0:T(8,128)(2,1)S(1)}, bf16[64,1024]{1,0:T(8,128)(2,1)S(1)}) custom-call(bf16[128,256]{1,0:T(8,128)(2,1)S(1)} %get-tuple-element.77.refs_0_, bf16[256,8192]{1,0:T(8,128)(2,1)S(1)} %bitcast.15, f32[64,128,128]{2,1,0:T(8,128)S(1)} %get-tuple-element.61.refs_10_.refs_2_, f32[8,128,128]{2,1,0:T(8,128)S(1)} %get-tuple-element.63.refs_3_, ...), custom_call_target="tpu_custom_call" | custom-call | flops 67108864 | bytes 1048576 | tf_op jit(solution)/shard_map/join/pallas_call | solution.py:39
  52.4 1.5 %collective-permute-start.12 = (bf16[64,1024]{1,0:T(8,128)(2,1)S(1)}, bf16[64,1024]{1,0:T(8,128)(2,1)S(1)}, u32[]{:S(2)}, u32[]{:S(2)}) collective-permute-start(bf16[64,1024]{1,0:T(8,128)(2,1)S(1)} %get-tuple-element.73), channel_id=1, source_target_pairs={{4,0},{8,4},{12,8},{14,12},{10,14},{6,10},{2,6},{0,2},{5,1},{9,5},... | collective-permute-start | bytes 393224 | tf_op jit(solution)/shard_map/ppermute | solution.py:438
  54.5 1.2 %join.13 = (bf16[64,1024]{1,0:T(8,128)(2,1)S(1)}, bf16[64,1024]{1,0:T(8,128)(2,1)S(1)}) custom-call(bf16[128,256]{1,0:T(8,128)(2,1)S(1)} %get-tuple-element.77.refs_0_, bf16[256,8192]{1,0:T(8,128)(2,1)S(1)} %bitcast.16, f32[64,128,128]{2,1,0:T(8,128)S(1)} %get-tuple-element.61.refs_10_.refs_2_, f32[8,128,128]{2,1,0:T(8,128)S(1)} %get-tuple-element.63.refs_3_, ...), custom_call_target="tpu_custom_call" | custom-call | flops 67108864 | bytes 1048576 | tf_op jit(solution)/shard_map/join/pallas_call | solution.py:39
  56.5 1.3 %collective-permute-start.21 = (bf16[64,1024]{1,0:T(8,128)(2,1)S(1)}, bf16[64,1024]{1,0:T(8,128)(2,1)S(1)}, u32[]{:S(2)}, u32[]{:S(2)}) collective-permute-start(bf16[64,1024]{1,0:T(8,128)(2,1)S(1)} %get-tuple-element.86), channel_id=1, source_target_pairs={{4,0},{8,4},{12,8},{14,12},{10,14},{6,10},{2,6},{0,2},{5,1},{9,5},... | collective-permute-start | bytes 393224 | tf_op jit(solution)/shard_map/ppermute | solution.py:441
  58.2 1.5 %collective-permute-done.13.refs_10_ = bf16[64,1024]{1,0:T(8,128)(2,1)S(1)} collective-permute-done((bf16[64,1024]{1,0:T(8,128)(2,1)S(1)}, bf16[64,1024]{1,0:T(8,128)(2,1)S(1)}, u32[]{:S(2)}, u32[]{:S(2)}) %collective-permute-start.13) | collective-permute-done | bytes 131104 | tf_op jit(solution)/shard_map/ppermute | solution.py:438
  59.7 1.2 %join.9 = (bf16[64,1024]{1,0:T(8,128)(2,1)S(1)}, bf16[64,1024]{1,0:T(8,128)(2,1)S(1)}) custom-call(bf16[128,256]{1,0:T(8,128)(2,1)S(1)} %get-tuple-element.77.refs_0_, bf16[256,8192]{1,0:T(8,128)(2,1)S(1)} %bitcast.17, f32[64,128,128]{2,1,0:T(8,128)S(1)} %get-tuple-element.61.refs_10_.refs_2_, f32[8,128,128]{2,1,0:T(8,128)S(1)} %get-tuple-element.63.refs_3_, ...), custom_call_target="tpu_custom_call" | custom-call | flops 67108864 | bytes 1048576 | tf_op jit(solution)/shard_map/join/pallas_call | solution.py:39
  61.0 1.8 %collective-permute-start.14 = (bf16[64,1024]{1,0:T(8,128)(2,1)S(1)}, bf16[64,1024]{1,0:T(8,128)(2,1)S(1)}, u32[]{:S(2)}, u32[]{:S(2)}) collective-permute-start(bf16[64,1024]{1,0:T(8,128)(2,1)S(1)} %get-tuple-element.75), channel_id=1, source_target_pairs={{4,0},{8,4},{12,8},{14,12},{10,14},{6,10},{2,6},{0,2},{5,1},{9,5},... | collective-permute-start | bytes 393224 | tf_op jit(solution)/shard_map/ppermute | solution.py:438
  63.0 1.3 %join.10 = (f32[64,1024]{1,0:T(8,128)S(1)}, f32[64,1024]{1,0:T(8,128)S(1)}) custom-call(bf16[128,256]{1,0:T(8,128)(2,1)S(1)} %get-tuple-element.77.refs_0_, bf16[256,8192]{1,0:T(8,128)(2,1)S(1)} %bitcast.18, f32[64,128,128]{2,1,0:T(8,128)S(1)} %get-tuple-element.61.refs_10_.refs_2_, f32[8,128,128]{2,1,0:T(8,128)S(1)} %get-tuple-element.63.refs_3_, ...), custom_call_target="tpu_custom_call" | custom-call | flops 67108864 | bytes 1048576 | tf_op jit(solution)/shard_map/join/pallas_call | solution.py:39
  64.3 1.7 %collective-permute-done.14.refs_0_ = bf16[64,1024]{1,0:T(8,128)(2,1)S(1)} collective-permute-done((bf16[64,1024]{1,0:T(8,128)(2,1)S(1)}, bf16[64,1024]{1,0:T(8,128)(2,1)S(1)}, u32[]{:S(2)}, u32[]{:S(2)}) %collective-permute-start.14) | collective-permute-done | bytes 131104 | tf_op jit(solution)/shard_map/ppermute | solution.py:438
  66.0 1.7 %collective-permute-done.15.refs_1_ = bf16[64,1024]{1,0:T(8,128)(2,1)S(1)} collective-permute-done((bf16[64,1024]{1,0:T(8,128)(2,1)S(1)}, bf16[64,1024]{1,0:T(8,128)(2,1)S(1)}, u32[]{:S(2)}, u32[]{:S(2)}) %collective-permute-start.15) | collective-permute-done | bytes 131104 | tf_op jit(solution)/shard_map/ppermute | solution.py:438
  (47 shorter events, 9.9 us)
Async XLA Ops:
  0.0 16.3 %copy-start.6 = (s32[4,16,1]{1,2,0:T(1,128)S(1)}, s32[4,16,1]{1,2,0:T(1,128)}, u32[]{:S(2)}) copy-start(s32[4,16,1]{1,2,0:T(1,128)} %param.28) | copy-start | bytes 772
  0.0 16.3 %copy-start.7 = (s32[128]{0:T(128)S(1)}, s32[128]{0:T(128)}, u32[]{:S(2)}) copy-start(s32[128]{0:T(128)} %param.21) | copy-start | bytes 1540
  0.0 16.3 %copy-start.8 = (s32[32]{0:T(128)S(1)}, s32[32]{0:T(128)}, u32[]{:S(2)}) copy-start(s32[32]{0:T(128)} %refs_3_.1) | copy-start | bytes 388
  4.8 9.5 %collective-permute-start.3 = (bf16[8,128,128]{2,1,0:T(8,128)(2,1)}, bf16[8,128,128]{2,1,0:T(8,128)(2,1)S(1)}, u32[]{:S(2)}, u32[]{:S(2)}) collective-permute-start(bf16[8,128,128]{2,1,0:T(8,128)(2,1)} %attend.1.refs_0_), channel_id=1, source_target_pairs={{0,4},{4,8},{8,12},{12,14},{14,10},{10,6},{6,2},{2,0},{1,5},{5,9},... | collective-permute-start | bytes 786440 | tf_op jit(solution)/shard_map/ppermute | solution.py:362
  7.8 8.3 %collective-permute-start = (bf16[8,128,128]{2,1,0:T(8,128)(2,1)}, bf16[8,128,128]{2,1,0:T(8,128)(2,1)S(1)}, u32[]{:S(2)}, u32[]{:S(2)}) collective-permute-start(bf16[8,128,128]{2,1,0:T(8,128)(2,1)} %attend.1.refs_0_), channel_id=1, source_target_pairs={{4,0},{8,4},{12,8},{14,12},{10,14},{6,10},{2,6},{0,2},{5,1},{9,5},... | collective-permute-start | bytes 786440 | tf_op jit(solution)/shard_map/ppermute | solution.py:361
  7.9 1.0 %copy-start.3 = (bf16[8,128,128]{2,1,0:T(8,128)(2,1)S(1)}, bf16[8,128,128]{2,1,0:T(8,128)(2,1)}, u32[]{:S(2)}) copy-start(bf16[8,128,128]{2,1,0:T(8,128)(2,1)} %attend.1.refs_0_) | copy-start | bytes 786436
  14.3 7.5 %collective-permute-start.4 = (bf16[8,128,128]{2,1,0:T(8,128)(2,1)S(1)}, bf16[8,128,128]{2,1,0:T(8,128)(2,1)S(1)}, u32[]{:S(2)}, u32[]{:S(2)}) collective-permute-start(bf16[8,128,128]{2,1,0:T(8,128)(2,1)S(1)} %collective-permute-done.3.refs_2_), channel_id=1, source_target_pairs={{0,4},{4,8},{8,12},{12,14},{14,10},{10,6},{6,2},{2,0},{1,5},{5,9},... | collective-permute-start | bytes 786440 | tf_op jit(solution)/shard_map/ppermute | solution.py:362
  16.1 7.2 %collective-permute-start.1 = (bf16[8,128,128]{2,1,0:T(8,128)(2,1)S(1)}, bf16[8,128,128]{2,1,0:T(8,128)(2,1)S(1)}, u32[]{:S(2)}, u32[]{:S(2)}) collective-permute-start(bf16[8,128,128]{2,1,0:T(8,128)(2,1)S(1)} %collective-permute-done.refs_1_), channel_id=1, source_target_pairs={{4,0},{8,4},{12,8},{14,12},{10,14},{6,10},{2,6},{0,2},{5,1},{9,5},... | collective-permute-start | bytes 786440 | tf_op jit(solution)/shard_map/ppermute | solution.py:361
  21.8 4.7 %copy-start.1 = (bf16[4,8192,64]{1,2,0:T(8,128)(2,1)S(1)}, bf16[4,8192,64]{1,2,0:T(8,128)(2,1)}, u32[]{:S(2)}) copy-start(bf16[4,8192,64]{1,2,0:T(8,128)(2,1)} %param.24) | copy-start | bytes 12582916
  21.8 4.7 %copy-start.2 = (bf16[4,16,128,128]{3,2,1,0:T(8,128)(2,1)S(1)}, bf16[4,16,128,128]{3,2,1,0:T(8,128)(2,1)}, u32[]{:S(2)}) copy-start(bf16[4,16,128,128]{3,2,1,0:T(8,128)(2,1)} %refs_4_.10) | copy-start | bytes 6291460
  21.8 4.7 %copy-start.4 = (f32[4,16]{1,0:T(4,128)S(1)}, f32[4,16]{1,0:T(4,128)}, u32[]{:S(2)}) copy-start(f32[4,16]{1,0:T(4,128)} %refs_4_.17) | copy-start | bytes 772
  21.8 4.7 %copy-start.5 = (s32[4,16]{1,0:T(4,128)S(1)}, s32[4,16]{1,0:T(4,128)}, u32[]{:S(2)}) copy-start(s32[4,16]{1,0:T(4,128)} %refs_5_.17) | copy-start | bytes 772
  21.8 6.9 %collective-permute-start.6 = (bf16[8,128,128]{2,1,0:T(8,128)(2,1)S(1)}, bf16[8,128,128]{2,1,0:T(8,128)(2,1)S(1)}, u32[]{:S(2)}, u32[]{:S(2)}) collective-permute-start(bf16[8,128,128]{2,1,0:T(8,128)(2,1)S(1)} %collective-permute-done.4.refs_4_), channel_id=1, source_target_pairs={{0,4},{4,8},{8,12},{12,14},{14,10},{10,6},{6,2},{2,0},{1,5},{5,9},... | collective-permute-start | bytes 786440 | tf_op jit(solution)/shard_map/ppermute | solution.py:362
  23.3 6.9 %collective-permute-start.2 = (bf16[8,128,128]{2,1,0:T(8,128)(2,1)S(1)}, bf16[8,128,128]{2,1,0:T(8,128)(2,1)S(1)}, u32[]{:S(2)}, u32[]{:S(2)}) collective-permute-start(bf16[8,128,128]{2,1,0:T(8,128)(2,1)S(1)} %collective-permute-done.1.refs_3_), channel_id=1, source_target_pairs={{4,0},{8,4},{12,8},{14,12},{10,14},{6,10},{2,6},{0,2},{5,1},{9,5},... | collective-permute-start | bytes 786440 | tf_op jit(solution)/shard_map/ppermute | solution.py:361
  28.7 5.0 %collective-permute-start.7 = (bf16[4,128,128]{2,1,0:T(8,128)(2,1)S(1)}, bf16[4,128,128]{2,1,0:T(8,128)(2,1)S(1)}, u32[]{:S(2)}, u32[]{:S(2)}) collective-permute-start(bf16[4,128,128]{2,1,0:T(8,128)(2,1)S(1)} %slice.7), channel_id=1, source_target_pairs={{0,4},{4,8},{8,12},{12,14},{14,10},{10,6},{6,2},{2,0},{1,5},{5,9},... | collective-permute-start | bytes 393224 | tf_op jit(solution)/shard_map/ppermute | solution.py:393
  30.3 5.0 %collective-permute-start.5 = (bf16[4,128,128]{2,1,0:T(8,128)(2,1)S(1)}, bf16[4,128,128]{2,1,0:T(8,128)(2,1)S(1)}, u32[]{:S(2)}, u32[]{:S(2)}) collective-permute-start(bf16[4,128,128]{2,1,0:T(8,128)(2,1)S(1)} %slice.6), channel_id=1, source_target_pairs={{4,0},{8,4},{12,8},{14,12},{10,14},{6,10},{2,6},{0,2},{5,1},{9,5},... | collective-permute-start | bytes 393224 | tf_op jit(solution)/shard_map/ppermute | solution.py:392
  30.9 4.4 %copy-start = (bf16[4,64,8192]{2,1,0:T(8,128)(2,1)S(1)}, bf16[4,64,8192]{2,1,0:T(8,128)(2,1)}, u32[]{:S(2)}) copy-start(bf16[4,64,8192]{2,1,0:T(8,128)(2,1)} %param.25) | copy-start | bytes 12582916
  36.7 5.4 %collective-permute-start.8 = (bf16[64,1024]{1,0:T(8,128)(2,1)S(1)}, bf16[64,1024]{1,0:T(8,128)(2,1)S(1)}, u32[]{:S(2)}, u32[]{:S(2)}) collective-permute-start(bf16[64,1024]{1,0:T(8,128)(2,1)S(1)} %get-tuple-element.69), channel_id=1, source_target_pairs={{4,0},{8,4},{12,8},{14,12},{10,14},{6,10},{2,6},{0,2},{5,1},{9,5},... | collective-permute-start | bytes 393224 | tf_op jit(solution)/shard_map/ppermute | solution.py:438
  37.3 5.0 %collective-permute-start.9 = (bf16[64,1024]{1,0:T(8,128)(2,1)S(1)}, bf16[64,1024]{1,0:T(8,128)(2,1)S(1)}, u32[]{:S(2)}, u32[]{:S(2)}) collective-permute-start(bf16[64,1024]{1,0:T(8,128)(2,1)S(1)} %get-tuple-element.70), channel_id=1, source_target_pairs={{0,4},{4,8},{8,12},{12,14},{14,10},{10,6},{6,2},{2,0},{1,5},{5,9},... | collective-permute-start | bytes 393224 | tf_op jit(solution)/shard_map/ppermute | solution.py:438
  40.0 5.7 %collective-permute-start.16 = (bf16[64,1024]{1,0:T(8,128)(2,1)S(1)}, bf16[64,1024]{1,0:T(8,128)(2,1)S(1)}, u32[]{:S(2)}, u32[]{:S(2)}) collective-permute-start(bf16[64,1024]{1,0:T(8,128)(2,1)S(1)} %get-tuple-element.81), channel_id=1, source_target_pairs={{4,0},{8,4},{12,8},{14,12},{10,14},{6,10},{2,6},{0,2},{5,1},{9,5},... | collective-permute-start | bytes 393224 | tf_op jit(solution)/shard_map/ppermute | solution.py:441
  40.6 5.2 %collective-permute-start.17 = (bf16[64,1024]{1,0:T(8,128)(2,1)S(1)}, bf16[64,1024]{1,0:T(8,128)(2,1)S(1)}, u32[]{:S(2)}, u32[]{:S(2)}) collective-permute-start(bf16[64,1024]{1,0:T(8,128)(2,1)S(1)} %get-tuple-element.82), channel_id=1, source_target_pairs={{0,4},{4,8},{8,12},{12,14},{14,10},{10,6},{6,2},{2,0},{1,5},{5,9},... | collective-permute-start | bytes 393224 | tf_op jit(solution)/shard_map/ppermute | solution.py:441
  43.5 6.0 %collective-permute-start.10 = (bf16[64,1024]{1,0:T(8,128)(2,1)S(1)}, bf16[64,1024]{1,0:T(8,128)(2,1)S(1)}, u32[]{:S(2)}, u32[]{:S(2)}) collective-permute-start(bf16[64,1024]{1,0:T(8,128)(2,1)S(1)} %get-tuple-element.71), channel_id=1, source_target_pairs={{4,0},{8,4},{12,8},{14,12},{10,14},{6,10},{2,6},{0,2},{5,1},{9,5},... | collective-permute-start | bytes 393224 | tf_op jit(solution)/shard_map/ppermute | solution.py:438
  45.0 6.1 %collective-permute-start.11 = (bf16[64,1024]{1,0:T(8,128)(2,1)S(1)}, bf16[64,1024]{1,0:T(8,128)(2,1)S(1)}, u32[]{:S(2)}, u32[]{:S(2)}) collective-permute-start(bf16[64,1024]{1,0:T(8,128)(2,1)S(1)} %get-tuple-element.72), channel_id=1, source_target_pairs={{0,4},{4,8},{8,12},{12,14},{14,10},{10,6},{6,2},{2,0},{1,5},{5,9},... | collective-permute-start | bytes 393224 | tf_op jit(solution)/shard_map/ppermute | solution.py:438
  47.1 7.3 %collective-permute-start.18 = (bf16[64,1024]{1,0:T(8,128)(2,1)S(1)}, bf16[64,1024]{1,0:T(8,128)(2,1)S(1)}, u32[]{:S(2)}, u32[]{:S(2)}) collective-permute-start(bf16[64,1024]{1,0:T(8,128)(2,1)S(1)} %get-tuple-element.83), channel_id=1, source_target_pairs={{4,0},{8,4},{12,8},{14,12},{10,14},{6,10},{2,6},{0,2},{5,1},{9,5},... | collective-permute-start | bytes 393224 | tf_op jit(solution)/shard_map/ppermute | solution.py:441
  48.4 6.0 %collective-permute-start.19 = (bf16[64,1024]{1,0:T(8,128)(2,1)S(1)}, bf16[64,1024]{1,0:T(8,128)(2,1)S(1)}, u32[]{:S(2)}, u32[]{:S(2)}) collective-permute-start(bf16[64,1024]{1,0:T(8,128)(2,1)S(1)} %get-tuple-element.84), channel_id=1, source_target_pairs={{0,4},{4,8},{8,12},{12,14},{14,10},{10,6},{6,2},{2,0},{1,5},{5,9},... | collective-permute-start | bytes 393224 | tf_op jit(solution)/shard_map/ppermute | solution.py:441
  52.4 5.9 %collective-permute-start.12 = (bf16[64,1024]{1,0:T(8,128)(2,1)S(1)}, bf16[64,1024]{1,0:T(8,128)(2,1)S(1)}, u32[]{:S(2)}, u32[]{:S(2)}) collective-permute-start(bf16[64,1024]{1,0:T(8,128)(2,1)S(1)} %get-tuple-element.73), channel_id=1, source_target_pairs={{4,0},{8,4},{12,8},{14,12},{10,14},{6,10},{2,6},{0,2},{5,1},{9,5},... | collective-permute-start | bytes 393224 | tf_op jit(solution)/shard_map/ppermute | solution.py:438
  53.9 5.8 %collective-permute-start.13 = (bf16[64,1024]{1,0:T(8,128)(2,1)S(1)}, bf16[64,1024]{1,0:T(8,128)(2,1)S(1)}, u32[]{:S(2)}, u32[]{:S(2)}) collective-permute-start(bf16[64,1024]{1,0:T(8,128)(2,1)S(1)} %get-tuple-element.74), channel_id=1, source_target_pairs={{0,4},{4,8},{8,12},{12,14},{14,10},{10,6},{6,2},{2,0},{1,5},{5,9},... | collective-permute-start | bytes 393224 | tf_op jit(solution)/shard_map/ppermute | solution.py:438
  55.7 8.6 %collective-permute-start.20 = (bf16[64,1024]{1,0:T(8,128)(2,1)S(1)}, bf16[64,1024]{1,0:T(8,128)(2,1)S(1)}, u32[]{:S(2)}, u32[]{:S(2)}) collective-permute-start(bf16[64,1024]{1,0:T(8,128)(2,1)S(1)} %get-tuple-element.85), channel_id=1, source_target_pairs={{0,4},{4,8},{8,12},{12,14},{14,10},{10,6},{6,2},{2,0},{1,5},{5,9},... | collective-permute-start | bytes 393224 | tf_op jit(solution)/shard_map/ppermute | solution.py:441
  56.5 7.8 %collective-permute-start.21 = (bf16[64,1024]{1,0:T(8,128)(2,1)S(1)}, bf16[64,1024]{1,0:T(8,128)(2,1)S(1)}, u32[]{:S(2)}, u32[]{:S(2)}) collective-permute-start(bf16[64,1024]{1,0:T(8,128)(2,1)S(1)} %get-tuple-element.86), channel_id=1, source_target_pairs={{4,0},{8,4},{12,8},{14,12},{10,14},{6,10},{2,6},{0,2},{5,1},{9,5},... | collective-permute-start | bytes 393224 | tf_op jit(solution)/shard_map/ppermute | solution.py:441
  61.0 5.0 %collective-permute-start.14 = (bf16[64,1024]{1,0:T(8,128)(2,1)S(1)}, bf16[64,1024]{1,0:T(8,128)(2,1)S(1)}, u32[]{:S(2)}, u32[]{:S(2)}) collective-permute-start(bf16[64,1024]{1,0:T(8,128)(2,1)S(1)} %get-tuple-element.75), channel_id=1, source_target_pairs={{4,0},{8,4},{12,8},{14,12},{10,14},{6,10},{2,6},{0,2},{5,1},{9,5},... | collective-permute-start | bytes 393224 | tf_op jit(solution)/shard_map/ppermute | solution.py:438
  62.8 5.0 %collective-permute-start.15 = (bf16[64,1024]{1,0:T(8,128)(2,1)S(1)}, bf16[64,1024]{1,0:T(8,128)(2,1)S(1)}, u32[]{:S(2)}, u32[]{:S(2)}) collective-permute-start(bf16[64,1024]{1,0:T(8,128)(2,1)S(1)} %get-tuple-element.76), channel_id=1, source_target_pairs={{0,4},{4,8},{8,12},{12,14},{14,10},{10,6},{6,2},{2,0},{1,5},{5,9},... | collective-permute-start | bytes 393224 | tf_op jit(solution)/shard_map/ppermute | solution.py:438

commit v6 on v5

--- a/solution.py
+++ b/solution.py
@@ -105,14 +105,14 @@
 
 
 def dense_kernel(distances, count, listing, *refs):
-    x_hbm, weight_ref = refs[:2]
+    x_ref, weight_ref = refs[:2]
     if listing:
         variant_ref, holder_ref, owner_ref = refs[2:5]
-        outs, slot_ref, table_ref = refs[5 : 5 + len(distances)], refs[-6], refs[-5]
+        outs, slot_ref, table_ref = refs[5 : 5 + len(distances)], refs[-4], refs[-3]
     else:
         outs = refs[2 : 2 + len(distances)]
-    x_ref, buffers, sems, x_sem = refs[-4:]
-    heads, rows, side = x_hbm.shape
+    buffers, sems = refs[-2:]
+    heads, rows, side = x_ref.shape
     width = heads * side
     depth = buffers.shape[0]
     piece = buffers.shape[2]
@@ -126,8 +126,6 @@
             sems.at[i % depth],
         )
 
-    own = pltpu.make_async_copy(x_hbm, x_ref, x_sem)
-    own.start()
     total = len(distances) * cuts
     for i in range(min(depth, total)):
         fetch(i).start()
@@ -149,7 +147,6 @@
                 return carry
 
             lax.fori_loop(0, owner_ref.shape[1], note, 0)
-    own.wait()
     x = jnp.concatenate([x_ref[h] for h in range(heads)], axis=1)
     for i in range(total):
         fetch(i).wait()
@@ -254,8 +251,10 @@
     low_out[...] = low
     part_for(distance, count, low_out, second_ref, dense_ref, block_ref, extra_out, columns,
              slice(0, rows), farthest)
-    top_out[...] = farthest[: rows // 2].astype(BF16)
-    bottom_out[...] = farthest[rows // 2 :].astype(BF16)
+    for i in range(2 * half):
+        tile = farthest[:, i * side : (i + 1) * side].astype(BF16)
+        top_out[i] = tile[: rows // 2]
+        bottom_out[i] = tile[rows // 2 :]
 
 
 def join_kernel(jobs, count, slots, *refs):
@@ -270,23 +269,26 @@
         here = slice(half * rows // 2, (half + 1) * rows // 2)
         part_for(distance, count, low_ref, second_ref, dense_refs[n], block_ref, extra_ref, columns,
                  here, totals[n])
-        total = totals[n][...]
-        if came:
-            total = total + came[n][...].astype(F32)
-        outs[n][...] = total.astype(outs[n].dtype)
+        side = width // heads
+        for i in range(heads):
+            total = totals[n][:, i * side : (i + 1) * side]
+            if came:
+                total = total + came[n][i].astype(F32)
+            outs[n][i] = total.astype(outs[n].dtype)
 
 
 def sum_kernel(upper_ref, lower_ref, *refs):
     out_ref = refs[-1]
-    cut = upper_ref.shape[0]
-    upper, lower = upper_ref[...], lower_ref[...]
-    for n, ref in enumerate(refs[:-1]):
-        if n in (0, 2):
-            upper = upper + ref[...].astype(F32)
-        else:
-            lower = lower + ref[...].astype(F32)
-    out_ref[:cut] = upper.astype(BF16)
-    out_ref[cut:] = lower.astype(BF16)
+    heads, cut, side = upper_ref.shape
+    for i in range(heads):
+        upper, lower = upper_ref[i], lower_ref[i]
+        for n, ref in enumerate(refs[:-1]):
+            if n in (0, 2):
+                upper = upper + ref[i].astype(F32)
+            else:
+                lower = lower + ref[i].astype(F32)
+        out_ref[:cut, i * side : (i + 1) * side] = upper.astype(BF16)
+        out_ref[cut:, i * side : (i + 1) * side] = lower.astype(BF16)
 
 
 def after(value, *others):
@@ -341,10 +343,9 @@
             "dense",
             [shape((rows, width), F32)] * len(distances) + extra_shapes * listing,
             (x, out_weight) + extra_ins * listing,
-            [ANY, ANY] + [VMEM, SMEM, SMEM] * listing,
+            [VMEM, ANY] + [VMEM, SMEM, SMEM] * listing,
             [VMEM] * len(distances) + [VMEM, SMEM] * listing,
-            [pltpu.VMEM((heads, rows, side), BF16), pltpu.VMEM((4, width, piece), BF16),
-             pltpu.SemaphoreType.DMA((4,)), pltpu.SemaphoreType.DMA],
+            [pltpu.VMEM((4, width, piece), BF16), pltpu.SemaphoreType.DMA((4,))],
             limit=40,
             flops=2 * rows * width * width * len(distances),
             moved=2 * width * width * len(distances),
@@ -368,7 +369,6 @@
     slot, table = dense_for(wanted[third : 2 * third], after(attended, token), True)
     for step in range(3, half):
         pass_on(step, slot)
-    token = dense_for(wanted[2 * third :], after(attended, slot))
 
     factor_t = jnp.swapaxes(factor_in, 1, 2).reshape(low_width, -1)
     second = second_factor.reshape(low_width, complete)
@@ -389,8 +389,10 @@
         flops=rows * low_width * complete,
         moved=4 * MIB,
     )
-    front = lax.ppermute(after(chunks[half - 1], low, token)[: heads // 2], "tp", to_left)
-    back = lax.ppermute(after(chunks[count - half + 1], low, token)[heads // 2 :], "tp", to_right)
+    front = lax.ppermute(after(chunks[half - 1], low)[: heads // 2], "tp", to_left)
+    back = lax.ppermute(after(chunks[count - half + 1], low)[heads // 2 :], "tp", to_right)
+    if len(wanted) > 2 * third + 1:
+        token = dense_for(wanted[2 * third : -1], after(attended, low))
     low, blocks = call(
         functools.partial(fold_kernel, late, count, False),
         "fold_late",
@@ -401,12 +403,13 @@
         flops=rows * low_width * width * 4,
         moved=MIB,
     )
+    low = after(low, token)
     extras = shape((slots * CAP, rows, side), F32)
     low, extra, top, bottom = call(
         functools.partial(finish_kernel, half, count),
         "finish",
         [shape((rows, low_width), BF16), extras]
-        + [shape((rows // 2, width), BF16)] * 2,
+        + [shape((heads, rows // 2, side), BF16)] * 2,
         (front, back, *tables, second, low, blocks, dense[half]),
         [VMEM] * 2 + table_specs + [VMEM] * 4,
         [VMEM] * 4,
@@ -420,7 +423,7 @@
         return call(
             functools.partial(join_kernel, jobs, count, slots),
             "join",
-            [shape((rows // 2, width), kind)] * len(jobs),
+            [shape((heads, rows // 2, side), kind)] * len(jobs),
             (low, second, blocks, extra, block_scale, block_cell, table,
              *[dense[distance] for distance, _ in jobs], *came),
             [VMEM] * 4 + [SMEM] * 3 + [VMEM] * (len(jobs) + len(came)),
@@ -439,6 +442,7 @@
         if distance > 1:
             near = join([(count - distance + 1, 1), (distance - 1, 0)], near, low)
             near = [lax.ppermute(near[0], "tp", to_left), lax.ppermute(near[1], "tp", to_right)]
+    dense_for([0], after(attended, *ready))
     own = join([(0, 0), (0, 1)], (), after(low, *ready), F32)
     up_left, low_right = far
     if half > 1:

time: 68.7 us -> 69.4 us (1.010)
  Pallas kernels: 29.7 us -> 31.9 us
  waiting for transfers between devices: 13.6 us -> 12 us
    pallas_call x15 -> x16, Pallas kernels: 29.7 us -> 31.9 us  [call(): pl.pallas_call(kernel, out_shape=outs, in_specs=specs, out_specs=out_spec...]
    ppermute x4, waiting for transfers between devices: 2.37 us -> 0.19 us  [body(): lax.ppermute(far[0], 'tp', to_left)]
    ppermute x2, waiting for transfers between devices: 2.97 us -> 1.05 us  [the longest x1 1.05 us: body(): lax.ppermute(after(chunks[half - 1], low)[:heads // 2], 'tp', to_left)]
    ppermute x3, waiting for transfers between devices: 3.04 us -> 4.67 us  [pass_on(): chunks[count - step] = lax.ppermute(left, 'tp', to_right)]
    ppermute x3, starting transfers between devices: 3.11 us -> 1.91 us  [body(): lax.ppermute(near[1], 'tp', to_right)]
    ppermute x3, starting transfers between devices: 3.19 us -> 4.32 us  [body(): lax.ppermute(near[0], 'tp', to_left)]
    ppermute x4, starting transfers between devices: 2.96 us -> 2.13 us  [body(): lax.ppermute(far[1], 'tp', to_right)]
    ppermute x4, starting transfers between devices: 5.44 us -> 6.19 us  [body(): lax.ppermute(far[0], 'tp', to_left)]
  transfers between devices with their start and end apart: 22 -> 22, of which waited for: 12 -> 10; matrix products, arithmetic and copies ran while one was open for 0% -> 0% of each run, Pallas kernels for 33% -> 36%
where the time goes in v6:
time: 69.4 us; the launch traced here: 69.1 us
  Pallas kernels  31.9 us (46%)
  starting transfers between devices  23.9 us (34%)
  waiting for transfers between devices  12 us (17%)
  local copies, waits for them, and re-layouts  1.06 us (2%)
    pallas_call x16, Pallas kernels, call(): pl.pallas_call(kernel, out_shape=outs, in_specs=specs, out_specs=out_spec...  31.9 us
    ppermute x3, starting transfers between devices, pass_on(): chunks[count - step] = lax.ppermute(left, 'tp', to_right)  6.7 us
    ppermute x4, starting transfers between devices, body(): lax.ppermute(far[0], 'tp', to_left)  6.19 us
    ppermute x4, waiting for transfers between devices, body(): lax.ppermute(far[1], 'tp', to_right)  5.4 us
    ppermute x3, waiting for transfers between devices, pass_on(): chunks[count - step] = lax.ppermute(left, 'tp', to_right)  4.67 us
    ppermute x3, starting transfers between devices, body(): lax.ppermute(near[0], 'tp', to_left)  4.32 us
    ppermute x4, starting transfers between devices, body(): lax.ppermute(far[1], 'tp', to_right)  2.13 us
    ppermute x3, starting transfers between devices, body(): lax.ppermute(near[1], 'tp', to_right)  1.91 us
  transfers between devices with their start and end apart: 22, of which 10 were waited for; matrix products, arithmetic and copies ran while one was open for 0% of the time, Pallas kernels for 36%

profile of v6, /device:TPU:0, one launch (start us, length us, event | category | flops | bytes accessed | tf_op | source)
XLA Modules:
  0.0 69.1 jit_solution(11563744684859713693)
XLA Ops:
  0.0 4.8 %attend.1.refs_0_ = bf16[8,128,128]{2,1,0:T(8,128)(2,1)} custom-call(bf16[128,1024]{1,0:T(8,128)(2,1)} %query_hbm.1, bf16[4096,128]{1,0:T(8,128)(2,1)} %bitcast.24, bf16[4096,128]{1,0:T(8,128)(2,1)} %bitcast.25, bf16[128,128]{1,0:T(8,128)(2,1)} %bitcast.26, bf16[128,128]{1,0:T(8,128)(2,1)} %bitcast.27, s32[1,128]{1,0:T(1,128)} %bitcast.28), custom_call_target="tpu_custom_call" | custom-call | tf_op jit(solution)/shard_map/attend/pallas_call | solution.py:39
  4.8 3.1 %collective-permute-start.3 = (bf16[8,128,128]{2,1,0:T(8,128)(2,1)}, bf16[8,128,128]{2,1,0:T(8,128)(2,1)S(1)}, u32[]{:S(2)}, u32[]{:S(2)}) collective-permute-start(bf16[8,128,128]{2,1,0:T(8,128)(2,1)} %attend.1.refs_0_), channel_id=1, source_target_pairs={{0,4},{4,8},{8,12},{12,14},{14,10},{10,6},{6,2},{2,0},{1,5},{5,9},... | collective-permute-start | bytes 786440 | tf_op jit(solution)/shard_map/ppermute | solution.py:363
  8.9 3.5 %dense.4 = (f32[128,1024]{1,0:T(8,128)S(1)}, f32[128,1024]{1,0:T(8,128)S(1)}, f32[128,1024]{1,0:T(8,128)S(1)}) custom-call(bf16[8,128,128]{2,1,0:T(8,128)(2,1)S(1)} %copy-done.3, bf16[1024,8192]{1,0:T(8,128)(2,1)} %refs_1_.7), custom_call_target="tpu_custom_call" | custom-call | flops 805306368 | bytes 6291456 | tf_op jit(solution)/shard_map/dense/pallas_call | solution.py:39
  12.3 2.0 %collective-permute-done.3.refs_2_ = bf16[8,128,128]{2,1,0:T(8,128)(2,1)S(1)} collective-permute-done((bf16[8,128,128]{2,1,0:T(8,128)(2,1)}, bf16[8,128,128]{2,1,0:T(8,128)(2,1)S(1)}, u32[]{:S(2)}, u32[]{:S(2)}) %collective-permute-start.3) | collective-permute-done | bytes 262176 | tf_op jit(solution)/shard_map/ppermute | solution.py:363
  14.3 1.8 %collective-permute-start.4 = (bf16[8,128,128]{2,1,0:T(8,128)(2,1)S(1)}, bf16[8,128,128]{2,1,0:T(8,128)(2,1)S(1)}, u32[]{:S(2)}, u32[]{:S(2)}) collective-permute-start(bf16[8,128,128]{2,1,0:T(8,128)(2,1)S(1)} %collective-permute-done.3.refs_2_), channel_id=1, source_target_pairs={{0,4},{4,8},{8,12},{12,14},{14,10},{10,6},{6,2},{2,0},{1,5},{5,9},... | collective-permute-start | bytes 786440 | tf_op jit(solution)/shard_map/ppermute | solution.py:363
  16.4 5.4 %dense.5 = (f32[128,1024]{1,0:T(8,128)S(1)}, f32[128,1024]{1,0:T(8,128)S(1)}, f32[128,1024]{1,0:T(8,128)S(1)}, s32[128,128]{1,0:T(8,128)S(1)}, s32[64]{0:T(128)S(1)}) custom-call(bf16[8,128,128]{2,1,0:T(8,128)(2,1)S(1)} %copy-done.3, bf16[1024,8192]{1,0:T(8,128)(2,1)} %refs_1_.7, s32[1,128]{1,0:T(1,128)S(1)} %bitcast.23, s32[32]{0:T(128)S(1)} %copy-done.8, ...), custom_call_target="tpu_custom_call" | custom-call | flops 805306368 | bytes 6291456 | tf_op jit(solution)/shard_map/dense/pallas_call | solution.py:39
  21.8 1.8 %collective-permute-start.6 = (bf16[8,128,128]{2,1,0:T(8,128)(2,1)S(1)}, bf16[8,128,128]{2,1,0:T(8,128)(2,1)S(1)}, u32[]{:S(2)}, u32[]{:S(2)}) collective-permute-start(bf16[8,128,128]{2,1,0:T(8,128)(2,1)S(1)} %collective-permute-done.4.refs_4_), channel_id=1, source_target_pairs={{0,4},{4,8},{8,12},{12,14},{14,10},{10,6},{6,2},{2,0},{1,5},{5,9},... | collective-permute-start | bytes 786440 | tf_op jit(solution)/shard_map/ppermute | solution.py:363
  23.9 2.2 %fold_early.1 = (f32[128,256]{1,0:T(8,128)S(1)}, f32[64,128,128]{2,1,0:T(8,128)S(1)}) custom-call(bf16[8,128,128]{2,1,0:T(8,128)(2,1)S(1)} %copy-done.3, bf16[8,128,128]{2,1,0:T(8,128)(2,1)S(1)} %collective-permute-done.refs_1_, bf16[8,128,128]{2,1,0:T(8,128)(2,1)S(1)} %collective-permute-done.3.refs_2_, ...), custom_call_target="tpu_custom_call" | custom-call | flops 268435456 | bytes 4194304 | tf_op jit(solution)/shard_map/fold_early/pallas_call | solution.py:39
  26.1 2.7 %collective-permute-done.6.refs_1_ = bf16[8,128,128]{2,1,0:T(8,128)(2,1)S(1)} collective-permute-done((bf16[8,128,128]{2,1,0:T(8,128)(2,1)S(1)}, bf16[8,128,128]{2,1,0:T(8,128)(2,1)S(1)}, u32[]{:S(2)}, u32[]{:S(2)}) %collective-permute-start.6) | collective-permute-done | bytes 262176 | tf_op jit(solution)/shard_map/ppermute | solution.py:363
  28.8 1.5 %collective-permute-start.7 = (bf16[4,128,128]{2,1,0:T(8,128)(2,1)S(1)}, bf16[4,128,128]{2,1,0:T(8,128)(2,1)S(1)}, u32[]{:S(2)}, u32[]{:S(2)}) collective-permute-start(bf16[4,128,128]{2,1,0:T(8,128)(2,1)S(1)} %slice.7), channel_id=1, source_target_pairs={{0,4},{4,8},{8,12},{12,14},{14,10},{10,6},{6,2},{2,0},{1,5},{5,9},... | collective-permute-start | bytes 393224 | tf_op jit(solution)/shard_map/ppermute | solution.py:393
  31.0 1.9 %dense.6.refs_7_ = f32[128,1024]{1,0:T(8,128)S(1)} custom-call(bf16[8,128,128]{2,1,0:T(8,128)(2,1)S(1)} %copy-done.3, bf16[1024,8192]{1,0:T(8,128)(2,1)} %refs_1_.7), custom_call_target="tpu_custom_call" | custom-call | flops 268435456 | bytes 2097152 | tf_op jit(solution)/shard_map/dense/pallas_call | solution.py:39
  32.9 1.4 %fold_late.1 = (f32[128,256]{1,0:T(8,128)S(1)}, f32[64,128,128]{2,1,0:T(8,128)S(1)}) custom-call(bf16[8,128,128]{2,1,0:T(8,128)(2,1)S(1)} %collective-permute-done.2.refs_0_, bf16[8,128,128]{2,1,0:T(8,128)(2,1)S(1)} %collective-permute-done.6.refs_1_, s32[128,128]{1,0:T(8,128)S(1)} %get-tuple-element.49.refs_5_.refs_2_, bf16[256,8192]{1,0:T(8,128)(2,1)S(1)} %bitcast.20, ...), custom_call_target="tpu_custom_call" | custom-call | flops 134217728 | bytes 1048576 | tf_op jit(solution)/shard_map/fold_late/pallas_call | solution.py:39
  34.4 1.0 %collective-permute-done.5.refs_0_ = bf16[4,128,128]{2,1,0:T(8,128)(2,1)S(1)} collective-permute-done((bf16[4,128,128]{2,1,0:T(8,128)(2,1)S(1)}, bf16[4,128,128]{2,1,0:T(8,128)(2,1)S(1)}, u32[]{:S(2)}, u32[]{:S(2)}) %collective-permute-start.5) | collective-permute-done | bytes 131104 | tf_op jit(solution)/shard_map/ppermute | solution.py:392
  35.4 1.4 %finish.1 = (bf16[128,256]{1,0:T(8,128)(2,1)S(1)}, f32[8,128,128]{2,1,0:T(8,128)S(1)}, bf16[8,64,128]{2,1,0:T(8,128)(2,1)S(1)}, bf16[8,64,128]{2,1,0:T(8,128)(2,1)S(1)}) custom-call(bf16[4,128,128]{2,1,0:T(8,128)(2,1)S(1)} %collective-permute-done.5.refs_0_, bf16[4,128,128]{2,1,0:T(8,128)(2,1)S(1)} %collective-permute-done.7.refs_1_, ...), custom_call_target="tpu_custom_call" | custom-call | flops 268435456 | bytes 2097152 | tf_op jit(solution)/shard_map/finish/pallas_call | solution.py:39
  36.8 1.2 %collective-permute-start.8 = (bf16[8,64,128]{2,1,0:T(8,128)(2,1)S(1)}, bf16[8,64,128]{2,1,0:T(8,128)(2,1)S(1)}, u32[]{:S(2)}, u32[]{:S(2)}) collective-permute-start(bf16[8,64,128]{2,1,0:T(8,128)(2,1)S(1)} %get-tuple-element.69), channel_id=1, source_target_pairs={{4,0},{8,4},{12,8},{14,12},{10,14},{6,10},{2,6},{0,2},{5,1},{9,5},... | collective-permute-start | bytes 393224 | tf_op jit(solution)/shard_map/ppermute | solution.py:441
  38.9 1.2 %join.11 = (bf16[8,64,128]{2,1,0:T(8,128)(2,1)S(1)}, bf16[8,64,128]{2,1,0:T(8,128)(2,1)S(1)}) custom-call(bf16[128,256]{1,0:T(8,128)(2,1)S(1)} %get-tuple-element.77.refs_0_, bf16[256,8192]{1,0:T(8,128)(2,1)S(1)} %bitcast.12, f32[64,128,128]{2,1,0:T(8,128)S(1)} %get-tuple-element.61.refs_10_.refs_2_, f32[8,128,128]{2,1,0:T(8,128)S(1)} %get-tuple-element.63.refs_3_, ...), custom_call_target="tpu_custom_call" | custom-call | flops 67108864 | bytes 1048576 | tf_op jit(solution)/shard_map/join/pallas_call | solution.py:39
  40.1 1.2 %collective-permute-start.16 = (bf16[8,64,128]{2,1,0:T(8,128)(2,1)S(1)}, bf16[8,64,128]{2,1,0:T(8,128)(2,1)S(1)}, u32[]{:S(2)}, u32[]{:S(2)}) collective-permute-start(bf16[8,64,128]{2,1,0:T(8,128)(2,1)S(1)} %get-tuple-element.81), channel_id=1, source_target_pairs={{4,0},{8,4},{12,8},{14,12},{10,14},{6,10},{2,6},{0,2},{5,1},{9,5},... | collective-permute-start | bytes 393224 | tf_op jit(solution)/shard_map/ppermute | solution.py:444
  42.9 1.2 %join.7 = (bf16[8,64,128]{2,1,0:T(8,128)(2,1)S(1)}, bf16[8,64,128]{2,1,0:T(8,128)(2,1)S(1)}) custom-call(bf16[128,256]{1,0:T(8,128)(2,1)S(1)} %get-tuple-element.77.refs_0_, bf16[256,8192]{1,0:T(8,128)(2,1)S(1)} %bitcast.13, f32[64,128,128]{2,1,0:T(8,128)S(1)} %get-tuple-element.61.refs_10_.refs_2_, f32[8,128,128]{2,1,0:T(8,128)S(1)} %get-tuple-element.63.refs_3_, ...), custom_call_target="tpu_custom_call" | custom-call | flops 67108864 | bytes 1048576 | tf_op jit(solution)/shard_map/join/pallas_call | solution.py:39
  44.2 1.6 %collective-permute-start.10 = (bf16[8,64,128]{2,1,0:T(8,128)(2,1)S(1)}, bf16[8,64,128]{2,1,0:T(8,128)(2,1)S(1)}, u32[]{:S(2)}, u32[]{:S(2)}) collective-permute-start(bf16[8,64,128]{2,1,0:T(8,128)(2,1)S(1)} %get-tuple-element.71), channel_id=1, source_target_pairs={{4,0},{8,4},{12,8},{14,12},{10,14},{6,10},{2,6},{0,2},{5,1},{9,5},... | collective-permute-start | bytes 393224 | tf_op jit(solution)/shard_map/ppermute | solution.py:441
  46.4 1.2 %join.12 = (bf16[8,64,128]{2,1,0:T(8,128)(2,1)S(1)}, bf16[8,64,128]{2,1,0:T(8,128)(2,1)S(1)}) custom-call(bf16[128,256]{1,0:T(8,128)(2,1)S(1)} %get-tuple-element.77.refs_0_, bf16[256,8192]{1,0:T(8,128)(2,1)S(1)} %bitcast.14, f32[64,128,128]{2,1,0:T(8,128)S(1)} %get-tuple-element.61.refs_10_.refs_2_, f32[8,128,128]{2,1,0:T(8,128)S(1)} %get-tuple-element.63.refs_3_, ...), custom_call_target="tpu_custom_call" | custom-call | flops 67108864 | bytes 1048576 | tf_op jit(solution)/shard_map/join/pallas_call | solution.py:39
  47.7 1.6 %collective-permute-start.18 = (bf16[8,64,128]{2,1,0:T(8,128)(2,1)S(1)}, bf16[8,64,128]{2,1,0:T(8,128)(2,1)S(1)}, u32[]{:S(2)}, u32[]{:S(2)}) collective-permute-start(bf16[8,64,128]{2,1,0:T(8,128)(2,1)S(1)} %get-tuple-element.83), channel_id=1, source_target_pairs={{4,0},{8,4},{12,8},{14,12},{10,14},{6,10},{2,6},{0,2},{5,1},{9,5},... | collective-permute-start | bytes 393224 | tf_op jit(solution)/shard_map/ppermute | solution.py:444
  49.7 1.3 %collective-permute-done.11.refs_10_ = bf16[8,64,128]{2,1,0:T(8,128)(2,1)S(1)} collective-permute-done((bf16[8,64,128]{2,1,0:T(8,128)(2,1)S(1)}, bf16[8,64,128]{2,1,0:T(8,128)(2,1)S(1)}, u32[]{:S(2)}, u32[]{:S(2)}) %collective-permute-start.11) | collective-permute-done | bytes 131104 | tf_op jit(solution)/shard_map/ppermute | solution.py:441
  51.1 1.2 %join.8 = (bf16[8,64,128]{2,1,0:T(8,128)(2,1)S(1)}, bf16[8,64,128]{2,1,0:T(8,128)(2,1)S(1)}) custom-call(bf16[128,256]{1,0:T(8,128)(2,1)S(1)} %get-tuple-element.77.refs_0_, bf16[256,8192]{1,0:T(8,128)(2,1)S(1)} %bitcast.15, f32[64,128,128]{2,1,0:T(8,128)S(1)} %get-tuple-element.61.refs_10_.refs_2_, f32[8,128,128]{2,1,0:T(8,128)S(1)} %get-tuple-element.63.refs_3_, ...), custom_call_target="tpu_custom_call" | custom-call | flops 67108864 | bytes 1048576 | tf_op jit(solution)/shard_map/join/pallas_call | solution.py:39
  52.3 1.6 %collective-permute-start.12 = (bf16[8,64,128]{2,1,0:T(8,128)(2,1)S(1)}, bf16[8,64,128]{2,1,0:T(8,128)(2,1)S(1)}, u32[]{:S(2)}, u32[]{:S(2)}) collective-permute-start(bf16[8,64,128]{2,1,0:T(8,128)(2,1)S(1)} %get-tuple-element.73), channel_id=1, source_target_pairs={{4,0},{8,4},{12,8},{14,12},{10,14},{6,10},{2,6},{0,2},{5,1},{9,5},... | collective-permute-start | bytes 393224 | tf_op jit(solution)/shard_map/ppermute | solution.py:441
  55.0 1.2 %join.13 = (bf16[8,64,128]{2,1,0:T(8,128)(2,1)S(1)}, bf16[8,64,128]{2,1,0:T(8,128)(2,1)S(1)}) custom-call(bf16[128,256]{1,0:T(8,128)(2,1)S(1)} %get-tuple-element.77.refs_0_, bf16[256,8192]{1,0:T(8,128)(2,1)S(1)} %bitcast.16, f32[64,128,128]{2,1,0:T(8,128)S(1)} %get-tuple-element.61.refs_10_.refs_2_, f32[8,128,128]{2,1,0:T(8,128)S(1)} %get-tuple-element.63.refs_3_, ...), custom_call_target="tpu_custom_call" | custom-call | flops 67108864 | bytes 1048576 | tf_op jit(solution)/shard_map/join/pallas_call | solution.py:39
  56.8 1.5 %collective-permute-start.21 = (bf16[8,64,128]{2,1,0:T(8,128)(2,1)S(1)}, bf16[8,64,128]{2,1,0:T(8,128)(2,1)S(1)}, u32[]{:S(2)}, u32[]{:S(2)}) collective-permute-start(bf16[8,64,128]{2,1,0:T(8,128)(2,1)S(1)} %get-tuple-element.86), channel_id=1, source_target_pairs={{4,0},{8,4},{12,8},{14,12},{10,14},{6,10},{2,6},{0,2},{5,1},{9,5},... | collective-permute-start | bytes 393224 | tf_op jit(solution)/shard_map/ppermute | solution.py:444
  58.5 1.8 %collective-permute-done.13.refs_10_ = bf16[8,64,128]{2,1,0:T(8,128)(2,1)S(1)} collective-permute-done((bf16[8,64,128]{2,1,0:T(8,128)(2,1)S(1)}, bf16[8,64,128]{2,1,0:T(8,128)(2,1)S(1)}, u32[]{:S(2)}, u32[]{:S(2)}) %collective-permute-start.13) | collective-permute-done | bytes 131104 | tf_op jit(solution)/shard_map/ppermute | solution.py:441
  60.3 1.2 %join.9 = (bf16[8,64,128]{2,1,0:T(8,128)(2,1)S(1)}, bf16[8,64,128]{2,1,0:T(8,128)(2,1)S(1)}) custom-call(bf16[128,256]{1,0:T(8,128)(2,1)S(1)} %get-tuple-element.77.refs_0_, bf16[256,8192]{1,0:T(8,128)(2,1)S(1)} %bitcast.17, f32[64,128,128]{2,1,0:T(8,128)S(1)} %get-tuple-element.61.refs_10_.refs_2_, f32[8,128,128]{2,1,0:T(8,128)S(1)} %get-tuple-element.63.refs_3_, ...), custom_call_target="tpu_custom_call" | custom-call | flops 67108864 | bytes 1048576 | tf_op jit(solution)/shard_map/join/pallas_call | solution.py:39
  61.5 1.8 %collective-permute-start.14 = (bf16[8,64,128]{2,1,0:T(8,128)(2,1)S(1)}, bf16[8,64,128]{2,1,0:T(8,128)(2,1)S(1)}, u32[]{:S(2)}, u32[]{:S(2)}) collective-permute-start(bf16[8,64,128]{2,1,0:T(8,128)(2,1)S(1)} %get-tuple-element.75), channel_id=1, source_target_pairs={{4,0},{8,4},{12,8},{14,12},{10,14},{6,10},{2,6},{0,2},{5,1},{9,5},... | collective-permute-start | bytes 393224 | tf_op jit(solution)/shard_map/ppermute | solution.py:441
  63.6 1.9 %dense.7.refs_7_.refs_8_ = f32[128,1024]{1,0:T(8,128)S(1)} custom-call(bf16[8,128,128]{2,1,0:T(8,128)(2,1)S(1)} %copy-done.3, bf16[1024,8192]{1,0:T(8,128)(2,1)} %refs_1_.7), custom_call_target="tpu_custom_call" | custom-call | flops 268435456 | bytes 2097152 | tf_op jit(solution)/shard_map/dense/pallas_call | solution.py:39
  65.5 1.2 %join.10 = (f32[8,64,128]{2,1,0:T(8,128)S(1)}, f32[8,64,128]{2,1,0:T(8,128)S(1)}) custom-call(bf16[128,256]{1,0:T(8,128)(2,1)S(1)} %get-tuple-element.77.refs_0_, bf16[256,8192]{1,0:T(8,128)(2,1)S(1)} %bitcast.18, f32[64,128,128]{2,1,0:T(8,128)S(1)} %get-tuple-element.61.refs_10_.refs_2_, f32[8,128,128]{2,1,0:T(8,128)S(1)} %get-tuple-element.63.refs_3_, ...), custom_call_target="tpu_custom_call" | custom-call | flops 67108864 | bytes 1048576 | tf_op jit(solution)/shard_map/join/pallas_call | solution.py:39
  66.8 1.5 %collective-permute-done.15.refs_1_ = bf16[8,64,128]{2,1,0:T(8,128)(2,1)S(1)} collective-permute-done((bf16[8,64,128]{2,1,0:T(8,128)(2,1)S(1)}, bf16[8,64,128]{2,1,0:T(8,128)(2,1)S(1)}, u32[]{:S(2)}, u32[]{:S(2)}) %collective-permute-start.15) | collective-permute-done | bytes 131104 | tf_op jit(solution)/shard_map/ppermute | solution.py:441
  (48 shorter events, 8.7 us)
Async XLA Ops:
  0.0 16.3 %copy-start.6 = (s32[4,16,1]{1,2,0:T(1,128)S(1)}, s32[4,16,1]{1,2,0:T(1,128)}, u32[]{:S(2)}) copy-start(s32[4,16,1]{1,2,0:T(1,128)} %param.28) | copy-start | bytes 772
  0.0 16.3 %copy-start.7 = (s32[128]{0:T(128)S(1)}, s32[128]{0:T(128)}, u32[]{:S(2)}) copy-start(s32[128]{0:T(128)} %param.21) | copy-start | bytes 1540
  0.0 16.3 %copy-start.8 = (s32[32]{0:T(128)S(1)}, s32[32]{0:T(128)}, u32[]{:S(2)}) copy-start(s32[32]{0:T(128)} %refs_3_.1) | copy-start | bytes 388
  4.8 9.5 %collective-permute-start.3 = (bf16[8,128,128]{2,1,0:T(8,128)(2,1)}, bf16[8,128,128]{2,1,0:T(8,128)(2,1)S(1)}, u32[]{:S(2)}, u32[]{:S(2)}) collective-permute-start(bf16[8,128,128]{2,1,0:T(8,128)(2,1)} %attend.1.refs_0_), channel_id=1, source_target_pairs={{0,4},{4,8},{8,12},{12,14},{14,10},{10,6},{6,2},{2,0},{1,5},{5,9},... | collective-permute-start | bytes 786440 | tf_op jit(solution)/shard_map/ppermute | solution.py:363
  7.8 8.3 %collective-permute-start = (bf16[8,128,128]{2,1,0:T(8,128)(2,1)}, bf16[8,128,128]{2,1,0:T(8,128)(2,1)S(1)}, u32[]{:S(2)}, u32[]{:S(2)}) collective-permute-start(bf16[8,128,128]{2,1,0:T(8,128)(2,1)} %attend.1.refs_0_), channel_id=1, source_target_pairs={{4,0},{8,4},{12,8},{14,12},{10,14},{6,10},{2,6},{0,2},{5,1},{9,5},... | collective-permute-start | bytes 786440 | tf_op jit(solution)/shard_map/ppermute | solution.py:362
  7.9 1.0 %copy-start.3 = (bf16[8,128,128]{2,1,0:T(8,128)(2,1)S(1)}, bf16[8,128,128]{2,1,0:T(8,128)(2,1)}, u32[]{:S(2)}) copy-start(bf16[8,128,128]{2,1,0:T(8,128)(2,1)} %attend.1.refs_0_) | copy-start | bytes 786436
  14.3 7.5 %collective-permute-start.4 = (bf16[8,128,128]{2,1,0:T(8,128)(2,1)S(1)}, bf16[8,128,128]{2,1,0:T(8,128)(2,1)S(1)}, u32[]{:S(2)}, u32[]{:S(2)}) collective-permute-start(bf16[8,128,128]{2,1,0:T(8,128)(2,1)S(1)} %collective-permute-done.3.refs_2_), channel_id=1, source_target_pairs={{0,4},{4,8},{8,12},{12,14},{14,10},{10,6},{6,2},{2,0},{1,5},{5,9},... | collective-permute-start | bytes 786440 | tf_op jit(solution)/shard_map/ppermute | solution.py:363
  16.1 7.6 %collective-permute-start.1 = (bf16[8,128,128]{2,1,0:T(8,128)(2,1)S(1)}, bf16[8,128,128]{2,1,0:T(8,128)(2,1)S(1)}, u32[]{:S(2)}, u32[]{:S(2)}) collective-permute-start(bf16[8,128,128]{2,1,0:T(8,128)(2,1)S(1)} %collective-permute-done.refs_1_), channel_id=1, source_target_pairs={{4,0},{8,4},{12,8},{14,12},{10,14},{6,10},{2,6},{0,2},{5,1},{9,5},... | collective-permute-start | bytes 786440 | tf_op jit(solution)/shard_map/ppermute | solution.py:362
  16.3 7.6 %copy-start.1 = (bf16[4,8192,64]{1,2,0:T(8,128)(2,1)S(1)}, bf16[4,8192,64]{1,2,0:T(8,128)(2,1)}, u32[]{:S(2)}) copy-start(bf16[4,8192,64]{1,2,0:T(8,128)(2,1)} %param.24) | copy-start | bytes 12582916
  16.4 7.6 %copy-start.2 = (bf16[4,16,128,128]{3,2,1,0:T(8,128)(2,1)S(1)}, bf16[4,16,128,128]{3,2,1,0:T(8,128)(2,1)}, u32[]{:S(2)}) copy-start(bf16[4,16,128,128]{3,2,1,0:T(8,128)(2,1)} %refs_4_.10) | copy-start | bytes 6291460
  16.4 7.6 %copy-start.4 = (f32[4,16]{1,0:T(4,128)S(1)}, f32[4,16]{1,0:T(4,128)}, u32[]{:S(2)}) copy-start(f32[4,16]{1,0:T(4,128)} %refs_4_.17) | copy-start | bytes 772
  16.4 7.6 %copy-start.5 = (s32[4,16]{1,0:T(4,128)S(1)}, s32[4,16]{1,0:T(4,128)}, u32[]{:S(2)}) copy-start(s32[4,16]{1,0:T(4,128)} %refs_5_.17) | copy-start | bytes 772
  21.8 7.0 %collective-permute-start.6 = (bf16[8,128,128]{2,1,0:T(8,128)(2,1)S(1)}, bf16[8,128,128]{2,1,0:T(8,128)(2,1)S(1)}, u32[]{:S(2)}, u32[]{:S(2)}) collective-permute-start(bf16[8,128,128]{2,1,0:T(8,128)(2,1)S(1)} %collective-permute-done.4.refs_4_), channel_id=1, source_target_pairs={{0,4},{4,8},{8,12},{12,14},{14,10},{10,6},{6,2},{2,0},{1,5},{5,9},... | collective-permute-start | bytes 786440 | tf_op jit(solution)/shard_map/ppermute | solution.py:363
  23.7 6.7 %collective-permute-start.2 = (bf16[8,128,128]{2,1,0:T(8,128)(2,1)S(1)}, bf16[8,128,128]{2,1,0:T(8,128)(2,1)S(1)}, u32[]{:S(2)}, u32[]{:S(2)}) collective-permute-start(bf16[8,128,128]{2,1,0:T(8,128)(2,1)S(1)} %collective-permute-done.1.refs_3_), channel_id=1, source_target_pairs={{4,0},{8,4},{12,8},{14,12},{10,14},{6,10},{2,6},{0,2},{5,1},{9,5},... | collective-permute-start | bytes 786440 | tf_op jit(solution)/shard_map/ppermute | solution.py:362
  28.8 5.5 %collective-permute-start.7 = (bf16[4,128,128]{2,1,0:T(8,128)(2,1)S(1)}, bf16[4,128,128]{2,1,0:T(8,128)(2,1)S(1)}, u32[]{:S(2)}, u32[]{:S(2)}) collective-permute-start(bf16[4,128,128]{2,1,0:T(8,128)(2,1)S(1)} %slice.7), channel_id=1, source_target_pairs={{0,4},{4,8},{8,12},{12,14},{14,10},{10,6},{6,2},{2,0},{1,5},{5,9},... | collective-permute-start | bytes 393224 | tf_op jit(solution)/shard_map/ppermute | solution.py:393
  30.4 5.0 %collective-permute-start.5 = (bf16[4,128,128]{2,1,0:T(8,128)(2,1)S(1)}, bf16[4,128,128]{2,1,0:T(8,128)(2,1)S(1)}, u32[]{:S(2)}, u32[]{:S(2)}) collective-permute-start(bf16[4,128,128]{2,1,0:T(8,128)(2,1)S(1)} %slice.6), channel_id=1, source_target_pairs={{4,0},{8,4},{12,8},{14,12},{10,14},{6,10},{2,6},{0,2},{5,1},{9,5},... | collective-permute-start | bytes 393224 | tf_op jit(solution)/shard_map/ppermute | solution.py:392
  32.9 2.5 %copy-start = (bf16[4,64,8192]{2,1,0:T(8,128)(2,1)S(1)}, bf16[4,64,8192]{2,1,0:T(8,128)(2,1)}, u32[]{:S(2)}) copy-start(bf16[4,64,8192]{2,1,0:T(8,128)(2,1)} %param.25) | copy-start | bytes 12582916
  36.8 5.4 %collective-permute-start.8 = (bf16[8,64,128]{2,1,0:T(8,128)(2,1)S(1)}, bf16[8,64,128]{2,1,0:T(8,128)(2,1)S(1)}, u32[]{:S(2)}, u32[]{:S(2)}) collective-permute-start(bf16[8,64,128]{2,1,0:T(8,128)(2,1)S(1)} %get-tuple-element.69), channel_id=1, source_target_pairs={{4,0},{8,4},{12,8},{14,12},{10,14},{6,10},{2,6},{0,2},{5,1},{9,5},... | collective-permute-start | bytes 393224 | tf_op jit(solution)/shard_map/ppermute | solution.py:441
  38.0 5.0 %collective-permute-start.9 = (bf16[8,64,128]{2,1,0:T(8,128)(2,1)S(1)}, bf16[8,64,128]{2,1,0:T(8,128)(2,1)S(1)}, u32[]{:S(2)}, u32[]{:S(2)}) collective-permute-start(bf16[8,64,128]{2,1,0:T(8,128)(2,1)S(1)} %get-tuple-element.70), channel_id=1, source_target_pairs={{0,4},{4,8},{8,12},{12,14},{14,10},{10,6},{6,2},{2,0},{1,5},{5,9},... | collective-permute-start | bytes 393224 | tf_op jit(solution)/shard_map/ppermute | solution.py:441
  40.1 6.1 %collective-permute-start.16 = (bf16[8,64,128]{2,1,0:T(8,128)(2,1)S(1)}, bf16[8,64,128]{2,1,0:T(8,128)(2,1)S(1)}, u32[]{:S(2)}, u32[]{:S(2)}) collective-permute-start(bf16[8,64,128]{2,1,0:T(8,128)(2,1)S(1)} %get-tuple-element.81), channel_id=1, source_target_pairs={{4,0},{8,4},{12,8},{14,12},{10,14},{6,10},{2,6},{0,2},{5,1},{9,5},... | collective-permute-start | bytes 393224 | tf_op jit(solution)/shard_map/ppermute | solution.py:444
  41.3 5.1 %collective-permute-start.17 = (bf16[8,64,128]{2,1,0:T(8,128)(2,1)S(1)}, bf16[8,64,128]{2,1,0:T(8,128)(2,1)S(1)}, u32[]{:S(2)}, u32[]{:S(2)}) collective-permute-start(bf16[8,64,128]{2,1,0:T(8,128)(2,1)S(1)} %get-tuple-element.82), channel_id=1, source_target_pairs={{0,4},{4,8},{8,12},{12,14},{14,10},{10,6},{6,2},{2,0},{1,5},{5,9},... | collective-permute-start | bytes 393224 | tf_op jit(solution)/shard_map/ppermute | solution.py:444
  44.2 5.5 %collective-permute-start.10 = (bf16[8,64,128]{2,1,0:T(8,128)(2,1)S(1)}, bf16[8,64,128]{2,1,0:T(8,128)(2,1)S(1)}, u32[]{:S(2)}, u32[]{:S(2)}) collective-permute-start(bf16[8,64,128]{2,1,0:T(8,128)(2,1)S(1)} %get-tuple-element.71), channel_id=1, source_target_pairs={{4,0},{8,4},{12,8},{14,12},{10,14},{6,10},{2,6},{0,2},{5,1},{9,5},... | collective-permute-start | bytes 393224 | tf_op jit(solution)/shard_map/ppermute | solution.py:441
  45.8 5.3 %collective-permute-start.11 = (bf16[8,64,128]{2,1,0:T(8,128)(2,1)S(1)}, bf16[8,64,128]{2,1,0:T(8,128)(2,1)S(1)}, u32[]{:S(2)}, u32[]{:S(2)}) collective-permute-start(bf16[8,64,128]{2,1,0:T(8,128)(2,1)S(1)} %get-tuple-element.72), channel_id=1, source_target_pairs={{0,4},{4,8},{8,12},{12,14},{14,10},{10,6},{6,2},{2,0},{1,5},{5,9},... | collective-permute-start | bytes 393224 | tf_op jit(solution)/shard_map/ppermute | solution.py:441
  47.7 6.7 %collective-permute-start.18 = (bf16[8,64,128]{2,1,0:T(8,128)(2,1)S(1)}, bf16[8,64,128]{2,1,0:T(8,128)(2,1)S(1)}, u32[]{:S(2)}, u32[]{:S(2)}) collective-permute-start(bf16[8,64,128]{2,1,0:T(8,128)(2,1)S(1)} %get-tuple-element.83), channel_id=1, source_target_pairs={{4,0},{8,4},{12,8},{14,12},{10,14},{6,10},{2,6},{0,2},{5,1},{9,5},... | collective-permute-start | bytes 393224 | tf_op jit(solution)/shard_map/ppermute | solution.py:444
  49.3 5.7 %collective-permute-start.19 = (bf16[8,64,128]{2,1,0:T(8,128)(2,1)S(1)}, bf16[8,64,128]{2,1,0:T(8,128)(2,1)S(1)}, u32[]{:S(2)}, u32[]{:S(2)}) collective-permute-start(bf16[8,64,128]{2,1,0:T(8,128)(2,1)S(1)} %get-tuple-element.84), channel_id=1, source_target_pairs={{0,4},{4,8},{8,12},{12,14},{14,10},{10,6},{6,2},{2,0},{1,5},{5,9},... | collective-permute-start | bytes 393224 | tf_op jit(solution)/shard_map/ppermute | solution.py:444
  52.3 6.2 %collective-permute-start.12 = (bf16[8,64,128]{2,1,0:T(8,128)(2,1)S(1)}, bf16[8,64,128]{2,1,0:T(8,128)(2,1)S(1)}, u32[]{:S(2)}, u32[]{:S(2)}) collective-permute-start(bf16[8,64,128]{2,1,0:T(8,128)(2,1)S(1)} %get-tuple-element.73), channel_id=1, source_target_pairs={{4,0},{8,4},{12,8},{14,12},{10,14},{6,10},{2,6},{0,2},{5,1},{9,5},... | collective-permute-start | bytes 393224 | tf_op jit(solution)/shard_map/ppermute | solution.py:441
  53.9 6.4 %collective-permute-start.13 = (bf16[8,64,128]{2,1,0:T(8,128)(2,1)S(1)}, bf16[8,64,128]{2,1,0:T(8,128)(2,1)S(1)}, u32[]{:S(2)}, u32[]{:S(2)}) collective-permute-start(bf16[8,64,128]{2,1,0:T(8,128)(2,1)S(1)} %get-tuple-element.74), channel_id=1, source_target_pairs={{0,4},{4,8},{8,12},{12,14},{14,10},{10,6},{6,2},{2,0},{1,5},{5,9},... | collective-permute-start | bytes 393224 | tf_op jit(solution)/shard_map/ppermute | solution.py:441
  56.2 10.5 %collective-permute-start.20 = (bf16[8,64,128]{2,1,0:T(8,128)(2,1)S(1)}, bf16[8,64,128]{2,1,0:T(8,128)(2,1)S(1)}, u32[]{:S(2)}, u32[]{:S(2)}) collective-permute-start(bf16[8,64,128]{2,1,0:T(8,128)(2,1)S(1)} %get-tuple-element.85), channel_id=1, source_target_pairs={{0,4},{4,8},{8,12},{12,14},{14,10},{10,6},{6,2},{2,0},{1,5},{5,9},... | collective-permute-start | bytes 393224 | tf_op jit(solution)/shard_map/ppermute | solution.py:444
  56.8 10.0 %collective-permute-start.21 = (bf16[8,64,128]{2,1,0:T(8,128)(2,1)S(1)}, bf16[8,64,128]{2,1,0:T(8,128)(2,1)S(1)}, u32[]{:S(2)}, u32[]{:S(2)}) collective-permute-start(bf16[8,64,128]{2,1,0:T(8,128)(2,1)S(1)} %get-tuple-element.86), channel_id=1, source_target_pairs={{4,0},{8,4},{12,8},{14,12},{10,14},{6,10},{2,6},{0,2},{5,1},{9,5},... | collective-permute-start | bytes 393224 | tf_op jit(solution)/shard_map/ppermute | solution.py:444
  61.5 5.2 %collective-permute-start.14 = (bf16[8,64,128]{2,1,0:T(8,128)(2,1)S(1)}, bf16[8,64,128]{2,1,0:T(8,128)(2,1)S(1)}, u32[]{:S(2)}, u32[]{:S(2)}) collective-permute-start(bf16[8,64,128]{2,1,0:T(8,128)(2,1)S(1)} %get-tuple-element.75), channel_id=1, source_target_pairs={{4,0},{8,4},{12,8},{14,12},{10,14},{6,10},{2,6},{0,2},{5,1},{9,5},... | collective-permute-start | bytes 393224 | tf_op jit(solution)/shard_map/ppermute | solution.py:441
  63.3 5.0 %collective-permute-start.15 = (bf16[8,64,128]{2,1,0:T(8,128)(2,1)S(1)}, bf16[8,64,128]{2,1,0:T(8,128)(2,1)S(1)}, u32[]{:S(2)}, u32[]{:S(2)}) collective-permute-start(bf16[8,64,128]{2,1,0:T(8,128)(2,1)S(1)} %get-tuple-element.76), channel_id=1, source_target_pairs={{0,4},{4,8},{8,12},{12,14},{14,10},{10,6},{6,2},{2,0},{1,5},{5,9},... | collective-permute-start | bytes 393224 | tf_op jit(solution)/shard_map/ppermute | solution.py:441

commit v7 on v6

--- a/solution.py
+++ b/solution.py
@@ -207,17 +207,16 @@
             block_ref[column] += product
 
 
-def part_for(distance, count, low_ref, second_ref, dense_ref, block_ref, extra_ref, columns, rows,
-             out_ref):
+def part_for(distance, count, low_ref, second_ref, dense_ref, block_ref, extra_ref, columns, out_ref):
     width = dense_ref.shape[1]
     side = block_ref.shape[2]
     heads = width // side
     owner = owner_at(distance, count)
     start = pl.multiple_of(owner * width, width)
-    blocks = jnp.concatenate([block_ref[owner * heads + i, rows] for i in range(heads)], axis=1)
+    blocks = jnp.concatenate([block_ref[owner * heads + i] for i in range(heads)], axis=1)
     out_ref[...] = (
-        jnp.dot(low_ref[rows], second_ref[:, pl.ds(start, width)], preferred_element_type=F32)
-        + dense_ref[rows]
+        jnp.dot(low_ref[...], second_ref[:, pl.ds(start, width)], preferred_element_type=F32)
+        + dense_ref[...]
         + blocks
     )
     for e, column in enumerate(columns):
@@ -225,20 +224,21 @@
         @pl.when(lax.div(column, heads) == owner)
         def _(e=e, column=column):
             place = pl.ds(pl.multiple_of(lax.rem(column, heads) * side, side), side)
-            out_ref[:, place] += extra_ref[e, rows]
-
-
-def finish_kernel(distance, count, *refs):
+            out_ref[:, place] += extra_ref[e]
+
+
+def finish_kernel(distances, count, *refs):
     front_ref, back_ref, slot_ref, factor_ref, values_ref, scale_ref, cell_ref, table_ref = refs[:8]
     second_ref, low_in, block_ref = refs[8:11]
-    dense_ref, low_out, extra_out, top_out, bottom_out = refs[11:16]
-    chunk, low_sum, farthest = refs[-3:]
+    dense_refs, refs = refs[11 : 11 + len(distances)], refs[11 + len(distances) :]
+    low_out, extra_out, front_out, back_out = refs[:4]
+    outs, (chunk, low_sum, total) = refs[4:-3], refs[-3:]
     half, rows, side = front_ref.shape
     chunk[:half] = front_ref[...]
     chunk[half:] = back_ref[...]
     low_sum[...] = low_in[...]
     slot = slot_ref[...]
-    added = fold_chunk(distance, count, chunk, slot, factor_ref, values_ref, scale_ref, cell_ref,
+    added = fold_chunk(distances[0], count, chunk, slot, factor_ref, values_ref, scale_ref, cell_ref,
                        table_ref, low_sum)
     for e, (_, product) in enumerate(added):
         extra_out[e] = product
@@ -249,46 +249,42 @@
     slots_wide = jnp.concatenate([slot] * -(-low_width // side), axis=1)[:, :low_width]
     low = jnp.where(slots_wide == held, low_sum[...], 0.0).astype(BF16)
     low_out[...] = low
-    part_for(distance, count, low_out, second_ref, dense_ref, block_ref, extra_out, columns,
-             slice(0, rows), farthest)
-    for i in range(2 * half):
-        tile = farthest[:, i * side : (i + 1) * side].astype(BF16)
-        top_out[i] = tile[: rows // 2]
-        bottom_out[i] = tile[rows // 2 :]
-
-
-def join_kernel(jobs, count, slots, *refs):
+    for n, (distance, dense_ref) in enumerate(zip(distances, dense_refs)):
+        part_for(distance, count, low_out, second_ref, dense_ref, block_ref, extra_out, columns,
+                 total.at[n])
+        for i in range(2 * half):
+            tile = total[n, :, i * side : (i + 1) * side].astype(BF16)
+            if n:
+                outs[n - 1][i] = tile
+            elif i < half:
+                front_out[i] = tile
+            else:
+                back_out[i - half] = tile
+
+
+def part_kernel(distances, count, slots, *refs):
     low_ref, second_ref, block_ref, extra_ref, scale_ref, cell_ref, table_ref = refs[:7]
-    dense_refs, refs = refs[7 : 7 + len(jobs)], refs[7 + len(jobs) :]
-    came, outs, totals = refs[: -2 * len(jobs)], refs[-2 * len(jobs) : -len(jobs)], refs[-len(jobs) :]
-    rows, width = dense_refs[0].shape
-    heads = width // block_ref.shape[2]
+    dense_refs, refs = refs[7 : 7 + len(distances)], refs[7 + len(distances) :]
+    outs, total = refs[:-1], refs[-1]
+    side = block_ref.shape[2]
+    heads = dense_refs[0].shape[1] // side
     listed = held_blocks(count // 2, count, slots, heads, scale_ref, cell_ref, table_ref)
     columns = [entry[-1] for entry in listed]
-    for n, (distance, half) in enumerate(jobs):
-        here = slice(half * rows // 2, (half + 1) * rows // 2)
-        part_for(distance, count, low_ref, second_ref, dense_refs[n], block_ref, extra_ref, columns,
-                 here, totals[n])
-        side = width // heads
+    for n, (distance, dense_ref) in enumerate(zip(distances, dense_refs)):
+        part_for(distance, count, low_ref, second_ref, dense_ref, block_ref, extra_ref, columns,
+                 total.at[n])
         for i in range(heads):
-            total = totals[n][:, i * side : (i + 1) * side]
-            if came:
-                total = total + came[n][i].astype(F32)
-            outs[n][i] = total.astype(outs[n].dtype)
-
-
-def sum_kernel(upper_ref, lower_ref, *refs):
+            outs[n][i] = total[n, :, i * side : (i + 1) * side].astype(outs[n].dtype)
+
+
+def sum_kernel(own_ref, *refs):
     out_ref = refs[-1]
-    heads, cut, side = upper_ref.shape
+    heads, _, side = own_ref.shape
     for i in range(heads):
-        upper, lower = upper_ref[i], lower_ref[i]
-        for n, ref in enumerate(refs[:-1]):
-            if n in (0, 2):
-                upper = upper + ref[i].astype(F32)
-            else:
-                lower = lower + ref[i].astype(F32)
-        out_ref[:cut, i * side : (i + 1) * side] = upper.astype(BF16)
-        out_ref[cut:, i * side : (i + 1) * side] = lower.astype(BF16)
+        total = own_ref[i]
+        for ref in refs[:-1]:
+            total = total + ref[i].astype(F32)
+        out_ref[:, i * side : (i + 1) * side] = total.astype(BF16)
 
 
 def after(value, *others):
@@ -302,8 +298,6 @@
     count = lax.axis_size("tp")
     half = count // 2
     ring = ring_order(count)
-    to_right = [(ring[i], ring[(i + 1) % count]) for i in range(count)]
-    to_left = [(ring[(i + 1) % count], ring[i]) for i in range(count)]
     rows, width = queries.shape
     side = key_cache.shape[3]
     cache = key_cache.shape[2]
@@ -353,22 +347,33 @@
         dense.update(zip(distances, got))
         return got[len(distances) :] if listing else got[0]
 
+    def come(value, distance):
+        return lax.ppermute(
+            value, "tp", [(ring[(i + distance) % count], ring[i]) for i in range(count)]
+        )
+
+    short = count == 8
     chunks = {0: attended}
-
-    def pass_on(step, *done):
-        right, left = chunks[step - 1], chunks[(count - step + 1) % count]
-        if done:
-            right, left = after(right, *done), after(left, *done)
-        chunks[step] = lax.ppermute(right, "tp", to_left)
-        chunks[count - step] = lax.ppermute(left, "tp", to_right)
-
-    third = -(-3 * count // 8)
-    pass_on(1)
-    token = dense_for(wanted[:third], attended)
-    pass_on(2, token)
-    slot, table = dense_for(wanted[third : 2 * third], after(attended, token), True)
-    for step in range(3, half):
-        pass_on(step, slot)
+    if short:
+        for distance in (2, 6, 1, 7):
+            chunks[distance] = come(attended, distance if distance <= half else distance - count)
+        wanted = [4, 3, 5, 1, 7, 2, 6, 0]
+        cuts = [5, 7]
+    else:
+        chunks[1], chunks[count - 1] = come(attended, 1), come(attended, -1)
+        cuts = [count // 2, count - 1]
+    token = dense_for(wanted[: cuts[0]], attended)
+    if short:
+        right, left = after(chunks[2], token), after(chunks[6], token)
+        chunks[3], chunks[5] = come(right, 1), come(left, -1)
+        front, back = come(right[: heads // 2], 2), come(left[heads // 2 :], -2)
+    else:
+        for step in range(2, half):
+            right, left = after(chunks[step - 1], token), after(chunks[count - step + 1], token)
+            chunks[step], chunks[count - step] = come(right, 1), come(left, -1)
+        right, left = chunks[half - 1], chunks[half + 1]
+        front, back = come(right[: heads // 2], 1), come(left[heads // 2 :], -1)
+    slot, table = dense_for(wanted[cuts[0] : cuts[1]], after(attended, token), True)
 
     factor_t = jnp.swapaxes(factor_in, 1, 2).reshape(low_width, -1)
     second = second_factor.reshape(low_width, complete)
@@ -389,10 +394,6 @@
         flops=rows * low_width * complete,
         moved=4 * MIB,
     )
-    front = lax.ppermute(after(chunks[half - 1], low)[: heads // 2], "tp", to_left)
-    back = lax.ppermute(after(chunks[count - half + 1], low)[heads // 2 :], "tp", to_right)
-    if len(wanted) > 2 * third + 1:
-        token = dense_for(wanted[2 * third : -1], after(attended, low))
     low, blocks = call(
         functools.partial(fold_kernel, late, count, False),
         "fold_late",
@@ -403,57 +404,80 @@
         flops=rows * low_width * width * 4,
         moved=MIB,
     )
-    low = after(low, token)
     extras = shape((slots * CAP, rows, side), F32)
-    low, extra, top, bottom = call(
-        functools.partial(finish_kernel, half, count),
+    first = [half, half - 1, half + 1] if half > 1 else [half]
+    travelling = shape((heads, rows, side), BF16)
+    low, extra, front, back, *sums = call(
+        functools.partial(finish_kernel, first, count),
         "finish",
         [shape((rows, low_width), BF16), extras]
-        + [shape((heads, rows // 2, side), BF16)] * 2,
-        (front, back, *tables, second, low, blocks, dense[half]),
-        [VMEM] * 2 + table_specs + [VMEM] * 4,
-        [VMEM] * 4,
+        + [shape((heads // 2, rows, side), BF16)] * 2
+        + [travelling] * (len(first) - 1),
+        (front, back, *tables, second, low, blocks, *[dense[d] for d in first]),
+        [VMEM] * 2 + table_specs + [VMEM] * (3 + len(first)),
+        [VMEM] * (3 + len(first)),
         [pltpu.VMEM((heads, rows, side), BF16), pltpu.VMEM((rows, low_width), F32),
-         pltpu.VMEM((rows, width), F32)],
+         pltpu.VMEM((len(first), rows, width), F32)],
         flops=rows * low_width * width * 8,
         moved=2 * MIB,
     )
-
-    def join(jobs, came, low, kind=BF16):
-        return call(
-            functools.partial(join_kernel, jobs, count, slots),
-            "join",
-            [shape((heads, rows // 2, side), kind)] * len(jobs),
+    parts = dict(zip(first[1:], sums))
+
+    def parts_for(distances, low, kind):
+        got = call(
+            functools.partial(part_kernel, distances, count, slots),
+            "part",
+            [shape((heads, rows, side), kind)] * len(distances),
             (low, second, blocks, extra, block_scale, block_cell, table,
-             *[dense[distance] for distance, _ in jobs], *came),
-            [VMEM] * 4 + [SMEM] * 3 + [VMEM] * (len(jobs) + len(came)),
-            [VMEM] * len(jobs),
-            [pltpu.VMEM((rows // 2, width), F32)] * len(jobs),
+             *[dense[distance] for distance in distances]),
+            [VMEM] * 4 + [SMEM] * 3 + [VMEM] * len(distances),
+            [VMEM] * len(distances),
+            [pltpu.VMEM((len(distances), rows, width), F32)],
             flops=rows * low_width * width * 2,
             moved=MIB,
         )
-
-    far, near = (top, bottom), ()
-    for distance in range(half, 0, -1):
-        if distance < half:
-            far = join([(count - distance, 0), (distance, 1)], far, low)
-        ready = far
-        far = [lax.ppermute(far[0], "tp", to_left), lax.ppermute(far[1], "tp", to_right)]
-        if distance > 1:
-            near = join([(count - distance + 1, 1), (distance - 1, 0)], near, low)
-            near = [lax.ppermute(near[0], "tp", to_left), lax.ppermute(near[1], "tp", to_right)]
-    dense_for([0], after(attended, *ready))
-    own = join([(0, 0), (0, 1)], (), after(low, *ready), F32)
-    up_left, low_right = far
-    if half > 1:
-        low_left, up_right = near
-    came = [up_left, low_right] if half == 1 else [up_left, low_right, up_right, low_left]
+        parts.update(zip(distances, got))
+
+    def joined(part, *came):
+        total = part.astype(F32)
+        for value, place in came:
+            value = value.astype(F32)
+            if place is not None:
+                none = jnp.zeros_like(value)
+                value = jnp.concatenate([none, value] if place else [value, none], axis=0)
+            total = total + value
+        return total.astype(BF16)
+
+    if short:
+        from_left, from_right = come(parts[3], -1), come(parts[5], 1)
+        front, back = come(front, -2), come(back, 2)
+        parts_for([1, 7], low, BF16)
+        came = [come(parts[1], -1), come(parts[7], 1)]
+        parts_for([2, 6], after(low, parts[1]), F32)
+        from_left, from_right, front, back = lax.optimization_barrier(
+            (from_left, from_right, front, back)
+        )
+        right = joined(parts[2], (from_left, None), (front, 0))
+        left = joined(parts[6], (from_right, None), (back, 1))
+        came += [come(right, -2), come(left, 2)]
+    else:
+        left, right = (front, 0), (back, 1)
+        left, right = (come(front, 1), 0), (come(back, -1), 1)
+        for distance in range(half - 1, 0, -1):
+            left = joined(parts[count - distance], left)
+            right = joined(parts[distance], right)
+            if distance > 1:
+                parts_for([distance - 1, count - distance + 1], after(low, right), F32)
+            left, right = (come(left, 1), None), (come(right, -1), None)
+        came = [left[0], right[0]]
+    dense_for([0], after(attended, right if short else parts[1]))
+    parts_for([0], low, F32)
     return call(
         sum_kernel,
         "sum_up",
         shape((rows, width), BF16),
-        (*own, *came),
-        [VMEM] * (2 + len(came)),
+        (parts[0], *came),
+        [VMEM] * (1 + len(came)),
         VMEM,
         flops=1,
         moved=1,

time: 69.4 us -> 72.8 us (1.049)
  waiting for transfers between devices: 12 us -> 24.8 us
  Pallas kernels: 31.9 us -> 25.5 us
  starting transfers between devices: 23.9 us -> 19.9 us
    ppermute x22 -> x16, waiting for transfers between devices: 12 us -> 24.8 us  [come(): lax.ppermute(value, 'tp', [(ring[(i + distance) % count], ring[i]) for i...]
    pallas_call x16 -> x11, Pallas kernels: 31.9 us -> 25.5 us  [call(): pl.pallas_call(kernel, out_shape=outs, in_specs=specs, out_specs=out_spec...]
    ppermute x22 -> x16, starting transfers between devices: 23.9 us -> 19.9 us  [come(): lax.ppermute(value, 'tp', [(ring[(i + distance) % count], ring[i]) for i...]
  transfers between devices with their start and end apart: 22 -> 16, of which waited for: 10 -> 8; matrix products, arithmetic and copies ran while one was open for 0% -> 0% of each run, Pallas kernels for 36% -> 25%
where the time goes in v7:
time: 72.8 us; the launch traced here: 71.9 us
  Pallas kernels  25.5 us (35%)
  waiting for transfers between devices  24.8 us (34%)
  starting transfers between devices  19.9 us (27%)
  local copies, waits for them, and re-layouts  1.41 us (2%)
    pallas_call x11, Pallas kernels, call(): pl.pallas_call(kernel, out_shape=outs, in_specs=specs, out_specs=out_spec...  25.5 us
    ppermute x16, waiting for transfers between devices, come(): lax.ppermute(value, 'tp', [(ring[(i + distance) % count], ring[i]) for i...  24.8 us
    ppermute x16, starting transfers between devices, come(): lax.ppermute(value, 'tp', [(ring[(i + distance) % count], ring[i]) for i...  19.9 us
  transfers between devices with their start and end apart: 16, of which 8 were waited for; matrix products, arithmetic and copies ran while one was open for 0% of the time, Pallas kernels for 25%

profile of v7, /device:TPU:0, one launch (start us, length us, event | category | flops | bytes accessed | tf_op | source)
XLA Modules:
  0.0 71.9 jit_solution(3279757981256387894)
XLA Ops:
  0.0 4.8 %attend.1.refs_0_ = bf16[8,128,128]{2,1,0:T(8,128)(2,1)} custom-call(bf16[128,1024]{1,0:T(8,128)(2,1)} %query_hbm.1, bf16[4096,128]{1,0:T(8,128)(2,1)} %bitcast.20, bf16[4096,128]{1,0:T(8,128)(2,1)} %bitcast.21, bf16[128,128]{1,0:T(8,128)(2,1)} %bitcast.22, bf16[128,128]{1,0:T(8,128)(2,1)} %bitcast.23, s32[1,128]{1,0:T(1,128)} %bitcast.24), custom_call_target="tpu_custom_call" | custom-call | tf_op jit(solution)/shard_map/attend/pallas_call | solution.py:39
  4.8 4.1 %collective-permute-start.2 = (bf16[8,128,128]{2,1,0:T(8,128)(2,1)}, bf16[8,128,128]{2,1,0:T(8,128)(2,1)S(1)}, u32[]{:S(2)}, u32[]{:S(2)}) collective-permute-start(bf16[8,128,128]{2,1,0:T(8,128)(2,1)} %attend.1.refs_0_), channel_id=1, source_target_pairs={{6,0},{2,4},{0,8},{4,12},{8,14},{12,10},{14,6},{10,2},{7,1},{3,5},... | collective-permute-start | bytes 786440 | tf_op jit(solution)/shard_map/ppermute | solution.py:351
  8.9 1.9 %collective-permute-start.7 = (bf16[8,128,128]{2,1,0:T(8,128)(2,1)}, bf16[8,128,128]{2,1,0:T(8,128)(2,1)S(1)}, u32[]{:S(2)}, u32[]{:S(2)}) collective-permute-start(bf16[8,128,128]{2,1,0:T(8,128)(2,1)} %attend.1.refs_0_), channel_id=1, source_target_pairs={{2,0},{0,4},{4,8},{8,12},{12,14},{14,10},{10,6},{6,2},{3,1},{1,5},... | collective-permute-start | bytes 786440 | tf_op jit(solution)/shard_map/ppermute | solution.py:351
  10.9 1.0 %copy-done.3 = bf16[8,128,128]{2,1,0:T(8,128)(2,1)S(1)} copy-done((bf16[8,128,128]{2,1,0:T(8,128)(2,1)S(1)}, bf16[8,128,128]{2,1,0:T(8,128)(2,1)}, u32[]{:S(2)}) %copy-start.3) | copy-done | bytes 262168
  11.9 5.0 %dense.3 = (f32[128,1024]{1,0:T(8,128)S(1)}, f32[128,1024]{1,0:T(8,128)S(1)}, f32[128,1024]{1,0:T(8,128)S(1)}, f32[128,1024]{1,0:T(8,128)S(1)}, f32[128,1024]{1,0:T(8,128)S(1)}) custom-call(bf16[8,128,128]{2,1,0:T(8,128)(2,1)S(1)} %copy-done.3, bf16[1024,8192]{1,0:T(8,128)(2,1)} %refs_1_.5), custom_call_target="tpu_custom_call" | custom-call | flops 1342177280 | bytes 10485760 | tf_op jit(solution)/shard_map/dense/pallas_call | solution.py:39
  16.9 1.1 %collective-permute-done.2.refs_4_ = bf16[8,128,128]{2,1,0:T(8,128)(2,1)S(1)} collective-permute-done((bf16[8,128,128]{2,1,0:T(8,128)(2,1)}, bf16[8,128,128]{2,1,0:T(8,128)(2,1)S(1)}, u32[]{:S(2)}, u32[]{:S(2)}) %collective-permute-start.2) | collective-permute-done | bytes 262176 | tf_op jit(solution)/shard_map/ppermute | solution.py:351
  18.1 6.8 %collective-permute-done.refs_3_ = bf16[8,128,128]{2,1,0:T(8,128)(2,1)S(1)} collective-permute-done((bf16[8,128,128]{2,1,0:T(8,128)(2,1)}, bf16[8,128,128]{2,1,0:T(8,128)(2,1)S(1)}, u32[]{:S(2)}, u32[]{:S(2)}) %collective-permute-start) | collective-permute-done | bytes 262176 | tf_op jit(solution)/shard_map/ppermute | solution.py:351
  24.8 2.0 %collective-permute-start.5 = (bf16[8,128,128]{2,1,0:T(8,128)(2,1)S(1)}, bf16[8,128,128]{2,1,0:T(8,128)(2,1)S(1)}, u32[]{:S(2)}, u32[]{:S(2)}) collective-permute-start(bf16[8,128,128]{2,1,0:T(8,128)(2,1)S(1)} %collective-permute-done.2.refs_4_), channel_id=1, source_target_pairs={{2,0},{0,4},{4,8},{8,12},{12,14},{14,10},{10,6},{6,2},{3,1},{1,5},... | collective-permute-start | bytes 786440 | tf_op jit(solution)/shard_map/ppermute | solution.py:351
  26.9 0.2 collective-permute-done.7.refs_2_
  27.2 2.7 %collective-permute-start.1 = (bf16[4,128,128]{2,1,0:T(8,128)(2,1)S(1)}, bf16[4,128,128]{2,1,0:T(8,128)(2,1)S(1)}, u32[]{:S(2)}, u32[]{:S(2)}) collective-permute-start(bf16[4,128,128]{2,1,0:T(8,128)(2,1)S(1)} %slice.6), channel_id=1, source_target_pairs={{8,0},{12,4},{14,8},{10,12},{6,14},{2,10},{0,6},{4,2},{9,1},{13,5}... | collective-permute-start | bytes 393224 | tf_op jit(solution)/shard_map/ppermute | solution.py:351
  29.9 3.7 %dense.4 = (f32[128,1024]{1,0:T(8,128)S(1)}, f32[128,1024]{1,0:T(8,128)S(1)}, s32[128,128]{1,0:T(8,128)S(1)}, s32[64]{0:T(128)S(1)}) custom-call(bf16[8,128,128]{2,1,0:T(8,128)(2,1)S(1)} %copy-done.3, bf16[1024,8192]{1,0:T(8,128)(2,1)} %refs_1_.5, s32[1,128]{1,0:T(1,128)S(1)} %bitcast.19, s32[32]{0:T(128)S(1)} %copy-done.9, s32[4,16]{1,0:T(4,128)S(1)} %bitcast.18), custom_call_target="tpu_custom_call" | custom-call | flops 536870912 | bytes 4194304 | tf_op jit(solution)/shard_map/dense/pallas_call | solution.py:39
  33.7 0.4 copy-done.2
  34.0 2.1 %fold_early.1 = (f32[128,256]{1,0:T(8,128)S(1)}, f32[64,128,128]{2,1,0:T(8,128)S(1)}) custom-call(bf16[8,128,128]{2,1,0:T(8,128)(2,1)S(1)} %copy-done.3, bf16[8,128,128]{2,1,0:T(8,128)(2,1)S(1)} %collective-permute-done.6.refs_1_, bf16[8,128,128]{2,1,0:T(8,128)(2,1)S(1)} %collective-permute-done.7.refs_2_, ...), custom_call_target="tpu_custom_call" | custom-call | flops 268435456 | bytes 4194304 | tf_op jit(solution)/shard_map/fold_early/pallas_call | solution.py:39
  36.3 1.4 %fold_late.1 = (f32[128,256]{1,0:T(8,128)S(1)}, f32[64,128,128]{2,1,0:T(8,128)S(1)}) custom-call(bf16[8,128,128]{2,1,0:T(8,128)(2,1)S(1)} %collective-permute-done.4.refs_0_, bf16[8,128,128]{2,1,0:T(8,128)(2,1)S(1)} %collective-permute-done.5.refs_1_, s32[128,128]{1,0:T(8,128)S(1)} %get-tuple-element.41.refs_5_.refs_2_, bf16[256,8192]{1,0:T(8,128)(2,1)S(1)} %bitcast.16, ...), custom_call_target="tpu_custom_call" | custom-call | flops 134217728 | bytes 1048576 | tf_op jit(solution)/shard_map/fold_late/pallas_call | solution.py:39
  37.7 2.5 %collective-permute-done.1.refs_0_ = bf16[4,128,128]{2,1,0:T(8,128)(2,1)S(1)} collective-permute-done((bf16[4,128,128]{2,1,0:T(8,128)(2,1)S(1)}, bf16[4,128,128]{2,1,0:T(8,128)(2,1)S(1)}, u32[]{:S(2)}, u32[]{:S(2)}) %collective-permute-start.1) | collective-permute-done | bytes 131104 | tf_op jit(solution)/shard_map/ppermute | solution.py:351
  40.3 2.0 %finish.1 = (bf16[128,256]{1,0:T(8,128)(2,1)S(1)}, f32[8,128,128]{2,1,0:T(8,128)S(1)}, bf16[4,128,128]{2,1,0:T(8,128)(2,1)S(1)}, bf16[4,128,128]{2,1,0:T(8,128)(...) custom-call(bf16[4,128,128]{2,1,0:T(8,128)(2,1)S(1)} %collective-permute-done.1.refs_0_, ...), custom_call_target="tpu_custom_call" | custom-call | flops 268435456 | bytes 2097152 | tf_op jit(solution)/shard_map/finish/pallas_call | solution.py:39
  42.3 0.5 collective-permute-start.8
  42.7 1.6 %collective-permute-start.9 = (bf16[8,128,128]{2,1,0:T(8,128)(2,1)S(1)}, bf16[8,128,128]{2,1,0:T(8,128)(2,1)S(1)}, u32[]{:S(2)}, u32[]{:S(2)}) collective-permute-start(bf16[8,128,128]{2,1,0:T(8,128)(2,1)S(1)} %get-tuple-element.59), channel_id=1, source_target_pairs={{4,0},{8,4},{12,8},{14,12},{10,14},{6,10},{2,6},{0,2},{5,1},{9,5},... | collective-permute-start | bytes 786440 | tf_op jit(solution)/shard_map/ppermute | solution.py:351
  44.4 0.2 collective-permute-start.10
  44.6 2.7 %collective-permute-start.11 = (bf16[4,128,128]{2,1,0:T(8,128)(2,1)S(1)}, bf16[4,128,128]{2,1,0:T(8,128)(2,1)S(1)}, u32[]{:S(2)}, u32[]{:S(2)}) collective-permute-start(bf16[4,128,128]{2,1,0:T(8,128)(2,1)S(1)} %get-tuple-element.61), channel_id=1, source_target_pairs={{8,0},{12,4},{14,8},{10,12},{6,14},{2,10},{0,6},{4,2},{9,1},{13,5}... | collective-permute-start | bytes 393224 | tf_op jit(solution)/shard_map/ppermute | solution.py:351
  47.3 1.3 %part.3 = (bf16[8,128,128]{2,1,0:T(8,128)(2,1)S(1)}, bf16[8,128,128]{2,1,0:T(8,128)(2,1)S(1)}) custom-call(bf16[128,256]{1,0:T(8,128)(2,1)S(1)} %get-tuple-element.54.refs_0_, bf16[256,8192]{1,0:T(8,128)(2,1)S(1)} %bitcast.12, f32[64,128,128]{2,1,0:T(8,128)S(1)} %get-tuple-element.46.refs_10_.refs_2_, f32[8,128,128]{2,1,0:T(8,128)S(1)} %get-tuple-element.50.refs_3_, ...), custom_call_target="tpu_custom_call" | custom-call | flops 67108864 | bytes 1048576 | tf_op jit(solution)/shard_map/part/pallas_call | solution.py:39
  48.6 0.5 collective-permute-start.12
  49.1 1.3 %part.4 = (f32[8,128,128]{2,1,0:T(8,128)S(1)}, f32[8,128,128]{2,1,0:T(8,128)S(1)}) custom-call(bf16[128,256]{1,0:T(8,128)(2,1)S(1)} %get-tuple-element.54.refs_0_, bf16[256,8192]{1,0:T(8,128)(2,1)S(1)} %bitcast.13, f32[64,128,128]{2,1,0:T(8,128)S(1)} %get-tuple-element.46.refs_10_.refs_2_, f32[8,128,128]{2,1,0:T(8,128)S(1)} %get-tuple-element.50.refs_3_, ...), custom_call_target="tpu_custom_call" | custom-call | flops 67108864 | bytes 1048576 | tf_op jit(solution)/shard_map/part/pallas_call | solution.py:39
  50.4 6.5 %collective-permute-done.10 = bf16[4,128,128]{2,1,0:T(8,128)(2,1)S(1)} collective-permute-done((bf16[4,128,128]{2,1,0:T(8,128)(2,1)S(1)}, bf16[4,128,128]{2,1,0:T(8,128)(2,1)S(1)}, u32[]{:S(2)}, u32[]{:S(2)}) %collective-permute-start.10) | collective-permute-done | bytes 131104 | tf_op jit(solution)/shard_map/ppermute | solution.py:351
  56.9 0.5 collective-permute-start.13
  57.5 1.0 %collective-permute-start.14 = (bf16[8,128,128]{2,1,0:T(8,128)(2,1)S(1)}, bf16[8,128,128]{2,1,0:T(8,128)(2,1)S(1)}, u32[]{:S(2)}, u32[]{:S(2)}) collective-permute-start(bf16[8,128,128]{2,1,0:T(8,128)(2,1)S(1)} %add_convert_fusion.1), channel_id=1, source_target_pairs={{6,0},{2,4},{0,8},{4,12},{8,14},{12,10},{14,6},{10,2},{7,1},{3,5},... | collective-permute-start | bytes 786440 | tf_op jit(solution)/shard_map/ppermute | solution.py:351
  58.6 2.0 %collective-permute-start.15 = (bf16[8,128,128]{2,1,0:T(8,128)(2,1)S(1)}, bf16[8,128,128]{2,1,0:T(8,128)(2,1)S(1)}, u32[]{:S(2)}, u32[]{:S(2)}) collective-permute-start(bf16[8,128,128]{2,1,0:T(8,128)(2,1)S(1)} %add_convert_fusion), channel_id=1, source_target_pairs={{8,0},{12,4},{14,8},{10,12},{6,14},{2,10},{0,6},{4,2},{9,1},{13,5}... | collective-permute-start | bytes 786440 | tf_op jit(solution)/shard_map/ppermute | solution.py:351
  60.6 1.9 %dense.5.refs_7_ = f32[128,1024]{1,0:T(8,128)S(1)} custom-call(bf16[8,128,128]{2,1,0:T(8,128)(2,1)S(1)} %copy-done.4, bf16[1024,8192]{1,0:T(8,128)(2,1)} %refs_1_.5), custom_call_target="tpu_custom_call" | custom-call | flops 268435456 | bytes 2097152 | tf_op jit(solution)/shard_map/dense/pallas_call | solution.py:39
  62.5 1.0 %part.5.own_ref = f32[8,128,128]{2,1,0:T(8,128)S(1)} custom-call(bf16[128,256]{1,0:T(8,128)(2,1)S(1)} %get-tuple-element.54.refs_0_, bf16[256,8192]{1,0:T(8,128)(2,1)S(1)} %bitcast.14, f32[64,128,128]{2,1,0:T(8,128)S(1)} %get-tuple-element.46.refs_10_.refs_2_, f32[8,128,128]{2,1,0:T(8,128)S(1)} %get-tuple-element.50.refs_3_, f32[4,16]{1,0:T(4,128)S(1)} %copy-done.5, ...), custom_call_target="tpu_custom_call" | custom-call | flops 67108864 | bytes 1048576 | tf_op jit(solution)/shard_map/part/pallas_call | solution.py:39
  63.5 6.9 %collective-permute-done.13.refs_1_ = bf16[8,128,128]{2,1,0:T(8,128)(2,1)S(1)} collective-permute-done((bf16[8,128,128]{2,1,0:T(8,128)(2,1)S(1)}, bf16[8,128,128]{2,1,0:T(8,128)(2,1)S(1)}, u32[]{:S(2)}, u32[]{:S(2)}) %collective-permute-start.13) | collective-permute-done | bytes 262176 | tf_op jit(solution)/shard_map/ppermute | solution.py:351
  70.4 0.7 collective-permute-done.14.refs_2_
  71.1 0.9 %sum_up.1 = bf16[128,1024]{1,0:T(8,128)(2,1)} custom-call(f32[8,128,128]{2,1,0:T(8,128)S(1)} %part.5.own_ref, bf16[8,128,128]{2,1,0:T(8,128)(2,1)S(1)} %collective-permute-done.12.refs_0_, bf16[8,128,128]{2,1,0:T(8,128)(2,1)S(1)} %collective-permute-done.13.refs_1_, bf16[8,128,128]{2,1,0:T(8,128)(2,1)S(1)} %collective-permute-done.14.refs_2_, ...), custom_call_target="tpu_custom_call" | custom-call | flops 1 | bytes 1 | tf_op jit(solution)/shard_map/sum_up/pallas_call | solution.py:39
  (35 shorter events, 0.5 us)
Async XLA Ops:
  0.0 29.9 %copy-start.7 = (s32[4,16,1]{1,2,0:T(1,128)S(1)}, s32[4,16,1]{1,2,0:T(1,128)}, u32[]{:S(2)}) copy-start(s32[4,16,1]{1,2,0:T(1,128)} %param.28) | copy-start | bytes 772
  0.0 29.9 %copy-start.8 = (s32[128]{0:T(128)S(1)}, s32[128]{0:T(128)}, u32[]{:S(2)}) copy-start(s32[128]{0:T(128)} %param.21) | copy-start | bytes 1540
  0.0 29.9 %copy-start.9 = (s32[32]{0:T(128)S(1)}, s32[32]{0:T(128)}, u32[]{:S(2)}) copy-start(s32[32]{0:T(128)} %refs_3_.1) | copy-start | bytes 388
  4.8 13.3 %collective-permute-start.2 = (bf16[8,128,128]{2,1,0:T(8,128)(2,1)}, bf16[8,128,128]{2,1,0:T(8,128)(2,1)S(1)}, u32[]{:S(2)}, u32[]{:S(2)}) collective-permute-start(bf16[8,128,128]{2,1,0:T(8,128)(2,1)} %attend.1.refs_0_), channel_id=1, source_target_pairs={{6,0},{2,4},{0,8},{4,12},{8,14},{12,10},{14,6},{10,2},{7,1},{3,5},... | collective-permute-start | bytes 786440 | tf_op jit(solution)/shard_map/ppermute | solution.py:351
  8.9 16.0 %collective-permute-start = (bf16[8,128,128]{2,1,0:T(8,128)(2,1)}, bf16[8,128,128]{2,1,0:T(8,128)(2,1)S(1)}, u32[]{:S(2)}, u32[]{:S(2)}) collective-permute-start(bf16[8,128,128]{2,1,0:T(8,128)(2,1)} %attend.1.refs_0_), channel_id=1, source_target_pairs={{8,0},{12,4},{14,8},{10,12},{6,14},{2,10},{0,6},{4,2},{9,1},{13,5}... | collective-permute-start | bytes 786440 | tf_op jit(solution)/shard_map/ppermute | solution.py:351
  8.9 18.3 %collective-permute-start.7 = (bf16[8,128,128]{2,1,0:T(8,128)(2,1)}, bf16[8,128,128]{2,1,0:T(8,128)(2,1)S(1)}, u32[]{:S(2)}, u32[]{:S(2)}) collective-permute-start(bf16[8,128,128]{2,1,0:T(8,128)(2,1)} %attend.1.refs_0_), channel_id=1, source_target_pairs={{2,0},{0,4},{4,8},{8,12},{12,14},{14,10},{10,6},{6,2},{3,1},{1,5},... | collective-permute-start | bytes 786440 | tf_op jit(solution)/shard_map/ppermute | solution.py:351
  10.8 22.9 %collective-permute-start.6 = (bf16[8,128,128]{2,1,0:T(8,128)(2,1)}, bf16[8,128,128]{2,1,0:T(8,128)(2,1)S(1)}, u32[]{:S(2)}, u32[]{:S(2)}) collective-permute-start(bf16[8,128,128]{2,1,0:T(8,128)(2,1)} %attend.1.refs_0_), channel_id=1, source_target_pairs={{4,0},{8,4},{12,8},{14,12},{10,14},{6,10},{2,6},{0,2},{5,1},{9,5},... | collective-permute-start | bytes 786440 | tf_op jit(solution)/shard_map/ppermute | solution.py:351
  10.9 1.0 %copy-start.3 = (bf16[8,128,128]{2,1,0:T(8,128)(2,1)S(1)}, bf16[8,128,128]{2,1,0:T(8,128)(2,1)}, u32[]{:S(2)}) copy-start(bf16[8,128,128]{2,1,0:T(8,128)(2,1)} %attend.1.refs_0_) | copy-start | bytes 786436
  24.8 11.5 %collective-permute-start.4 = (bf16[8,128,128]{2,1,0:T(8,128)(2,1)S(1)}, bf16[8,128,128]{2,1,0:T(8,128)(2,1)S(1)}, u32[]{:S(2)}, u32[]{:S(2)}) collective-permute-start(bf16[8,128,128]{2,1,0:T(8,128)(2,1)S(1)} %collective-permute-done.refs_3_), channel_id=1, source_target_pairs={{4,0},{8,4},{12,8},{14,12},{10,14},{6,10},{2,6},{0,2},{5,1},{9,5},... | collective-permute-start | bytes 786440 | tf_op jit(solution)/shard_map/ppermute | solution.py:351
  24.8 11.5 %collective-permute-start.5 = (bf16[8,128,128]{2,1,0:T(8,128)(2,1)S(1)}, bf16[8,128,128]{2,1,0:T(8,128)(2,1)S(1)}, u32[]{:S(2)}, u32[]{:S(2)}) collective-permute-start(bf16[8,128,128]{2,1,0:T(8,128)(2,1)S(1)} %collective-permute-done.2.refs_4_), channel_id=1, source_target_pairs={{2,0},{0,4},{4,8},{8,12},{12,14},{14,10},{10,6},{6,2},{3,1},{1,5},... | collective-permute-start | bytes 786440 | tf_op jit(solution)/shard_map/ppermute | solution.py:351
  26.9 10.8 %collective-permute-start.3 = (bf16[4,128,128]{2,1,0:T(8,128)(2,1)S(1)}, bf16[4,128,128]{2,1,0:T(8,128)(2,1)S(1)}, u32[]{:S(2)}, u32[]{:S(2)}) collective-permute-start(bf16[4,128,128]{2,1,0:T(8,128)(2,1)S(1)} %slice.7), channel_id=1, source_target_pairs={{6,0},{2,4},{0,8},{4,12},{8,14},{12,10},{14,6},{10,2},{7,1},{3,5},... | collective-permute-start | bytes 393224 | tf_op jit(solution)/shard_map/ppermute | solution.py:351
  27.2 13.1 %collective-permute-start.1 = (bf16[4,128,128]{2,1,0:T(8,128)(2,1)S(1)}, bf16[4,128,128]{2,1,0:T(8,128)(2,1)S(1)}, u32[]{:S(2)}, u32[]{:S(2)}) collective-permute-start(bf16[4,128,128]{2,1,0:T(8,128)(2,1)S(1)} %slice.6), channel_id=1, source_target_pairs={{8,0},{12,4},{14,8},{10,12},{6,14},{2,10},{0,6},{4,2},{9,1},{13,5}... | collective-permute-start | bytes 393224 | tf_op jit(solution)/shard_map/ppermute | solution.py:351
  29.9 3.8 %copy-start.1 = (bf16[4,8192,64]{1,2,0:T(8,128)(2,1)S(1)}, bf16[4,8192,64]{1,2,0:T(8,128)(2,1)}, u32[]{:S(2)}) copy-start(bf16[4,8192,64]{1,2,0:T(8,128)(2,1)} %param.24) | copy-start | bytes 12582916
  29.9 4.2 %copy-start.2 = (bf16[4,16,128,128]{3,2,1,0:T(8,128)(2,1)S(1)}, bf16[4,16,128,128]{3,2,1,0:T(8,128)(2,1)}, u32[]{:S(2)}) copy-start(bf16[4,16,128,128]{3,2,1,0:T(8,128)(2,1)} %refs_4_.6) | copy-start | bytes 6291460
  29.9 4.1 %copy-start.5 = (f32[4,16]{1,0:T(4,128)S(1)}, f32[4,16]{1,0:T(4,128)}, u32[]{:S(2)}) copy-start(f32[4,16]{1,0:T(4,128)} %refs_4_.9) | copy-start | bytes 772
  29.9 4.1 %copy-start.6 = (s32[4,16]{1,0:T(4,128)S(1)}, s32[4,16]{1,0:T(4,128)}, u32[]{:S(2)}) copy-start(s32[4,16]{1,0:T(4,128)} %refs_5_.9) | copy-start | bytes 772
  36.3 4.0 %copy-start = (bf16[4,64,8192]{2,1,0:T(8,128)(2,1)S(1)}, bf16[4,64,8192]{2,1,0:T(8,128)(2,1)}, u32[]{:S(2)}) copy-start(bf16[4,64,8192]{2,1,0:T(8,128)(2,1)} %param.25) | copy-start | bytes 12582916
  42.3 15.1 %collective-permute-start.8 = (bf16[8,128,128]{2,1,0:T(8,128)(2,1)S(1)}, bf16[8,128,128]{2,1,0:T(8,128)(2,1)S(1)}, u32[]{:S(2)}, u32[]{:S(2)}) collective-permute-start(bf16[8,128,128]{2,1,0:T(8,128)(2,1)S(1)} %get-tuple-element.58), channel_id=1, source_target_pairs={{2,0},{0,4},{4,8},{8,12},{12,14},{14,10},{10,6},{6,2},{3,1},{1,5},... | collective-permute-start | bytes 786440 | tf_op jit(solution)/shard_map/ppermute | solution.py:351
  42.7 14.7 %collective-permute-start.9 = (bf16[8,128,128]{2,1,0:T(8,128)(2,1)S(1)}, bf16[8,128,128]{2,1,0:T(8,128)(2,1)S(1)}, u32[]{:S(2)}, u32[]{:S(2)}) collective-permute-start(bf16[8,128,128]{2,1,0:T(8,128)(2,1)S(1)} %get-tuple-element.59), channel_id=1, source_target_pairs={{4,0},{8,4},{12,8},{14,12},{10,14},{6,10},{2,6},{0,2},{5,1},{9,5},... | collective-permute-start | bytes 786440 | tf_op jit(solution)/shard_map/ppermute | solution.py:351
  44.4 12.5 %collective-permute-start.10 = (bf16[4,128,128]{2,1,0:T(8,128)(2,1)S(1)}, bf16[4,128,128]{2,1,0:T(8,128)(2,1)S(1)}, u32[]{:S(2)}, u32[]{:S(2)}) collective-permute-start(bf16[4,128,128]{2,1,0:T(8,128)(2,1)S(1)} %get-tuple-element.60), channel_id=1, source_target_pairs={{6,0},{2,4},{0,8},{4,12},{8,14},{12,10},{14,6},{10,2},{7,1},{3,5},... | collective-permute-start | bytes 393224 | tf_op jit(solution)/shard_map/ppermute | solution.py:351
  44.6 12.8 %collective-permute-start.11 = (bf16[4,128,128]{2,1,0:T(8,128)(2,1)S(1)}, bf16[4,128,128]{2,1,0:T(8,128)(2,1)S(1)}, u32[]{:S(2)}, u32[]{:S(2)}) collective-permute-start(bf16[4,128,128]{2,1,0:T(8,128)(2,1)S(1)} %get-tuple-element.61), channel_id=1, source_target_pairs={{8,0},{12,4},{14,8},{10,12},{6,14},{2,10},{0,6},{4,2},{9,1},{13,5}... | collective-permute-start | bytes 393224 | tf_op jit(solution)/shard_map/ppermute | solution.py:351
  48.6 21.8 %collective-permute-start.12 = (bf16[8,128,128]{2,1,0:T(8,128)(2,1)S(1)}, bf16[8,128,128]{2,1,0:T(8,128)(2,1)S(1)}, u32[]{:S(2)}, u32[]{:S(2)}) collective-permute-start(bf16[8,128,128]{2,1,0:T(8,128)(2,1)S(1)} %get-tuple-element.53), channel_id=1, source_target_pairs={{2,0},{0,4},{4,8},{8,12},{12,14},{14,10},{10,6},{6,2},{3,1},{1,5},... | collective-permute-start | bytes 786440 | tf_op jit(solution)/shard_map/ppermute | solution.py:351
  49.1 11.5 %copy-start.4 = (bf16[8,128,128]{2,1,0:T(8,128)(2,1)S(1)}, bf16[8,128,128]{2,1,0:T(8,128)(2,1)}, u32[]{:S(2)}) copy-start(bf16[8,128,128]{2,1,0:T(8,128)(2,1)} %attend.1.refs_0_) | copy-start | bytes 786436
  56.9 13.5 %collective-permute-start.13 = (bf16[8,128,128]{2,1,0:T(8,128)(2,1)S(1)}, bf16[8,128,128]{2,1,0:T(8,128)(2,1)S(1)}, u32[]{:S(2)}, u32[]{:S(2)}) collective-permute-start(bf16[8,128,128]{2,1,0:T(8,128)(2,1)S(1)} %get-tuple-element.65), channel_id=1, source_target_pairs={{4,0},{8,4},{12,8},{14,12},{10,14},{6,10},{2,6},{0,2},{5,1},{9,5},... | collective-permute-start | bytes 786440 | tf_op jit(solution)/shard_map/ppermute | solution.py:351
  57.5 13.6 %collective-permute-start.14 = (bf16[8,128,128]{2,1,0:T(8,128)(2,1)S(1)}, bf16[8,128,128]{2,1,0:T(8,128)(2,1)S(1)}, u32[]{:S(2)}, u32[]{:S(2)}) collective-permute-start(bf16[8,128,128]{2,1,0:T(8,128)(2,1)S(1)} %add_convert_fusion.1), channel_id=1, source_target_pairs={{6,0},{2,4},{0,8},{4,12},{8,14},{12,10},{14,6},{10,2},{7,1},{3,5},... | collective-permute-start | bytes 786440 | tf_op jit(solution)/shard_map/ppermute | solution.py:351
  58.6 12.5 %collective-permute-start.15 = (bf16[8,128,128]{2,1,0:T(8,128)(2,1)S(1)}, bf16[8,128,128]{2,1,0:T(8,128)(2,1)S(1)}, u32[]{:S(2)}, u32[]{:S(2)}) collective-permute-start(bf16[8,128,128]{2,1,0:T(8,128)(2,1)S(1)} %add_convert_fusion), channel_id=1, source_target_pairs={{8,0},{12,4},{14,8},{10,12},{6,14},{2,10},{0,6},{4,2},{9,1},{13,5}... | collective-permute-start | bytes 786440 | tf_op jit(solution)/shard_map/ppermute | solution.py:351

commit v8 on v7

--- a/solution.py
+++ b/solution.py
@@ -352,28 +352,17 @@
             value, "tp", [(ring[(i + distance) % count], ring[i]) for i in range(count)]
         )
 
-    short = count == 8
     chunks = {0: attended}
-    if short:
-        for distance in (2, 6, 1, 7):
-            chunks[distance] = come(attended, distance if distance <= half else distance - count)
-        wanted = [4, 3, 5, 1, 7, 2, 6, 0]
-        cuts = [5, 7]
-    else:
-        chunks[1], chunks[count - 1] = come(attended, 1), come(attended, -1)
-        cuts = [count // 2, count - 1]
-    token = dense_for(wanted[: cuts[0]], attended)
-    if short:
-        right, left = after(chunks[2], token), after(chunks[6], token)
-        chunks[3], chunks[5] = come(right, 1), come(left, -1)
-        front, back = come(right[: heads // 2], 2), come(left[heads // 2 :], -2)
-    else:
-        for step in range(2, half):
-            right, left = after(chunks[step - 1], token), after(chunks[count - step + 1], token)
-            chunks[step], chunks[count - step] = come(right, 1), come(left, -1)
-        right, left = chunks[half - 1], chunks[half + 1]
-        front, back = come(right[: heads // 2], 1), come(left[heads // 2 :], -1)
-    slot, table = dense_for(wanted[cuts[0] : cuts[1]], after(attended, token), True)
+    chunks[1], chunks[count - 1] = come(attended, 1), come(attended, -1)
+    token = dense_for(wanted[:3], attended)
+    for step in range(2, half):
+        right, left = after(chunks[step - 1], token), after(chunks[count - step + 1], token)
+        if step == half - 1:
+            front, back = come(right[: heads // 2], 2), come(left[heads // 2 :], -2)
+        chunks[step], chunks[count - step] = come(right, 1), come(left, -1)
+        if step == 2:
+            slot, table = dense_for(wanted[3:5], after(attended, token), True)
+            token = slot
 
     factor_t = jnp.swapaxes(factor_in, 1, 2).reshape(low_width, -1)
     second = second_factor.reshape(low_width, complete)
@@ -405,7 +394,7 @@
         moved=MIB,
     )
     extras = shape((slots * CAP, rows, side), F32)
-    first = [half, half - 1, half + 1] if half > 1 else [half]
+    first = wanted[:3]
     travelling = shape((heads, rows, side), BF16)
     low, extra, front, back, *sums = call(
         functools.partial(finish_kernel, first, count),
@@ -448,30 +437,25 @@
             total = total + value
         return total.astype(BF16)
 
-    if short:
-        from_left, from_right = come(parts[3], -1), come(parts[5], 1)
-        front, back = come(front, -2), come(back, 2)
-        parts_for([1, 7], low, BF16)
-        came = [come(parts[1], -1), come(parts[7], 1)]
-        parts_for([2, 6], after(low, parts[1]), F32)
-        from_left, from_right, front, back = lax.optimization_barrier(
-            (from_left, from_right, front, back)
-        )
-        right = joined(parts[2], (from_left, None), (front, 0))
-        left = joined(parts[6], (from_right, None), (back, 1))
-        came += [come(right, -2), come(left, 2)]
-    else:
-        left, right = (front, 0), (back, 1)
-        left, right = (come(front, 1), 0), (come(back, -1), 1)
-        for distance in range(half - 1, 0, -1):
-            left = joined(parts[count - distance], left)
-            right = joined(parts[distance], right)
-            if distance > 1:
-                parts_for([distance - 1, count - distance + 1], after(low, right), F32)
-            left, right = (come(left, 1), None), (come(right, -1), None)
-        came = [left[0], right[0]]
-    dense_for([0], after(attended, right if short else parts[1]))
-    parts_for([0], low, F32)
+    front, back = come(front, -2), come(back, 2)
+    from_left, from_right = come(parts[half - 1], -1), come(parts[half + 1], 1)
+    parts_for([half - 2, half + 2], low, F32)
+    token = dense_for(wanted[5:-1], after(attended, low))
+    from_left, from_right, front, back, token = lax.optimization_barrier(
+        (from_left, from_right, front, back, token)
+    )
+    right = joined(parts[half - 2], (from_left, None), (front, 0))
+    left = joined(parts[half + 2], (from_right, None), (back, 1))
+    for distance in range(half - 2, 0, -1):
+        nearer = distance - 1
+        if distance == half - 2:
+            dense_for([0], after(attended, right))
+        parts_for([nearer, count - nearer] if nearer else [0], after(low, right), F32)
+        from_left, from_right = come(right, -1), come(left, 1)
+        if nearer:
+            right = joined(parts[nearer], (from_left, None))
+            left = joined(parts[count - nearer], (from_right, None))
+    came = [from_left, from_right]
     return call(
         sum_kernel,
         "sum_up",

time: 72.8 us -> 68.5 us (0.941)
  waiting for transfers between devices: 24.8 us -> 20.9 us
  Pallas kernels: 25.5 us -> 26.4 us
    ppermute x16, waiting for transfers between devices: 24.8 us -> 20.9 us  [come(): lax.ppermute(value, 'tp', [(ring[(i + distance) % count], ring[i]) for i...]
    pallas_call x11 -> x12, Pallas kernels: 25.5 us -> 26.4 us  [call(): pl.pallas_call(kernel, out_shape=outs, in_specs=specs, out_specs=out_spec...]
  transfers between devices with their start and end apart: 16 -> 16, of which waited for: 8 -> 10; matrix products, arithmetic and copies ran while one was open for 0% -> 0% of each run, Pallas kernels for 25% -> 28%
where the time goes in v8:
time: 68.5 us; the launch traced here: 68.3 us
  Pallas kernels  26.4 us (39%)
  waiting for transfers between devices  20.9 us (31%)
  starting transfers between devices  19.4 us (28%)
  local copies, waits for them, and re-layouts  1.06 us (2%)
    pallas_call x12, Pallas kernels, call(): pl.pallas_call(kernel, out_shape=outs, in_specs=specs, out_specs=out_spec...  26.4 us
    ppermute x16, waiting for transfers between devices, come(): lax.ppermute(value, 'tp', [(ring[(i + distance) % count], ring[i]) for i...  20.9 us
    ppermute x16, starting transfers between devices, come(): lax.ppermute(value, 'tp', [(ring[(i + distance) % count], ring[i]) for i...  19.4 us
  transfers between devices with their start and end apart: 16, of which 10 were waited for; matrix products, arithmetic and copies ran while one was open for 0% of the time, Pallas kernels for 28%

profile of v8, /device:TPU:0, one launch (start us, length us, event | category | flops | bytes accessed | tf_op | source)
XLA Modules:
  0.0 68.3 jit_solution(17146184330627945249)
XLA Ops:
  0.0 4.8 %attend.1.refs_0_ = bf16[8,128,128]{2,1,0:T(8,128)(2,1)} custom-call(bf16[128,1024]{1,0:T(8,128)(2,1)} %query_hbm.1, bf16[4096,128]{1,0:T(8,128)(2,1)} %bitcast.20, bf16[4096,128]{1,0:T(8,128)(2,1)} %bitcast.21, bf16[128,128]{1,0:T(8,128)(2,1)} %bitcast.22, bf16[128,128]{1,0:T(8,128)(2,1)} %bitcast.23, s32[1,128]{1,0:T(1,128)} %bitcast.24), custom_call_target="tpu_custom_call" | custom-call | tf_op jit(solution)/shard_map/attend/pallas_call | solution.py:39
  4.8 3.1 %collective-permute-start.3 = (bf16[8,128,128]{2,1,0:T(8,128)(2,1)}, bf16[8,128,128]{2,1,0:T(8,128)(2,1)S(1)}, u32[]{:S(2)}, u32[]{:S(2)}) collective-permute-start(bf16[8,128,128]{2,1,0:T(8,128)(2,1)} %attend.1.refs_0_), channel_id=1, source_target_pairs={{2,0},{0,4},{4,8},{8,12},{12,14},{14,10},{10,6},{6,2},{3,1},{1,5},... | collective-permute-start | bytes 786440 | tf_op jit(solution)/shard_map/ppermute | solution.py:351
  7.9 1.0 %copy-done.3 = bf16[8,128,128]{2,1,0:T(8,128)(2,1)S(1)} copy-done((bf16[8,128,128]{2,1,0:T(8,128)(2,1)S(1)}, bf16[8,128,128]{2,1,0:T(8,128)(2,1)}, u32[]{:S(2)}) %copy-start.3) | copy-done | bytes 262168
  8.9 3.5 %dense.4 = (f32[128,1024]{1,0:T(8,128)S(1)}, f32[128,1024]{1,0:T(8,128)S(1)}, f32[128,1024]{1,0:T(8,128)S(1)}) custom-call(bf16[8,128,128]{2,1,0:T(8,128)(2,1)S(1)} %copy-done.3, bf16[1024,8192]{1,0:T(8,128)(2,1)} %refs_1_.7), custom_call_target="tpu_custom_call" | custom-call | flops 805306368 | bytes 6291456 | tf_op jit(solution)/shard_map/dense/pallas_call | solution.py:39
  12.3 2.0 %collective-permute-done.3.refs_2_ = bf16[8,128,128]{2,1,0:T(8,128)(2,1)S(1)} collective-permute-done((bf16[8,128,128]{2,1,0:T(8,128)(2,1)}, bf16[8,128,128]{2,1,0:T(8,128)(2,1)S(1)}, u32[]{:S(2)}, u32[]{:S(2)}) %collective-permute-start.3) | collective-permute-done | bytes 262176 | tf_op jit(solution)/shard_map/ppermute | solution.py:351
  14.3 1.8 %collective-permute-start.4 = (bf16[8,128,128]{2,1,0:T(8,128)(2,1)S(1)}, bf16[8,128,128]{2,1,0:T(8,128)(2,1)S(1)}, u32[]{:S(2)}, u32[]{:S(2)}) collective-permute-start(bf16[8,128,128]{2,1,0:T(8,128)(2,1)S(1)} %collective-permute-done.3.refs_2_), channel_id=1, source_target_pairs={{2,0},{0,4},{4,8},{8,12},{12,14},{14,10},{10,6},{6,2},{3,1},{1,5},... | collective-permute-start | bytes 786440 | tf_op jit(solution)/shard_map/ppermute | solution.py:351
  16.4 3.7 %dense.5 = (f32[128,1024]{1,0:T(8,128)S(1)}, f32[128,1024]{1,0:T(8,128)S(1)}, s32[128,128]{1,0:T(8,128)S(1)}, s32[64]{0:T(128)S(1)}) custom-call(bf16[8,128,128]{2,1,0:T(8,128)(2,1)S(1)} %copy-done.3, bf16[1024,8192]{1,0:T(8,128)(2,1)} %refs_1_.7, s32[1,128]{1,0:T(1,128)S(1)} %bitcast.19, s32[32]{0:T(128)S(1)} %copy-done.9, s32[4,16]{1,0:T(4,128)S(1)} %bitcast.18), custom_call_target="tpu_custom_call" | custom-call | flops 536870912 | bytes 4194304 | tf_op jit(solution)/shard_map/dense/pallas_call | solution.py:39
  20.1 1.7 %collective-permute-done.4.refs_4_ = bf16[8,128,128]{2,1,0:T(8,128)(2,1)S(1)} collective-permute-done((bf16[8,128,128]{2,1,0:T(8,128)(2,1)S(1)}, bf16[8,128,128]{2,1,0:T(8,128)(2,1)S(1)}, u32[]{:S(2)}, u32[]{:S(2)}) %collective-permute-start.4) | collective-permute-done | bytes 262176 | tf_op jit(solution)/shard_map/ppermute | solution.py:351
  21.8 1.2 %collective-permute-done.1.refs_3_ = bf16[8,128,128]{2,1,0:T(8,128)(2,1)S(1)} collective-permute-done((bf16[8,128,128]{2,1,0:T(8,128)(2,1)S(1)}, bf16[8,128,128]{2,1,0:T(8,128)(2,1)S(1)}, u32[]{:S(2)}, u32[]{:S(2)}) %collective-permute-start.1) | collective-permute-done | bytes 262176 | tf_op jit(solution)/shard_map/ppermute | solution.py:351
  23.0 0.6 collective-permute-start.6
  23.6 1.5 %collective-permute-start.7 = (bf16[8,128,128]{2,1,0:T(8,128)(2,1)S(1)}, bf16[8,128,128]{2,1,0:T(8,128)(2,1)S(1)}, u32[]{:S(2)}, u32[]{:S(2)}) collective-permute-start(bf16[8,128,128]{2,1,0:T(8,128)(2,1)S(1)} %collective-permute-done.4.refs_4_), channel_id=1, source_target_pairs={{2,0},{0,4},{4,8},{8,12},{12,14},{14,10},{10,6},{6,2},{3,1},{1,5},... | collective-permute-start | bytes 786440 | tf_op jit(solution)/shard_map/ppermute | solution.py:351
  25.1 2.6 %collective-permute-start.5 = (bf16[4,128,128]{2,1,0:T(8,128)(2,1)S(1)}, bf16[4,128,128]{2,1,0:T(8,128)(2,1)S(1)}, u32[]{:S(2)}, u32[]{:S(2)}) collective-permute-start(bf16[4,128,128]{2,1,0:T(8,128)(2,1)S(1)} %slice.7), channel_id=1, source_target_pairs={{6,0},{2,4},{0,8},{4,12},{8,14},{12,10},{14,6},{10,2},{7,1},{3,5},... | collective-permute-start | bytes 393224 | tf_op jit(solution)/shard_map/ppermute | solution.py:351
  28.0 2.1 %fold_early.1 = (f32[128,256]{1,0:T(8,128)S(1)}, f32[64,128,128]{2,1,0:T(8,128)S(1)}) custom-call(bf16[8,128,128]{2,1,0:T(8,128)(2,1)S(1)} %copy-done.3, bf16[8,128,128]{2,1,0:T(8,128)(2,1)S(1)} %collective-permute-done.refs_1_, bf16[8,128,128]{2,1,0:T(8,128)(2,1)S(1)} %collective-permute-done.3.refs_2_, ...), custom_call_target="tpu_custom_call" | custom-call | flops 268435456 | bytes 4194304 | tf_op jit(solution)/shard_map/fold_early/pallas_call | solution.py:39
  30.2 2.0 %collective-permute-done.6.refs_0_ = bf16[8,128,128]{2,1,0:T(8,128)(2,1)S(1)} collective-permute-done((bf16[8,128,128]{2,1,0:T(8,128)(2,1)S(1)}, bf16[8,128,128]{2,1,0:T(8,128)(2,1)S(1)}, u32[]{:S(2)}, u32[]{:S(2)}) %collective-permute-start.6) | collective-permute-done | bytes 262176 | tf_op jit(solution)/shard_map/ppermute | solution.py:351
  32.2 1.4 %fold_late.1 = (f32[128,256]{1,0:T(8,128)S(1)}, f32[64,128,128]{2,1,0:T(8,128)S(1)}) custom-call(bf16[8,128,128]{2,1,0:T(8,128)(2,1)S(1)} %collective-permute-done.6.refs_0_, bf16[8,128,128]{2,1,0:T(8,128)(2,1)S(1)} %collective-permute-done.7.refs_1_, s32[128,128]{1,0:T(8,128)S(1)} %get-tuple-element.44.refs_5_.refs_2_, bf16[256,8192]{1,0:T(8,128)(2,1)S(1)} %bitcast.16, ...), custom_call_target="tpu_custom_call" | custom-call | flops 134217728 | bytes 1048576 | tf_op jit(solution)/shard_map/fold_late/pallas_call | solution.py:39
  33.6 1.9 %collective-permute-done.5.refs_1_ = bf16[4,128,128]{2,1,0:T(8,128)(2,1)S(1)} collective-permute-done((bf16[4,128,128]{2,1,0:T(8,128)(2,1)S(1)}, bf16[4,128,128]{2,1,0:T(8,128)(2,1)S(1)}, u32[]{:S(2)}, u32[]{:S(2)}) %collective-permute-start.5) | collective-permute-done | bytes 131104 | tf_op jit(solution)/shard_map/ppermute | solution.py:351
  35.5 2.0 %finish.1 = (bf16[128,256]{1,0:T(8,128)(2,1)S(1)}, f32[8,128,128]{2,1,0:T(8,128)S(1)}, bf16[4,128,128]{2,1,0:T(8,128)(2,1)S(1)}, bf16[4,128,128]{2,1,0:T(8,128)(...) custom-call(bf16[4,128,128]{2,1,0:T(8,128)(2,1)S(1)} %collective-permute-done.2.refs_0_, ...), custom_call_target="tpu_custom_call" | custom-call | flops 268435456 | bytes 2097152 | tf_op jit(solution)/shard_map/finish/pallas_call | solution.py:39
  37.5 1.7 %collective-permute-start.8 = (bf16[8,128,128]{2,1,0:T(8,128)(2,1)S(1)}, bf16[8,128,128]{2,1,0:T(8,128)(2,1)S(1)}, u32[]{:S(2)}, u32[]{:S(2)}) collective-permute-start(bf16[8,128,128]{2,1,0:T(8,128)(2,1)S(1)} %get-tuple-element.60), channel_id=1, source_target_pairs={{2,0},{0,4},{4,8},{8,12},{12,14},{14,10},{10,6},{6,2},{3,1},{1,5},... | collective-permute-start | bytes 786440 | tf_op jit(solution)/shard_map/ppermute | solution.py:351
  39.6 3.0 %collective-permute-start.10 = (bf16[4,128,128]{2,1,0:T(8,128)(2,1)S(1)}, bf16[4,128,128]{2,1,0:T(8,128)(2,1)S(1)}, u32[]{:S(2)}, u32[]{:S(2)}) collective-permute-start(bf16[4,128,128]{2,1,0:T(8,128)(2,1)S(1)} %get-tuple-element.62), channel_id=1, source_target_pairs={{6,0},{2,4},{0,8},{4,12},{8,14},{12,10},{14,6},{10,2},{7,1},{3,5},... | collective-permute-start | bytes 393224 | tf_op jit(solution)/shard_map/ppermute | solution.py:351
  42.6 1.3 %part.3 = (f32[8,128,128]{2,1,0:T(8,128)S(1)}, f32[8,128,128]{2,1,0:T(8,128)S(1)}) custom-call(bf16[128,256]{1,0:T(8,128)(2,1)S(1)} %get-tuple-element.71.refs_0_, bf16[256,8192]{1,0:T(8,128)(2,1)S(1)} %bitcast.12, f32[64,128,128]{2,1,0:T(8,128)S(1)} %get-tuple-element.52.refs_10_.refs_2_, f32[8,128,128]{2,1,0:T(8,128)S(1)} %get-tuple-element.56.refs_3_, ...), custom_call_target="tpu_custom_call" | custom-call | flops 67108864 | bytes 1048576 | tf_op jit(solution)/shard_map/part/pallas_call | solution.py:39
  43.9 2.6 %dense.6 = (f32[128,1024]{1,0:T(8,128)S(1)}, f32[128,1024]{1,0:T(8,128)S(1)}) custom-call(bf16[8,128,128]{2,1,0:T(8,128)(2,1)S(1)} %copy-done.4, bf16[1024,8192]{1,0:T(8,128)(2,1)} %refs_1_.7), custom_call_target="tpu_custom_call" | custom-call | flops 536870912 | bytes 4194304 | tf_op jit(solution)/shard_map/dense/pallas_call | solution.py:39
  46.5 2.9 %collective-permute-done.10 = bf16[4,128,128]{2,1,0:T(8,128)(2,1)S(1)} collective-permute-done((bf16[4,128,128]{2,1,0:T(8,128)(2,1)S(1)}, bf16[4,128,128]{2,1,0:T(8,128)(2,1)S(1)}, u32[]{:S(2)}, u32[]{:S(2)}) %collective-permute-start.10) | collective-permute-done | bytes 131104 | tf_op jit(solution)/shard_map/ppermute | solution.py:351
  49.4 1.9 %collective-permute-done.11 = bf16[4,128,128]{2,1,0:T(8,128)(2,1)S(1)} collective-permute-done((bf16[4,128,128]{2,1,0:T(8,128)(2,1)S(1)}, bf16[4,128,128]{2,1,0:T(8,128)(2,1)S(1)}, u32[]{:S(2)}, u32[]{:S(2)}) %collective-permute-start.11) | collective-permute-done | bytes 131104 | tf_op jit(solution)/shard_map/ppermute | solution.py:351
  51.8 1.8 %collective-permute-start.14 = (bf16[8,128,128]{2,1,0:T(8,128)(2,1)S(1)}, bf16[8,128,128]{2,1,0:T(8,128)(2,1)S(1)}, u32[]{:S(2)}, u32[]{:S(2)}) collective-permute-start(bf16[8,128,128]{2,1,0:T(8,128)(2,1)S(1)} %add_convert_fusion.1), channel_id=1, source_target_pairs={{4,0},{8,4},{12,8},{14,12},{10,14},{6,10},{2,6},{0,2},{5,1},{9,5},... | collective-permute-start | bytes 786440 | tf_op jit(solution)/shard_map/ppermute | solution.py:351
  53.6 1.3 %part.4 = (f32[8,128,128]{2,1,0:T(8,128)S(1)}, f32[8,128,128]{2,1,0:T(8,128)S(1)}) custom-call(bf16[128,256]{1,0:T(8,128)(2,1)S(1)} %get-tuple-element.71.refs_0_, bf16[256,8192]{1,0:T(8,128)(2,1)S(1)} %bitcast.13, f32[64,128,128]{2,1,0:T(8,128)S(1)} %get-tuple-element.52.refs_10_.refs_2_, f32[8,128,128]{2,1,0:T(8,128)S(1)} %get-tuple-element.56.refs_3_, ...), custom_call_target="tpu_custom_call" | custom-call | flops 67108864 | bytes 1048576 | tf_op jit(solution)/shard_map/part/pallas_call | solution.py:39
  55.0 4.2 %collective-permute-done.12 = bf16[8,128,128]{2,1,0:T(8,128)(2,1)S(1)} collective-permute-done((bf16[8,128,128]{2,1,0:T(8,128)(2,1)S(1)}, bf16[8,128,128]{2,1,0:T(8,128)(2,1)S(1)}, u32[]{:S(2)}, u32[]{:S(2)}) %collective-permute-start.12) | collective-permute-done | bytes 262176 | tf_op jit(solution)/shard_map/ppermute | solution.py:351
  59.3 1.8 %collective-permute-start.13 = (bf16[8,128,128]{2,1,0:T(8,128)(2,1)S(1)}, bf16[8,128,128]{2,1,0:T(8,128)(2,1)S(1)}, u32[]{:S(2)}, u32[]{:S(2)}) collective-permute-start(bf16[8,128,128]{2,1,0:T(8,128)(2,1)S(1)} %add_convert_fusion.2), channel_id=1, source_target_pairs={{2,0},{0,4},{4,8},{8,12},{12,14},{14,10},{10,6},{6,2},{3,1},{1,5},... | collective-permute-start | bytes 786440 | tf_op jit(solution)/shard_map/ppermute | solution.py:351
  61.5 1.9 %dense.7.refs_7_ = f32[128,1024]{1,0:T(8,128)S(1)} custom-call(bf16[8,128,128]{2,1,0:T(8,128)(2,1)S(1)} %copy-done.4, bf16[1024,8192]{1,0:T(8,128)(2,1)} %refs_1_.7), custom_call_target="tpu_custom_call" | custom-call | flops 268435456 | bytes 2097152 | tf_op jit(solution)/shard_map/dense/pallas_call | solution.py:39
  63.4 1.0 %part.5.own_ref = f32[8,128,128]{2,1,0:T(8,128)S(1)} custom-call(bf16[128,256]{1,0:T(8,128)(2,1)S(1)} %get-tuple-element.71.refs_0_, bf16[256,8192]{1,0:T(8,128)(2,1)S(1)} %bitcast.14, f32[64,128,128]{2,1,0:T(8,128)S(1)} %get-tuple-element.52.refs_10_.refs_2_, f32[8,128,128]{2,1,0:T(8,128)S(1)} %get-tuple-element.56.refs_3_, f32[4,16]{1,0:T(4,128)S(1)} %copy-done.5, ...), custom_call_target="tpu_custom_call" | custom-call | flops 67108864 | bytes 1048576 | tf_op jit(solution)/shard_map/part/pallas_call | solution.py:39
  64.4 1.3 %collective-permute-done.13.refs_0_ = bf16[8,128,128]{2,1,0:T(8,128)(2,1)S(1)} collective-permute-done((bf16[8,128,128]{2,1,0:T(8,128)(2,1)S(1)}, bf16[8,128,128]{2,1,0:T(8,128)(2,1)S(1)}, u32[]{:S(2)}, u32[]{:S(2)}) %collective-permute-start.13) | collective-permute-done | bytes 262176 | tf_op jit(solution)/shard_map/ppermute | solution.py:351
  65.7 1.8 %collective-permute-done.15.refs_1_ = bf16[8,128,128]{2,1,0:T(8,128)(2,1)S(1)} collective-permute-done((bf16[8,128,128]{2,1,0:T(8,128)(2,1)S(1)}, bf16[8,128,128]{2,1,0:T(8,128)(2,1)S(1)}, u32[]{:S(2)}, u32[]{:S(2)}) %collective-permute-start.15) | collective-permute-done | bytes 262176 | tf_op jit(solution)/shard_map/ppermute | solution.py:351
  67.5 0.8 %sum_up.1 = bf16[128,1024]{1,0:T(8,128)(2,1)} custom-call(f32[8,128,128]{2,1,0:T(8,128)S(1)} %part.5.own_ref, bf16[8,128,128]{2,1,0:T(8,128)(2,1)S(1)} %collective-permute-done.13.refs_0_, bf16[8,128,128]{2,1,0:T(8,128)(2,1)S(1)} %collective-permute-done.15.refs_1_), custom_call_target="tpu_custom_call" | custom-call | flops 1 | bytes 1 | tf_op jit(solution)/shard_map/sum_up/pallas_call | solution.py:39
  (38 shorter events, 2.0 us)
Async XLA Ops:
  0.0 16.3 %copy-start.7 = (s32[4,16,1]{1,2,0:T(1,128)S(1)}, s32[4,16,1]{1,2,0:T(1,128)}, u32[]{:S(2)}) copy-start(s32[4,16,1]{1,2,0:T(1,128)} %param.28) | copy-start | bytes 772
  0.0 16.3 %copy-start.8 = (s32[128]{0:T(128)S(1)}, s32[128]{0:T(128)}, u32[]{:S(2)}) copy-start(s32[128]{0:T(128)} %param.21) | copy-start | bytes 1540
  0.0 16.3 %copy-start.9 = (s32[32]{0:T(128)S(1)}, s32[32]{0:T(128)}, u32[]{:S(2)}) copy-start(s32[32]{0:T(128)} %refs_3_.1) | copy-start | bytes 388
  4.8 9.5 %collective-permute-start.3 = (bf16[8,128,128]{2,1,0:T(8,128)(2,1)}, bf16[8,128,128]{2,1,0:T(8,128)(2,1)S(1)}, u32[]{:S(2)}, u32[]{:S(2)}) collective-permute-start(bf16[8,128,128]{2,1,0:T(8,128)(2,1)} %attend.1.refs_0_), channel_id=1, source_target_pairs={{2,0},{0,4},{4,8},{8,12},{12,14},{14,10},{10,6},{6,2},{3,1},{1,5},... | collective-permute-start | bytes 786440 | tf_op jit(solution)/shard_map/ppermute | solution.py:351
  7.8 8.3 %collective-permute-start = (bf16[8,128,128]{2,1,0:T(8,128)(2,1)}, bf16[8,128,128]{2,1,0:T(8,128)(2,1)S(1)}, u32[]{:S(2)}, u32[]{:S(2)}) collective-permute-start(bf16[8,128,128]{2,1,0:T(8,128)(2,1)} %attend.1.refs_0_), channel_id=1, source_target_pairs={{4,0},{8,4},{12,8},{14,12},{10,14},{6,10},{2,6},{0,2},{5,1},{9,5},... | collective-permute-start | bytes 786440 | tf_op jit(solution)/shard_map/ppermute | solution.py:351
  7.9 1.0 %copy-start.3 = (bf16[8,128,128]{2,1,0:T(8,128)(2,1)S(1)}, bf16[8,128,128]{2,1,0:T(8,128)(2,1)}, u32[]{:S(2)}) copy-start(bf16[8,128,128]{2,1,0:T(8,128)(2,1)} %attend.1.refs_0_) | copy-start | bytes 786436
  14.3 7.5 %collective-permute-start.4 = (bf16[8,128,128]{2,1,0:T(8,128)(2,1)S(1)}, bf16[8,128,128]{2,1,0:T(8,128)(2,1)S(1)}, u32[]{:S(2)}, u32[]{:S(2)}) collective-permute-start(bf16[8,128,128]{2,1,0:T(8,128)(2,1)S(1)} %collective-permute-done.3.refs_2_), channel_id=1, source_target_pairs={{2,0},{0,4},{4,8},{8,12},{12,14},{14,10},{10,6},{6,2},{3,1},{1,5},... | collective-permute-start | bytes 786440 | tf_op jit(solution)/shard_map/ppermute | solution.py:351
  16.1 6.9 %collective-permute-start.1 = (bf16[8,128,128]{2,1,0:T(8,128)(2,1)S(1)}, bf16[8,128,128]{2,1,0:T(8,128)(2,1)S(1)}, u32[]{:S(2)}, u32[]{:S(2)}) collective-permute-start(bf16[8,128,128]{2,1,0:T(8,128)(2,1)S(1)} %collective-permute-done.refs_1_), channel_id=1, source_target_pairs={{4,0},{8,4},{12,8},{14,12},{10,14},{6,10},{2,6},{0,2},{5,1},{9,5},... | collective-permute-start | bytes 786440 | tf_op jit(solution)/shard_map/ppermute | solution.py:351
  16.3 11.7 %copy-start.1 = (bf16[4,8192,64]{1,2,0:T(8,128)(2,1)S(1)}, bf16[4,8192,64]{1,2,0:T(8,128)(2,1)}, u32[]{:S(2)}) copy-start(bf16[4,8192,64]{1,2,0:T(8,128)(2,1)} %param.24) | copy-start | bytes 12582916
  16.4 11.7 %copy-start.2 = (bf16[4,16,128,128]{3,2,1,0:T(8,128)(2,1)S(1)}, bf16[4,16,128,128]{3,2,1,0:T(8,128)(2,1)}, u32[]{:S(2)}) copy-start(bf16[4,16,128,128]{3,2,1,0:T(8,128)(2,1)} %refs_4_.6) | copy-start | bytes 6291460
  16.4 11.7 %copy-start.5 = (f32[4,16]{1,0:T(4,128)S(1)}, f32[4,16]{1,0:T(4,128)}, u32[]{:S(2)}) copy-start(f32[4,16]{1,0:T(4,128)} %refs_4_.9) | copy-start | bytes 772
  16.4 11.7 %copy-start.6 = (s32[4,16]{1,0:T(4,128)S(1)}, s32[4,16]{1,0:T(4,128)}, u32[]{:S(2)}) copy-start(s32[4,16]{1,0:T(4,128)} %refs_5_.9) | copy-start | bytes 772
  23.0 9.2 %collective-permute-start.6 = (bf16[8,128,128]{2,1,0:T(8,128)(2,1)S(1)}, bf16[8,128,128]{2,1,0:T(8,128)(2,1)S(1)}, u32[]{:S(2)}, u32[]{:S(2)}) collective-permute-start(bf16[8,128,128]{2,1,0:T(8,128)(2,1)S(1)} %collective-permute-done.1.refs_3_), channel_id=1, source_target_pairs={{4,0},{8,4},{12,8},{14,12},{10,14},{6,10},{2,6},{0,2},{5,1},{9,5},... | collective-permute-start | bytes 786440 | tf_op jit(solution)/shard_map/ppermute | solution.py:351
  23.6 8.6 %collective-permute-start.7 = (bf16[8,128,128]{2,1,0:T(8,128)(2,1)S(1)}, bf16[8,128,128]{2,1,0:T(8,128)(2,1)S(1)}, u32[]{:S(2)}, u32[]{:S(2)}) collective-permute-start(bf16[8,128,128]{2,1,0:T(8,128)(2,1)S(1)} %collective-permute-done.4.refs_4_), channel_id=1, source_target_pairs={{2,0},{0,4},{4,8},{8,12},{12,14},{14,10},{10,6},{6,2},{3,1},{1,5},... | collective-permute-start | bytes 786440 | tf_op jit(solution)/shard_map/ppermute | solution.py:351
  25.1 10.4 %collective-permute-start.5 = (bf16[4,128,128]{2,1,0:T(8,128)(2,1)S(1)}, bf16[4,128,128]{2,1,0:T(8,128)(2,1)S(1)}, u32[]{:S(2)}, u32[]{:S(2)}) collective-permute-start(bf16[4,128,128]{2,1,0:T(8,128)(2,1)S(1)} %slice.7), channel_id=1, source_target_pairs={{6,0},{2,4},{0,8},{4,12},{8,14},{12,10},{14,6},{10,2},{7,1},{3,5},... | collective-permute-start | bytes 393224 | tf_op jit(solution)/shard_map/ppermute | solution.py:351
  27.7 7.8 %collective-permute-start.2 = (bf16[4,128,128]{2,1,0:T(8,128)(2,1)S(1)}, bf16[4,128,128]{2,1,0:T(8,128)(2,1)S(1)}, u32[]{:S(2)}, u32[]{:S(2)}) collective-permute-start(bf16[4,128,128]{2,1,0:T(8,128)(2,1)S(1)} %slice.6), channel_id=1, source_target_pairs={{8,0},{12,4},{14,8},{10,12},{6,14},{2,10},{0,6},{4,2},{9,1},{13,5}... | collective-permute-start | bytes 393224 | tf_op jit(solution)/shard_map/ppermute | solution.py:351
  32.2 3.3 %copy-start = (bf16[4,64,8192]{2,1,0:T(8,128)(2,1)S(1)}, bf16[4,64,8192]{2,1,0:T(8,128)(2,1)}, u32[]{:S(2)}) copy-start(bf16[4,64,8192]{2,1,0:T(8,128)(2,1)} %param.25) | copy-start | bytes 12582916
  37.5 13.8 %collective-permute-start.8 = (bf16[8,128,128]{2,1,0:T(8,128)(2,1)S(1)}, bf16[8,128,128]{2,1,0:T(8,128)(2,1)S(1)}, u32[]{:S(2)}, u32[]{:S(2)}) collective-permute-start(bf16[8,128,128]{2,1,0:T(8,128)(2,1)S(1)} %get-tuple-element.60), channel_id=1, source_target_pairs={{2,0},{0,4},{4,8},{8,12},{12,14},{14,10},{10,6},{6,2},{3,1},{1,5},... | collective-permute-start | bytes 786440 | tf_op jit(solution)/shard_map/ppermute | solution.py:351
  39.2 12.1 %collective-permute-start.9 = (bf16[8,128,128]{2,1,0:T(8,128)(2,1)S(1)}, bf16[8,128,128]{2,1,0:T(8,128)(2,1)S(1)}, u32[]{:S(2)}, u32[]{:S(2)}) collective-permute-start(bf16[8,128,128]{2,1,0:T(8,128)(2,1)S(1)} %get-tuple-element.61), channel_id=1, source_target_pairs={{4,0},{8,4},{12,8},{14,12},{10,14},{6,10},{2,6},{0,2},{5,1},{9,5},... | collective-permute-start | bytes 786440 | tf_op jit(solution)/shard_map/ppermute | solution.py:351
  39.6 9.8 %collective-permute-start.10 = (bf16[4,128,128]{2,1,0:T(8,128)(2,1)S(1)}, bf16[4,128,128]{2,1,0:T(8,128)(2,1)S(1)}, u32[]{:S(2)}, u32[]{:S(2)}) collective-permute-start(bf16[4,128,128]{2,1,0:T(8,128)(2,1)S(1)} %get-tuple-element.62), channel_id=1, source_target_pairs={{6,0},{2,4},{0,8},{4,12},{8,14},{12,10},{14,6},{10,2},{7,1},{3,5},... | collective-permute-start | bytes 393224 | tf_op jit(solution)/shard_map/ppermute | solution.py:351
  42.6 8.8 %collective-permute-start.11 = (bf16[4,128,128]{2,1,0:T(8,128)(2,1)S(1)}, bf16[4,128,128]{2,1,0:T(8,128)(2,1)S(1)}, u32[]{:S(2)}, u32[]{:S(2)}) collective-permute-start(bf16[4,128,128]{2,1,0:T(8,128)(2,1)S(1)} %get-tuple-element.63), channel_id=1, source_target_pairs={{8,0},{12,4},{14,8},{10,12},{6,14},{2,10},{0,6},{4,2},{9,1},{13,5}... | collective-permute-start | bytes 393224 | tf_op jit(solution)/shard_map/ppermute | solution.py:351
  42.6 1.4 %copy-start.4 = (bf16[8,128,128]{2,1,0:T(8,128)(2,1)S(1)}, bf16[8,128,128]{2,1,0:T(8,128)(2,1)}, u32[]{:S(2)}) copy-start(bf16[8,128,128]{2,1,0:T(8,128)(2,1)} %attend.1.refs_0_) | copy-start | bytes 786436
  51.4 7.8 %collective-permute-start.12 = (bf16[8,128,128]{2,1,0:T(8,128)(2,1)S(1)}, bf16[8,128,128]{2,1,0:T(8,128)(2,1)S(1)}, u32[]{:S(2)}, u32[]{:S(2)}) collective-permute-start(bf16[8,128,128]{2,1,0:T(8,128)(2,1)S(1)} %add_convert_fusion.3), channel_id=1, source_target_pairs={{2,0},{0,4},{4,8},{8,12},{12,14},{14,10},{10,6},{6,2},{3,1},{1,5},... | collective-permute-start | bytes 786440 | tf_op jit(solution)/shard_map/ppermute | solution.py:351
  51.8 9.2 %collective-permute-start.14 = (bf16[8,128,128]{2,1,0:T(8,128)(2,1)S(1)}, bf16[8,128,128]{2,1,0:T(8,128)(2,1)S(1)}, u32[]{:S(2)}, u32[]{:S(2)}) collective-permute-start(bf16[8,128,128]{2,1,0:T(8,128)(2,1)S(1)} %add_convert_fusion.1), channel_id=1, source_target_pairs={{4,0},{8,4},{12,8},{14,12},{10,14},{6,10},{2,6},{0,2},{5,1},{9,5},... | collective-permute-start | bytes 786440 | tf_op jit(solution)/shard_map/ppermute | solution.py:351
  59.3 6.4 %collective-permute-start.13 = (bf16[8,128,128]{2,1,0:T(8,128)(2,1)S(1)}, bf16[8,128,128]{2,1,0:T(8,128)(2,1)S(1)}, u32[]{:S(2)}, u32[]{:S(2)}) collective-permute-start(bf16[8,128,128]{2,1,0:T(8,128)(2,1)S(1)} %add_convert_fusion.2), channel_id=1, source_target_pairs={{2,0},{0,4},{4,8},{8,12},{12,14},{14,10},{10,6},{6,2},{3,1},{1,5},... | collective-permute-start | bytes 786440 | tf_op jit(solution)/shard_map/ppermute | solution.py:351
  61.1 6.4 %collective-permute-start.15 = (bf16[8,128,128]{2,1,0:T(8,128)(2,1)S(1)}, bf16[8,128,128]{2,1,0:T(8,128)(2,1)S(1)}, u32[]{:S(2)}, u32[]{:S(2)}) collective-permute-start(bf16[8,128,128]{2,1,0:T(8,128)(2,1)S(1)} %add_convert_fusion), channel_id=1, source_target_pairs={{4,0},{8,4},{12,8},{14,12},{10,14},{6,10},{2,6},{0,2},{5,1},{9,5},... | collective-permute-start | bytes 786440 | tf_op jit(solution)/shard_map/ppermute | solution.py:351

commit v9 on v8

--- a/solution.py
+++ b/solution.py
@@ -104,19 +104,16 @@
             out_ref[h, here, :] = attended[h * ROW_BLOCK : (h + 1) * ROW_BLOCK]
 
 
-def dense_kernel(distances, count, listing, *refs):
+def dense_kernel(distances, count, listing, turn, *refs):
     x_ref, weight_ref = refs[:2]
-    if listing:
-        variant_ref, holder_ref, owner_ref = refs[2:5]
-        outs, slot_ref, table_ref = refs[5 : 5 + len(distances)], refs[-4], refs[-3]
-    else:
-        outs = refs[2 : 2 + len(distances)]
+    outs = refs[-2 - 2 * listing - len(distances) : -2 - 2 * listing]
     buffers, sems = refs[-2:]
     heads, rows, side = x_ref.shape
     width = heads * side
     depth = buffers.shape[0]
     piece = buffers.shape[2]
     cuts = width // piece
+    total = len(distances) * cuts
 
     def fetch(i):
         start = pl.multiple_of(owner_at(distances[i // cuts], count) * width, width) + i % cuts * piece
@@ -126,35 +123,53 @@
             sems.at[i % depth],
         )
 
-    total = len(distances) * cuts
-    for i in range(min(depth, total)):
-        fetch(i).start()
-    if listing:
-        slots = owner_ref.shape[0]
-        variant = variant_ref[...]
-        slot_row = jnp.zeros(variant.shape, jnp.int32)
-        for v in range(holder_ref.shape[0]):
-            slot_row = jnp.where(variant == v, holder_ref[v], slot_row)
-        slot_row = (slot_row - lax.axis_index("tp") * slots).astype(F32)
-        slot_ref[...] = jnp.transpose(jnp.broadcast_to(slot_row, (rows, rows))).astype(jnp.int32)
-        for e in range(table_ref.shape[0]):
-            table_ref[e] = -1
-        for j in range(slots):
-
-            def note(b, carry, j=j):
-                e = (owner_ref[j, b] * slots + j) * CAP
-                table_ref[e + jnp.where(table_ref[e] >= 0, 1, 0)] = b
-                return carry
-
-            lax.fori_loop(0, owner_ref.shape[1], note, 0)
-    x = jnp.concatenate([x_ref[h] for h in range(heads)], axis=1)
-    for i in range(total):
-        fetch(i).wait()
-        outs[i // cuts][:, i % cuts * piece : (i % cuts + 1) * piece] = jnp.dot(
-            x, buffers[i % depth], preferred_element_type=F32
-        )
-        if i + depth < total:
-            fetch(i + depth).start()
+    def compute():
+        for i in range(min(depth, total)):
+            fetch(i).start()
+        if listing:
+            list_blocks(refs[2], refs[3], refs[4], refs[-4], refs[-3])
+        x = jnp.concatenate([x_ref[h] for h in range(heads)], axis=1)
+        for i in range(total):
+            fetch(i).wait()
+            outs[i // cuts][:, i % cuts * piece : (i % cuts + 1) * piece] = jnp.dot(
+                x, buffers[i % depth], preferred_element_type=F32
+            )
+            if i + depth < total:
+                fetch(i + depth).start()
+
+    if turn is None:
+        compute()
+        return
+    here = lax.axis_index("rep") == turn
+    pl.when(here)(compute)
+    handed = refs[2 : -2 - len(distances)]
+    if handed:
+
+        @pl.when(jnp.logical_not(here))
+        def _():
+            for source, target in zip(handed, outs):
+                target[...] = source[...]
+
+
+def list_blocks(variant_ref, holder_ref, owner_ref, slot_ref, table_ref):
+    rows = slot_ref.shape[0]
+    slots = owner_ref.shape[0]
+    variant = variant_ref[...]
+    slot_row = jnp.zeros(variant.shape, jnp.int32)
+    for v in range(holder_ref.shape[0]):
+        slot_row = jnp.where(variant == v, holder_ref[v], slot_row)
+    slot_row = (slot_row - lax.axis_index("tp") * slots).astype(F32)
+    slot_ref[...] = jnp.transpose(jnp.broadcast_to(slot_row, (rows, rows))).astype(jnp.int32)
+    for e in range(table_ref.shape[0]):
+        table_ref[e] = -1
+    for j in range(slots):
+
+        def note(b, carry, j=j):
+            e = (owner_ref[j, b] * slots + j) * CAP
+            table_ref[e + jnp.where(table_ref[e] >= 0, 1, 0)] = b
+            return carry
+
+        lax.fori_loop(0, owner_ref.shape[1], note, 0)
 
 
 def held_blocks(distance, count, slots, heads, scale_ref, cell_ref, table_ref):
@@ -329,15 +344,15 @@
     piece = width // 2 if width >= 512 else width
     dense = {}
 
-    def dense_for(distances, x, listing=False):
+    def dense_for(distances, x, listing=False, turn=None, handed=()):
         extra_shapes = [shape((rows, rows), jnp.int32), shape((count * slots * CAP,), jnp.int32)]
         extra_ins = (request_variant[None, :], holder_slot, block_owner[:, :, 0])
         got = call(
-            functools.partial(dense_kernel, distances, count, listing),
+            functools.partial(dense_kernel, distances, count, listing, turn),
             "dense",
             [shape((rows, width), F32)] * len(distances) + extra_shapes * listing,
-            (x, out_weight) + extra_ins * listing,
-            [VMEM, ANY] + [VMEM, SMEM, SMEM] * listing,
+            (x, out_weight) + extra_ins * listing + tuple(handed),
+            [VMEM, ANY] + [VMEM, SMEM, SMEM] * listing + [VMEM] * len(handed),
             [VMEM] * len(distances) + [VMEM, SMEM] * listing,
             [pltpu.VMEM((4, width, piece), BF16), pltpu.SemaphoreType.DMA((4,))],
             limit=40,
@@ -345,24 +360,25 @@
             moved=2 * width * width * len(distances),
         )
         dense.update(zip(distances, got))
-        return got[len(distances) :] if listing else got[0]
+        return got[len(distances) :] if listing else got
 
     def come(value, distance):
         return lax.ppermute(
             value, "tp", [(ring[(i + distance) % count], ring[i]) for i in range(count)]
         )
 
+    begun = dense_for(wanted[:3], attended, turn=1)
+    attended = after(attended, begun[0])
     chunks = {0: attended}
     chunks[1], chunks[count - 1] = come(attended, 1), come(attended, -1)
-    token = dense_for(wanted[:3], attended)
+    (token, *_) = dense_for(wanted[:3], attended, turn=0, handed=begun)
     for step in range(2, half):
         right, left = after(chunks[step - 1], token), after(chunks[count - step + 1], token)
-        if step == half - 1:
-            front, back = come(right[: heads // 2], 2), come(left[heads // 2 :], -2)
         chunks[step], chunks[count - step] = come(right, 1), come(left, -1)
         if step == 2:
             slot, table = dense_for(wanted[3:5], after(attended, token), True)
             token = slot
+    right, left = chunks[half - 1], chunks[half + 1]
 
     factor_t = jnp.swapaxes(factor_in, 1, 2).reshape(low_width, -1)
     second = second_factor.reshape(low_width, complete)
@@ -383,6 +399,8 @@
         flops=rows * low_width * complete,
         moved=4 * MIB,
     )
+    right, left = after(right, low), after(left, low)
+    front, back = come(right[: heads // 2], 1), come(left[heads // 2 :], -1)
     low, blocks = call(
         functools.partial(fold_kernel, late, count, False),
         "fold_late",
@@ -394,7 +412,7 @@
         moved=MIB,
     )
     extras = shape((slots * CAP, rows, side), F32)
-    first = wanted[:3]
+    first = wanted[:1]
     travelling = shape((heads, rows, side), BF16)
     low, extra, front, back, *sums = call(
         functools.partial(finish_kernel, first, count),
@@ -437,25 +455,22 @@
             total = total + value
         return total.astype(BF16)
 
-    front, back = come(front, -2), come(back, 2)
-    from_left, from_right = come(parts[half - 1], -1), come(parts[half + 1], 1)
-    parts_for([half - 2, half + 2], low, F32)
-    token = dense_for(wanted[5:-1], after(attended, low))
-    from_left, from_right, front, back, token = lax.optimization_barrier(
-        (from_left, from_right, front, back, token)
-    )
-    right = joined(parts[half - 2], (from_left, None), (front, 0))
-    left = joined(parts[half + 2], (from_right, None), (back, 1))
-    for distance in range(half - 2, 0, -1):
+    begun = dense_for(wanted[5:-1], after(attended, low), turn=1)
+    front, back = after(front, begun[0]), after(back, begun[0])
+    left, right = (come(front, 1), 0), (come(back, -1), 1)
+    parts_for([half - 1, half + 1], after(low, begun[0]), F32)
+    for distance in range(half - 1, 0, -1):
+        left = joined(parts[count - distance], left)
+        right = joined(parts[distance], right)
         nearer = distance - 1
+        kept = after(low, right)
+        parts_for([nearer, count - nearer] if nearer else [0], kept, F32)
+        if distance == half - 1:
+            dense_for(wanted[5:-1], after(attended, right), turn=0, handed=begun)
         if distance == half - 2:
             dense_for([0], after(attended, right))
-        parts_for([nearer, count - nearer] if nearer else [0], after(low, right), F32)
-        from_left, from_right = come(right, -1), come(left, 1)
-        if nearer:
-            right = joined(parts[nearer], (from_left, None))
-            left = joined(parts[count - nearer], (from_right, None))
-    came = [from_left, from_right]
+        left, right = (come(left, 1), None), (come(right, -1), None)
+    came = [left[0], right[0]]
     return call(
         sum_kernel,
         "sum_up",

time: 68.5 us -> 71.8 us (1.048)
  waiting for transfers between devices: 20.9 us -> 24.4 us
  starting transfers between devices: 19.4 us -> 18.4 us
  Pallas kernels: 26.4 us -> 27.3 us
    ppermute x16, waiting for transfers between devices: 20.9 us -> 24.4 us  [come(): lax.ppermute(value, 'tp', [(ring[(i + distance) % count], ring[i]) for i...]
    ppermute x16, starting transfers between devices: 19.4 us -> 18.4 us  [come(): lax.ppermute(value, 'tp', [(ring[(i + distance) % count], ring[i]) for i...]
    pallas_call x12 -> x15, Pallas kernels: 26.4 us -> 27.3 us  [call(): pl.pallas_call(kernel, out_shape=outs, in_specs=specs, out_specs=out_spec...]
  transfers between devices with their start and end apart: 16 -> 16, of which waited for: 10 -> 15; matrix products, arithmetic and copies ran while one was open for 0% -> 0% of each run, Pallas kernels for 28% -> 28%
where the time goes in v9:
time: 71.8 us; the launch traced here: 71.6 us
  Pallas kernels  27.3 us (38%)
  waiting for transfers between devices  24.4 us (34%)
  starting transfers between devices  18.4 us (26%)
  local copies, waits for them, and re-layouts  1.01 us (1%)
    pallas_call x15, Pallas kernels, call(): pl.pallas_call(kernel, out_shape=outs, in_specs=specs, out_specs=out_spec...  27.3 us
    ppermute x16, waiting for transfers between devices, come(): lax.ppermute(value, 'tp', [(ring[(i + distance) % count], ring[i]) for i...  24.4 us
    ppermute x16, starting transfers between devices, come(): lax.ppermute(value, 'tp', [(ring[(i + distance) % count], ring[i]) for i...  18.4 us
  transfers between devices with their start and end apart: 16, of which 15 were waited for; matrix products, arithmetic and copies ran while one was open for 0% of the time, Pallas kernels for 28%

profile of v9, /device:TPU:0, one launch (start us, length us, event | category | flops | bytes accessed | tf_op | source)
XLA Modules:
  0.0 71.6 jit_solution(10122541533217504310)
XLA Ops:
  0.0 4.7 %attend.1.refs_0_ = bf16[8,128,128]{2,1,0:T(8,128)(2,1)} custom-call(bf16[128,1024]{1,0:T(8,128)(2,1)} %query_hbm.1, bf16[4096,128]{1,0:T(8,128)(2,1)} %bitcast.21, bf16[4096,128]{1,0:T(8,128)(2,1)} %bitcast.22, bf16[128,128]{1,0:T(8,128)(2,1)} %bitcast.23, bf16[128,128]{1,0:T(8,128)(2,1)} %bitcast.24, s32[1,128]{1,0:T(1,128)} %bitcast.25), custom_call_target="tpu_custom_call" | custom-call | tf_op jit(solution)/shard_map/attend/pallas_call | solution.py:39
  4.7 0.9 %copy-done.3 = bf16[8,128,128]{2,1,0:T(8,128)(2,1)S(1)} copy-done((bf16[8,128,128]{2,1,0:T(8,128)(2,1)S(1)}, bf16[8,128,128]{2,1,0:T(8,128)(2,1)}, u32[]{:S(2)}) %copy-start.3) | copy-done | bytes 262168
  5.7 3.1 %collective-permute-start.3 = (bf16[8,128,128]{2,1,0:T(8,128)(2,1)S(1)}, bf16[8,128,128]{2,1,0:T(8,128)(2,1)S(1)}, u32[]{:S(2)}, u32[]{:S(2)}) collective-permute-start(bf16[8,128,128]{2,1,0:T(8,128)(2,1)S(1)} %copy-done.3), channel_id=1, source_target_pairs={{2,0},{0,4},{4,8},{8,12},{12,14},{14,10},{10,6},{6,2},{3,1},{1,5},... | collective-permute-start | bytes 786440 | tf_op jit(solution)/shard_map/ppermute | solution.py:366
  8.8 3.5 %dense.7 = (f32[128,1024]{1,0:T(8,128)S(1)}, f32[128,1024]{1,0:T(8,128)S(1)}, f32[128,1024]{1,0:T(8,128)S(1)}) custom-call(bf16[8,128,128]{2,1,0:T(8,128)(2,1)S(1)} %copy-done.3, bf16[1024,8192]{1,0:T(8,128)(2,1)} %refs_1_.11, f32[128,1024]{1,0:T(8,128)S(1)} %get-tuple-element.50.refs_2_, f32[128,1024]{1,0:T(8,128)S(1)} %get-tuple-element.52.refs_3_, ...), custom_call_target="tpu_custom_call" | custom-call | flops 805306368 | bytes 6291456 | tf_op jit(solution)/shard_map/dense/pallas_call | solution.py:39
  12.3 0.9 %collective-permute-done.3.refs_2_ = bf16[8,128,128]{2,1,0:T(8,128)(2,1)S(1)} collective-permute-done((bf16[8,128,128]{2,1,0:T(8,128)(2,1)S(1)}, bf16[8,128,128]{2,1,0:T(8,128)(2,1)S(1)}, u32[]{:S(2)}, u32[]{:S(2)}) %collective-permute-start.3) | collective-permute-done | bytes 262176 | tf_op jit(solution)/shard_map/ppermute | solution.py:366
  13.3 2.4 %collective-permute-start.4 = (bf16[8,128,128]{2,1,0:T(8,128)(2,1)S(1)}, bf16[8,128,128]{2,1,0:T(8,128)(2,1)S(1)}, u32[]{:S(2)}, u32[]{:S(2)}) collective-permute-start(bf16[8,128,128]{2,1,0:T(8,128)(2,1)S(1)} %collective-permute-done.3.refs_2_), channel_id=1, source_target_pairs={{2,0},{0,4},{4,8},{8,12},{12,14},{14,10},{10,6},{6,2},{3,1},{1,5},... | collective-permute-start | bytes 786440 | tf_op jit(solution)/shard_map/ppermute | solution.py:366
  16.0 3.7 %dense.8 = (f32[128,1024]{1,0:T(8,128)S(1)}, f32[128,1024]{1,0:T(8,128)S(1)}, s32[128,128]{1,0:T(8,128)S(1)}, s32[64]{0:T(128)S(1)}) custom-call(bf16[8,128,128]{2,1,0:T(8,128)(2,1)S(1)} %copy-done.3, bf16[1024,8192]{1,0:T(8,128)(2,1)} %refs_1_.11, s32[1,128]{1,0:T(1,128)S(1)} %bitcast.20, s32[32]{0:T(128)S(1)} %copy-done.8, s32[4,16]{1,0:T(4,128)S(1)} %bitcast.19), custom_call_target="tpu_custom_call" | custom-call | flops 536870912 | bytes 4194304 | tf_op jit(solution)/shard_map/dense/pallas_call | solution.py:39
  19.7 1.4 %collective-permute-done.4.refs_4_ = bf16[8,128,128]{2,1,0:T(8,128)(2,1)S(1)} collective-permute-done((bf16[8,128,128]{2,1,0:T(8,128)(2,1)S(1)}, bf16[8,128,128]{2,1,0:T(8,128)(2,1)S(1)}, u32[]{:S(2)}, u32[]{:S(2)}) %collective-permute-start.4) | collective-permute-done | bytes 262176 | tf_op jit(solution)/shard_map/ppermute | solution.py:366
  21.1 2.4 %collective-permute-start.6 = (bf16[8,128,128]{2,1,0:T(8,128)(2,1)S(1)}, bf16[8,128,128]{2,1,0:T(8,128)(2,1)S(1)}, u32[]{:S(2)}, u32[]{:S(2)}) collective-permute-start(bf16[8,128,128]{2,1,0:T(8,128)(2,1)S(1)} %collective-permute-done.4.refs_4_), channel_id=1, source_target_pairs={{2,0},{0,4},{4,8},{8,12},{12,14},{14,10},{10,6},{6,2},{3,1},{1,5},... | collective-permute-start | bytes 786440 | tf_op jit(solution)/shard_map/ppermute | solution.py:366
  23.9 2.2 %fold_early.1 = (f32[128,256]{1,0:T(8,128)S(1)}, f32[64,128,128]{2,1,0:T(8,128)S(1)}) custom-call(bf16[8,128,128]{2,1,0:T(8,128)(2,1)S(1)} %copy-done.3, bf16[8,128,128]{2,1,0:T(8,128)(2,1)S(1)} %collective-permute-done.refs_1_, bf16[8,128,128]{2,1,0:T(8,128)(2,1)S(1)} %collective-permute-done.3.refs_2_, ...), custom_call_target="tpu_custom_call" | custom-call | flops 268435456 | bytes 4194304 | tf_op jit(solution)/shard_map/fold_early/pallas_call | solution.py:39
  26.1 4.3 %collective-permute-done.6.refs_1_ = bf16[8,128,128]{2,1,0:T(8,128)(2,1)S(1)} collective-permute-done((bf16[8,128,128]{2,1,0:T(8,128)(2,1)S(1)}, bf16[8,128,128]{2,1,0:T(8,128)(2,1)S(1)}, u32[]{:S(2)}, u32[]{:S(2)}) %collective-permute-start.6) | collective-permute-done | bytes 262176 | tf_op jit(solution)/shard_map/ppermute | solution.py:366
  30.4 2.2 %collective-permute-start.7 = (bf16[4,128,128]{2,1,0:T(8,128)(2,1)S(1)}, bf16[4,128,128]{2,1,0:T(8,128)(2,1)S(1)}, u32[]{:S(2)}, u32[]{:S(2)}) collective-permute-start(bf16[4,128,128]{2,1,0:T(8,128)(2,1)S(1)} %slice.7), channel_id=1, source_target_pairs={{2,0},{0,4},{4,8},{8,12},{12,14},{14,10},{10,6},{6,2},{3,1},{1,5},... | collective-permute-start | bytes 393224 | tf_op jit(solution)/shard_map/ppermute | solution.py:366
  32.8 1.4 %fold_late.1 = (f32[128,256]{1,0:T(8,128)S(1)}, f32[64,128,128]{2,1,0:T(8,128)S(1)}) custom-call(bf16[8,128,128]{2,1,0:T(8,128)(2,1)S(1)} %collective-permute-done.2.refs_0_, bf16[8,128,128]{2,1,0:T(8,128)(2,1)S(1)} %collective-permute-done.6.refs_1_, s32[128,128]{1,0:T(8,128)S(1)} %get-tuple-element.57.refs_5_.refs_2_, bf16[256,8192]{1,0:T(8,128)(2,1)S(1)} %bitcast.17, ...), custom_call_target="tpu_custom_call" | custom-call | flops 134217728 | bytes 1048576 | tf_op jit(solution)/shard_map/fold_late/pallas_call | solution.py:39
  34.3 2.2 %collective-permute-done.7.refs_1_ = bf16[4,128,128]{2,1,0:T(8,128)(2,1)S(1)} collective-permute-done((bf16[4,128,128]{2,1,0:T(8,128)(2,1)S(1)}, bf16[4,128,128]{2,1,0:T(8,128)(2,1)S(1)}, u32[]{:S(2)}, u32[]{:S(2)}) %collective-permute-start.7) | collective-permute-done | bytes 131104 | tf_op jit(solution)/shard_map/ppermute | solution.py:366
  36.4 1.9 %collective-permute-done.5.refs_0_ = bf16[4,128,128]{2,1,0:T(8,128)(2,1)S(1)} collective-permute-done((bf16[4,128,128]{2,1,0:T(8,128)(2,1)S(1)}, bf16[4,128,128]{2,1,0:T(8,128)(2,1)S(1)}, u32[]{:S(2)}, u32[]{:S(2)}) %collective-permute-start.5) | collective-permute-done | bytes 131104 | tf_op jit(solution)/shard_map/ppermute | solution.py:366
  38.3 1.4 %finish.1 = (bf16[128,256]{1,0:T(8,128)(2,1)S(1)}, f32[8,128,128]{2,1,0:T(8,128)S(1)}, bf16[4,128,128]{2,1,0:T(8,128)(2,1)S(1)}, bf16[4,128,128]{2,1,0:T(8,128)(2,1)S(1)}) custom-call(bf16[4,128,128]{2,1,0:T(8,128)(2,1)S(1)} %collective-permute-done.5.refs_0_, bf16[4,128,128]{2,1,0:T(8,128)(2,1)S(1)} %collective-permute-done.7.refs_1_, ...), custom_call_target="tpu_custom_call" | custom-call | flops 268435456 | bytes 2097152 | tf_op jit(solution)/shard_map/finish/pallas_call | solution.py:39
  40.1 1.8 %collective-permute-start.8 = (bf16[4,128,128]{2,1,0:T(8,128)(2,1)S(1)}, bf16[4,128,128]{2,1,0:T(8,128)(2,1)S(1)}, u32[]{:S(2)}, u32[]{:S(2)}) collective-permute-start(bf16[4,128,128]{2,1,0:T(8,128)(2,1)S(1)} %get-tuple-element.77), channel_id=1, source_target_pairs={{2,0},{0,4},{4,8},{8,12},{12,14},{14,10},{10,6},{6,2},{3,1},{1,5},... | collective-permute-start | bytes 393224 | tf_op jit(solution)/shard_map/ppermute | solution.py:366
  41.9 1.3 %part.4 = (f32[8,128,128]{2,1,0:T(8,128)S(1)}, f32[8,128,128]{2,1,0:T(8,128)S(1)}) custom-call(bf16[128,256]{1,0:T(8,128)(2,1)S(1)} %get-tuple-element.88.refs_0_, bf16[256,8192]{1,0:T(8,128)(2,1)S(1)} %bitcast.12, f32[64,128,128]{2,1,0:T(8,128)S(1)} %get-tuple-element.67.refs_10_.refs_2_, f32[8,128,128]{2,1,0:T(8,128)S(1)} %get-tuple-element.72.refs_3_, ...), custom_call_target="tpu_custom_call" | custom-call | flops 67108864 | bytes 1048576 | tf_op jit(solution)/shard_map/part/pallas_call | solution.py:39
  43.2 2.2 %collective-permute-done.11 = bf16[4,128,128]{2,1,0:T(8,128)(2,1)S(1)} collective-permute-done((bf16[4,128,128]{2,1,0:T(8,128)(2,1)S(1)}, bf16[4,128,128]{2,1,0:T(8,128)(2,1)S(1)}, u32[]{:S(2)}, u32[]{:S(2)}) %collective-permute-start.11) | collective-permute-done | bytes 131104 | tf_op jit(solution)/shard_map/ppermute | solution.py:366
  45.7 2.2 %collective-permute-start.9 = (bf16[8,128,128]{2,1,0:T(8,128)(2,1)S(1)}, bf16[8,128,128]{2,1,0:T(8,128)(2,1)S(1)}, u32[]{:S(2)}, u32[]{:S(2)}) collective-permute-start(bf16[8,128,128]{2,1,0:T(8,128)(2,1)S(1)} %add_convert_fusion.5), channel_id=1, source_target_pairs={{2,0},{0,4},{4,8},{8,12},{12,14},{14,10},{10,6},{6,2},{3,1},{1,5},... | collective-permute-start | bytes 786440 | tf_op jit(solution)/shard_map/ppermute | solution.py:366
  47.8 1.3 %part.5 = (f32[8,128,128]{2,1,0:T(8,128)S(1)}, f32[8,128,128]{2,1,0:T(8,128)S(1)}) custom-call(bf16[128,256]{1,0:T(8,128)(2,1)S(1)} %get-tuple-element.88.refs_0_, bf16[256,8192]{1,0:T(8,128)(2,1)S(1)} %bitcast.13, f32[64,128,128]{2,1,0:T(8,128)S(1)} %get-tuple-element.67.refs_10_.refs_2_, f32[8,128,128]{2,1,0:T(8,128)S(1)} %get-tuple-element.72.refs_3_, ...), custom_call_target="tpu_custom_call" | custom-call | flops 67108864 | bytes 1048576 | tf_op jit(solution)/shard_map/part/pallas_call | solution.py:39
  49.2 5.2 %collective-permute-done.12 = bf16[8,128,128]{2,1,0:T(8,128)(2,1)S(1)} collective-permute-done((bf16[8,128,128]{2,1,0:T(8,128)(2,1)S(1)}, bf16[8,128,128]{2,1,0:T(8,128)(2,1)S(1)}, u32[]{:S(2)}, u32[]{:S(2)}) %collective-permute-start.12) | collective-permute-done | bytes 262176 | tf_op jit(solution)/shard_map/ppermute | solution.py:366
  54.9 1.8 %collective-permute-start.10 = (bf16[8,128,128]{2,1,0:T(8,128)(2,1)S(1)}, bf16[8,128,128]{2,1,0:T(8,128)(2,1)S(1)}, u32[]{:S(2)}, u32[]{:S(2)}) collective-permute-start(bf16[8,128,128]{2,1,0:T(8,128)(2,1)S(1)} %add_convert_fusion.4), channel_id=1, source_target_pairs={{2,0},{0,4},{4,8},{8,12},{12,14},{14,10},{10,6},{6,2},{3,1},{1,5},... | collective-permute-start | bytes 786440 | tf_op jit(solution)/shard_map/ppermute | solution.py:366
  56.7 2.5 %dense.10 = (f32[128,1024]{1,0:T(8,128)S(1)}, f32[128,1024]{1,0:T(8,128)S(1)}) custom-call(bf16[8,128,128]{2,1,0:T(8,128)(2,1)S(1)} %copy-done.3, bf16[1024,8192]{1,0:T(8,128)(2,1)} %refs_1_.11, f32[128,1024]{1,0:T(8,128)S(1)} %get-tuple-element.70.refs_2_, f32[128,1024]{1,0:T(8,128)S(1)} %get-tuple-element.84.refs_3_), custom_call_target="tpu_custom_call" | custom-call | flops 536870912 | bytes 4194304 | tf_op jit(solution)/shard_map/dense/pallas_call | solution.py:39
  59.2 1.3 %part.6 = (f32[8,128,128]{2,1,0:T(8,128)S(1)}, f32[8,128,128]{2,1,0:T(8,128)S(1)}) custom-call(bf16[128,256]{1,0:T(8,128)(2,1)S(1)} %get-tuple-element.88.refs_0_, bf16[256,8192]{1,0:T(8,128)(2,1)S(1)} %bitcast.14, f32[64,128,128]{2,1,0:T(8,128)S(1)} %get-tuple-element.67.refs_10_.refs_2_, f32[8,128,128]{2,1,0:T(8,128)S(1)} %get-tuple-element.72.refs_3_, ...), custom_call_target="tpu_custom_call" | custom-call | flops 67108864 | bytes 1048576 | tf_op jit(solution)/shard_map/part/pallas_call | solution.py:39
  60.5 2.1 %collective-permute-done.13 = bf16[8,128,128]{2,1,0:T(8,128)(2,1)S(1)} collective-permute-done((bf16[8,128,128]{2,1,0:T(8,128)(2,1)S(1)}, bf16[8,128,128]{2,1,0:T(8,128)(2,1)S(1)}, u32[]{:S(2)}, u32[]{:S(2)}) %collective-permute-start.13) | collective-permute-done | bytes 262176 | tf_op jit(solution)/shard_map/ppermute | solution.py:366
  62.7 0.5 collective-permute-start.14
  63.3 1.6 %collective-permute-start.15 = (bf16[8,128,128]{2,1,0:T(8,128)(2,1)S(1)}, bf16[8,128,128]{2,1,0:T(8,128)(2,1)S(1)}, u32[]{:S(2)}, u32[]{:S(2)}) collective-permute-start(bf16[8,128,128]{2,1,0:T(8,128)(2,1)S(1)} %add_convert_fusion.3), channel_id=1, source_target_pairs={{2,0},{0,4},{4,8},{8,12},{12,14},{14,10},{10,6},{6,2},{3,1},{1,5},... | collective-permute-start | bytes 786440 | tf_op jit(solution)/shard_map/ppermute | solution.py:366
  64.9 1.9 %dense.11.refs_7_ = f32[128,1024]{1,0:T(8,128)S(1)} custom-call(bf16[8,128,128]{2,1,0:T(8,128)(2,1)S(1)} %copy-done.3, bf16[1024,8192]{1,0:T(8,128)(2,1)} %refs_1_.11), custom_call_target="tpu_custom_call" | custom-call | flops 268435456 | bytes 2097152 | tf_op jit(solution)/shard_map/dense/pallas_call | solution.py:39
  66.8 1.0 %part.7.own_ref = f32[8,128,128]{2,1,0:T(8,128)S(1)} custom-call(bf16[128,256]{1,0:T(8,128)(2,1)S(1)} %get-tuple-element.88.refs_0_, bf16[256,8192]{1,0:T(8,128)(2,1)S(1)} %bitcast.15, f32[64,128,128]{2,1,0:T(8,128)S(1)} %get-tuple-element.67.refs_10_.refs_2_, f32[8,128,128]{2,1,0:T(8,128)S(1)} %get-tuple-element.72.refs_3_, f32[4,16]{1,0:T(4,128)S(1)} %copy-done.4, ...), custom_call_target="tpu_custom_call" | custom-call | flops 67108864 | bytes 1048576 | tf_op jit(solution)/shard_map/part/pallas_call | solution.py:39
  67.8 2.6 %collective-permute-done.14.refs_0_ = bf16[8,128,128]{2,1,0:T(8,128)(2,1)S(1)} collective-permute-done((bf16[8,128,128]{2,1,0:T(8,128)(2,1)S(1)}, bf16[8,128,128]{2,1,0:T(8,128)(2,1)S(1)}, u32[]{:S(2)}, u32[]{:S(2)}) %collective-permute-start.14) | collective-permute-done | bytes 262176 | tf_op jit(solution)/shard_map/ppermute | solution.py:366
  70.8 0.8 %sum_up.1 = bf16[128,1024]{1,0:T(8,128)(2,1)} custom-call(f32[8,128,128]{2,1,0:T(8,128)S(1)} %part.7.own_ref, bf16[8,128,128]{2,1,0:T(8,128)(2,1)S(1)} %collective-permute-done.14.refs_0_, bf16[8,128,128]{2,1,0:T(8,128)(2,1)S(1)} %collective-permute-done.15.refs_1_), custom_call_target="tpu_custom_call" | custom-call | flops 1 | bytes 1 | tf_op jit(solution)/shard_map/sum_up/pallas_call | solution.py:39
  (41 shorter events, 2.5 us)
Async XLA Ops:
  4.7 1.0 %copy-start.3 = (bf16[8,128,128]{2,1,0:T(8,128)(2,1)S(1)}, bf16[8,128,128]{2,1,0:T(8,128)(2,1)}, u32[]{:S(2)}) copy-start(bf16[8,128,128]{2,1,0:T(8,128)(2,1)} %attend.1.refs_0_) | copy-start | bytes 786436
  5.7 7.5 %collective-permute-start.3 = (bf16[8,128,128]{2,1,0:T(8,128)(2,1)S(1)}, bf16[8,128,128]{2,1,0:T(8,128)(2,1)S(1)}, u32[]{:S(2)}, u32[]{:S(2)}) collective-permute-start(bf16[8,128,128]{2,1,0:T(8,128)(2,1)S(1)} %copy-done.3), channel_id=1, source_target_pairs={{2,0},{0,4},{4,8},{8,12},{12,14},{14,10},{10,6},{6,2},{3,1},{1,5},... | collective-permute-start | bytes 786440 | tf_op jit(solution)/shard_map/ppermute | solution.py:366
  8.8 7.1 %collective-permute-start = (bf16[8,128,128]{2,1,0:T(8,128)(2,1)S(1)}, bf16[8,128,128]{2,1,0:T(8,128)(2,1)S(1)}, u32[]{:S(2)}, u32[]{:S(2)}) collective-permute-start(bf16[8,128,128]{2,1,0:T(8,128)(2,1)S(1)} %copy-done.3), channel_id=1, source_target_pairs={{4,0},{8,4},{12,8},{14,12},{10,14},{6,10},{2,6},{0,2},{5,1},{9,5},... | collective-permute-start | bytes 786440 | tf_op jit(solution)/shard_map/ppermute | solution.py:366
  8.8 7.1 %copy-start.6 = (s32[4,16,1]{1,2,0:T(1,128)S(1)}, s32[4,16,1]{1,2,0:T(1,128)}, u32[]{:S(2)}) copy-start(s32[4,16,1]{1,2,0:T(1,128)} %param.28) | copy-start | bytes 772
  8.8 7.1 %copy-start.7 = (s32[128]{0:T(128)S(1)}, s32[128]{0:T(128)}, u32[]{:S(2)}) copy-start(s32[128]{0:T(128)} %param.21) | copy-start | bytes 1540
  8.8 7.1 %copy-start.8 = (s32[32]{0:T(128)S(1)}, s32[32]{0:T(128)}, u32[]{:S(2)}) copy-start(s32[32]{0:T(128)} %refs_3_.1) | copy-start | bytes 388
  13.3 7.9 %collective-permute-start.4 = (bf16[8,128,128]{2,1,0:T(8,128)(2,1)S(1)}, bf16[8,128,128]{2,1,0:T(8,128)(2,1)S(1)}, u32[]{:S(2)}, u32[]{:S(2)}) collective-permute-start(bf16[8,128,128]{2,1,0:T(8,128)(2,1)S(1)} %collective-permute-done.3.refs_2_), channel_id=1, source_target_pairs={{2,0},{0,4},{4,8},{8,12},{12,14},{14,10},{10,6},{6,2},{3,1},{1,5},... | collective-permute-start | bytes 786440 | tf_op jit(solution)/shard_map/ppermute | solution.py:366
  15.9 7.9 %collective-permute-start.1 = (bf16[8,128,128]{2,1,0:T(8,128)(2,1)S(1)}, bf16[8,128,128]{2,1,0:T(8,128)(2,1)S(1)}, u32[]{:S(2)}, u32[]{:S(2)}) collective-permute-start(bf16[8,128,128]{2,1,0:T(8,128)(2,1)S(1)} %collective-permute-done.refs_1_), channel_id=1, source_target_pairs={{4,0},{8,4},{12,8},{14,12},{10,14},{6,10},{2,6},{0,2},{5,1},{9,5},... | collective-permute-start | bytes 786440 | tf_op jit(solution)/shard_map/ppermute | solution.py:366
  15.9 7.9 %copy-start.1 = (bf16[4,8192,64]{1,2,0:T(8,128)(2,1)S(1)}, bf16[4,8192,64]{1,2,0:T(8,128)(2,1)}, u32[]{:S(2)}) copy-start(bf16[4,8192,64]{1,2,0:T(8,128)(2,1)} %param.24) | copy-start | bytes 12582916
  15.9 7.9 %copy-start.2 = (bf16[4,16,128,128]{3,2,1,0:T(8,128)(2,1)S(1)}, bf16[4,16,128,128]{3,2,1,0:T(8,128)(2,1)}, u32[]{:S(2)}) copy-start(bf16[4,16,128,128]{3,2,1,0:T(8,128)(2,1)} %refs_4_.7) | copy-start | bytes 6291460
  16.0 7.9 %copy-start.4 = (f32[4,16]{1,0:T(4,128)S(1)}, f32[4,16]{1,0:T(4,128)}, u32[]{:S(2)}) copy-start(f32[4,16]{1,0:T(4,128)} %refs_4_.11) | copy-start | bytes 772
  16.0 7.9 %copy-start.5 = (s32[4,16]{1,0:T(4,128)S(1)}, s32[4,16]{1,0:T(4,128)}, u32[]{:S(2)}) copy-start(s32[4,16]{1,0:T(4,128)} %refs_5_.11) | copy-start | bytes 772
  21.1 9.2 %collective-permute-start.6 = (bf16[8,128,128]{2,1,0:T(8,128)(2,1)S(1)}, bf16[8,128,128]{2,1,0:T(8,128)(2,1)S(1)}, u32[]{:S(2)}, u32[]{:S(2)}) collective-permute-start(bf16[8,128,128]{2,1,0:T(8,128)(2,1)S(1)} %collective-permute-done.4.refs_4_), channel_id=1, source_target_pairs={{2,0},{0,4},{4,8},{8,12},{12,14},{14,10},{10,6},{6,2},{3,1},{1,5},... | collective-permute-start | bytes 786440 | tf_op jit(solution)/shard_map/ppermute | solution.py:366
  23.8 8.9 %collective-permute-start.2 = (bf16[8,128,128]{2,1,0:T(8,128)(2,1)S(1)}, bf16[8,128,128]{2,1,0:T(8,128)(2,1)S(1)}, u32[]{:S(2)}, u32[]{:S(2)}) collective-permute-start(bf16[8,128,128]{2,1,0:T(8,128)(2,1)S(1)} %collective-permute-done.1.refs_3_), channel_id=1, source_target_pairs={{4,0},{8,4},{12,8},{14,12},{10,14},{6,10},{2,6},{0,2},{5,1},{9,5},... | collective-permute-start | bytes 786440 | tf_op jit(solution)/shard_map/ppermute | solution.py:366
  30.4 6.1 %collective-permute-start.7 = (bf16[4,128,128]{2,1,0:T(8,128)(2,1)S(1)}, bf16[4,128,128]{2,1,0:T(8,128)(2,1)S(1)}, u32[]{:S(2)}, u32[]{:S(2)}) collective-permute-start(bf16[4,128,128]{2,1,0:T(8,128)(2,1)S(1)} %slice.7), channel_id=1, source_target_pairs={{2,0},{0,4},{4,8},{8,12},{12,14},{14,10},{10,6},{6,2},{3,1},{1,5},... | collective-permute-start | bytes 393224 | tf_op jit(solution)/shard_map/ppermute | solution.py:366
  32.7 5.6 %collective-permute-start.5 = (bf16[4,128,128]{2,1,0:T(8,128)(2,1)S(1)}, bf16[4,128,128]{2,1,0:T(8,128)(2,1)S(1)}, u32[]{:S(2)}, u32[]{:S(2)}) collective-permute-start(bf16[4,128,128]{2,1,0:T(8,128)(2,1)S(1)} %slice.6), channel_id=1, source_target_pairs={{4,0},{8,4},{12,8},{14,12},{10,14},{6,10},{2,6},{0,2},{5,1},{9,5},... | collective-permute-start | bytes 393224 | tf_op jit(solution)/shard_map/ppermute | solution.py:366
  32.8 5.6 %copy-start = (bf16[4,64,8192]{2,1,0:T(8,128)(2,1)S(1)}, bf16[4,64,8192]{2,1,0:T(8,128)(2,1)}, u32[]{:S(2)}) copy-start(bf16[4,64,8192]{2,1,0:T(8,128)(2,1)} %param.25) | copy-start | bytes 12582916
  39.8 5.6 %collective-permute-start.11 = (bf16[4,128,128]{2,1,0:T(8,128)(2,1)S(1)}, bf16[4,128,128]{2,1,0:T(8,128)(2,1)S(1)}, u32[]{:S(2)}, u32[]{:S(2)}) collective-permute-start(bf16[4,128,128]{2,1,0:T(8,128)(2,1)S(1)} %get-tuple-element.94), channel_id=1, source_target_pairs={{4,0},{8,4},{12,8},{14,12},{10,14},{6,10},{2,6},{0,2},{5,1},{9,5},... | collective-permute-start | bytes 393224 | tf_op jit(solution)/shard_map/ppermute | solution.py:366
  40.1 5.5 %collective-permute-start.8 = (bf16[4,128,128]{2,1,0:T(8,128)(2,1)S(1)}, bf16[4,128,128]{2,1,0:T(8,128)(2,1)S(1)}, u32[]{:S(2)}, u32[]{:S(2)}) collective-permute-start(bf16[4,128,128]{2,1,0:T(8,128)(2,1)S(1)} %get-tuple-element.77), channel_id=1, source_target_pairs={{2,0},{0,4},{4,8},{8,12},{12,14},{14,10},{10,6},{6,2},{3,1},{1,5},... | collective-permute-start | bytes 393224 | tf_op jit(solution)/shard_map/ppermute | solution.py:366
  45.4 9.0 %collective-permute-start.12 = (bf16[8,128,128]{2,1,0:T(8,128)(2,1)S(1)}, bf16[8,128,128]{2,1,0:T(8,128)(2,1)S(1)}, u32[]{:S(2)}, u32[]{:S(2)}) collective-permute-start(bf16[8,128,128]{2,1,0:T(8,128)(2,1)S(1)} %add_convert_fusion.2), channel_id=1, source_target_pairs={{4,0},{8,4},{12,8},{14,12},{10,14},{6,10},{2,6},{0,2},{5,1},{9,5},... | collective-permute-start | bytes 786440 | tf_op jit(solution)/shard_map/ppermute | solution.py:366
  45.7 9.2 %collective-permute-start.9 = (bf16[8,128,128]{2,1,0:T(8,128)(2,1)S(1)}, bf16[8,128,128]{2,1,0:T(8,128)(2,1)S(1)}, u32[]{:S(2)}, u32[]{:S(2)}) collective-permute-start(bf16[8,128,128]{2,1,0:T(8,128)(2,1)S(1)} %add_convert_fusion.5), channel_id=1, source_target_pairs={{2,0},{0,4},{4,8},{8,12},{12,14},{14,10},{10,6},{6,2},{3,1},{1,5},... | collective-permute-start | bytes 786440 | tf_op jit(solution)/shard_map/ppermute | solution.py:366
  54.5 8.2 %collective-permute-start.13 = (bf16[8,128,128]{2,1,0:T(8,128)(2,1)S(1)}, bf16[8,128,128]{2,1,0:T(8,128)(2,1)S(1)}, u32[]{:S(2)}, u32[]{:S(2)}) collective-permute-start(bf16[8,128,128]{2,1,0:T(8,128)(2,1)S(1)} %add_convert_fusion.1), channel_id=1, source_target_pairs={{4,0},{8,4},{12,8},{14,12},{10,14},{6,10},{2,6},{0,2},{5,1},{9,5},... | collective-permute-start | bytes 786440 | tf_op jit(solution)/shard_map/ppermute | solution.py:366
  54.9 8.3 %collective-permute-start.10 = (bf16[8,128,128]{2,1,0:T(8,128)(2,1)S(1)}, bf16[8,128,128]{2,1,0:T(8,128)(2,1)S(1)}, u32[]{:S(2)}, u32[]{:S(2)}) collective-permute-start(bf16[8,128,128]{2,1,0:T(8,128)(2,1)S(1)} %add_convert_fusion.4), channel_id=1, source_target_pairs={{2,0},{0,4},{4,8},{8,12},{12,14},{14,10},{10,6},{6,2},{3,1},{1,5},... | collective-permute-start | bytes 786440 | tf_op jit(solution)/shard_map/ppermute | solution.py:366
  62.7 7.7 %collective-permute-start.14 = (bf16[8,128,128]{2,1,0:T(8,128)(2,1)S(1)}, bf16[8,128,128]{2,1,0:T(8,128)(2,1)S(1)}, u32[]{:S(2)}, u32[]{:S(2)}) collective-permute-start(bf16[8,128,128]{2,1,0:T(8,128)(2,1)S(1)} %add_convert_fusion), channel_id=1, source_target_pairs={{4,0},{8,4},{12,8},{14,12},{10,14},{6,10},{2,6},{0,2},{5,1},{9,5},... | collective-permute-start | bytes 786440 | tf_op jit(solution)/shard_map/ppermute | solution.py:366
  63.3 7.5 %collective-permute-start.15 = (bf16[8,128,128]{2,1,0:T(8,128)(2,1)S(1)}, bf16[8,128,128]{2,1,0:T(8,128)(2,1)S(1)}, u32[]{:S(2)}, u32[]{:S(2)}) collective-permute-start(bf16[8,128,128]{2,1,0:T(8,128)(2,1)S(1)} %add_convert_fusion.3), channel_id=1, source_target_pairs={{2,0},{0,4},{4,8},{8,12},{12,14},{14,10},{10,6},{6,2},{3,1},{1,5},... | collective-permute-start | bytes 786440 | tf_op jit(solution)/shard_map/ppermute | solution.py:366

commit v10 on v9

--- a/solution.py
+++ b/solution.py
@@ -104,32 +104,37 @@
             out_ref[h, here, :] = attended[h * ROW_BLOCK : (h + 1) * ROW_BLOCK]
 
 
-def dense_kernel(distances, count, listing, turn, *refs):
-    x_ref, weight_ref = refs[:2]
-    outs = refs[-2 - 2 * listing - len(distances) : -2 - 2 * listing]
-    buffers, sems = refs[-2:]
+def dense_kernel(distances, count, listing, turn, kept, *refs):
+    x_hbm, weight_ref = refs[:2]
+    outs = refs[-4 - 2 * listing - len(distances) : -4 - 2 * listing]
+    x_ref, buffers, sems, x_sem = refs[-4:]
     heads, rows, side = x_ref.shape
     width = heads * side
     depth = buffers.shape[0]
     piece = buffers.shape[2]
     cuts = width // piece
-    total = len(distances) * cuts
-
-    def fetch(i):
-        start = pl.multiple_of(owner_at(distances[i // cuts], count) * width, width) + i % cuts * piece
-        return pltpu.make_async_copy(
-            weight_ref.at[:, pl.ds(pl.multiple_of(start, piece), piece)],
-            buffers.at[i % depth],
-            sems.at[i % depth],
-        )
-
-    def compute():
-        for i in range(min(depth, total)):
+
+    def compute(first):
+        total = len(distances) * cuts
+
+        def fetch(i):
+            owner = owner_at(distances[i // cuts], count)
+            start = pl.multiple_of(owner * width, width) + i % cuts * piece
+            return pltpu.make_async_copy(
+                weight_ref.at[:, pl.ds(pl.multiple_of(start, piece), piece)],
+                buffers.at[i % depth],
+                sems.at[i % depth],
+            )
+
+        own = pltpu.make_async_copy(x_hbm, x_ref, x_sem)
+        own.start()
+        for i in range(first * cuts, min(first * cuts + depth, total)):
             fetch(i).start()
         if listing:
-            list_blocks(refs[2], refs[3], refs[4], refs[-4], refs[-3])
+            list_blocks(refs[2], refs[3], refs[4], refs[-6], refs[-5])
+        own.wait()
         x = jnp.concatenate([x_ref[h] for h in range(heads)], axis=1)
-        for i in range(total):
+        for i in range(first * cuts, total):
             fetch(i).wait()
             outs[i // cuts][:, i % cuts * piece : (i % cuts + 1) * piece] = jnp.dot(
                 x, buffers[i % depth], preferred_element_type=F32
@@ -138,17 +143,18 @@
                 fetch(i + depth).start()
 
     if turn is None:
-        compute()
+        compute(0)
         return
     here = lax.axis_index("rep") == turn
-    pl.when(here)(compute)
-    handed = refs[2 : -2 - len(distances)]
-    if handed:
-
-        @pl.when(jnp.logical_not(here))
-        def _():
-            for source, target in zip(handed, outs):
-                target[...] = source[...]
+    pl.when(here)(functools.partial(compute, 0))
+
+    @pl.when(jnp.logical_not(here))
+    def _():
+        handed = refs[2 : -4 - len(distances)]
+        for source, target in zip(handed, outs):
+            target[...] = source[...]
+        if kept < len(distances):
+            compute(kept)
 
 
 def list_blocks(variant_ref, holder_ref, owner_ref, slot_ref, table_ref):
@@ -344,18 +350,19 @@
     piece = width // 2 if width >= 512 else width
     dense = {}
 
-    def dense_for(distances, x, listing=False, turn=None, handed=()):
+    def dense_for(distances, x, listing=False, turn=None, handed=(), kept=0, limit=40):
         extra_shapes = [shape((rows, rows), jnp.int32), shape((count * slots * CAP,), jnp.int32)]
         extra_ins = (request_variant[None, :], holder_slot, block_owner[:, :, 0])
         got = call(
-            functools.partial(dense_kernel, distances, count, listing, turn),
+            functools.partial(dense_kernel, distances, count, listing, turn, kept),
             "dense",
             [shape((rows, width), F32)] * len(distances) + extra_shapes * listing,
             (x, out_weight) + extra_ins * listing + tuple(handed),
-            [VMEM, ANY] + [VMEM, SMEM, SMEM] * listing + [VMEM] * len(handed),
+            [ANY, ANY] + [VMEM, SMEM, SMEM] * listing + [VMEM] * len(handed),
             [VMEM] * len(distances) + [VMEM, SMEM] * listing,
-            [pltpu.VMEM((4, width, piece), BF16), pltpu.SemaphoreType.DMA((4,))],
-            limit=40,
+            [pltpu.VMEM((heads, rows, side), BF16), pltpu.VMEM((4, width, piece), BF16),
+             pltpu.SemaphoreType.DMA((4,)), pltpu.SemaphoreType.DMA],
+            limit=limit,
             flops=2 * rows * width * width * len(distances),
             moved=2 * width * width * len(distances),
         )
@@ -367,11 +374,11 @@
             value, "tp", [(ring[(i + distance) % count], ring[i]) for i in range(count)]
         )
 
-    begun = dense_for(wanted[:3], attended, turn=1)
+    begun = dense_for(wanted[:1], attended, turn=0, kept=1, limit=60)
     attended = after(attended, begun[0])
     chunks = {0: attended}
     chunks[1], chunks[count - 1] = come(attended, 1), come(attended, -1)
-    (token, *_) = dense_for(wanted[:3], attended, turn=0, handed=begun)
+    (token, *_) = dense_for(wanted[:3], attended, turn=1, handed=begun, kept=1)
     for step in range(2, half):
         right, left = after(chunks[step - 1], token), after(chunks[count - step + 1], token)
         chunks[step], chunks[count - step] = come(right, 1), come(left, -1)
@@ -455,7 +462,8 @@
             total = total + value
         return total.astype(BF16)
 
-    begun = dense_for(wanted[5:-1], after(attended, low), turn=1)
+    near = wanted[5:-1]
+    begun = dense_for(near, after(attended, low), turn=1, kept=len(near))
     front, back = after(front, begun[0]), after(back, begun[0])
     left, right = (come(front, 1), 0), (come(back, -1), 1)
     parts_for([half - 1, half + 1], after(low, begun[0]), F32)
@@ -466,7 +474,7 @@
         kept = after(low, right)
         parts_for([nearer, count - nearer] if nearer else [0], kept, F32)
         if distance == half - 1:
-            dense_for(wanted[5:-1], after(attended, right), turn=0, handed=begun)
+            dense_for(near, after(attended, right), turn=0, handed=begun, kept=len(near))
         if distance == half - 2:
             dense_for([0], after(attended, right))
         left, right = (come(left, 1), None), (come(right, -1), None)

time: 71.8 us -> 70.9 us (0.987)
  waiting for transfers between devices: 24.4 us -> 22.1 us
  Pallas kernels: 27.3 us -> 29.3 us
  starting transfers between devices: 18.4 us -> 17.5 us
    ppermute x16, waiting for transfers between devices: 24.4 us -> 22.1 us  [come(): lax.ppermute(value, 'tp', [(ring[(i + distance) % count], ring[i]) for i...]
    pallas_call x15, Pallas kernels: 27.3 us -> 29.3 us  [call(): pl.pallas_call(kernel, out_shape=outs, in_specs=specs, out_specs=out_spec...]
    ppermute x16, starting transfers between devices: 18.4 us -> 17.5 us  [come(): lax.ppermute(value, 'tp', [(ring[(i + distance) % count], ring[i]) for i...]
  transfers between devices with their start and end apart: 16 -> 16, of which waited for: 15 -> 16; matrix products, arithmetic and copies ran while one was open for 0% -> 0% of each run, Pallas kernels for 28% -> 28%
where the time goes in v10:
time: 70.9 us; the launch traced here: 70.6 us
  Pallas kernels  29.3 us (41%)
  waiting for transfers between devices  22.1 us (31%)
  starting transfers between devices  17.5 us (25%)
  local copies, waits for them, and re-layouts  1.12 us (2%)
    pallas_call x15, Pallas kernels, call(): pl.pallas_call(kernel, out_shape=outs, in_specs=specs, out_specs=out_spec...  29.3 us
    ppermute x16, waiting for transfers between devices, come(): lax.ppermute(value, 'tp', [(ring[(i + distance) % count], ring[i]) for i...  22.1 us
    ppermute x16, starting transfers between devices, come(): lax.ppermute(value, 'tp', [(ring[(i + distance) % count], ring[i]) for i...  17.5 us
  transfers between devices with their start and end apart: 16, of which 16 were waited for; matrix products, arithmetic and copies ran while one was open for 0% of the time, Pallas kernels for 28%

profile of v10, /device:TPU:0, one launch (start us, length us, event | category | flops | bytes accessed | tf_op | source)
XLA Modules:
  0.0 70.6 jit_solution(2796664165955883425)
XLA Ops:
  0.0 4.7 %attend.1.refs_0_ = bf16[8,128,128]{2,1,0:T(8,128)(2,1)} custom-call(bf16[128,1024]{1,0:T(8,128)(2,1)} %query_hbm.1, bf16[4096,128]{1,0:T(8,128)(2,1)} %bitcast.21, bf16[4096,128]{1,0:T(8,128)(2,1)} %bitcast.22, bf16[128,128]{1,0:T(8,128)(2,1)} %bitcast.23, bf16[128,128]{1,0:T(8,128)(2,1)} %bitcast.24, s32[1,128]{1,0:T(1,128)} %bitcast.25), custom_call_target="tpu_custom_call" | custom-call | tf_op jit(solution)/shard_map/attend/pallas_call | solution.py:39
  4.8 2.8 %dense.6.refs_2_ = f32[128,1024]{1,0:T(8,128)} custom-call(bf16[8,128,128]{2,1,0:T(8,128)(2,1)} %attend.1.refs_0_, bf16[1024,8192]{1,0:T(8,128)(2,1)} %refs_1_.11), custom_call_target="tpu_custom_call" | custom-call | flops 268435456 | bytes 2097152 | tf_op jit(solution)/shard_map/dense/pallas_call | solution.py:39
  7.6 3.1 %collective-permute-start.3 = (bf16[8,128,128]{2,1,0:T(8,128)(2,1)S(1)}, bf16[8,128,128]{2,1,0:T(8,128)(2,1)S(1)}, u32[]{:S(2)}, u32[]{:S(2)}) collective-permute-start(bf16[8,128,128]{2,1,0:T(8,128)(2,1)S(1)} %copy-done.3), channel_id=1, source_target_pairs={{2,0},{0,4},{4,8},{8,12},{12,14},{14,10},{10,6},{6,2},{3,1},{1,5},... | collective-permute-start | bytes 786440 | tf_op jit(solution)/shard_map/ppermute | solution.py:373
  10.7 1.0 %copy-done.4 = f32[128,1024]{1,0:T(8,128)S(1)} copy-done((f32[128,1024]{1,0:T(8,128)S(1)}, f32[128,1024]{1,0:T(8,128)}, u32[]{:S(2)}) %copy-start.4) | copy-done | bytes 524312
  11.8 2.6 %dense.7 = (f32[128,1024]{1,0:T(8,128)S(1)}, f32[128,1024]{1,0:T(8,128)S(1)}, f32[128,1024]{1,0:T(8,128)S(1)}) custom-call(bf16[8,128,128]{2,1,0:T(8,128)(2,1)S(1)} %copy-done.3, bf16[1024,8192]{1,0:T(8,128)(2,1)} %refs_1_.11, f32[128,1024]{1,0:T(8,128)S(1)} %copy-done.4), custom_call_target="tpu_custom_call" | custom-call | flops 805306368 | bytes 6291456 | tf_op jit(solution)/shard_map/dense/pallas_call | solution.py:39
  15.0 2.1 %collective-permute-start.4 = (bf16[8,128,128]{2,1,0:T(8,128)(2,1)S(1)}, bf16[8,128,128]{2,1,0:T(8,128)(2,1)S(1)}, u32[]{:S(2)}, u32[]{:S(2)}) collective-permute-start(bf16[8,128,128]{2,1,0:T(8,128)(2,1)S(1)} %collective-permute-done.3.refs_2_), channel_id=1, source_target_pairs={{2,0},{0,4},{4,8},{8,12},{12,14},{14,10},{10,6},{6,2},{3,1},{1,5},... | collective-permute-start | bytes 786440 | tf_op jit(solution)/shard_map/ppermute | solution.py:373
  17.2 3.8 %dense.8 = (f32[128,1024]{1,0:T(8,128)S(1)}, f32[128,1024]{1,0:T(8,128)S(1)}, s32[128,128]{1,0:T(8,128)S(1)}, s32[64]{0:T(128)S(1)}) custom-call(bf16[8,128,128]{2,1,0:T(8,128)(2,1)S(1)} %copy-done.3, bf16[1024,8192]{1,0:T(8,128)(2,1)} %refs_1_.11, s32[1,128]{1,0:T(1,128)S(1)} %bitcast.20, s32[32]{0:T(128)S(1)} %copy-done.9, s32[4,16]{1,0:T(4,128)S(1)} %bitcast.19), custom_call_target="tpu_custom_call" | custom-call | flops 536870912 | bytes 4194304 | tf_op jit(solution)/shard_map/dense/pallas_call | solution.py:39
  21.0 0.8 %collective-permute-done.4.refs_4_ = bf16[8,128,128]{2,1,0:T(8,128)(2,1)S(1)} collective-permute-done((bf16[8,128,128]{2,1,0:T(8,128)(2,1)S(1)}, bf16[8,128,128]{2,1,0:T(8,128)(2,1)S(1)}, u32[]{:S(2)}, u32[]{:S(2)}) %collective-permute-start.4) | collective-permute-done | bytes 262176 | tf_op jit(solution)/shard_map/ppermute | solution.py:373
  21.9 2.4 %collective-permute-start.6 = (bf16[8,128,128]{2,1,0:T(8,128)(2,1)S(1)}, bf16[8,128,128]{2,1,0:T(8,128)(2,1)S(1)}, u32[]{:S(2)}, u32[]{:S(2)}) collective-permute-start(bf16[8,128,128]{2,1,0:T(8,128)(2,1)S(1)} %collective-permute-done.4.refs_4_), channel_id=1, source_target_pairs={{2,0},{0,4},{4,8},{8,12},{12,14},{14,10},{10,6},{6,2},{3,1},{1,5},... | collective-permute-start | bytes 786440 | tf_op jit(solution)/shard_map/ppermute | solution.py:373
  24.4 2.2 %fold_early.1 = (f32[128,256]{1,0:T(8,128)S(1)}, f32[64,128,128]{2,1,0:T(8,128)S(1)}) custom-call(bf16[8,128,128]{2,1,0:T(8,128)(2,1)S(1)} %copy-done.3, bf16[8,128,128]{2,1,0:T(8,128)(2,1)S(1)} %collective-permute-done.refs_1_, bf16[8,128,128]{2,1,0:T(8,128)(2,1)S(1)} %collective-permute-done.3.refs_2_, ...), custom_call_target="tpu_custom_call" | custom-call | flops 268435456 | bytes 4194304 | tf_op jit(solution)/shard_map/fold_early/pallas_call | solution.py:39
  26.6 3.3 %collective-permute-done.6.refs_1_ = bf16[8,128,128]{2,1,0:T(8,128)(2,1)S(1)} collective-permute-done((bf16[8,128,128]{2,1,0:T(8,128)(2,1)S(1)}, bf16[8,128,128]{2,1,0:T(8,128)(2,1)S(1)}, u32[]{:S(2)}, u32[]{:S(2)}) %collective-permute-start.6) | collective-permute-done | bytes 262176 | tf_op jit(solution)/shard_map/ppermute | solution.py:373
  30.0 2.1 %collective-permute-start.7 = (bf16[4,128,128]{2,1,0:T(8,128)(2,1)S(1)}, bf16[4,128,128]{2,1,0:T(8,128)(2,1)S(1)}, u32[]{:S(2)}, u32[]{:S(2)}) collective-permute-start(bf16[4,128,128]{2,1,0:T(8,128)(2,1)S(1)} %slice.7), channel_id=1, source_target_pairs={{2,0},{0,4},{4,8},{8,12},{12,14},{14,10},{10,6},{6,2},{3,1},{1,5},... | collective-permute-start | bytes 393224 | tf_op jit(solution)/shard_map/ppermute | solution.py:373
  32.3 1.5 %fold_late.1 = (f32[128,256]{1,0:T(8,128)S(1)}, f32[64,128,128]{2,1,0:T(8,128)S(1)}) custom-call(bf16[8,128,128]{2,1,0:T(8,128)(2,1)S(1)} %collective-permute-done.2.refs_0_, bf16[8,128,128]{2,1,0:T(8,128)(2,1)S(1)} %collective-permute-done.6.refs_1_, s32[128,128]{1,0:T(8,128)S(1)} %get-tuple-element.51.refs_5_.refs_2_, bf16[256,8192]{1,0:T(8,128)(2,1)S(1)} %bitcast.17, ...), custom_call_target="tpu_custom_call" | custom-call | flops 134217728 | bytes 1048576 | tf_op jit(solution)/shard_map/fold_late/pallas_call | solution.py:39
  33.7 1.3 %collective-permute-done.7.refs_1_ = bf16[4,128,128]{2,1,0:T(8,128)(2,1)S(1)} collective-permute-done((bf16[4,128,128]{2,1,0:T(8,128)(2,1)S(1)}, bf16[4,128,128]{2,1,0:T(8,128)(2,1)S(1)}, u32[]{:S(2)}, u32[]{:S(2)}) %collective-permute-start.7) | collective-permute-done | bytes 131104 | tf_op jit(solution)/shard_map/ppermute | solution.py:373
  35.0 2.2 %collective-permute-done.5.refs_0_ = bf16[4,128,128]{2,1,0:T(8,128)(2,1)S(1)} collective-permute-done((bf16[4,128,128]{2,1,0:T(8,128)(2,1)S(1)}, bf16[4,128,128]{2,1,0:T(8,128)(2,1)S(1)}, u32[]{:S(2)}, u32[]{:S(2)}) %collective-permute-start.5) | collective-permute-done | bytes 131104 | tf_op jit(solution)/shard_map/ppermute | solution.py:373
  37.2 1.4 %finish.1 = (bf16[128,256]{1,0:T(8,128)(2,1)S(1)}, f32[8,128,128]{2,1,0:T(8,128)S(1)}, bf16[4,128,128]{2,1,0:T(8,128)(2,1)S(1)}, bf16[4,128,128]{2,1,0:T(8,128)(2,1)S(1)}) custom-call(bf16[4,128,128]{2,1,0:T(8,128)(2,1)S(1)} %collective-permute-done.5.refs_0_, bf16[4,128,128]{2,1,0:T(8,128)(2,1)S(1)} %collective-permute-done.7.refs_1_, ...), custom_call_target="tpu_custom_call" | custom-call | flops 268435456 | bytes 2097152 | tf_op jit(solution)/shard_map/finish/pallas_call | solution.py:39
  38.8 2.0 %collective-permute-start.8 = (bf16[4,128,128]{2,1,0:T(8,128)(2,1)S(1)}, bf16[4,128,128]{2,1,0:T(8,128)(2,1)S(1)}, u32[]{:S(2)}, u32[]{:S(2)}) collective-permute-start(bf16[4,128,128]{2,1,0:T(8,128)(2,1)S(1)} %get-tuple-element.71), channel_id=1, source_target_pairs={{2,0},{0,4},{4,8},{8,12},{12,14},{14,10},{10,6},{6,2},{3,1},{1,5},... | collective-permute-start | bytes 393224 | tf_op jit(solution)/shard_map/ppermute | solution.py:373
  40.8 1.3 %part.4 = (f32[8,128,128]{2,1,0:T(8,128)S(1)}, f32[8,128,128]{2,1,0:T(8,128)S(1)}) custom-call(bf16[128,256]{1,0:T(8,128)(2,1)S(1)} %get-tuple-element.82.refs_0_, bf16[256,8192]{1,0:T(8,128)(2,1)S(1)} %bitcast.12, f32[64,128,128]{2,1,0:T(8,128)S(1)} %get-tuple-element.61.refs_10_.refs_2_, f32[8,128,128]{2,1,0:T(8,128)S(1)} %get-tuple-element.66.refs_3_, ...), custom_call_target="tpu_custom_call" | custom-call | flops 67108864 | bytes 1048576 | tf_op jit(solution)/shard_map/part/pallas_call | solution.py:39
  42.1 2.7 %collective-permute-done.11 = bf16[4,128,128]{2,1,0:T(8,128)(2,1)S(1)} collective-permute-done((bf16[4,128,128]{2,1,0:T(8,128)(2,1)S(1)}, bf16[4,128,128]{2,1,0:T(8,128)(2,1)S(1)}, u32[]{:S(2)}, u32[]{:S(2)}) %collective-permute-start.11) | collective-permute-done | bytes 131104 | tf_op jit(solution)/shard_map/ppermute | solution.py:373
  45.2 1.9 %collective-permute-start.9 = (bf16[8,128,128]{2,1,0:T(8,128)(2,1)S(1)}, bf16[8,128,128]{2,1,0:T(8,128)(2,1)S(1)}, u32[]{:S(2)}, u32[]{:S(2)}) collective-permute-start(bf16[8,128,128]{2,1,0:T(8,128)(2,1)S(1)} %add_convert_fusion.5), channel_id=1, source_target_pairs={{2,0},{0,4},{4,8},{8,12},{12,14},{14,10},{10,6},{6,2},{3,1},{1,5},... | collective-permute-start | bytes 786440 | tf_op jit(solution)/shard_map/ppermute | solution.py:373
  47.1 1.3 %part.5 = (f32[8,128,128]{2,1,0:T(8,128)S(1)}, f32[8,128,128]{2,1,0:T(8,128)S(1)}) custom-call(bf16[128,256]{1,0:T(8,128)(2,1)S(1)} %get-tuple-element.82.refs_0_, bf16[256,8192]{1,0:T(8,128)(2,1)S(1)} %bitcast.13, f32[64,128,128]{2,1,0:T(8,128)S(1)} %get-tuple-element.61.refs_10_.refs_2_, f32[8,128,128]{2,1,0:T(8,128)S(1)} %get-tuple-element.66.refs_3_, ...), custom_call_target="tpu_custom_call" | custom-call | flops 67108864 | bytes 1048576 | tf_op jit(solution)/shard_map/part/pallas_call | solution.py:39
  48.4 5.1 %collective-permute-done.12 = bf16[8,128,128]{2,1,0:T(8,128)(2,1)S(1)} collective-permute-done((bf16[8,128,128]{2,1,0:T(8,128)(2,1)S(1)}, bf16[8,128,128]{2,1,0:T(8,128)(2,1)S(1)}, u32[]{:S(2)}, u32[]{:S(2)}) %collective-permute-start.12) | collective-permute-done | bytes 262176 | tf_op jit(solution)/shard_map/ppermute | solution.py:373
  54.4 1.7 %collective-permute-start.10 = (bf16[8,128,128]{2,1,0:T(8,128)(2,1)S(1)}, bf16[8,128,128]{2,1,0:T(8,128)(2,1)S(1)}, u32[]{:S(2)}, u32[]{:S(2)}) collective-permute-start(bf16[8,128,128]{2,1,0:T(8,128)(2,1)S(1)} %add_convert_fusion.4), channel_id=1, source_target_pairs={{2,0},{0,4},{4,8},{8,12},{12,14},{14,10},{10,6},{6,2},{3,1},{1,5},... | collective-permute-start | bytes 786440 | tf_op jit(solution)/shard_map/ppermute | solution.py:373
  56.0 2.6 %dense.10 = (f32[128,1024]{1,0:T(8,128)S(1)}, f32[128,1024]{1,0:T(8,128)S(1)}) custom-call(bf16[8,128,128]{2,1,0:T(8,128)(2,1)S(1)} %copy-done.3, bf16[1024,8192]{1,0:T(8,128)(2,1)} %refs_1_.11, f32[128,1024]{1,0:T(8,128)S(1)} %get-tuple-element.64.refs_2_, f32[128,1024]{1,0:T(8,128)S(1)} %get-tuple-element.78.refs_3_), custom_call_target="tpu_custom_call" | custom-call | flops 536870912 | bytes 4194304 | tf_op jit(solution)/shard_map/dense/pallas_call | solution.py:39
  58.6 1.3 %part.6 = (f32[8,128,128]{2,1,0:T(8,128)S(1)}, f32[8,128,128]{2,1,0:T(8,128)S(1)}) custom-call(bf16[128,256]{1,0:T(8,128)(2,1)S(1)} %get-tuple-element.82.refs_0_, bf16[256,8192]{1,0:T(8,128)(2,1)S(1)} %bitcast.14, f32[64,128,128]{2,1,0:T(8,128)S(1)} %get-tuple-element.61.refs_10_.refs_2_, f32[8,128,128]{2,1,0:T(8,128)S(1)} %get-tuple-element.66.refs_3_, ...), custom_call_target="tpu_custom_call" | custom-call | flops 67108864 | bytes 1048576 | tf_op jit(solution)/shard_map/part/pallas_call | solution.py:39
  60.0 2.5 %collective-permute-done.13 = bf16[8,128,128]{2,1,0:T(8,128)(2,1)S(1)} collective-permute-done((bf16[8,128,128]{2,1,0:T(8,128)(2,1)S(1)}, bf16[8,128,128]{2,1,0:T(8,128)(2,1)S(1)}, u32[]{:S(2)}, u32[]{:S(2)}) %collective-permute-start.13) | collective-permute-done | bytes 262176 | tf_op jit(solution)/shard_map/ppermute | solution.py:373
  63.4 1.4 %collective-permute-start.15 = (bf16[8,128,128]{2,1,0:T(8,128)(2,1)S(1)}, bf16[8,128,128]{2,1,0:T(8,128)(2,1)S(1)}, u32[]{:S(2)}, u32[]{:S(2)}) collective-permute-start(bf16[8,128,128]{2,1,0:T(8,128)(2,1)S(1)} %add_convert_fusion.3), channel_id=1, source_target_pairs={{2,0},{0,4},{4,8},{8,12},{12,14},{14,10},{10,6},{6,2},{3,1},{1,5},... | collective-permute-start | bytes 786440 | tf_op jit(solution)/shard_map/ppermute | solution.py:373
  64.8 1.9 %dense.11.refs_7_ = f32[128,1024]{1,0:T(8,128)S(1)} custom-call(bf16[8,128,128]{2,1,0:T(8,128)(2,1)S(1)} %copy-done.3, bf16[1024,8192]{1,0:T(8,128)(2,1)} %refs_1_.11), custom_call_target="tpu_custom_call" | custom-call | flops 268435456 | bytes 2097152 | tf_op jit(solution)/shard_map/dense/pallas_call | solution.py:39
  66.7 1.0 %part.7.own_ref = f32[8,128,128]{2,1,0:T(8,128)S(1)} custom-call(bf16[128,256]{1,0:T(8,128)(2,1)S(1)} %get-tuple-element.82.refs_0_, bf16[256,8192]{1,0:T(8,128)(2,1)S(1)} %bitcast.15, f32[64,128,128]{2,1,0:T(8,128)S(1)} %get-tuple-element.61.refs_10_.refs_2_, f32[8,128,128]{2,1,0:T(8,128)S(1)} %get-tuple-element.66.refs_3_, f32[4,16]{1,0:T(4,128)S(1)} %copy-done.5, ...), custom_call_target="tpu_custom_call" | custom-call | flops 67108864 | bytes 1048576 | tf_op jit(solution)/shard_map/part/pallas_call | solution.py:39
  67.7 1.3 %collective-permute-done.14.refs_0_ = bf16[8,128,128]{2,1,0:T(8,128)(2,1)S(1)} collective-permute-done((bf16[8,128,128]{2,1,0:T(8,128)(2,1)S(1)}, bf16[8,128,128]{2,1,0:T(8,128)(2,1)S(1)}, u32[]{:S(2)}, u32[]{:S(2)}) %collective-permute-start.14) | collective-permute-done | bytes 262176 | tf_op jit(solution)/shard_map/ppermute | solution.py:373
  69.0 0.8 %collective-permute-done.15.refs_1_ = bf16[8,128,128]{2,1,0:T(8,128)(2,1)S(1)} collective-permute-done((bf16[8,128,128]{2,1,0:T(8,128)(2,1)S(1)}, bf16[8,128,128]{2,1,0:T(8,128)(2,1)S(1)}, u32[]{:S(2)}, u32[]{:S(2)}) %collective-permute-start.15) | collective-permute-done | bytes 262176 | tf_op jit(solution)/shard_map/ppermute | solution.py:373
  69.8 0.8 %sum_up.1 = bf16[128,1024]{1,0:T(8,128)(2,1)} custom-call(f32[8,128,128]{2,1,0:T(8,128)S(1)} %part.7.own_ref, bf16[8,128,128]{2,1,0:T(8,128)(2,1)S(1)} %collective-permute-done.14.refs_0_, bf16[8,128,128]{2,1,0:T(8,128)(2,1)S(1)} %collective-permute-done.15.refs_1_), custom_call_target="tpu_custom_call" | custom-call | flops 1 | bytes 1 | tf_op jit(solution)/shard_map/sum_up/pallas_call | solution.py:39
  (43 shorter events, 3.3 us)
Async XLA Ops:
  4.7 2.9 %copy-start.3 = (bf16[8,128,128]{2,1,0:T(8,128)(2,1)S(1)}, bf16[8,128,128]{2,1,0:T(8,128)(2,1)}, u32[]{:S(2)}) copy-start(bf16[8,128,128]{2,1,0:T(8,128)(2,1)} %attend.1.refs_0_) | copy-start | bytes 786436
  4.7 12.4 %copy-start.7 = (s32[4,16,1]{1,2,0:T(1,128)S(1)}, s32[4,16,1]{1,2,0:T(1,128)}, u32[]{:S(2)}) copy-start(s32[4,16,1]{1,2,0:T(1,128)} %param.28) | copy-start | bytes 772
  4.8 12.4 %copy-start.8 = (s32[128]{0:T(128)S(1)}, s32[128]{0:T(128)}, u32[]{:S(2)}) copy-start(s32[128]{0:T(128)} %param.21) | copy-start | bytes 1540
  4.8 12.4 %copy-start.9 = (s32[32]{0:T(128)S(1)}, s32[32]{0:T(128)}, u32[]{:S(2)}) copy-start(s32[32]{0:T(128)} %refs_3_.1) | copy-start | bytes 388
  7.6 7.4 %collective-permute-start.3 = (bf16[8,128,128]{2,1,0:T(8,128)(2,1)S(1)}, bf16[8,128,128]{2,1,0:T(8,128)(2,1)S(1)}, u32[]{:S(2)}, u32[]{:S(2)}) collective-permute-start(bf16[8,128,128]{2,1,0:T(8,128)(2,1)S(1)} %copy-done.3), channel_id=1, source_target_pairs={{2,0},{0,4},{4,8},{8,12},{12,14},{14,10},{10,6},{6,2},{3,1},{1,5},... | collective-permute-start | bytes 786440 | tf_op jit(solution)/shard_map/ppermute | solution.py:373
  10.7 6.5 %collective-permute-start = (bf16[8,128,128]{2,1,0:T(8,128)(2,1)S(1)}, bf16[8,128,128]{2,1,0:T(8,128)(2,1)S(1)}, u32[]{:S(2)}, u32[]{:S(2)}) collective-permute-start(bf16[8,128,128]{2,1,0:T(8,128)(2,1)S(1)} %copy-done.3), channel_id=1, source_target_pairs={{4,0},{8,4},{12,8},{14,12},{10,14},{6,10},{2,6},{0,2},{5,1},{9,5},... | collective-permute-start | bytes 786440 | tf_op jit(solution)/shard_map/ppermute | solution.py:373
  10.7 1.0 %copy-start.4 = (f32[128,1024]{1,0:T(8,128)S(1)}, f32[128,1024]{1,0:T(8,128)}, u32[]{:S(2)}) copy-start(f32[128,1024]{1,0:T(8,128)} %dense.6.refs_2_) | copy-start | bytes 1572868
  15.0 6.8 %collective-permute-start.4 = (bf16[8,128,128]{2,1,0:T(8,128)(2,1)S(1)}, bf16[8,128,128]{2,1,0:T(8,128)(2,1)S(1)}, u32[]{:S(2)}, u32[]{:S(2)}) collective-permute-start(bf16[8,128,128]{2,1,0:T(8,128)(2,1)S(1)} %collective-permute-done.3.refs_2_), channel_id=1, source_target_pairs={{2,0},{0,4},{4,8},{8,12},{12,14},{14,10},{10,6},{6,2},{3,1},{1,5},... | collective-permute-start | bytes 786440 | tf_op jit(solution)/shard_map/ppermute | solution.py:373
  17.2 7.2 %collective-permute-start.1 = (bf16[8,128,128]{2,1,0:T(8,128)(2,1)S(1)}, bf16[8,128,128]{2,1,0:T(8,128)(2,1)S(1)}, u32[]{:S(2)}, u32[]{:S(2)}) collective-permute-start(bf16[8,128,128]{2,1,0:T(8,128)(2,1)S(1)} %collective-permute-done.refs_1_), channel_id=1, source_target_pairs={{4,0},{8,4},{12,8},{14,12},{10,14},{6,10},{2,6},{0,2},{5,1},{9,5},... | collective-permute-start | bytes 786440 | tf_op jit(solution)/shard_map/ppermute | solution.py:373
  17.2 7.2 %copy-start.1 = (bf16[4,8192,64]{1,2,0:T(8,128)(2,1)S(1)}, bf16[4,8192,64]{1,2,0:T(8,128)(2,1)}, u32[]{:S(2)}) copy-start(bf16[4,8192,64]{1,2,0:T(8,128)(2,1)} %param.24) | copy-start | bytes 12582916
  17.2 7.2 %copy-start.2 = (bf16[4,16,128,128]{3,2,1,0:T(8,128)(2,1)S(1)}, bf16[4,16,128,128]{3,2,1,0:T(8,128)(2,1)}, u32[]{:S(2)}) copy-start(bf16[4,16,128,128]{3,2,1,0:T(8,128)(2,1)} %refs_4_.7) | copy-start | bytes 6291460
  17.2 7.2 %copy-start.5 = (f32[4,16]{1,0:T(4,128)S(1)}, f32[4,16]{1,0:T(4,128)}, u32[]{:S(2)}) copy-start(f32[4,16]{1,0:T(4,128)} %refs_4_.11) | copy-start | bytes 772
  17.2 7.2 %copy-start.6 = (s32[4,16]{1,0:T(4,128)S(1)}, s32[4,16]{1,0:T(4,128)}, u32[]{:S(2)}) copy-start(s32[4,16]{1,0:T(4,128)} %refs_5_.11) | copy-start | bytes 772
  21.9 8.1 %collective-permute-start.6 = (bf16[8,128,128]{2,1,0:T(8,128)(2,1)S(1)}, bf16[8,128,128]{2,1,0:T(8,128)(2,1)S(1)}, u32[]{:S(2)}, u32[]{:S(2)}) collective-permute-start(bf16[8,128,128]{2,1,0:T(8,128)(2,1)S(1)} %collective-permute-done.4.refs_4_), channel_id=1, source_target_pairs={{2,0},{0,4},{4,8},{8,12},{12,14},{14,10},{10,6},{6,2},{3,1},{1,5},... | collective-permute-start | bytes 786440 | tf_op jit(solution)/shard_map/ppermute | solution.py:373
  24.4 7.8 %collective-permute-start.2 = (bf16[8,128,128]{2,1,0:T(8,128)(2,1)S(1)}, bf16[8,128,128]{2,1,0:T(8,128)(2,1)S(1)}, u32[]{:S(2)}, u32[]{:S(2)}) collective-permute-start(bf16[8,128,128]{2,1,0:T(8,128)(2,1)S(1)} %collective-permute-done.1.refs_3_), channel_id=1, source_target_pairs={{4,0},{8,4},{12,8},{14,12},{10,14},{6,10},{2,6},{0,2},{5,1},{9,5},... | collective-permute-start | bytes 786440 | tf_op jit(solution)/shard_map/ppermute | solution.py:373
  30.0 5.0 %collective-permute-start.7 = (bf16[4,128,128]{2,1,0:T(8,128)(2,1)S(1)}, bf16[4,128,128]{2,1,0:T(8,128)(2,1)S(1)}, u32[]{:S(2)}, u32[]{:S(2)}) collective-permute-start(bf16[4,128,128]{2,1,0:T(8,128)(2,1)S(1)} %slice.7), channel_id=1, source_target_pairs={{2,0},{0,4},{4,8},{8,12},{12,14},{14,10},{10,6},{6,2},{3,1},{1,5},... | collective-permute-start | bytes 393224 | tf_op jit(solution)/shard_map/ppermute | solution.py:373
  32.2 5.0 %collective-permute-start.5 = (bf16[4,128,128]{2,1,0:T(8,128)(2,1)S(1)}, bf16[4,128,128]{2,1,0:T(8,128)(2,1)S(1)}, u32[]{:S(2)}, u32[]{:S(2)}) collective-permute-start(bf16[4,128,128]{2,1,0:T(8,128)(2,1)S(1)} %slice.6), channel_id=1, source_target_pairs={{4,0},{8,4},{12,8},{14,12},{10,14},{6,10},{2,6},{0,2},{5,1},{9,5},... | collective-permute-start | bytes 393224 | tf_op jit(solution)/shard_map/ppermute | solution.py:373
  32.3 5.0 %copy-start = (bf16[4,64,8192]{2,1,0:T(8,128)(2,1)S(1)}, bf16[4,64,8192]{2,1,0:T(8,128)(2,1)}, u32[]{:S(2)}) copy-start(bf16[4,64,8192]{2,1,0:T(8,128)(2,1)} %param.25) | copy-start | bytes 12582916
  38.7 6.1 %collective-permute-start.11 = (bf16[4,128,128]{2,1,0:T(8,128)(2,1)S(1)}, bf16[4,128,128]{2,1,0:T(8,128)(2,1)S(1)}, u32[]{:S(2)}, u32[]{:S(2)}) collective-permute-start(bf16[4,128,128]{2,1,0:T(8,128)(2,1)S(1)} %get-tuple-element.88), channel_id=1, source_target_pairs={{4,0},{8,4},{12,8},{14,12},{10,14},{6,10},{2,6},{0,2},{5,1},{9,5},... | collective-permute-start | bytes 393224 | tf_op jit(solution)/shard_map/ppermute | solution.py:373
  38.8 6.4 %collective-permute-start.8 = (bf16[4,128,128]{2,1,0:T(8,128)(2,1)S(1)}, bf16[4,128,128]{2,1,0:T(8,128)(2,1)S(1)}, u32[]{:S(2)}, u32[]{:S(2)}) collective-permute-start(bf16[4,128,128]{2,1,0:T(8,128)(2,1)S(1)} %get-tuple-element.71), channel_id=1, source_target_pairs={{2,0},{0,4},{4,8},{8,12},{12,14},{14,10},{10,6},{6,2},{3,1},{1,5},... | collective-permute-start | bytes 393224 | tf_op jit(solution)/shard_map/ppermute | solution.py:373
  44.8 8.7 %collective-permute-start.12 = (bf16[8,128,128]{2,1,0:T(8,128)(2,1)S(1)}, bf16[8,128,128]{2,1,0:T(8,128)(2,1)S(1)}, u32[]{:S(2)}, u32[]{:S(2)}) collective-permute-start(bf16[8,128,128]{2,1,0:T(8,128)(2,1)S(1)} %add_convert_fusion.2), channel_id=1, source_target_pairs={{4,0},{8,4},{12,8},{14,12},{10,14},{6,10},{2,6},{0,2},{5,1},{9,5},... | collective-permute-start | bytes 786440 | tf_op jit(solution)/shard_map/ppermute | solution.py:373
  45.2 9.2 %collective-permute-start.9 = (bf16[8,128,128]{2,1,0:T(8,128)(2,1)S(1)}, bf16[8,128,128]{2,1,0:T(8,128)(2,1)S(1)}, u32[]{:S(2)}, u32[]{:S(2)}) collective-permute-start(bf16[8,128,128]{2,1,0:T(8,128)(2,1)S(1)} %add_convert_fusion.5), channel_id=1, source_target_pairs={{2,0},{0,4},{4,8},{8,12},{12,14},{14,10},{10,6},{6,2},{3,1},{1,5},... | collective-permute-start | bytes 786440 | tf_op jit(solution)/shard_map/ppermute | solution.py:373
  53.6 8.9 %collective-permute-start.13 = (bf16[8,128,128]{2,1,0:T(8,128)(2,1)S(1)}, bf16[8,128,128]{2,1,0:T(8,128)(2,1)S(1)}, u32[]{:S(2)}, u32[]{:S(2)}) collective-permute-start(bf16[8,128,128]{2,1,0:T(8,128)(2,1)S(1)} %add_convert_fusion.1), channel_id=1, source_target_pairs={{4,0},{8,4},{12,8},{14,12},{10,14},{6,10},{2,6},{0,2},{5,1},{9,5},... | collective-permute-start | bytes 786440 | tf_op jit(solution)/shard_map/ppermute | solution.py:373
  54.4 8.9 %collective-permute-start.10 = (bf16[8,128,128]{2,1,0:T(8,128)(2,1)S(1)}, bf16[8,128,128]{2,1,0:T(8,128)(2,1)S(1)}, u32[]{:S(2)}, u32[]{:S(2)}) collective-permute-start(bf16[8,128,128]{2,1,0:T(8,128)(2,1)S(1)} %add_convert_fusion.4), channel_id=1, source_target_pairs={{2,0},{0,4},{4,8},{8,12},{12,14},{14,10},{10,6},{6,2},{3,1},{1,5},... | collective-permute-start | bytes 786440 | tf_op jit(solution)/shard_map/ppermute | solution.py:373
  62.6 6.4 %collective-permute-start.14 = (bf16[8,128,128]{2,1,0:T(8,128)(2,1)S(1)}, bf16[8,128,128]{2,1,0:T(8,128)(2,1)S(1)}, u32[]{:S(2)}, u32[]{:S(2)}) collective-permute-start(bf16[8,128,128]{2,1,0:T(8,128)(2,1)S(1)} %add_convert_fusion), channel_id=1, source_target_pairs={{4,0},{8,4},{12,8},{14,12},{10,14},{6,10},{2,6},{0,2},{5,1},{9,5},... | collective-permute-start | bytes 786440 | tf_op jit(solution)/shard_map/ppermute | solution.py:373
  63.4 6.4 %collective-permute-start.15 = (bf16[8,128,128]{2,1,0:T(8,128)(2,1)S(1)}, bf16[8,128,128]{2,1,0:T(8,128)(2,1)S(1)}, u32[]{:S(2)}, u32[]{:S(2)}) collective-permute-start(bf16[8,128,128]{2,1,0:T(8,128)(2,1)S(1)} %add_convert_fusion.3), channel_id=1, source_target_pairs={{2,0},{0,4},{4,8},{8,12},{12,14},{14,10},{10,6},{6,2},{3,1},{1,5},... | collective-permute-start | bytes 786440 | tf_op jit(solution)/shard_map/ppermute | solution.py:373

commit v11 on v9

--- a/solution.py
+++ b/solution.py
@@ -104,7 +104,7 @@
             out_ref[h, here, :] = attended[h * ROW_BLOCK : (h + 1) * ROW_BLOCK]
 
 
-def dense_kernel(distances, count, listing, turn, *refs):
+def dense_kernel(distances, count, listing, *refs):
     x_ref, weight_ref = refs[:2]
     outs = refs[-2 - 2 * listing - len(distances) : -2 - 2 * listing]
     buffers, sems = refs[-2:]
@@ -123,32 +123,18 @@
             sems.at[i % depth],
         )
 
-    def compute():
-        for i in range(min(depth, total)):
-            fetch(i).start()
-        if listing:
-            list_blocks(refs[2], refs[3], refs[4], refs[-4], refs[-3])
-        x = jnp.concatenate([x_ref[h] for h in range(heads)], axis=1)
-        for i in range(total):
-            fetch(i).wait()
-            outs[i // cuts][:, i % cuts * piece : (i % cuts + 1) * piece] = jnp.dot(
-                x, buffers[i % depth], preferred_element_type=F32
-            )
-            if i + depth < total:
-                fetch(i + depth).start()
-
-    if turn is None:
-        compute()
-        return
-    here = lax.axis_index("rep") == turn
-    pl.when(here)(compute)
-    handed = refs[2 : -2 - len(distances)]
-    if handed:
-
-        @pl.when(jnp.logical_not(here))
-        def _():
-            for source, target in zip(handed, outs):
-                target[...] = source[...]
+    for i in range(min(depth, total)):
+        fetch(i).start()
+    if listing:
+        list_blocks(refs[2], refs[3], refs[4], refs[-4], refs[-3])
+    x = jnp.concatenate([x_ref[h] for h in range(heads)], axis=1)
+    for i in range(total):
+        fetch(i).wait()
+        outs[i // cuts][:, i % cuts * piece : (i % cuts + 1) * piece] = jnp.dot(
+            x, buffers[i % depth], preferred_element_type=F32
+        )
+        if i + depth < total:
+            fetch(i + depth).start()
 
 
 def list_blocks(variant_ref, holder_ref, owner_ref, slot_ref, table_ref):
@@ -268,13 +254,13 @@
         part_for(distance, count, low_out, second_ref, dense_ref, block_ref, extra_out, columns,
                  total.at[n])
         for i in range(2 * half):
-            tile = total[n, :, i * side : (i + 1) * side].astype(BF16)
+            tile = total[n, :, i * side : (i + 1) * side]
             if n:
-                outs[n - 1][i] = tile
+                outs[2 * n - 2 + i // half][i % half] = tile
             elif i < half:
-                front_out[i] = tile
+                front_out[i] = tile.astype(BF16)
             else:
-                back_out[i - half] = tile
+                back_out[i - half] = tile.astype(BF16)
 
 
 def part_kernel(distances, count, slots, *refs):
@@ -289,16 +275,16 @@
         part_for(distance, count, low_ref, second_ref, dense_ref, block_ref, extra_ref, columns,
                  total.at[n])
         for i in range(heads):
-            outs[n][i] = total[n, :, i * side : (i + 1) * side].astype(outs[n].dtype)
-
-
-def sum_kernel(own_ref, *refs):
+            outs[2 * n + 2 * i // heads][i % (heads // 2)] = total[n, :, i * side : (i + 1) * side]
+
+
+def sum_kernel(*refs):
     out_ref = refs[-1]
-    heads, _, side = own_ref.shape
-    for i in range(heads):
-        total = own_ref[i]
-        for ref in refs[:-1]:
-            total = total + ref[i].astype(F32)
+    half, _, side = refs[0].shape
+    for i in range(2 * half):
+        total = refs[i // half][i % half]
+        for ref in refs[2 + i // half : -1 : 2]:
+            total = total + ref[i % half].astype(F32)
         out_ref[:, i * side : (i + 1) * side] = total.astype(BF16)
 
 
@@ -344,15 +330,15 @@
     piece = width // 2 if width >= 512 else width
     dense = {}
 
-    def dense_for(distances, x, listing=False, turn=None, handed=()):
+    def dense_for(distances, x, listing=False):
         extra_shapes = [shape((rows, rows), jnp.int32), shape((count * slots * CAP,), jnp.int32)]
         extra_ins = (request_variant[None, :], holder_slot, block_owner[:, :, 0])
         got = call(
-            functools.partial(dense_kernel, distances, count, listing, turn),
+            functools.partial(dense_kernel, distances, count, listing),
             "dense",
             [shape((rows, width), F32)] * len(distances) + extra_shapes * listing,
-            (x, out_weight) + extra_ins * listing + tuple(handed),
-            [VMEM, ANY] + [VMEM, SMEM, SMEM] * listing + [VMEM] * len(handed),
+            (x, out_weight) + extra_ins * listing,
+            [VMEM, ANY] + [VMEM, SMEM, SMEM] * listing,
             [VMEM] * len(distances) + [VMEM, SMEM] * listing,
             [pltpu.VMEM((4, width, piece), BF16), pltpu.SemaphoreType.DMA((4,))],
             limit=40,
@@ -367,11 +353,9 @@
             value, "tp", [(ring[(i + distance) % count], ring[i]) for i in range(count)]
         )
 
-    begun = dense_for(wanted[:3], attended, turn=1)
-    attended = after(attended, begun[0])
     chunks = {0: attended}
     chunks[1], chunks[count - 1] = come(attended, 1), come(attended, -1)
-    (token, *_) = dense_for(wanted[:3], attended, turn=0, handed=begun)
+    (token, *_) = dense_for(wanted[:3], attended)
     for step in range(2, half):
         right, left = after(chunks[step - 1], token), after(chunks[count - step + 1], token)
         chunks[step], chunks[count - step] = come(right, 1), come(left, -1)
@@ -412,71 +396,69 @@
         moved=MIB,
     )
     extras = shape((slots * CAP, rows, side), F32)
-    first = wanted[:1]
-    travelling = shape((heads, rows, side), BF16)
+    first = wanted[:3]
+    part_half = shape((heads // 2, rows, side), F32)
     low, extra, front, back, *sums = call(
         functools.partial(finish_kernel, first, count),
         "finish",
         [shape((rows, low_width), BF16), extras]
         + [shape((heads // 2, rows, side), BF16)] * 2
-        + [travelling] * (len(first) - 1),
+        + [part_half] * (2 * len(first) - 2),
         (front, back, *tables, second, low, blocks, *[dense[d] for d in first]),
         [VMEM] * 2 + table_specs + [VMEM] * (3 + len(first)),
-        [VMEM] * (3 + len(first)),
+        [VMEM] * (2 + 2 * len(first)),
         [pltpu.VMEM((heads, rows, side), BF16), pltpu.VMEM((rows, low_width), F32),
          pltpu.VMEM((len(first), rows, width), F32)],
         flops=rows * low_width * width * 8,
         moved=2 * MIB,
     )
-    parts = dict(zip(first[1:], sums))
-
-    def parts_for(distances, low, kind):
+    parts = {d: sums[2 * n : 2 * n + 2] for n, d in enumerate(first[1:])}
+
+    def parts_for(distances, low):
         got = call(
             functools.partial(part_kernel, distances, count, slots),
             "part",
-            [shape((heads, rows, side), kind)] * len(distances),
+            [part_half] * (2 * len(distances)),
             (low, second, blocks, extra, block_scale, block_cell, table,
              *[dense[distance] for distance in distances]),
             [VMEM] * 4 + [SMEM] * 3 + [VMEM] * len(distances),
-            [VMEM] * len(distances),
+            [VMEM] * (2 * len(distances)),
             [pltpu.VMEM((len(distances), rows, width), F32)],
             flops=rows * low_width * width * 2,
             moved=MIB,
         )
-        parts.update(zip(distances, got))
-
-    def joined(part, *came):
-        total = part.astype(F32)
-        for value, place in came:
-            value = value.astype(F32)
-            if place is not None:
-                none = jnp.zeros_like(value)
-                value = jnp.concatenate([none, value] if place else [value, none], axis=0)
-            total = total + value
-        return total.astype(BF16)
-
-    begun = dense_for(wanted[5:-1], after(attended, low), turn=1)
-    front, back = after(front, begun[0]), after(back, begun[0])
-    left, right = (come(front, 1), 0), (come(back, -1), 1)
-    parts_for([half - 1, half + 1], after(low, begun[0]), F32)
-    for distance in range(half - 1, 0, -1):
-        left = joined(parts[count - distance], left)
-        right = joined(parts[distance], right)
+        parts.update((d, got[2 * n : 2 * n + 2]) for n, d in enumerate(distances))
+
+    def joined(part, came):
+        return (part if came is None else part + came.astype(F32)).astype(BF16)
+
+    far, near = (front, back), (None, None)
+    for distance in range(half, 0, -1):
         nearer = distance - 1
-        kept = after(low, right)
-        parts_for([nearer, count - nearer] if nearer else [0], kept, F32)
+        if distance < half:
+            far = lax.optimization_barrier(
+                (joined(parts[count - distance][0], far[0]), joined(parts[distance][1], far[1]))
+            )
         if distance == half - 1:
-            dense_for(wanted[5:-1], after(attended, right), turn=0, handed=begun)
-        if distance == half - 2:
-            dense_for([0], after(attended, right))
-        left, right = (come(left, 1), None), (come(right, -1), None)
-    came = [left[0], right[0]]
+            dense_for(wanted[5:-1], after(attended, *far))
+        if nearer and nearer < half - 1:
+            parts_for([nearer, count - nearer], after(low, *far))
+        if not nearer:
+            dense_for([0], after(attended, *far))
+            parts_for([0], after(low, *far))
+        far = come(far[0], 1), come(far[1], -1)
+        if nearer:
+            near = lax.optimization_barrier(
+                (joined(parts[count - nearer][1], near[0]), joined(parts[nearer][0], near[1]))
+            )
+            near = come(near[0], 1), come(near[1], -1)
+    came = [far[0], near[0], near[1], far[1]] if half > 1 else [far[0], far[1]]
     return call(
         sum_kernel,
         "sum_up",
         shape((rows, width), BF16),
-        (parts[0], *came),
-        [VMEM] * (1 + len(came)),
+        (*parts[0], *came),
+        [VMEM] * (2 + len(came)),
         VMEM,
         flops=1,
         moved=1,

time: 71.8 us -> 67.6 us (0.942)
  waiting for transfers between devices: 24.4 us -> 15.4 us
  starting transfers between devices: 18.4 us -> 23.8 us
  Pallas kernels: 27.3 us -> 26.5 us
    ppermute x16 -> x22, waiting for transfers between devices: 24.4 us -> 15.4 us  [come(): lax.ppermute(value, 'tp', [(ring[(i + distance) % count], ring[i]) for i...]
    ppermute x16 -> x22, starting transfers between devices: 18.4 us -> 23.8 us  [come(): lax.ppermute(value, 'tp', [(ring[(i + distance) % count], ring[i]) for i...]
    pallas_call x15 -> x12, Pallas kernels: 27.3 us -> 26.5 us  [call(): pl.pallas_call(kernel, out_shape=outs, in_specs=specs, out_specs=out_spec...]
  transfers between devices with their start and end apart: 16 -> 22, of which waited for: 15 -> 9; matrix products, arithmetic and copies ran while one was open for 0% -> 1% of each run, Pallas kernels for 28% -> 28%
where the time goes in v11:
time: 67.6 us; the launch traced here: 67.4 us
  Pallas kernels  26.5 us (39%)
  starting transfers between devices  23.8 us (35%)
  waiting for transfers between devices  15.4 us (23%)
  local copies, waits for them, and re-layouts  1.06 us (2%)
    pallas_call x12, Pallas kernels, call(): pl.pallas_call(kernel, out_shape=outs, in_specs=specs, out_specs=out_spec...  26.5 us
    ppermute x22, starting transfers between devices, come(): lax.ppermute(value, 'tp', [(ring[(i + distance) % count], ring[i]) for i...  23.8 us
    ppermute x22, waiting for transfers between devices, come(): lax.ppermute(value, 'tp', [(ring[(i + distance) % count], ring[i]) for i...  15.4 us
  transfers between devices with their start and end apart: 22, of which 9 were waited for; matrix products, arithmetic and copies ran while one was open for 1% of the time, Pallas kernels for 28%

profile of v11, /device:TPU:0, one launch (start us, length us, event | category | flops | bytes accessed | tf_op | source)
XLA Modules:
  0.0 67.4 jit_solution(5598880138649170370)
XLA Ops:
  0.0 4.8 %attend.1.refs_0_ = bf16[8,128,128]{2,1,0:T(8,128)(2,1)} custom-call(bf16[128,1024]{1,0:T(8,128)(2,1)} %query_hbm.1, bf16[4096,128]{1,0:T(8,128)(2,1)} %bitcast.20, bf16[4096,128]{1,0:T(8,128)(2,1)} %bitcast.21, bf16[128,128]{1,0:T(8,128)(2,1)} %bitcast.22, bf16[128,128]{1,0:T(8,128)(2,1)} %bitcast.23, s32[1,128]{1,0:T(1,128)} %bitcast.24), custom_call_target="tpu_custom_call" | custom-call | tf_op jit(solution)/shard_map/attend/pallas_call | solution.py:39
  4.8 3.1 %collective-permute-start.3 = (bf16[8,128,128]{2,1,0:T(8,128)(2,1)}, bf16[8,128,128]{2,1,0:T(8,128)(2,1)S(1)}, u32[]{:S(2)}, u32[]{:S(2)}) collective-permute-start(bf16[8,128,128]{2,1,0:T(8,128)(2,1)} %attend.1.refs_0_), channel_id=1, source_target_pairs={{2,0},{0,4},{4,8},{8,12},{12,14},{14,10},{10,6},{6,2},{3,1},{1,5},... | collective-permute-start | bytes 786440 | tf_op jit(solution)/shard_map/ppermute | solution.py:352
  7.9 1.0 %copy-done.3 = bf16[8,128,128]{2,1,0:T(8,128)(2,1)S(1)} copy-done((bf16[8,128,128]{2,1,0:T(8,128)(2,1)S(1)}, bf16[8,128,128]{2,1,0:T(8,128)(2,1)}, u32[]{:S(2)}) %copy-start.3) | copy-done | bytes 262168
  8.9 3.5 %dense.4 = (f32[128,1024]{1,0:T(8,128)S(1)}, f32[128,1024]{1,0:T(8,128)S(1)}, f32[128,1024]{1,0:T(8,128)S(1)}) custom-call(bf16[8,128,128]{2,1,0:T(8,128)(2,1)S(1)} %copy-done.3, bf16[1024,8192]{1,0:T(8,128)(2,1)} %refs_1_.7), custom_call_target="tpu_custom_call" | custom-call | flops 805306368 | bytes 6291456 | tf_op jit(solution)/shard_map/dense/pallas_call | solution.py:39
  12.3 2.0 %collective-permute-done.3.refs_2_ = bf16[8,128,128]{2,1,0:T(8,128)(2,1)S(1)} collective-permute-done((bf16[8,128,128]{2,1,0:T(8,128)(2,1)}, bf16[8,128,128]{2,1,0:T(8,128)(2,1)S(1)}, u32[]{:S(2)}, u32[]{:S(2)}) %collective-permute-start.3) | collective-permute-done | bytes 262176 | tf_op jit(solution)/shard_map/ppermute | solution.py:352
  14.3 1.8 %collective-permute-start.4 = (bf16[8,128,128]{2,1,0:T(8,128)(2,1)S(1)}, bf16[8,128,128]{2,1,0:T(8,128)(2,1)S(1)}, u32[]{:S(2)}, u32[]{:S(2)}) collective-permute-start(bf16[8,128,128]{2,1,0:T(8,128)(2,1)S(1)} %collective-permute-done.3.refs_2_), channel_id=1, source_target_pairs={{2,0},{0,4},{4,8},{8,12},{12,14},{14,10},{10,6},{6,2},{3,1},{1,5},... | collective-permute-start | bytes 786440 | tf_op jit(solution)/shard_map/ppermute | solution.py:352
  16.4 3.7 %dense.5 = (f32[128,1024]{1,0:T(8,128)S(1)}, f32[128,1024]{1,0:T(8,128)S(1)}, s32[128,128]{1,0:T(8,128)S(1)}, s32[64]{0:T(128)S(1)}) custom-call(bf16[8,128,128]{2,1,0:T(8,128)(2,1)S(1)} %copy-done.3, bf16[1024,8192]{1,0:T(8,128)(2,1)} %refs_1_.7, s32[1,128]{1,0:T(1,128)S(1)} %bitcast.19, s32[32]{0:T(128)S(1)} %copy-done.8, s32[4,16]{1,0:T(4,128)S(1)} %bitcast.18), custom_call_target="tpu_custom_call" | custom-call | flops 536870912 | bytes 4194304 | tf_op jit(solution)/shard_map/dense/pallas_call | solution.py:39
  20.1 1.7 %collective-permute-done.4.refs_4_ = bf16[8,128,128]{2,1,0:T(8,128)(2,1)S(1)} collective-permute-done((bf16[8,128,128]{2,1,0:T(8,128)(2,1)S(1)}, bf16[8,128,128]{2,1,0:T(8,128)(2,1)S(1)}, u32[]{:S(2)}, u32[]{:S(2)}) %collective-permute-start.4) | collective-permute-done | bytes 262176 | tf_op jit(solution)/shard_map/ppermute | solution.py:352
  21.8 1.5 %collective-permute-start.6 = (bf16[8,128,128]{2,1,0:T(8,128)(2,1)S(1)}, bf16[8,128,128]{2,1,0:T(8,128)(2,1)S(1)}, u32[]{:S(2)}, u32[]{:S(2)}) collective-permute-start(bf16[8,128,128]{2,1,0:T(8,128)(2,1)S(1)} %collective-permute-done.4.refs_4_), channel_id=1, source_target_pairs={{2,0},{0,4},{4,8},{8,12},{12,14},{14,10},{10,6},{6,2},{3,1},{1,5},... | collective-permute-start | bytes 786440 | tf_op jit(solution)/shard_map/ppermute | solution.py:352
  23.8 2.2 %fold_early.1 = (f32[128,256]{1,0:T(8,128)S(1)}, f32[64,128,128]{2,1,0:T(8,128)S(1)}) custom-call(bf16[8,128,128]{2,1,0:T(8,128)(2,1)S(1)} %copy-done.3, bf16[8,128,128]{2,1,0:T(8,128)(2,1)S(1)} %collective-permute-done.refs_1_, bf16[8,128,128]{2,1,0:T(8,128)(2,1)S(1)} %collective-permute-done.3.refs_2_, ...), custom_call_target="tpu_custom_call" | custom-call | flops 268435456 | bytes 4194304 | tf_op jit(solution)/shard_map/fold_early/pallas_call | solution.py:39
  26.0 2.3 %collective-permute-done.6.refs_1_ = bf16[8,128,128]{2,1,0:T(8,128)(2,1)S(1)} collective-permute-done((bf16[8,128,128]{2,1,0:T(8,128)(2,1)S(1)}, bf16[8,128,128]{2,1,0:T(8,128)(2,1)S(1)}, u32[]{:S(2)}, u32[]{:S(2)}) %collective-permute-start.6) | collective-permute-done | bytes 262176 | tf_op jit(solution)/shard_map/ppermute | solution.py:352
  28.4 1.7 %collective-permute-start.7 = (bf16[4,128,128]{2,1,0:T(8,128)(2,1)S(1)}, bf16[4,128,128]{2,1,0:T(8,128)(2,1)S(1)}, u32[]{:S(2)}, u32[]{:S(2)}) collective-permute-start(bf16[4,128,128]{2,1,0:T(8,128)(2,1)S(1)} %slice.7), channel_id=1, source_target_pairs={{2,0},{0,4},{4,8},{8,12},{12,14},{14,10},{10,6},{6,2},{3,1},{1,5},... | collective-permute-start | bytes 393224 | tf_op jit(solution)/shard_map/ppermute | solution.py:352
  30.5 1.4 %fold_late.1 = (f32[128,256]{1,0:T(8,128)S(1)}, f32[64,128,128]{2,1,0:T(8,128)S(1)}) custom-call(bf16[8,128,128]{2,1,0:T(8,128)(2,1)S(1)} %collective-permute-done.2.refs_0_, bf16[8,128,128]{2,1,0:T(8,128)(2,1)S(1)} %collective-permute-done.6.refs_1_, s32[128,128]{1,0:T(8,128)S(1)} %get-tuple-element.63.refs_5_.refs_2_, bf16[256,8192]{1,0:T(8,128)(2,1)S(1)} %bitcast.16, ...), custom_call_target="tpu_custom_call" | custom-call | flops 134217728 | bytes 1048576 | tf_op jit(solution)/shard_map/fold_late/pallas_call | solution.py:39
  32.0 1.4 %collective-permute-done.7.refs_1_ = bf16[4,128,128]{2,1,0:T(8,128)(2,1)S(1)} collective-permute-done((bf16[4,128,128]{2,1,0:T(8,128)(2,1)S(1)}, bf16[4,128,128]{2,1,0:T(8,128)(2,1)S(1)}, u32[]{:S(2)}, u32[]{:S(2)}) %collective-permute-start.7) | collective-permute-done | bytes 131104 | tf_op jit(solution)/shard_map/ppermute | solution.py:352
  33.4 1.7 %collective-permute-done.5.refs_0_ = bf16[4,128,128]{2,1,0:T(8,128)(2,1)S(1)} collective-permute-done((bf16[4,128,128]{2,1,0:T(8,128)(2,1)S(1)}, bf16[4,128,128]{2,1,0:T(8,128)(2,1)S(1)}, u32[]{:S(2)}, u32[]{:S(2)}) %collective-permute-start.5) | collective-permute-done | bytes 131104 | tf_op jit(solution)/shard_map/ppermute | solution.py:352
  35.1 2.0 %finish.1 = (bf16[128,256]{1,0:T(8,128)(2,1)S(1)}, f32[8,128,128]{2,1,0:T(8,128)S(1)}, bf16[4,128,128]{2,1,0:T(8,128)(2,1)S(1)}, bf16[4,128,128]{2,1,0:T(8,128)(...) custom-call(bf16[4,128,128]{2,1,0:T(8,128)(2,1)S(1)} %collective-per, ...), custom_call_target="tpu_custom_call" | custom-call | flops 268435456 | bytes 2097152 | tf_op jit(solution)/shard_map/finish/pallas_call | solution.py:39
  37.2 1.6 %collective-permute-start.9 = (bf16[4,128,128]{2,1,0:T(8,128)(2,1)S(1)}, bf16[4,128,128]{2,1,0:T(8,128)(2,1)S(1)}, u32[]{:S(2)}, u32[]{:S(2)}) collective-permute-start(bf16[4,128,128]{2,1,0:T(8,128)(2,1)S(1)} %get-tuple-element.80), channel_id=1, source_target_pairs={{2,0},{0,4},{4,8},{8,12},{12,14},{14,10},{10,6},{6,2},{3,1},{1,5},... | collective-permute-start | bytes 393224 | tf_op jit(solution)/shard_map/ppermute | solution.py:352
  38.9 1.6 %collective-permute-start.16 = (bf16[4,128,128]{2,1,0:T(8,128)(2,1)S(1)}, bf16[4,128,128]{2,1,0:T(8,128)(2,1)S(1)}, u32[]{:S(2)}, u32[]{:S(2)}) collective-permute-start(bf16[4,128,128]{2,1,0:T(8,128)(2,1)S(1)} %convert_element_type.79), channel_id=1, source_target_pairs={{2,0},{0,4},{4,8},{8,12},{12,14},{14,10},{10,6},{6,2},{3,1},{1,5},... | collective-permute-start | bytes 393224 | tf_op jit(solution)/shard_map/ppermute | solution.py:352
  42.2 4.0 %collective-permute-done.8 = bf16[4,128,128]{2,1,0:T(8,128)(2,1)S(1)} collective-permute-done((bf16[4,128,128]{2,1,0:T(8,128)(2,1)S(1)}, bf16[4,128,128]{2,1,0:T(8,128)(2,1)S(1)}, u32[]{:S(2)}, u32[]{:S(2)}) %collective-permute-start.8) | collective-permute-done | bytes 131104 | tf_op jit(solution)/shard_map/ppermute | solution.py:352
  46.3 1.0 %collective-permute-start.11 = (bf16[4,128,128]{2,1,0:T(8,128)(2,1)S(1)}, bf16[4,128,128]{2,1,0:T(8,128)(2,1)S(1)}, u32[]{:S(2)}, u32[]{:S(2)}) collective-permute-start(bf16[4,128,128]{2,1,0:T(8,128)(2,1)S(1)} %add_convert_fusion.8), channel_id=1, source_target_pairs={{2,0},{0,4},{4,8},{8,12},{12,14},{14,10},{10,6},{6,2},{3,1},{1,5},... | collective-permute-start | bytes 393224 | tf_op jit(solution)/shard_map/ppermute | solution.py:352
  47.2 1.1 %collective-permute-start.10 = (bf16[4,128,128]{2,1,0:T(8,128)(2,1)S(1)}, bf16[4,128,128]{2,1,0:T(8,128)(2,1)S(1)}, u32[]{:S(2)}, u32[]{:S(2)}) collective-permute-start(bf16[4,128,128]{2,1,0:T(8,128)(2,1)S(1)} %add_convert_fusion.9), channel_id=1, source_target_pairs={{4,0},{8,4},{12,8},{14,12},{10,14},{6,10},{2,6},{0,2},{5,1},{9,5},... | collective-permute-start | bytes 393224 | tf_op jit(solution)/shard_map/ppermute | solution.py:352
  48.4 1.3 %part.3 = (f32[4,128,128]{2,1,0:T(8,128)S(1)}, f32[4,128,128]{2,1,0:T(8,128)S(1)}, f32[4,128,128]{2,1,0:T(8,128)S(1)}, f32[4,128,128]{2,1,0:T(8,128)S(1)}) custom-call(bf16[128,256]{1,0:T(8,128)(2,1)S(1)} %get-tuple-element.99.refs_0_, bf16[256,8192]{1,0:T(8,128)(2,1)S(1)} %bitcast.12, f32[64,128,128]{2,1,0:T(8,128)S(1)} %get-tuple-element.73.refs_10_.refs_2_, ...), custom_call_target="tpu_custom_call" | custom-call | flops 67108864 | bytes 1048576 | tf_op jit(solution)/shard_map/part/pallas_call | solution.py:39
  49.8 1.0 %collective-permute-start.18 = (bf16[4,128,128]{2,1,0:T(8,128)(2,1)S(1)}, bf16[4,128,128]{2,1,0:T(8,128)(2,1)S(1)}, u32[]{:S(2)}, u32[]{:S(2)}) collective-permute-start(bf16[4,128,128]{2,1,0:T(8,128)(2,1)S(1)} %add_convert_fusion.2), channel_id=1, source_target_pairs={{2,0},{0,4},{4,8},{8,12},{12,14},{14,10},{10,6},{6,2},{3,1},{1,5},... | collective-permute-start | bytes 393224 | tf_op jit(solution)/shard_map/ppermute | solution.py:352
  50.8 1.1 %collective-permute-start.17 = (bf16[4,128,128]{2,1,0:T(8,128)(2,1)S(1)}, bf16[4,128,128]{2,1,0:T(8,128)(2,1)S(1)}, u32[]{:S(2)}, u32[]{:S(2)}) collective-permute-start(bf16[4,128,128]{2,1,0:T(8,128)(2,1)S(1)} %add_convert_fusion.3), channel_id=1, source_target_pairs={{4,0},{8,4},{12,8},{14,12},{10,14},{6,10},{2,6},{0,2},{5,1},{9,5},... | collective-permute-start | bytes 393224 | tf_op jit(solution)/shard_map/ppermute | solution.py:352
  51.9 2.6 %dense.6 = (f32[128,1024]{1,0:T(8,128)S(1)}, f32[128,1024]{1,0:T(8,128)S(1)}) custom-call(bf16[8,128,128]{2,1,0:T(8,128)(2,1)S(1)} %copy-done.3, bf16[1024,8192]{1,0:T(8,128)(2,1)} %refs_1_.7), custom_call_target="tpu_custom_call" | custom-call | flops 536870912 | bytes 4194304 | tf_op jit(solution)/shard_map/dense/pallas_call | solution.py:39
  55.5 1.1 %collective-permute-start.12 = (bf16[4,128,128]{2,1,0:T(8,128)(2,1)S(1)}, bf16[4,128,128]{2,1,0:T(8,128)(2,1)S(1)}, u32[]{:S(2)}, u32[]{:S(2)}) collective-permute-start(bf16[4,128,128]{2,1,0:T(8,128)(2,1)S(1)} %add_convert_fusion.7), channel_id=1, source_target_pairs={{4,0},{8,4},{12,8},{14,12},{10,14},{6,10},{2,6},{0,2},{5,1},{9,5},... | collective-permute-start | bytes 393224 | tf_op jit(solution)/shard_map/ppermute | solution.py:352
  56.6 1.3 %part.4 = (f32[4,128,128]{2,1,0:T(8,128)S(1)}, f32[4,128,128]{2,1,0:T(8,128)S(1)}, f32[4,128,128]{2,1,0:T(8,128)S(1)}, f32[4,128,128]{2,1,0:T(8,128)S(1)}) custom-call(bf16[128,256]{1,0:T(8,128)(2,1)S(1)} %get-tuple-element.99.refs_0_, bf16[256,8192]{1,0:T(8,128)(2,1)S(1)} %bitcast.13, f32[64,128,128]{2,1,0:T(8,128)S(1)} %get-tuple-element.73.refs_10_.refs_2_, ...), custom_call_target="tpu_custom_call" | custom-call | flops 67108864 | bytes 1048576 | tf_op jit(solution)/shard_map/part/pallas_call | solution.py:39
  58.5 1.6 %collective-permute-start.20 = (bf16[4,128,128]{2,1,0:T(8,128)(2,1)S(1)}, bf16[4,128,128]{2,1,0:T(8,128)(2,1)S(1)}, u32[]{:S(2)}, u32[]{:S(2)}) collective-permute-start(bf16[4,128,128]{2,1,0:T(8,128)(2,1)S(1)} %add_convert_fusion), channel_id=1, source_target_pairs={{2,0},{0,4},{4,8},{8,12},{12,14},{14,10},{10,6},{6,2},{3,1},{1,5},... | collective-permute-start | bytes 393224 | tf_op jit(solution)/shard_map/ppermute | solution.py:352
  60.5 1.2 %collective-permute-start.14 = (bf16[4,128,128]{2,1,0:T(8,128)(2,1)S(1)}, bf16[4,128,128]{2,1,0:T(8,128)(2,1)S(1)}, u32[]{:S(2)}, u32[]{:S(2)}) collective-permute-start(bf16[4,128,128]{2,1,0:T(8,128)(2,1)S(1)} %add_convert_fusion.5), channel_id=1, source_target_pairs={{4,0},{8,4},{12,8},{14,12},{10,14},{6,10},{2,6},{0,2},{5,1},{9,5},... | collective-permute-start | bytes 393224 | tf_op jit(solution)/shard_map/ppermute | solution.py:352
  62.6 1.9 %dense.7.refs_7_ = f32[128,1024]{1,0:T(8,128)S(1)} custom-call(bf16[8,128,128]{2,1,0:T(8,128)(2,1)S(1)} %copy-done.3, bf16[1024,8192]{1,0:T(8,128)(2,1)} %refs_1_.7), custom_call_target="tpu_custom_call" | custom-call | flops 268435456 | bytes 2097152 | tf_op jit(solution)/shard_map/dense/pallas_call | solution.py:39
  64.5 1.0 %part.5 = (f32[4,128,128]{2,1,0:T(8,128)S(1)}, f32[4,128,128]{2,1,0:T(8,128)S(1)}) custom-call(bf16[128,256]{1,0:T(8,128)(2,1)S(1)} %get-tuple-element.99.refs_0_, bf16[256,8192]{1,0:T(8,128)(2,1)S(1)} %bitcast.14, f32[64,128,128]{2,1,0:T(8,128)S(1)} %get-tuple-element.73.refs_10_.refs_2_, f32[8,128,128]{2,1,0:T(8,128)S(1)} %get-tuple-element.84.refs_3_, ...), custom_call_target="tpu_custom_call" | custom-call | flops 67108864 | bytes 1048576 | tf_op jit(solution)/shard_map/part/pallas_call | solution.py:39
  65.5 1.1 %collective-permute-done.21.refs_5_ = bf16[4,128,128]{2,1,0:T(8,128)(2,1)S(1)} collective-permute-done((bf16[4,128,128]{2,1,0:T(8,128)(2,1)S(1)}, bf16[4,128,128]{2,1,0:T(8,128)(2,1)S(1)}, u32[]{:S(2)}, u32[]{:S(2)}) %collective-permute-start.21) | collective-permute-done | bytes 131104 | tf_op jit(solution)/shard_map/ppermute | solution.py:352
  (56 shorter events, 6.8 us)
Async XLA Ops:
  0.0 16.3 %copy-start.6 = (s32[4,16,1]{1,2,0:T(1,128)S(1)}, s32[4,16,1]{1,2,0:T(1,128)}, u32[]{:S(2)}) copy-start(s32[4,16,1]{1,2,0:T(1,128)} %param.28) | copy-start | bytes 772
  0.0 16.3 %copy-start.7 = (s32[128]{0:T(128)S(1)}, s32[128]{0:T(128)}, u32[]{:S(2)}) copy-start(s32[128]{0:T(128)} %param.21) | copy-start | bytes 1540
  0.0 16.3 %copy-start.8 = (s32[32]{0:T(128)S(1)}, s32[32]{0:T(128)}, u32[]{:S(2)}) copy-start(s32[32]{0:T(128)} %refs_3_.1) | copy-start | bytes 388
  4.8 9.5 %collective-permute-start.3 = (bf16[8,128,128]{2,1,0:T(8,128)(2,1)}, bf16[8,128,128]{2,1,0:T(8,128)(2,1)S(1)}, u32[]{:S(2)}, u32[]{:S(2)}) collective-permute-start(bf16[8,128,128]{2,1,0:T(8,128)(2,1)} %attend.1.refs_0_), channel_id=1, source_target_pairs={{2,0},{0,4},{4,8},{8,12},{12,14},{14,10},{10,6},{6,2},{3,1},{1,5},... | collective-permute-start | bytes 786440 | tf_op jit(solution)/shard_map/ppermute | solution.py:352
  7.8 8.3 %collective-permute-start = (bf16[8,128,128]{2,1,0:T(8,128)(2,1)}, bf16[8,128,128]{2,1,0:T(8,128)(2,1)S(1)}, u32[]{:S(2)}, u32[]{:S(2)}) collective-permute-start(bf16[8,128,128]{2,1,0:T(8,128)(2,1)} %attend.1.refs_0_), channel_id=1, source_target_pairs={{4,0},{8,4},{12,8},{14,12},{10,14},{6,10},{2,6},{0,2},{5,1},{9,5},... | collective-permute-start | bytes 786440 | tf_op jit(solution)/shard_map/ppermute | solution.py:352
  7.9 1.0 %copy-start.3 = (bf16[8,128,128]{2,1,0:T(8,128)(2,1)S(1)}, bf16[8,128,128]{2,1,0:T(8,128)(2,1)}, u32[]{:S(2)}) copy-start(bf16[8,128,128]{2,1,0:T(8,128)(2,1)} %attend.1.refs_0_) | copy-start | bytes 786436
  14.3 7.5 %collective-permute-start.4 = (bf16[8,128,128]{2,1,0:T(8,128)(2,1)S(1)}, bf16[8,128,128]{2,1,0:T(8,128)(2,1)S(1)}, u32[]{:S(2)}, u32[]{:S(2)}) collective-permute-start(bf16[8,128,128]{2,1,0:T(8,128)(2,1)S(1)} %collective-permute-done.3.refs_2_), channel_id=1, source_target_pairs={{2,0},{0,4},{4,8},{8,12},{12,14},{14,10},{10,6},{6,2},{3,1},{1,5},... | collective-permute-start | bytes 786440 | tf_op jit(solution)/shard_map/ppermute | solution.py:352
  16.1 7.2 %collective-permute-start.1 = (bf16[8,128,128]{2,1,0:T(8,128)(2,1)S(1)}, bf16[8,128,128]{2,1,0:T(8,128)(2,1)S(1)}, u32[]{:S(2)}, u32[]{:S(2)}) collective-permute-start(bf16[8,128,128]{2,1,0:T(8,128)(2,1)S(1)} %collective-permute-done.refs_1_), channel_id=1, source_target_pairs={{4,0},{8,4},{12,8},{14,12},{10,14},{6,10},{2,6},{0,2},{5,1},{9,5},... | collective-permute-start | bytes 786440 | tf_op jit(solution)/shard_map/ppermute | solution.py:352
  16.3 7.5 %copy-start.1 = (bf16[4,8192,64]{1,2,0:T(8,128)(2,1)S(1)}, bf16[4,8192,64]{1,2,0:T(8,128)(2,1)}, u32[]{:S(2)}) copy-start(bf16[4,8192,64]{1,2,0:T(8,128)(2,1)} %param.24) | copy-start | bytes 12582916
  16.4 7.5 %copy-start.2 = (bf16[4,16,128,128]{3,2,1,0:T(8,128)(2,1)S(1)}, bf16[4,16,128,128]{3,2,1,0:T(8,128)(2,1)}, u32[]{:S(2)}) copy-start(bf16[4,16,128,128]{3,2,1,0:T(8,128)(2,1)} %refs_4_.6) | copy-start | bytes 6291460
  16.4 7.5 %copy-start.4 = (f32[4,16]{1,0:T(4,128)S(1)}, f32[4,16]{1,0:T(4,128)}, u32[]{:S(2)}) copy-start(f32[4,16]{1,0:T(4,128)} %refs_4_.9) | copy-start | bytes 772
  16.4 7.5 %copy-start.5 = (s32[4,16]{1,0:T(4,128)S(1)}, s32[4,16]{1,0:T(4,128)}, u32[]{:S(2)}) copy-start(s32[4,16]{1,0:T(4,128)} %refs_5_.9) | copy-start | bytes 772
  21.8 6.6 %collective-permute-start.6 = (bf16[8,128,128]{2,1,0:T(8,128)(2,1)S(1)}, bf16[8,128,128]{2,1,0:T(8,128)(2,1)S(1)}, u32[]{:S(2)}, u32[]{:S(2)}) collective-permute-start(bf16[8,128,128]{2,1,0:T(8,128)(2,1)S(1)} %collective-permute-done.4.refs_4_), channel_id=1, source_target_pairs={{2,0},{0,4},{4,8},{8,12},{12,14},{14,10},{10,6},{6,2},{3,1},{1,5},... | collective-permute-start | bytes 786440 | tf_op jit(solution)/shard_map/ppermute | solution.py:352
  23.3 6.8 %collective-permute-start.2 = (bf16[8,128,128]{2,1,0:T(8,128)(2,1)S(1)}, bf16[8,128,128]{2,1,0:T(8,128)(2,1)S(1)}, u32[]{:S(2)}, u32[]{:S(2)}) collective-permute-start(bf16[8,128,128]{2,1,0:T(8,128)(2,1)S(1)} %collective-permute-done.1.refs_3_), channel_id=1, source_target_pairs={{4,0},{8,4},{12,8},{14,12},{10,14},{6,10},{2,6},{0,2},{5,1},{9,5},... | collective-permute-start | bytes 786440 | tf_op jit(solution)/shard_map/ppermute | solution.py:352
  28.4 5.0 %collective-permute-start.7 = (bf16[4,128,128]{2,1,0:T(8,128)(2,1)S(1)}, bf16[4,128,128]{2,1,0:T(8,128)(2,1)S(1)}, u32[]{:S(2)}, u32[]{:S(2)}) collective-permute-start(bf16[4,128,128]{2,1,0:T(8,128)(2,1)S(1)} %slice.7), channel_id=1, source_target_pairs={{2,0},{0,4},{4,8},{8,12},{12,14},{14,10},{10,6},{6,2},{3,1},{1,5},... | collective-permute-start | bytes 393224 | tf_op jit(solution)/shard_map/ppermute | solution.py:352
  30.1 5.0 %collective-permute-start.5 = (bf16[4,128,128]{2,1,0:T(8,128)(2,1)S(1)}, bf16[4,128,128]{2,1,0:T(8,128)(2,1)S(1)}, u32[]{:S(2)}, u32[]{:S(2)}) collective-permute-start(bf16[4,128,128]{2,1,0:T(8,128)(2,1)S(1)} %slice.6), channel_id=1, source_target_pairs={{4,0},{8,4},{12,8},{14,12},{10,14},{6,10},{2,6},{0,2},{5,1},{9,5},... | collective-permute-start | bytes 393224 | tf_op jit(solution)/shard_map/ppermute | solution.py:352
  30.5 4.6 %copy-start = (bf16[4,64,8192]{2,1,0:T(8,128)(2,1)S(1)}, bf16[4,64,8192]{2,1,0:T(8,128)(2,1)}, u32[]{:S(2)}) copy-start(bf16[4,64,8192]{2,1,0:T(8,128)(2,1)} %param.25) | copy-start | bytes 12582916
  37.2 5.0 %collective-permute-start.9 = (bf16[4,128,128]{2,1,0:T(8,128)(2,1)S(1)}, bf16[4,128,128]{2,1,0:T(8,128)(2,1)S(1)}, u32[]{:S(2)}, u32[]{:S(2)}) collective-permute-start(bf16[4,128,128]{2,1,0:T(8,128)(2,1)S(1)} %get-tuple-element.80), channel_id=1, source_target_pairs={{2,0},{0,4},{4,8},{8,12},{12,14},{14,10},{10,6},{6,2},{3,1},{1,5},... | collective-permute-start | bytes 393224 | tf_op jit(solution)/shard_map/ppermute | solution.py:352
  38.9 10.8 %collective-permute-start.16 = (bf16[4,128,128]{2,1,0:T(8,128)(2,1)S(1)}, bf16[4,128,128]{2,1,0:T(8,128)(2,1)S(1)}, u32[]{:S(2)}, u32[]{:S(2)}) collective-permute-start(bf16[4,128,128]{2,1,0:T(8,128)(2,1)S(1)} %convert_element_type.79), channel_id=1, source_target_pairs={{2,0},{0,4},{4,8},{8,12},{12,14},{14,10},{10,6},{6,2},{3,1},{1,5},... | collective-permute-start | bytes 393224 | tf_op jit(solution)/shard_map/ppermute | solution.py:352
  40.5 5.8 %collective-permute-start.8 = (bf16[4,128,128]{2,1,0:T(8,128)(2,1)S(1)}, bf16[4,128,128]{2,1,0:T(8,128)(2,1)S(1)}, u32[]{:S(2)}, u32[]{:S(2)}) collective-permute-start(bf16[4,128,128]{2,1,0:T(8,128)(2,1)S(1)} %get-tuple-element.78), channel_id=1, source_target_pairs={{4,0},{8,4},{12,8},{14,12},{10,14},{6,10},{2,6},{0,2},{5,1},{9,5},... | collective-permute-start | bytes 393224 | tf_op jit(solution)/shard_map/ppermute | solution.py:352
  41.0 8.8 %collective-permute-start.15 = (bf16[4,128,128]{2,1,0:T(8,128)(2,1)S(1)}, bf16[4,128,128]{2,1,0:T(8,128)(2,1)S(1)}, u32[]{:S(2)}, u32[]{:S(2)}) collective-permute-start(bf16[4,128,128]{2,1,0:T(8,128)(2,1)S(1)} %convert_element_type.78), channel_id=1, source_target_pairs={{4,0},{8,4},{12,8},{14,12},{10,14},{6,10},{2,6},{0,2},{5,1},{9,5},... | collective-permute-start | bytes 393224 | tf_op jit(solution)/shard_map/ppermute | solution.py:352
  46.3 8.2 %collective-permute-start.11 = (bf16[4,128,128]{2,1,0:T(8,128)(2,1)S(1)}, bf16[4,128,128]{2,1,0:T(8,128)(2,1)S(1)}, u32[]{:S(2)}, u32[]{:S(2)}) collective-permute-start(bf16[4,128,128]{2,1,0:T(8,128)(2,1)S(1)} %add_convert_fusion.8), channel_id=1, source_target_pairs={{2,0},{0,4},{4,8},{8,12},{12,14},{14,10},{10,6},{6,2},{3,1},{1,5},... | collective-permute-start | bytes 393224 | tf_op jit(solution)/shard_map/ppermute | solution.py:352
  47.2 7.3 %collective-permute-start.10 = (bf16[4,128,128]{2,1,0:T(8,128)(2,1)S(1)}, bf16[4,128,128]{2,1,0:T(8,128)(2,1)S(1)}, u32[]{:S(2)}, u32[]{:S(2)}) collective-permute-start(bf16[4,128,128]{2,1,0:T(8,128)(2,1)S(1)} %add_convert_fusion.9), channel_id=1, source_target_pairs={{4,0},{8,4},{12,8},{14,12},{10,14},{6,10},{2,6},{0,2},{5,1},{9,5},... | collective-permute-start | bytes 393224 | tf_op jit(solution)/shard_map/ppermute | solution.py:352
  49.8 8.1 %collective-permute-start.18 = (bf16[4,128,128]{2,1,0:T(8,128)(2,1)S(1)}, bf16[4,128,128]{2,1,0:T(8,128)(2,1)S(1)}, u32[]{:S(2)}, u32[]{:S(2)}) collective-permute-start(bf16[4,128,128]{2,1,0:T(8,128)(2,1)S(1)} %add_convert_fusion.2), channel_id=1, source_target_pairs={{2,0},{0,4},{4,8},{8,12},{12,14},{14,10},{10,6},{6,2},{3,1},{1,5},... | collective-permute-start | bytes 393224 | tf_op jit(solution)/shard_map/ppermute | solution.py:352
  50.8 7.2 %collective-permute-start.17 = (bf16[4,128,128]{2,1,0:T(8,128)(2,1)S(1)}, bf16[4,128,128]{2,1,0:T(8,128)(2,1)S(1)}, u32[]{:S(2)}, u32[]{:S(2)}) collective-permute-start(bf16[4,128,128]{2,1,0:T(8,128)(2,1)S(1)} %add_convert_fusion.3), channel_id=1, source_target_pairs={{4,0},{8,4},{12,8},{14,12},{10,14},{6,10},{2,6},{0,2},{5,1},{9,5},... | collective-permute-start | bytes 393224 | tf_op jit(solution)/shard_map/ppermute | solution.py:352
  54.5 5.6 %collective-permute-start.13 = (bf16[4,128,128]{2,1,0:T(8,128)(2,1)S(1)}, bf16[4,128,128]{2,1,0:T(8,128)(2,1)S(1)}, u32[]{:S(2)}, u32[]{:S(2)}) collective-permute-start(bf16[4,128,128]{2,1,0:T(8,128)(2,1)S(1)} %add_convert_fusion.6), channel_id=1, source_target_pairs={{2,0},{0,4},{4,8},{8,12},{12,14},{14,10},{10,6},{6,2},{3,1},{1,5},... | collective-permute-start | bytes 393224 | tf_op jit(solution)/shard_map/ppermute | solution.py:352
  55.5 5.0 %collective-permute-start.12 = (bf16[4,128,128]{2,1,0:T(8,128)(2,1)S(1)}, bf16[4,128,128]{2,1,0:T(8,128)(2,1)S(1)}, u32[]{:S(2)}, u32[]{:S(2)}) collective-permute-start(bf16[4,128,128]{2,1,0:T(8,128)(2,1)S(1)} %add_convert_fusion.7), channel_id=1, source_target_pairs={{4,0},{8,4},{12,8},{14,12},{10,14},{6,10},{2,6},{0,2},{5,1},{9,5},... | collective-permute-start | bytes 393224 | tf_op jit(solution)/shard_map/ppermute | solution.py:352
  58.0 7.5 %collective-permute-start.19 = (bf16[4,128,128]{2,1,0:T(8,128)(2,1)S(1)}, bf16[4,128,128]{2,1,0:T(8,128)(2,1)S(1)}, u32[]{:S(2)}, u32[]{:S(2)}) collective-permute-start(bf16[4,128,128]{2,1,0:T(8,128)(2,1)S(1)} %add_convert_fusion.1), channel_id=1, source_target_pairs={{4,0},{8,4},{12,8},{14,12},{10,14},{6,10},{2,6},{0,2},{5,1},{9,5},... | collective-permute-start | bytes 393224 | tf_op jit(solution)/shard_map/ppermute | solution.py:352
  58.5 7.0 %collective-permute-start.20 = (bf16[4,128,128]{2,1,0:T(8,128)(2,1)S(1)}, bf16[4,128,128]{2,1,0:T(8,128)(2,1)S(1)}, u32[]{:S(2)}, u32[]{:S(2)}) collective-permute-start(bf16[4,128,128]{2,1,0:T(8,128)(2,1)S(1)} %add_convert_fusion), channel_id=1, source_target_pairs={{2,0},{0,4},{4,8},{8,12},{12,14},{14,10},{10,6},{6,2},{3,1},{1,5},... | collective-permute-start | bytes 393224 | tf_op jit(solution)/shard_map/ppermute | solution.py:352
  60.5 5.0 %collective-permute-start.14 = (bf16[4,128,128]{2,1,0:T(8,128)(2,1)S(1)}, bf16[4,128,128]{2,1,0:T(8,128)(2,1)S(1)}, u32[]{:S(2)}, u32[]{:S(2)}) collective-permute-start(bf16[4,128,128]{2,1,0:T(8,128)(2,1)S(1)} %add_convert_fusion.5), channel_id=1, source_target_pairs={{4,0},{8,4},{12,8},{14,12},{10,14},{6,10},{2,6},{0,2},{5,1},{9,5},... | collective-permute-start | bytes 393224 | tf_op jit(solution)/shard_map/ppermute | solution.py:352
  61.7 5.0 %collective-permute-start.21 = (bf16[4,128,128]{2,1,0:T(8,128)(2,1)S(1)}, bf16[4,128,128]{2,1,0:T(8,128)(2,1)S(1)}, u32[]{:S(2)}, u32[]{:S(2)}) collective-permute-start(bf16[4,128,128]{2,1,0:T(8,128)(2,1)S(1)} %add_convert_fusion.4), channel_id=1, source_target_pairs={{2,0},{0,4},{4,8},{8,12},{12,14},{14,10},{10,6},{6,2},{3,1},{1,5},... | collective-permute-start | bytes 393224 | tf_op jit(solution)/shard_map/ppermute | solution.py:352

commit v12 on v11

--- a/solution.py
+++ b/solution.py
@@ -12,7 +12,7 @@
 F32 = jnp.float32
 CAP = 2
 ROW_BLOCK = 16
-PIECES = 4
+PIECES = 2
 MIB = 1024 * 1024
 NT = (((1,), (1,)), ((), ()))
 VMEM = pl.BlockSpec(memory_space=pltpu.VMEM)
@@ -362,6 +362,7 @@
         if step == 2:
             slot, table = dense_for(wanted[3:5], after(attended, token), True)
             token = slot
+    (token, *_) = dense_for(wanted[5:-1], after(attended, chunks[half - 2], chunks[half + 2]))
     right, left = chunks[half - 1], chunks[half + 1]
 
     factor_t = jnp.swapaxes(factor_in, 1, 2).reshape(low_width, -1)
@@ -383,7 +384,7 @@
         flops=rows * low_width * complete,
         moved=4 * MIB,
     )
-    right, left = after(right, low), after(left, low)
+    right, left = after(right, low, token), after(left, low, token)
     front, back = come(right[: heads // 2], 1), come(left[heads // 2 :], -1)
     low, blocks = call(
         functools.partial(fold_kernel, late, count, False),
@@ -439,8 +440,6 @@
             far = lax.optimization_barrier(
                 (joined(parts[count - distance][0], far[0]), joined(parts[distance][1], far[1]))
             )
-        if distance == half - 1:
-            dense_for(wanted[5:-1], after(attended, *far))
         if nearer and nearer < half - 1:
             parts_for([nearer, count - nearer], after(low, *far))
         if not nearer:

time: 67.6 us -> 66.2 us (0.979)
  waiting for transfers between devices: 15.4 us -> 13.8 us
    ppermute x22, waiting for transfers between devices: 15.4 us -> 13.8 us  [come(): lax.ppermute(value, 'tp', [(ring[(i + distance) % count], ring[i]) for i...]
  transfers between devices with their start and end apart: 22 -> 22, of which waited for: 9 -> 9; matrix products, arithmetic and copies ran while one was open for 1% -> 1% of each run, Pallas kernels for 28% -> 29%
where the time goes in v12:
time: 66.2 us; the launch traced here: 66 us
  Pallas kernels  26.2 us (40%)
  starting transfers between devices  24.3 us (37%)
  waiting for transfers between devices  13.8 us (21%)
  local copies, waits for them, and re-layouts  1.07 us (2%)
    pallas_call x12, Pallas kernels, call(): pl.pallas_call(kernel, out_shape=outs, in_specs=specs, out_specs=out_spec...  26.2 us
    ppermute x22, starting transfers between devices, come(): lax.ppermute(value, 'tp', [(ring[(i + distance) % count], ring[i]) for i...  24.3 us
    ppermute x22, waiting for transfers between devices, come(): lax.ppermute(value, 'tp', [(ring[(i + distance) % count], ring[i]) for i...  13.8 us
  transfers between devices with their start and end apart: 22, of which 9 were waited for; matrix products, arithmetic and copies ran while one was open for 1% of the time, Pallas kernels for 29%

profile of v12, /device:TPU:0, one launch (start us, length us, event | category | flops | bytes accessed | tf_op | source)
XLA Modules:
  0.0 66.0 jit_solution(17542379875851144394)
XLA Ops:
  0.0 4.6 %attend.1.refs_0_ = bf16[8,128,128]{2,1,0:T(8,128)(2,1)} custom-call(bf16[128,1024]{1,0:T(8,128)(2,1)} %query_hbm.1, bf16[4096,128]{1,0:T(8,128)(2,1)} %bitcast.20, bf16[4096,128]{1,0:T(8,128)(2,1)} %bitcast.21, bf16[128,128]{1,0:T(8,128)(2,1)} %bitcast.22, bf16[128,128]{1,0:T(8,128)(2,1)} %bitcast.23, s32[1,128]{1,0:T(1,128)} %bitcast.24), custom_call_target="tpu_custom_call" | custom-call | tf_op jit(solution)/shard_map/attend/pallas_call | solution.py:39
  4.6 3.1 %collective-permute-start.3 = (bf16[8,128,128]{2,1,0:T(8,128)(2,1)}, bf16[8,128,128]{2,1,0:T(8,128)(2,1)S(1)}, u32[]{:S(2)}, u32[]{:S(2)}) collective-permute-start(bf16[8,128,128]{2,1,0:T(8,128)(2,1)} %attend.1.refs_0_), channel_id=1, source_target_pairs={{2,0},{0,4},{4,8},{8,12},{12,14},{14,10},{10,6},{6,2},{3,1},{1,5},... | collective-permute-start | bytes 786440 | tf_op jit(solution)/shard_map/ppermute | solution.py:352
  7.7 1.0 %copy-done.3 = bf16[8,128,128]{2,1,0:T(8,128)(2,1)S(1)} copy-done((bf16[8,128,128]{2,1,0:T(8,128)(2,1)S(1)}, bf16[8,128,128]{2,1,0:T(8,128)(2,1)}, u32[]{:S(2)}) %copy-start.3) | copy-done | bytes 262168
  8.7 3.5 %dense.4 = (f32[128,1024]{1,0:T(8,128)S(1)}, f32[128,1024]{1,0:T(8,128)S(1)}, f32[128,1024]{1,0:T(8,128)S(1)}) custom-call(bf16[8,128,128]{2,1,0:T(8,128)(2,1)S(1)} %copy-done.3, bf16[1024,8192]{1,0:T(8,128)(2,1)} %refs_1_.7), custom_call_target="tpu_custom_call" | custom-call | flops 805306368 | bytes 6291456 | tf_op jit(solution)/shard_map/dense/pallas_call | solution.py:39
  12.1 2.0 %collective-permute-done.3.refs_2_ = bf16[8,128,128]{2,1,0:T(8,128)(2,1)S(1)} collective-permute-done((bf16[8,128,128]{2,1,0:T(8,128)(2,1)}, bf16[8,128,128]{2,1,0:T(8,128)(2,1)S(1)}, u32[]{:S(2)}, u32[]{:S(2)}) %collective-permute-start.3) | collective-permute-done | bytes 262176 | tf_op jit(solution)/shard_map/ppermute | solution.py:352
  14.1 1.8 %collective-permute-start.4 = (bf16[8,128,128]{2,1,0:T(8,128)(2,1)S(1)}, bf16[8,128,128]{2,1,0:T(8,128)(2,1)S(1)}, u32[]{:S(2)}, u32[]{:S(2)}) collective-permute-start(bf16[8,128,128]{2,1,0:T(8,128)(2,1)S(1)} %collective-permute-done.3.refs_2_), channel_id=1, source_target_pairs={{2,0},{0,4},{4,8},{8,12},{12,14},{14,10},{10,6},{6,2},{3,1},{1,5},... | collective-permute-start | bytes 786440 | tf_op jit(solution)/shard_map/ppermute | solution.py:352
  16.2 3.7 %dense.5 = (f32[128,1024]{1,0:T(8,128)S(1)}, f32[128,1024]{1,0:T(8,128)S(1)}, s32[128,128]{1,0:T(8,128)S(1)}, s32[64]{0:T(128)S(1)}) custom-call(bf16[8,128,128]{2,1,0:T(8,128)(2,1)S(1)} %copy-done.3, bf16[1024,8192]{1,0:T(8,128)(2,1)} %refs_1_.7, s32[1,128]{1,0:T(1,128)S(1)} %bitcast.19, s32[32]{0:T(128)S(1)} %copy-done.8, s32[4,16]{1,0:T(4,128)S(1)} %bitcast.18), custom_call_target="tpu_custom_call" | custom-call | flops 536870912 | bytes 4194304 | tf_op jit(solution)/shard_map/dense/pallas_call | solution.py:39
  19.9 1.7 %collective-permute-done.4.refs_4_ = bf16[8,128,128]{2,1,0:T(8,128)(2,1)S(1)} collective-permute-done((bf16[8,128,128]{2,1,0:T(8,128)(2,1)S(1)}, bf16[8,128,128]{2,1,0:T(8,128)(2,1)S(1)}, u32[]{:S(2)}, u32[]{:S(2)}) %collective-permute-start.4) | collective-permute-done | bytes 262176 | tf_op jit(solution)/shard_map/ppermute | solution.py:352
  21.6 1.5 %collective-permute-start.6 = (bf16[8,128,128]{2,1,0:T(8,128)(2,1)S(1)}, bf16[8,128,128]{2,1,0:T(8,128)(2,1)S(1)}, u32[]{:S(2)}, u32[]{:S(2)}) collective-permute-start(bf16[8,128,128]{2,1,0:T(8,128)(2,1)S(1)} %collective-permute-done.4.refs_4_), channel_id=1, source_target_pairs={{2,0},{0,4},{4,8},{8,12},{12,14},{14,10},{10,6},{6,2},{3,1},{1,5},... | collective-permute-start | bytes 786440 | tf_op jit(solution)/shard_map/ppermute | solution.py:352
  23.6 2.1 %fold_early.1 = (f32[128,256]{1,0:T(8,128)S(1)}, f32[64,128,128]{2,1,0:T(8,128)S(1)}) custom-call(bf16[8,128,128]{2,1,0:T(8,128)(2,1)S(1)} %copy-done.3, bf16[8,128,128]{2,1,0:T(8,128)(2,1)S(1)} %collective-permute-done.refs_1_, bf16[8,128,128]{2,1,0:T(8,128)(2,1)S(1)} %collective-permute-done.3.refs_2_, ...), custom_call_target="tpu_custom_call" | custom-call | flops 268435456 | bytes 4194304 | tf_op jit(solution)/shard_map/fold_early/pallas_call | solution.py:39
  25.8 2.6 %dense.6 = (f32[128,1024]{1,0:T(8,128)S(1)}, f32[128,1024]{1,0:T(8,128)S(1)}) custom-call(bf16[8,128,128]{2,1,0:T(8,128)(2,1)S(1)} %copy-done.3, bf16[1024,8192]{1,0:T(8,128)(2,1)} %refs_1_.7), custom_call_target="tpu_custom_call" | custom-call | flops 536870912 | bytes 4194304 | tf_op jit(solution)/shard_map/dense/pallas_call | solution.py:39
  28.4 1.5 %collective-permute-start.7 = (bf16[4,128,128]{2,1,0:T(8,128)(2,1)S(1)}, bf16[4,128,128]{2,1,0:T(8,128)(2,1)S(1)}, u32[]{:S(2)}, u32[]{:S(2)}) collective-permute-start(bf16[4,128,128]{2,1,0:T(8,128)(2,1)S(1)} %slice.7), channel_id=1, source_target_pairs={{2,0},{0,4},{4,8},{8,12},{12,14},{14,10},{10,6},{6,2},{3,1},{1,5},... | collective-permute-start | bytes 393224 | tf_op jit(solution)/shard_map/ppermute | solution.py:352
  29.9 0.6 collective-permute-start.5
  30.5 1.4 %fold_late.1 = (f32[128,256]{1,0:T(8,128)S(1)}, f32[64,128,128]{2,1,0:T(8,128)S(1)}) custom-call(bf16[8,128,128]{2,1,0:T(8,128)(2,1)S(1)} %collective-permute-done.2.refs_0_, bf16[8,128,128]{2,1,0:T(8,128)(2,1)S(1)} %collective-permute-done.6.refs_1_, s32[128,128]{1,0:T(8,128)S(1)} %get-tuple-element.63.refs_5_.refs_2_, bf16[256,8192]{1,0:T(8,128)(2,1)S(1)} %bitcast.16, ...), custom_call_target="tpu_custom_call" | custom-call | flops 134217728 | bytes 1048576 | tf_op jit(solution)/shard_map/fold_late/pallas_call | solution.py:39
  32.0 1.4 %collective-permute-done.7.refs_1_ = bf16[4,128,128]{2,1,0:T(8,128)(2,1)S(1)} collective-permute-done((bf16[4,128,128]{2,1,0:T(8,128)(2,1)S(1)}, bf16[4,128,128]{2,1,0:T(8,128)(2,1)S(1)}, u32[]{:S(2)}, u32[]{:S(2)}) %collective-permute-start.7) | collective-permute-done | bytes 131104 | tf_op jit(solution)/shard_map/ppermute | solution.py:352
  33.4 1.5 %collective-permute-done.5.refs_0_ = bf16[4,128,128]{2,1,0:T(8,128)(2,1)S(1)} collective-permute-done((bf16[4,128,128]{2,1,0:T(8,128)(2,1)S(1)}, bf16[4,128,128]{2,1,0:T(8,128)(2,1)S(1)}, u32[]{:S(2)}, u32[]{:S(2)}) %collective-permute-start.5) | collective-permute-done | bytes 131104 | tf_op jit(solution)/shard_map/ppermute | solution.py:352
  34.9 2.0 %finish.1 = (bf16[128,256]{1,0:T(8,128)(2,1)S(1)}, f32[8,128,128]{2,1,0:T(8,128)S(1)}, bf16[4,128,128]{2,1,0:T(8,128)(2,1)S(1)}, bf16[4,128,128]{2,1,0:T(8,128)(...) custom-call(bf16[4,128,128]{2,1,0:T(8,128)(2,1)S(1)} %collective-per, ...), custom_call_target="tpu_custom_call" | custom-call | flops 268435456 | bytes 2097152 | tf_op jit(solution)/shard_map/finish/pallas_call | solution.py:39
  37.0 1.6 %collective-permute-start.9 = (bf16[4,128,128]{2,1,0:T(8,128)(2,1)S(1)}, bf16[4,128,128]{2,1,0:T(8,128)(2,1)S(1)}, u32[]{:S(2)}, u32[]{:S(2)}) collective-permute-start(bf16[4,128,128]{2,1,0:T(8,128)(2,1)S(1)} %get-tuple-element.82), channel_id=1, source_target_pairs={{2,0},{0,4},{4,8},{8,12},{12,14},{14,10},{10,6},{6,2},{3,1},{1,5},... | collective-permute-start | bytes 393224 | tf_op jit(solution)/shard_map/ppermute | solution.py:352
  38.7 1.6 %collective-permute-start.16 = (bf16[4,128,128]{2,1,0:T(8,128)(2,1)S(1)}, bf16[4,128,128]{2,1,0:T(8,128)(2,1)S(1)}, u32[]{:S(2)}, u32[]{:S(2)}) collective-permute-start(bf16[4,128,128]{2,1,0:T(8,128)(2,1)S(1)} %convert_element_type.79), channel_id=1, source_target_pairs={{2,0},{0,4},{4,8},{8,12},{12,14},{14,10},{10,6},{6,2},{3,1},{1,5},... | collective-permute-start | bytes 393224 | tf_op jit(solution)/shard_map/ppermute | solution.py:352
  41.2 0.8 %collective-permute-done.9 = bf16[4,128,128]{2,1,0:T(8,128)(2,1)S(1)} collective-permute-done((bf16[4,128,128]{2,1,0:T(8,128)(2,1)S(1)}, bf16[4,128,128]{2,1,0:T(8,128)(2,1)S(1)}, u32[]{:S(2)}, u32[]{:S(2)}) %collective-permute-start.9) | collective-permute-done | bytes 131104 | tf_op jit(solution)/shard_map/ppermute | solution.py:352
  42.0 4.3 %collective-permute-done.8 = bf16[4,128,128]{2,1,0:T(8,128)(2,1)S(1)} collective-permute-done((bf16[4,128,128]{2,1,0:T(8,128)(2,1)S(1)}, bf16[4,128,128]{2,1,0:T(8,128)(2,1)S(1)}, u32[]{:S(2)}, u32[]{:S(2)}) %collective-permute-start.8) | collective-permute-done | bytes 131104 | tf_op jit(solution)/shard_map/ppermute | solution.py:352
  46.9 1.5 %collective-permute-start.10 = (bf16[4,128,128]{2,1,0:T(8,128)(2,1)S(1)}, bf16[4,128,128]{2,1,0:T(8,128)(2,1)S(1)}, u32[]{:S(2)}, u32[]{:S(2)}) collective-permute-start(bf16[4,128,128]{2,1,0:T(8,128)(2,1)S(1)} %add_convert_fusion.9), channel_id=1, source_target_pairs={{4,0},{8,4},{12,8},{14,12},{10,14},{6,10},{2,6},{0,2},{5,1},{9,5},... | collective-permute-start | bytes 393224 | tf_op jit(solution)/shard_map/ppermute | solution.py:352
  48.4 1.3 %part.3 = (f32[4,128,128]{2,1,0:T(8,128)S(1)}, f32[4,128,128]{2,1,0:T(8,128)S(1)}, f32[4,128,128]{2,1,0:T(8,128)S(1)}, f32[4,128,128]{2,1,0:T(8,128)S(1)}) custom-call(bf16[128,256]{1,0:T(8,128)(2,1)S(1)} %get-tuple-element.99.refs_0_, bf16[256,8192]{1,0:T(8,128)(2,1)S(1)} %bitcast.12, f32[64,128,128]{2,1,0:T(8,128)S(1)} %get-tuple-element.75.refs_10_.refs_2_, ...), custom_call_target="tpu_custom_call" | custom-call | flops 67108864 | bytes 1048576 | tf_op jit(solution)/shard_map/part/pallas_call | solution.py:39
  50.4 1.5 %collective-permute-start.17 = (bf16[4,128,128]{2,1,0:T(8,128)(2,1)S(1)}, bf16[4,128,128]{2,1,0:T(8,128)(2,1)S(1)}, u32[]{:S(2)}, u32[]{:S(2)}) collective-permute-start(bf16[4,128,128]{2,1,0:T(8,128)(2,1)S(1)} %add_convert_fusion.3), channel_id=1, source_target_pairs={{4,0},{8,4},{12,8},{14,12},{10,14},{6,10},{2,6},{0,2},{5,1},{9,5},... | collective-permute-start | bytes 393224 | tf_op jit(solution)/shard_map/ppermute | solution.py:352
  52.6 2.1 %collective-permute-start.12 = (bf16[4,128,128]{2,1,0:T(8,128)(2,1)S(1)}, bf16[4,128,128]{2,1,0:T(8,128)(2,1)S(1)}, u32[]{:S(2)}, u32[]{:S(2)}) collective-permute-start(bf16[4,128,128]{2,1,0:T(8,128)(2,1)S(1)} %add_convert_fusion.7), channel_id=1, source_target_pairs={{4,0},{8,4},{12,8},{14,12},{10,14},{6,10},{2,6},{0,2},{5,1},{9,5},... | collective-permute-start | bytes 393224 | tf_op jit(solution)/shard_map/ppermute | solution.py:352
  54.7 1.3 %part.4 = (f32[4,128,128]{2,1,0:T(8,128)S(1)}, f32[4,128,128]{2,1,0:T(8,128)S(1)}, f32[4,128,128]{2,1,0:T(8,128)S(1)}, f32[4,128,128]{2,1,0:T(8,128)S(1)}) custom-call(bf16[128,256]{1,0:T(8,128)(2,1)S(1)} %get-tuple-element.99.refs_0_, bf16[256,8192]{1,0:T(8,128)(2,1)S(1)} %bitcast.13, f32[64,128,128]{2,1,0:T(8,128)S(1)} %get-tuple-element.75.refs_10_.refs_2_, ...), custom_call_target="tpu_custom_call" | custom-call | flops 67108864 | bytes 1048576 | tf_op jit(solution)/shard_map/part/pallas_call | solution.py:39
  56.2 1.9 %collective-permute-start.19 = (bf16[4,128,128]{2,1,0:T(8,128)(2,1)S(1)}, bf16[4,128,128]{2,1,0:T(8,128)(2,1)S(1)}, u32[]{:S(2)}, u32[]{:S(2)}) collective-permute-start(bf16[4,128,128]{2,1,0:T(8,128)(2,1)S(1)} %add_convert_fusion.1), channel_id=1, source_target_pairs={{4,0},{8,4},{12,8},{14,12},{10,14},{6,10},{2,6},{0,2},{5,1},{9,5},... | collective-permute-start | bytes 393224 | tf_op jit(solution)/shard_map/ppermute | solution.py:352
  58.4 1.9 %collective-permute-start.14 = (bf16[4,128,128]{2,1,0:T(8,128)(2,1)S(1)}, bf16[4,128,128]{2,1,0:T(8,128)(2,1)S(1)}, u32[]{:S(2)}, u32[]{:S(2)}) collective-permute-start(bf16[4,128,128]{2,1,0:T(8,128)(2,1)S(1)} %add_convert_fusion.5), channel_id=1, source_target_pairs={{4,0},{8,4},{12,8},{14,12},{10,14},{6,10},{2,6},{0,2},{5,1},{9,5},... | collective-permute-start | bytes 393224 | tf_op jit(solution)/shard_map/ppermute | solution.py:352
  60.5 1.9 %dense.7.refs_7_ = f32[128,1024]{1,0:T(8,128)S(1)} custom-call(bf16[8,128,128]{2,1,0:T(8,128)(2,1)S(1)} %copy-done.3, bf16[1024,8192]{1,0:T(8,128)(2,1)} %refs_1_.7), custom_call_target="tpu_custom_call" | custom-call | flops 268435456 | bytes 2097152 | tf_op jit(solution)/shard_map/dense/pallas_call | solution.py:39
  62.4 1.0 %part.5 = (f32[4,128,128]{2,1,0:T(8,128)S(1)}, f32[4,128,128]{2,1,0:T(8,128)S(1)}) custom-call(bf16[128,256]{1,0:T(8,128)(2,1)S(1)} %get-tuple-element.99.refs_0_, bf16[256,8192]{1,0:T(8,128)(2,1)S(1)} %bitcast.14, f32[64,128,128]{2,1,0:T(8,128)S(1)} %get-tuple-element.75.refs_10_.refs_2_, f32[8,128,128]{2,1,0:T(8,128)S(1)} %get-tuple-element.86.refs_3_, ...), custom_call_target="tpu_custom_call" | custom-call | flops 67108864 | bytes 1048576 | tf_op jit(solution)/shard_map/part/pallas_call | solution.py:39
  63.4 1.9 %collective-permute-done.21.refs_5_ = bf16[4,128,128]{2,1,0:T(8,128)(2,1)S(1)} collective-permute-done((bf16[4,128,128]{2,1,0:T(8,128)(2,1)S(1)}, bf16[4,128,128]{2,1,0:T(8,128)(2,1)S(1)}, u32[]{:S(2)}, u32[]{:S(2)}) %collective-permute-start.21) | collective-permute-done | bytes 131104 | tf_op jit(solution)/shard_map/ppermute | solution.py:352
  65.2 0.8 %sum_up.1 = bf16[128,1024]{1,0:T(8,128)(2,1)} custom-call(f32[4,128,128]{2,1,0:T(8,128)S(1)} %get-tuple-element.101.refs_0_, f32[4,128,128]{2,1,0:T(8,128)S(1)} %get-tuple-element.102.refs_1_, bf16[4,128,128]{2,1,0:T(8,128)(2,1)S(1)} %collective-permute-done.14.refs_2_, bf16[4,128,128]{2,1,0:T(8,128)(2,1)S(1)} %collective-permute-done.19.refs_3_, ...), custom_call_target="tpu_custom_call" | custom-call | flops 1 | bytes 1 | tf_op jit(solution)/shard_map/sum_up/pallas_call | solution.py:39
  (56 shorter events, 4.3 us)
Async XLA Ops:
  0.0 16.1 %copy-start.6 = (s32[4,16,1]{1,2,0:T(1,128)S(1)}, s32[4,16,1]{1,2,0:T(1,128)}, u32[]{:S(2)}) copy-start(s32[4,16,1]{1,2,0:T(1,128)} %param.28) | copy-start | bytes 772
  0.0 16.1 %copy-start.7 = (s32[128]{0:T(128)S(1)}, s32[128]{0:T(128)}, u32[]{:S(2)}) copy-start(s32[128]{0:T(128)} %param.21) | copy-start | bytes 1540
  0.0 16.1 %copy-start.8 = (s32[32]{0:T(128)S(1)}, s32[32]{0:T(128)}, u32[]{:S(2)}) copy-start(s32[32]{0:T(128)} %refs_3_.1) | copy-start | bytes 388
  4.6 9.5 %collective-permute-start.3 = (bf16[8,128,128]{2,1,0:T(8,128)(2,1)}, bf16[8,128,128]{2,1,0:T(8,128)(2,1)S(1)}, u32[]{:S(2)}, u32[]{:S(2)}) collective-permute-start(bf16[8,128,128]{2,1,0:T(8,128)(2,1)} %attend.1.refs_0_), channel_id=1, source_target_pairs={{2,0},{0,4},{4,8},{8,12},{12,14},{14,10},{10,6},{6,2},{3,1},{1,5},... | collective-permute-start | bytes 786440 | tf_op jit(solution)/shard_map/ppermute | solution.py:352
  7.6 8.3 %collective-permute-start = (bf16[8,128,128]{2,1,0:T(8,128)(2,1)}, bf16[8,128,128]{2,1,0:T(8,128)(2,1)S(1)}, u32[]{:S(2)}, u32[]{:S(2)}) collective-permute-start(bf16[8,128,128]{2,1,0:T(8,128)(2,1)} %attend.1.refs_0_), channel_id=1, source_target_pairs={{4,0},{8,4},{12,8},{14,12},{10,14},{6,10},{2,6},{0,2},{5,1},{9,5},... | collective-permute-start | bytes 786440 | tf_op jit(solution)/shard_map/ppermute | solution.py:352
  7.7 1.0 %copy-start.3 = (bf16[8,128,128]{2,1,0:T(8,128)(2,1)S(1)}, bf16[8,128,128]{2,1,0:T(8,128)(2,1)}, u32[]{:S(2)}) copy-start(bf16[8,128,128]{2,1,0:T(8,128)(2,1)} %attend.1.refs_0_) | copy-start | bytes 786436
  14.1 7.5 %collective-permute-start.4 = (bf16[8,128,128]{2,1,0:T(8,128)(2,1)S(1)}, bf16[8,128,128]{2,1,0:T(8,128)(2,1)S(1)}, u32[]{:S(2)}, u32[]{:S(2)}) collective-permute-start(bf16[8,128,128]{2,1,0:T(8,128)(2,1)S(1)} %collective-permute-done.3.refs_2_), channel_id=1, source_target_pairs={{2,0},{0,4},{4,8},{8,12},{12,14},{14,10},{10,6},{6,2},{3,1},{1,5},... | collective-permute-start | bytes 786440 | tf_op jit(solution)/shard_map/ppermute | solution.py:352
  15.9 7.2 %collective-permute-start.1 = (bf16[8,128,128]{2,1,0:T(8,128)(2,1)S(1)}, bf16[8,128,128]{2,1,0:T(8,128)(2,1)S(1)}, u32[]{:S(2)}, u32[]{:S(2)}) collective-permute-start(bf16[8,128,128]{2,1,0:T(8,128)(2,1)S(1)} %collective-permute-done.refs_1_), channel_id=1, source_target_pairs={{4,0},{8,4},{12,8},{14,12},{10,14},{6,10},{2,6},{0,2},{5,1},{9,5},... | collective-permute-start | bytes 786440 | tf_op jit(solution)/shard_map/ppermute | solution.py:352
  16.1 7.5 %copy-start.1 = (bf16[4,8192,64]{1,2,0:T(8,128)(2,1)S(1)}, bf16[4,8192,64]{1,2,0:T(8,128)(2,1)}, u32[]{:S(2)}) copy-start(bf16[4,8192,64]{1,2,0:T(8,128)(2,1)} %param.24) | copy-start | bytes 12582916
  16.1 7.5 %copy-start.2 = (bf16[4,16,128,128]{3,2,1,0:T(8,128)(2,1)S(1)}, bf16[4,16,128,128]{3,2,1,0:T(8,128)(2,1)}, u32[]{:S(2)}) copy-start(bf16[4,16,128,128]{3,2,1,0:T(8,128)(2,1)} %refs_4_.6) | copy-start | bytes 6291460
  16.2 7.5 %copy-start.4 = (f32[4,16]{1,0:T(4,128)S(1)}, f32[4,16]{1,0:T(4,128)}, u32[]{:S(2)}) copy-start(f32[4,16]{1,0:T(4,128)} %refs_4_.9) | copy-start | bytes 772
  16.2 7.5 %copy-start.5 = (s32[4,16]{1,0:T(4,128)S(1)}, s32[4,16]{1,0:T(4,128)}, u32[]{:S(2)}) copy-start(s32[4,16]{1,0:T(4,128)} %refs_5_.9) | copy-start | bytes 772
  21.6 6.8 %collective-permute-start.6 = (bf16[8,128,128]{2,1,0:T(8,128)(2,1)S(1)}, bf16[8,128,128]{2,1,0:T(8,128)(2,1)S(1)}, u32[]{:S(2)}, u32[]{:S(2)}) collective-permute-start(bf16[8,128,128]{2,1,0:T(8,128)(2,1)S(1)} %collective-permute-done.4.refs_4_), channel_id=1, source_target_pairs={{2,0},{0,4},{4,8},{8,12},{12,14},{14,10},{10,6},{6,2},{3,1},{1,5},... | collective-permute-start | bytes 786440 | tf_op jit(solution)/shard_map/ppermute | solution.py:352
  23.1 6.8 %collective-permute-start.2 = (bf16[8,128,128]{2,1,0:T(8,128)(2,1)S(1)}, bf16[8,128,128]{2,1,0:T(8,128)(2,1)S(1)}, u32[]{:S(2)}, u32[]{:S(2)}) collective-permute-start(bf16[8,128,128]{2,1,0:T(8,128)(2,1)S(1)} %collective-permute-done.1.refs_3_), channel_id=1, source_target_pairs={{4,0},{8,4},{12,8},{14,12},{10,14},{6,10},{2,6},{0,2},{5,1},{9,5},... | collective-permute-start | bytes 786440 | tf_op jit(solution)/shard_map/ppermute | solution.py:352
  28.4 5.0 %collective-permute-start.7 = (bf16[4,128,128]{2,1,0:T(8,128)(2,1)S(1)}, bf16[4,128,128]{2,1,0:T(8,128)(2,1)S(1)}, u32[]{:S(2)}, u32[]{:S(2)}) collective-permute-start(bf16[4,128,128]{2,1,0:T(8,128)(2,1)S(1)} %slice.7), channel_id=1, source_target_pairs={{2,0},{0,4},{4,8},{8,12},{12,14},{14,10},{10,6},{6,2},{3,1},{1,5},... | collective-permute-start | bytes 393224 | tf_op jit(solution)/shard_map/ppermute | solution.py:352
  29.9 5.0 %collective-permute-start.5 = (bf16[4,128,128]{2,1,0:T(8,128)(2,1)S(1)}, bf16[4,128,128]{2,1,0:T(8,128)(2,1)S(1)}, u32[]{:S(2)}, u32[]{:S(2)}) collective-permute-start(bf16[4,128,128]{2,1,0:T(8,128)(2,1)S(1)} %slice.6), channel_id=1, source_target_pairs={{4,0},{8,4},{12,8},{14,12},{10,14},{6,10},{2,6},{0,2},{5,1},{9,5},... | collective-permute-start | bytes 393224 | tf_op jit(solution)/shard_map/ppermute | solution.py:352
  30.5 4.4 %copy-start = (bf16[4,64,8192]{2,1,0:T(8,128)(2,1)S(1)}, bf16[4,64,8192]{2,1,0:T(8,128)(2,1)}, u32[]{:S(2)}) copy-start(bf16[4,64,8192]{2,1,0:T(8,128)(2,1)} %param.25) | copy-start | bytes 12582916
  37.0 5.0 %collective-permute-start.9 = (bf16[4,128,128]{2,1,0:T(8,128)(2,1)S(1)}, bf16[4,128,128]{2,1,0:T(8,128)(2,1)S(1)}, u32[]{:S(2)}, u32[]{:S(2)}) collective-permute-start(bf16[4,128,128]{2,1,0:T(8,128)(2,1)S(1)} %get-tuple-element.82), channel_id=1, source_target_pairs={{2,0},{0,4},{4,8},{8,12},{12,14},{14,10},{10,6},{6,2},{3,1},{1,5},... | collective-permute-start | bytes 393224 | tf_op jit(solution)/shard_map/ppermute | solution.py:352
  38.7 11.1 %collective-permute-start.16 = (bf16[4,128,128]{2,1,0:T(8,128)(2,1)S(1)}, bf16[4,128,128]{2,1,0:T(8,128)(2,1)S(1)}, u32[]{:S(2)}, u32[]{:S(2)}) collective-permute-start(bf16[4,128,128]{2,1,0:T(8,128)(2,1)S(1)} %convert_element_type.79), channel_id=1, source_target_pairs={{2,0},{0,4},{4,8},{8,12},{12,14},{14,10},{10,6},{6,2},{3,1},{1,5},... | collective-permute-start | bytes 393224 | tf_op jit(solution)/shard_map/ppermute | solution.py:352
  40.3 6.0 %collective-permute-start.8 = (bf16[4,128,128]{2,1,0:T(8,128)(2,1)S(1)}, bf16[4,128,128]{2,1,0:T(8,128)(2,1)S(1)}, u32[]{:S(2)}, u32[]{:S(2)}) collective-permute-start(bf16[4,128,128]{2,1,0:T(8,128)(2,1)S(1)} %get-tuple-element.80), channel_id=1, source_target_pairs={{4,0},{8,4},{12,8},{14,12},{10,14},{6,10},{2,6},{0,2},{5,1},{9,5},... | collective-permute-start | bytes 393224 | tf_op jit(solution)/shard_map/ppermute | solution.py:352
  40.7 9.1 %collective-permute-start.15 = (bf16[4,128,128]{2,1,0:T(8,128)(2,1)S(1)}, bf16[4,128,128]{2,1,0:T(8,128)(2,1)S(1)}, u32[]{:S(2)}, u32[]{:S(2)}) collective-permute-start(bf16[4,128,128]{2,1,0:T(8,128)(2,1)S(1)} %convert_element_type.78), channel_id=1, source_target_pairs={{4,0},{8,4},{12,8},{14,12},{10,14},{6,10},{2,6},{0,2},{5,1},{9,5},... | collective-permute-start | bytes 393224 | tf_op jit(solution)/shard_map/ppermute | solution.py:352
  46.4 5.6 %collective-permute-start.11 = (bf16[4,128,128]{2,1,0:T(8,128)(2,1)S(1)}, bf16[4,128,128]{2,1,0:T(8,128)(2,1)S(1)}, u32[]{:S(2)}, u32[]{:S(2)}) collective-permute-start(bf16[4,128,128]{2,1,0:T(8,128)(2,1)S(1)} %add_convert_fusion.8), channel_id=1, source_target_pairs={{2,0},{0,4},{4,8},{8,12},{12,14},{14,10},{10,6},{6,2},{3,1},{1,5},... | collective-permute-start | bytes 393224 | tf_op jit(solution)/shard_map/ppermute | solution.py:352
  46.9 5.2 %collective-permute-start.10 = (bf16[4,128,128]{2,1,0:T(8,128)(2,1)S(1)}, bf16[4,128,128]{2,1,0:T(8,128)(2,1)S(1)}, u32[]{:S(2)}, u32[]{:S(2)}) collective-permute-start(bf16[4,128,128]{2,1,0:T(8,128)(2,1)S(1)} %add_convert_fusion.9), channel_id=1, source_target_pairs={{4,0},{8,4},{12,8},{14,12},{10,14},{6,10},{2,6},{0,2},{5,1},{9,5},... | collective-permute-start | bytes 393224 | tf_op jit(solution)/shard_map/ppermute | solution.py:352
  49.9 6.2 %collective-permute-start.18 = (bf16[4,128,128]{2,1,0:T(8,128)(2,1)S(1)}, bf16[4,128,128]{2,1,0:T(8,128)(2,1)S(1)}, u32[]{:S(2)}, u32[]{:S(2)}) collective-permute-start(bf16[4,128,128]{2,1,0:T(8,128)(2,1)S(1)} %add_convert_fusion.2), channel_id=1, source_target_pairs={{2,0},{0,4},{4,8},{8,12},{12,14},{14,10},{10,6},{6,2},{3,1},{1,5},... | collective-permute-start | bytes 393224 | tf_op jit(solution)/shard_map/ppermute | solution.py:352
  50.4 5.7 %collective-permute-start.17 = (bf16[4,128,128]{2,1,0:T(8,128)(2,1)S(1)}, bf16[4,128,128]{2,1,0:T(8,128)(2,1)S(1)}, u32[]{:S(2)}, u32[]{:S(2)}) collective-permute-start(bf16[4,128,128]{2,1,0:T(8,128)(2,1)S(1)} %add_convert_fusion.3), channel_id=1, source_target_pairs={{4,0},{8,4},{12,8},{14,12},{10,14},{6,10},{2,6},{0,2},{5,1},{9,5},... | collective-permute-start | bytes 393224 | tf_op jit(solution)/shard_map/ppermute | solution.py:352
  52.1 6.2 %collective-permute-start.13 = (bf16[4,128,128]{2,1,0:T(8,128)(2,1)S(1)}, bf16[4,128,128]{2,1,0:T(8,128)(2,1)S(1)}, u32[]{:S(2)}, u32[]{:S(2)}) collective-permute-start(bf16[4,128,128]{2,1,0:T(8,128)(2,1)S(1)} %add_convert_fusion.6), channel_id=1, source_target_pairs={{2,0},{0,4},{4,8},{8,12},{12,14},{14,10},{10,6},{6,2},{3,1},{1,5},... | collective-permute-start | bytes 393224 | tf_op jit(solution)/shard_map/ppermute | solution.py:352
  52.6 5.7 %collective-permute-start.12 = (bf16[4,128,128]{2,1,0:T(8,128)(2,1)S(1)}, bf16[4,128,128]{2,1,0:T(8,128)(2,1)S(1)}, u32[]{:S(2)}, u32[]{:S(2)}) collective-permute-start(bf16[4,128,128]{2,1,0:T(8,128)(2,1)S(1)} %add_convert_fusion.7), channel_id=1, source_target_pairs={{4,0},{8,4},{12,8},{14,12},{10,14},{6,10},{2,6},{0,2},{5,1},{9,5},... | collective-permute-start | bytes 393224 | tf_op jit(solution)/shard_map/ppermute | solution.py:352
  56.2 7.2 %collective-permute-start.19 = (bf16[4,128,128]{2,1,0:T(8,128)(2,1)S(1)}, bf16[4,128,128]{2,1,0:T(8,128)(2,1)S(1)}, u32[]{:S(2)}, u32[]{:S(2)}) collective-permute-start(bf16[4,128,128]{2,1,0:T(8,128)(2,1)S(1)} %add_convert_fusion.1), channel_id=1, source_target_pairs={{4,0},{8,4},{12,8},{14,12},{10,14},{6,10},{2,6},{0,2},{5,1},{9,5},... | collective-permute-start | bytes 393224 | tf_op jit(solution)/shard_map/ppermute | solution.py:352
  58.1 5.3 %collective-permute-start.20 = (bf16[4,128,128]{2,1,0:T(8,128)(2,1)S(1)}, bf16[4,128,128]{2,1,0:T(8,128)(2,1)S(1)}, u32[]{:S(2)}, u32[]{:S(2)}) collective-permute-start(bf16[4,128,128]{2,1,0:T(8,128)(2,1)S(1)} %add_convert_fusion), channel_id=1, source_target_pairs={{2,0},{0,4},{4,8},{8,12},{12,14},{14,10},{10,6},{6,2},{3,1},{1,5},... | collective-permute-start | bytes 393224 | tf_op jit(solution)/shard_map/ppermute | solution.py:352
  58.4 5.0 %collective-permute-start.14 = (bf16[4,128,128]{2,1,0:T(8,128)(2,1)S(1)}, bf16[4,128,128]{2,1,0:T(8,128)(2,1)S(1)}, u32[]{:S(2)}, u32[]{:S(2)}) collective-permute-start(bf16[4,128,128]{2,1,0:T(8,128)(2,1)S(1)} %add_convert_fusion.5), channel_id=1, source_target_pairs={{4,0},{8,4},{12,8},{14,12},{10,14},{6,10},{2,6},{0,2},{5,1},{9,5},... | collective-permute-start | bytes 393224 | tf_op jit(solution)/shard_map/ppermute | solution.py:352
  60.3 5.0 %collective-permute-start.21 = (bf16[4,128,128]{2,1,0:T(8,128)(2,1)S(1)}, bf16[4,128,128]{2,1,0:T(8,128)(2,1)S(1)}, u32[]{:S(2)}, u32[]{:S(2)}) collective-permute-start(bf16[4,128,128]{2,1,0:T(8,128)(2,1)S(1)} %add_convert_fusion.4), channel_id=1, source_target_pairs={{2,0},{0,4},{4,8},{8,12},{12,14},{14,10},{10,6},{6,2},{3,1},{1,5},... | collective-permute-start | bytes 393224 | tf_op jit(solution)/shard_map/ppermute | solution.py:352

commit v13 on v12

--- a/solution.py
+++ b/solution.py
@@ -397,7 +397,7 @@
         moved=MIB,
     )
     extras = shape((slots * CAP, rows, side), F32)
-    first = wanted[:3]
+    first = wanted[:1]
     part_half = shape((heads // 2, rows, side), F32)
     low, extra, front, back, *sums = call(
         functools.partial(finish_kernel, first, count),
@@ -440,7 +440,7 @@
             far = lax.optimization_barrier(
                 (joined(parts[count - distance][0], far[0]), joined(parts[distance][1], far[1]))
             )
-        if nearer and nearer < half - 1:
+        if nearer:
             parts_for([nearer, count - nearer], after(low, *far))
         if not nearer:
             dense_for([0], after(attended, *far))

time: 66.2 us -> 65.4 us (0.988)
  waiting for transfers between devices: 13.8 us -> 12.7 us
  Pallas kernels: 26.2 us -> 26.9 us
    ppermute x22, waiting for transfers between devices: 13.8 us -> 12.7 us  [come(): lax.ppermute(value, 'tp', [(ring[(i + distance) % count], ring[i]) for i...]
    pallas_call x12 -> x13, Pallas kernels: 26.2 us -> 26.9 us  [call(): pl.pallas_call(kernel, out_shape=outs, in_specs=specs, out_specs=out_spec...]
  transfers between devices with their start and end apart: 22 -> 22, of which waited for: 9 -> 8; matrix products, arithmetic and copies ran while one was open for 1% -> 1% of each run, Pallas kernels for 29% -> 31%
where the time goes in v13:
time: 65.4 us; the launch traced here: 65.2 us
  Pallas kernels  26.9 us (41%)
  starting transfers between devices  23.8 us (36%)
  waiting for transfers between devices  12.7 us (19%)
  local copies, waits for them, and re-layouts  1.07 us (2%)
    pallas_call x13, Pallas kernels, call(): pl.pallas_call(kernel, out_shape=outs, in_specs=specs, out_specs=out_spec...  26.9 us
    ppermute x22, starting transfers between devices, come(): lax.ppermute(value, 'tp', [(ring[(i + distance) % count], ring[i]) for i...  23.8 us
    ppermute x22, waiting for transfers between devices, come(): lax.ppermute(value, 'tp', [(ring[(i + distance) % count], ring[i]) for i...  12.7 us
  transfers between devices with their start and end apart: 22, of which 8 were waited for; matrix products, arithmetic and copies ran while one was open for 1% of the time, Pallas kernels for 31%

profile of v13, /device:TPU:0, one launch (start us, length us, event | category | flops | bytes accessed | tf_op | source)
XLA Modules:
  0.0 65.2 jit_solution(9712762801633211251)
XLA Ops:
  0.0 4.6 %attend.1.refs_0_ = bf16[8,128,128]{2,1,0:T(8,128)(2,1)} custom-call(bf16[128,1024]{1,0:T(8,128)(2,1)} %query_hbm.1, bf16[4096,128]{1,0:T(8,128)(2,1)} %bitcast.21, bf16[4096,128]{1,0:T(8,128)(2,1)} %bitcast.22, bf16[128,128]{1,0:T(8,128)(2,1)} %bitcast.23, bf16[128,128]{1,0:T(8,128)(2,1)} %bitcast.24, s32[1,128]{1,0:T(1,128)} %bitcast.25), custom_call_target="tpu_custom_call" | custom-call | tf_op jit(solution)/shard_map/attend/pallas_call | solution.py:39
  4.6 3.1 %collective-permute-start.3 = (bf16[8,128,128]{2,1,0:T(8,128)(2,1)}, bf16[8,128,128]{2,1,0:T(8,128)(2,1)S(1)}, u32[]{:S(2)}, u32[]{:S(2)}) collective-permute-start(bf16[8,128,128]{2,1,0:T(8,128)(2,1)} %attend.1.refs_0_), channel_id=1, source_target_pairs={{2,0},{0,4},{4,8},{8,12},{12,14},{14,10},{10,6},{6,2},{3,1},{1,5},... | collective-permute-start | bytes 786440 | tf_op jit(solution)/shard_map/ppermute | solution.py:352
  7.7 1.0 %copy-done.3 = bf16[8,128,128]{2,1,0:T(8,128)(2,1)S(1)} copy-done((bf16[8,128,128]{2,1,0:T(8,128)(2,1)S(1)}, bf16[8,128,128]{2,1,0:T(8,128)(2,1)}, u32[]{:S(2)}) %copy-start.3) | copy-done | bytes 262168
  8.7 3.5 %dense.4 = (f32[128,1024]{1,0:T(8,128)S(1)}, f32[128,1024]{1,0:T(8,128)S(1)}, f32[128,1024]{1,0:T(8,128)S(1)}) custom-call(bf16[8,128,128]{2,1,0:T(8,128)(2,1)S(1)} %copy-done.3, bf16[1024,8192]{1,0:T(8,128)(2,1)} %refs_1_.7), custom_call_target="tpu_custom_call" | custom-call | flops 805306368 | bytes 6291456 | tf_op jit(solution)/shard_map/dense/pallas_call | solution.py:39
  12.1 2.0 %collective-permute-done.3.refs_2_ = bf16[8,128,128]{2,1,0:T(8,128)(2,1)S(1)} collective-permute-done((bf16[8,128,128]{2,1,0:T(8,128)(2,1)}, bf16[8,128,128]{2,1,0:T(8,128)(2,1)S(1)}, u32[]{:S(2)}, u32[]{:S(2)}) %collective-permute-start.3) | collective-permute-done | bytes 262176 | tf_op jit(solution)/shard_map/ppermute | solution.py:352
  14.1 1.8 %collective-permute-start.4 = (bf16[8,128,128]{2,1,0:T(8,128)(2,1)S(1)}, bf16[8,128,128]{2,1,0:T(8,128)(2,1)S(1)}, u32[]{:S(2)}, u32[]{:S(2)}) collective-permute-start(bf16[8,128,128]{2,1,0:T(8,128)(2,1)S(1)} %collective-permute-done.3.refs_2_), channel_id=1, source_target_pairs={{2,0},{0,4},{4,8},{8,12},{12,14},{14,10},{10,6},{6,2},{3,1},{1,5},... | collective-permute-start | bytes 786440 | tf_op jit(solution)/shard_map/ppermute | solution.py:352
  16.2 3.7 %dense.5 = (f32[128,1024]{1,0:T(8,128)S(1)}, f32[128,1024]{1,0:T(8,128)S(1)}, s32[128,128]{1,0:T(8,128)S(1)}, s32[64]{0:T(128)S(1)}) custom-call(bf16[8,128,128]{2,1,0:T(8,128)(2,1)S(1)} %copy-done.3, bf16[1024,8192]{1,0:T(8,128)(2,1)} %refs_1_.7, s32[1,128]{1,0:T(1,128)S(1)} %bitcast.20, s32[32]{0:T(128)S(1)} %copy-done.9, s32[4,16]{1,0:T(4,128)S(1)} %bitcast.19), custom_call_target="tpu_custom_call" | custom-call | flops 536870912 | bytes 4194304 | tf_op jit(solution)/shard_map/dense/pallas_call | solution.py:39
  19.9 1.7 %collective-permute-done.4.refs_4_ = bf16[8,128,128]{2,1,0:T(8,128)(2,1)S(1)} collective-permute-done((bf16[8,128,128]{2,1,0:T(8,128)(2,1)S(1)}, bf16[8,128,128]{2,1,0:T(8,128)(2,1)S(1)}, u32[]{:S(2)}, u32[]{:S(2)}) %collective-permute-start.4) | collective-permute-done | bytes 262176 | tf_op jit(solution)/shard_map/ppermute | solution.py:352
  21.6 1.5 %collective-permute-start.6 = (bf16[8,128,128]{2,1,0:T(8,128)(2,1)S(1)}, bf16[8,128,128]{2,1,0:T(8,128)(2,1)S(1)}, u32[]{:S(2)}, u32[]{:S(2)}) collective-permute-start(bf16[8,128,128]{2,1,0:T(8,128)(2,1)S(1)} %collective-permute-done.4.refs_4_), channel_id=1, source_target_pairs={{2,0},{0,4},{4,8},{8,12},{12,14},{14,10},{10,6},{6,2},{3,1},{1,5},... | collective-permute-start | bytes 786440 | tf_op jit(solution)/shard_map/ppermute | solution.py:352
  23.6 2.1 %fold_early.1 = (f32[128,256]{1,0:T(8,128)S(1)}, f32[64,128,128]{2,1,0:T(8,128)S(1)}) custom-call(bf16[8,128,128]{2,1,0:T(8,128)(2,1)S(1)} %copy-done.3, bf16[8,128,128]{2,1,0:T(8,128)(2,1)S(1)} %collective-permute-done.refs_1_, bf16[8,128,128]{2,1,0:T(8,128)(2,1)S(1)} %collective-permute-done.3.refs_2_, ...), custom_call_target="tpu_custom_call" | custom-call | flops 268435456 | bytes 4194304 | tf_op jit(solution)/shard_map/fold_early/pallas_call | solution.py:39
  25.8 2.6 %dense.6 = (f32[128,1024]{1,0:T(8,128)S(1)}, f32[128,1024]{1,0:T(8,128)S(1)}) custom-call(bf16[8,128,128]{2,1,0:T(8,128)(2,1)S(1)} %copy-done.3, bf16[1024,8192]{1,0:T(8,128)(2,1)} %refs_1_.7), custom_call_target="tpu_custom_call" | custom-call | flops 536870912 | bytes 4194304 | tf_op jit(solution)/shard_map/dense/pallas_call | solution.py:39
  28.4 1.5 %collective-permute-start.7 = (bf16[4,128,128]{2,1,0:T(8,128)(2,1)S(1)}, bf16[4,128,128]{2,1,0:T(8,128)(2,1)S(1)}, u32[]{:S(2)}, u32[]{:S(2)}) collective-permute-start(bf16[4,128,128]{2,1,0:T(8,128)(2,1)S(1)} %slice.7), channel_id=1, source_target_pairs={{2,0},{0,4},{4,8},{8,12},{12,14},{14,10},{10,6},{6,2},{3,1},{1,5},... | collective-permute-start | bytes 393224 | tf_op jit(solution)/shard_map/ppermute | solution.py:352
  30.5 1.4 %fold_late.1 = (f32[128,256]{1,0:T(8,128)S(1)}, f32[64,128,128]{2,1,0:T(8,128)S(1)}) custom-call(bf16[8,128,128]{2,1,0:T(8,128)(2,1)S(1)} %collective-permute-done.2.refs_0_, bf16[8,128,128]{2,1,0:T(8,128)(2,1)S(1)} %collective-permute-done.6.refs_1_, s32[128,128]{1,0:T(8,128)S(1)} %get-tuple-element.64.refs_5_.refs_2_, bf16[256,8192]{1,0:T(8,128)(2,1)S(1)} %bitcast.17, ...), custom_call_target="tpu_custom_call" | custom-call | flops 134217728 | bytes 1048576 | tf_op jit(solution)/shard_map/fold_late/pallas_call | solution.py:39
  32.0 1.4 %collective-permute-done.7.refs_1_ = bf16[4,128,128]{2,1,0:T(8,128)(2,1)S(1)} collective-permute-done((bf16[4,128,128]{2,1,0:T(8,128)(2,1)S(1)}, bf16[4,128,128]{2,1,0:T(8,128)(2,1)S(1)}, u32[]{:S(2)}, u32[]{:S(2)}) %collective-permute-start.7) | collective-permute-done | bytes 131104 | tf_op jit(solution)/shard_map/ppermute | solution.py:352
  33.4 1.5 %collective-permute-done.5.refs_0_ = bf16[4,128,128]{2,1,0:T(8,128)(2,1)S(1)} collective-permute-done((bf16[4,128,128]{2,1,0:T(8,128)(2,1)S(1)}, bf16[4,128,128]{2,1,0:T(8,128)(2,1)S(1)}, u32[]{:S(2)}, u32[]{:S(2)}) %collective-permute-start.5) | collective-permute-done | bytes 131104 | tf_op jit(solution)/shard_map/ppermute | solution.py:352
  34.9 1.4 %finish.1 = (bf16[128,256]{1,0:T(8,128)(2,1)S(1)}, f32[8,128,128]{2,1,0:T(8,128)S(1)}, bf16[4,128,128]{2,1,0:T(8,128)(2,1)S(1)}, bf16[4,128,128]{2,1,0:T(8,128)(2,1)S(1)}) custom-call(bf16[4,128,128]{2,1,0:T(8,128)(2,1)S(1)} %collective-permute-done.5.refs_0_, bf16[4,128,128]{2,1,0:T(8,128)(2,1)S(1)} %collective-permute-done.7.refs_1_, ...), custom_call_target="tpu_custom_call" | custom-call | flops 268435456 | bytes 2097152 | tf_op jit(solution)/shard_map/finish/pallas_call | solution.py:39
  36.3 1.6 %collective-permute-start.9 = (bf16[4,128,128]{2,1,0:T(8,128)(2,1)S(1)}, bf16[4,128,128]{2,1,0:T(8,128)(2,1)S(1)}, u32[]{:S(2)}, u32[]{:S(2)}) collective-permute-start(bf16[4,128,128]{2,1,0:T(8,128)(2,1)S(1)} %get-tuple-element.79), channel_id=1, source_target_pairs={{2,0},{0,4},{4,8},{8,12},{12,14},{14,10},{10,6},{6,2},{3,1},{1,5},... | collective-permute-start | bytes 393224 | tf_op jit(solution)/shard_map/ppermute | solution.py:352
  38.4 1.3 %part.4 = (f32[4,128,128]{2,1,0:T(8,128)S(1)}, f32[4,128,128]{2,1,0:T(8,128)S(1)}, f32[4,128,128]{2,1,0:T(8,128)S(1)}, f32[4,128,128]{2,1,0:T(8,128)S(1)}) custom-call(bf16[128,256]{1,0:T(8,128)(2,1)S(1)} %get-tuple-element.101.refs_0_, bf16[256,8192]{1,0:T(8,128)(2,1)S(1)} %bitcast.12, f32[64,128,128]{2,1,0:T(8,128)S(1)} %get-tuple-element.76.refs_10_.refs_2_, ...), custom_call_target="tpu_custom_call" | custom-call | flops 67108864 | bytes 1048576 | tf_op jit(solution)/shard_map/part/pallas_call | solution.py:39
  39.8 1.6 %collective-permute-start.16 = (bf16[4,128,128]{2,1,0:T(8,128)(2,1)S(1)}, bf16[4,128,128]{2,1,0:T(8,128)(2,1)S(1)}, u32[]{:S(2)}, u32[]{:S(2)}) collective-permute-start(bf16[4,128,128]{2,1,0:T(8,128)(2,1)S(1)} %convert_element_type.79), channel_id=1, source_target_pairs={{2,0},{0,4},{4,8},{8,12},{12,14},{14,10},{10,6},{6,2},{3,1},{1,5},... | collective-permute-start | bytes 393224 | tf_op jit(solution)/shard_map/ppermute | solution.py:352
  42.5 1.8 %collective-permute-done.8 = bf16[4,128,128]{2,1,0:T(8,128)(2,1)S(1)} collective-permute-done((bf16[4,128,128]{2,1,0:T(8,128)(2,1)S(1)}, bf16[4,128,128]{2,1,0:T(8,128)(2,1)S(1)}, u32[]{:S(2)}, u32[]{:S(2)}) %collective-permute-start.8) | collective-permute-done | bytes 131104 | tf_op jit(solution)/shard_map/ppermute | solution.py:352
  44.4 1.6 %collective-permute-start.11 = (bf16[4,128,128]{2,1,0:T(8,128)(2,1)S(1)}, bf16[4,128,128]{2,1,0:T(8,128)(2,1)S(1)}, u32[]{:S(2)}, u32[]{:S(2)}) collective-permute-start(bf16[4,128,128]{2,1,0:T(8,128)(2,1)S(1)} %add_convert_fusion.8), channel_id=1, source_target_pairs={{2,0},{0,4},{4,8},{8,12},{12,14},{14,10},{10,6},{6,2},{3,1},{1,5},... | collective-permute-start | bytes 393224 | tf_op jit(solution)/shard_map/ppermute | solution.py:352
  46.4 1.3 %part.5 = (f32[4,128,128]{2,1,0:T(8,128)S(1)}, f32[4,128,128]{2,1,0:T(8,128)S(1)}, f32[4,128,128]{2,1,0:T(8,128)S(1)}, f32[4,128,128]{2,1,0:T(8,128)S(1)}) custom-call(bf16[128,256]{1,0:T(8,128)(2,1)S(1)} %get-tuple-element.101.refs_0_, bf16[256,8192]{1,0:T(8,128)(2,1)S(1)} %bitcast.13, f32[64,128,128]{2,1,0:T(8,128)S(1)} %get-tuple-element.76.refs_10_.refs_2_, ...), custom_call_target="tpu_custom_call" | custom-call | flops 67108864 | bytes 1048576 | tf_op jit(solution)/shard_map/part/pallas_call | solution.py:39
  47.9 1.6 %collective-permute-start.18 = (bf16[4,128,128]{2,1,0:T(8,128)(2,1)S(1)}, bf16[4,128,128]{2,1,0:T(8,128)(2,1)S(1)}, u32[]{:S(2)}, u32[]{:S(2)}) collective-permute-start(bf16[4,128,128]{2,1,0:T(8,128)(2,1)S(1)} %add_convert_fusion.2), channel_id=1, source_target_pairs={{2,0},{0,4},{4,8},{8,12},{12,14},{14,10},{10,6},{6,2},{3,1},{1,5},... | collective-permute-start | bytes 393224 | tf_op jit(solution)/shard_map/ppermute | solution.py:352
  50.0 2.3 %collective-permute-done.10 = bf16[4,128,128]{2,1,0:T(8,128)(2,1)S(1)} collective-permute-done((bf16[4,128,128]{2,1,0:T(8,128)(2,1)S(1)}, bf16[4,128,128]{2,1,0:T(8,128)(2,1)S(1)}, u32[]{:S(2)}, u32[]{:S(2)}) %collective-permute-start.10) | collective-permute-done | bytes 131104 | tf_op jit(solution)/shard_map/ppermute | solution.py:352
  52.3 2.0 %collective-permute-start.12 = (bf16[4,128,128]{2,1,0:T(8,128)(2,1)S(1)}, bf16[4,128,128]{2,1,0:T(8,128)(2,1)S(1)}, u32[]{:S(2)}, u32[]{:S(2)}) collective-permute-start(bf16[4,128,128]{2,1,0:T(8,128)(2,1)S(1)} %add_convert_fusion.7), channel_id=1, source_target_pairs={{4,0},{8,4},{12,8},{14,12},{10,14},{6,10},{2,6},{0,2},{5,1},{9,5},... | collective-permute-start | bytes 393224 | tf_op jit(solution)/shard_map/ppermute | solution.py:352
  54.4 1.3 %part.6 = (f32[4,128,128]{2,1,0:T(8,128)S(1)}, f32[4,128,128]{2,1,0:T(8,128)S(1)}, f32[4,128,128]{2,1,0:T(8,128)S(1)}, f32[4,128,128]{2,1,0:T(8,128)S(1)}) custom-call(bf16[128,256]{1,0:T(8,128)(2,1)S(1)} %get-tuple-element.101.refs_0_, bf16[256,8192]{1,0:T(8,128)(2,1)S(1)} %bitcast.14, f32[64,128,128]{2,1,0:T(8,128)S(1)} %get-tuple-element.76.refs_10_.refs_2_, ...), custom_call_target="tpu_custom_call" | custom-call | flops 67108864 | bytes 1048576 | tf_op jit(solution)/shard_map/part/pallas_call | solution.py:39
  56.4 1.4 %collective-permute-start.20 = (bf16[4,128,128]{2,1,0:T(8,128)(2,1)S(1)}, bf16[4,128,128]{2,1,0:T(8,128)(2,1)S(1)}, u32[]{:S(2)}, u32[]{:S(2)}) collective-permute-start(bf16[4,128,128]{2,1,0:T(8,128)(2,1)S(1)} %add_convert_fusion), channel_id=1, source_target_pairs={{2,0},{0,4},{4,8},{8,12},{12,14},{14,10},{10,6},{6,2},{3,1},{1,5},... | collective-permute-start | bytes 393224 | tf_op jit(solution)/shard_map/ppermute | solution.py:352
  57.9 1.5 %collective-permute-start.14 = (bf16[4,128,128]{2,1,0:T(8,128)(2,1)S(1)}, bf16[4,128,128]{2,1,0:T(8,128)(2,1)S(1)}, u32[]{:S(2)}, u32[]{:S(2)}) collective-permute-start(bf16[4,128,128]{2,1,0:T(8,128)(2,1)S(1)} %add_convert_fusion.5), channel_id=1, source_target_pairs={{4,0},{8,4},{12,8},{14,12},{10,14},{6,10},{2,6},{0,2},{5,1},{9,5},... | collective-permute-start | bytes 393224 | tf_op jit(solution)/shard_map/ppermute | solution.py:352
  60.0 1.9 %dense.7.refs_7_ = f32[128,1024]{1,0:T(8,128)S(1)} custom-call(bf16[8,128,128]{2,1,0:T(8,128)(2,1)S(1)} %copy-done.4, bf16[1024,8192]{1,0:T(8,128)(2,1)} %refs_1_.7), custom_call_target="tpu_custom_call" | custom-call | flops 268435456 | bytes 2097152 | tf_op jit(solution)/shard_map/dense/pallas_call | solution.py:39
  61.9 1.0 %part.7 = (f32[4,128,128]{2,1,0:T(8,128)S(1)}, f32[4,128,128]{2,1,0:T(8,128)S(1)}) custom-call(bf16[128,256]{1,0:T(8,128)(2,1)S(1)} %get-tuple-element.101.refs_0_, bf16[256,8192]{1,0:T(8,128)(2,1)S(1)} %bitcast.15, f32[64,128,128]{2,1,0:T(8,128)S(1)} %get-tuple-element.76.refs_10_.refs_2_, f32[8,128,128]{2,1,0:T(8,128)S(1)} %get-tuple-element.81.refs_3_, ...), custom_call_target="tpu_custom_call" | custom-call | flops 67108864 | bytes 1048576 | tf_op jit(solution)/shard_map/part/pallas_call | solution.py:39
  63.0 1.4 %collective-permute-done.21.refs_5_ = bf16[4,128,128]{2,1,0:T(8,128)(2,1)S(1)} collective-permute-done((bf16[4,128,128]{2,1,0:T(8,128)(2,1)S(1)}, bf16[4,128,128]{2,1,0:T(8,128)(2,1)S(1)}, u32[]{:S(2)}, u32[]{:S(2)}) %collective-permute-start.21) | collective-permute-done | bytes 131104 | tf_op jit(solution)/shard_map/ppermute | solution.py:352
  64.4 0.8 %sum_up.1 = bf16[128,1024]{1,0:T(8,128)(2,1)} custom-call(f32[4,128,128]{2,1,0:T(8,128)S(1)} %get-tuple-element.103.refs_0_, f32[4,128,128]{2,1,0:T(8,128)S(1)} %get-tuple-element.104.refs_1_, bf16[4,128,128]{2,1,0:T(8,128)(2,1)S(1)} %collective-permute-done.14.refs_2_, bf16[4,128,128]{2,1,0:T(8,128)(2,1)S(1)} %collective-permute-done.19.refs_3_, ...), custom_call_target="tpu_custom_call" | custom-call | flops 1 | bytes 1 | tf_op jit(solution)/shard_map/sum_up/pallas_call | solution.py:39
  (59 shorter events, 5.6 us)
Async XLA Ops:
  0.0 16.1 %copy-start.7 = (s32[4,16,1]{1,2,0:T(1,128)S(1)}, s32[4,16,1]{1,2,0:T(1,128)}, u32[]{:S(2)}) copy-start(s32[4,16,1]{1,2,0:T(1,128)} %param.28) | copy-start | bytes 772
  0.0 16.1 %copy-start.8 = (s32[128]{0:T(128)S(1)}, s32[128]{0:T(128)}, u32[]{:S(2)}) copy-start(s32[128]{0:T(128)} %param.21) | copy-start | bytes 1540
  0.0 16.1 %copy-start.9 = (s32[32]{0:T(128)S(1)}, s32[32]{0:T(128)}, u32[]{:S(2)}) copy-start(s32[32]{0:T(128)} %refs_3_.1) | copy-start | bytes 388
  4.6 9.5 %collective-permute-start.3 = (bf16[8,128,128]{2,1,0:T(8,128)(2,1)}, bf16[8,128,128]{2,1,0:T(8,128)(2,1)S(1)}, u32[]{:S(2)}, u32[]{:S(2)}) collective-permute-start(bf16[8,128,128]{2,1,0:T(8,128)(2,1)} %attend.1.refs_0_), channel_id=1, source_target_pairs={{2,0},{0,4},{4,8},{8,12},{12,14},{14,10},{10,6},{6,2},{3,1},{1,5},... | collective-permute-start | bytes 786440 | tf_op jit(solution)/shard_map/ppermute | solution.py:352
  7.6 8.3 %collective-permute-start = (bf16[8,128,128]{2,1,0:T(8,128)(2,1)}, bf16[8,128,128]{2,1,0:T(8,128)(2,1)S(1)}, u32[]{:S(2)}, u32[]{:S(2)}) collective-permute-start(bf16[8,128,128]{2,1,0:T(8,128)(2,1)} %attend.1.refs_0_), channel_id=1, source_target_pairs={{4,0},{8,4},{12,8},{14,12},{10,14},{6,10},{2,6},{0,2},{5,1},{9,5},... | collective-permute-start | bytes 786440 | tf_op jit(solution)/shard_map/ppermute | solution.py:352
  7.7 1.0 %copy-start.3 = (bf16[8,128,128]{2,1,0:T(8,128)(2,1)S(1)}, bf16[8,128,128]{2,1,0:T(8,128)(2,1)}, u32[]{:S(2)}) copy-start(bf16[8,128,128]{2,1,0:T(8,128)(2,1)} %attend.1.refs_0_) | copy-start | bytes 786436
  14.1 7.5 %collective-permute-start.4 = (bf16[8,128,128]{2,1,0:T(8,128)(2,1)S(1)}, bf16[8,128,128]{2,1,0:T(8,128)(2,1)S(1)}, u32[]{:S(2)}, u32[]{:S(2)}) collective-permute-start(bf16[8,128,128]{2,1,0:T(8,128)(2,1)S(1)} %collective-permute-done.3.refs_2_), channel_id=1, source_target_pairs={{2,0},{0,4},{4,8},{8,12},{12,14},{14,10},{10,6},{6,2},{3,1},{1,5},... | collective-permute-start | bytes 786440 | tf_op jit(solution)/shard_map/ppermute | solution.py:352
  15.9 7.2 %collective-permute-start.1 = (bf16[8,128,128]{2,1,0:T(8,128)(2,1)S(1)}, bf16[8,128,128]{2,1,0:T(8,128)(2,1)S(1)}, u32[]{:S(2)}, u32[]{:S(2)}) collective-permute-start(bf16[8,128,128]{2,1,0:T(8,128)(2,1)S(1)} %collective-permute-done.refs_1_), channel_id=1, source_target_pairs={{4,0},{8,4},{12,8},{14,12},{10,14},{6,10},{2,6},{0,2},{5,1},{9,5},... | collective-permute-start | bytes 786440 | tf_op jit(solution)/shard_map/ppermute | solution.py:352
  16.1 7.5 %copy-start.1 = (bf16[4,8192,64]{1,2,0:T(8,128)(2,1)S(1)}, bf16[4,8192,64]{1,2,0:T(8,128)(2,1)}, u32[]{:S(2)}) copy-start(bf16[4,8192,64]{1,2,0:T(8,128)(2,1)} %param.24) | copy-start | bytes 12582916
  16.1 7.5 %copy-start.2 = (bf16[4,16,128,128]{3,2,1,0:T(8,128)(2,1)S(1)}, bf16[4,16,128,128]{3,2,1,0:T(8,128)(2,1)}, u32[]{:S(2)}) copy-start(bf16[4,16,128,128]{3,2,1,0:T(8,128)(2,1)} %refs_4_.7) | copy-start | bytes 6291460
  16.2 7.5 %copy-start.5 = (f32[4,16]{1,0:T(4,128)S(1)}, f32[4,16]{1,0:T(4,128)}, u32[]{:S(2)}) copy-start(f32[4,16]{1,0:T(4,128)} %refs_4_.11) | copy-start | bytes 772
  16.2 7.5 %copy-start.6 = (s32[4,16]{1,0:T(4,128)S(1)}, s32[4,16]{1,0:T(4,128)}, u32[]{:S(2)}) copy-start(s32[4,16]{1,0:T(4,128)} %refs_5_.11) | copy-start | bytes 772
  21.6 6.8 %collective-permute-start.6 = (bf16[8,128,128]{2,1,0:T(8,128)(2,1)S(1)}, bf16[8,128,128]{2,1,0:T(8,128)(2,1)S(1)}, u32[]{:S(2)}, u32[]{:S(2)}) collective-permute-start(bf16[8,128,128]{2,1,0:T(8,128)(2,1)S(1)} %collective-permute-done.4.refs_4_), channel_id=1, source_target_pairs={{2,0},{0,4},{4,8},{8,12},{12,14},{14,10},{10,6},{6,2},{3,1},{1,5},... | collective-permute-start | bytes 786440 | tf_op jit(solution)/shard_map/ppermute | solution.py:352
  23.1 6.8 %collective-permute-start.2 = (bf16[8,128,128]{2,1,0:T(8,128)(2,1)S(1)}, bf16[8,128,128]{2,1,0:T(8,128)(2,1)S(1)}, u32[]{:S(2)}, u32[]{:S(2)}) collective-permute-start(bf16[8,128,128]{2,1,0:T(8,128)(2,1)S(1)} %collective-permute-done.1.refs_3_), channel_id=1, source_target_pairs={{4,0},{8,4},{12,8},{14,12},{10,14},{6,10},{2,6},{0,2},{5,1},{9,5},... | collective-permute-start | bytes 786440 | tf_op jit(solution)/shard_map/ppermute | solution.py:352
  28.4 5.0 %collective-permute-start.7 = (bf16[4,128,128]{2,1,0:T(8,128)(2,1)S(1)}, bf16[4,128,128]{2,1,0:T(8,128)(2,1)S(1)}, u32[]{:S(2)}, u32[]{:S(2)}) collective-permute-start(bf16[4,128,128]{2,1,0:T(8,128)(2,1)S(1)} %slice.7), channel_id=1, source_target_pairs={{2,0},{0,4},{4,8},{8,12},{12,14},{14,10},{10,6},{6,2},{3,1},{1,5},... | collective-permute-start | bytes 393224 | tf_op jit(solution)/shard_map/ppermute | solution.py:352
  29.9 5.0 %collective-permute-start.5 = (bf16[4,128,128]{2,1,0:T(8,128)(2,1)S(1)}, bf16[4,128,128]{2,1,0:T(8,128)(2,1)S(1)}, u32[]{:S(2)}, u32[]{:S(2)}) collective-permute-start(bf16[4,128,128]{2,1,0:T(8,128)(2,1)S(1)} %slice.6), channel_id=1, source_target_pairs={{4,0},{8,4},{12,8},{14,12},{10,14},{6,10},{2,6},{0,2},{5,1},{9,5},... | collective-permute-start | bytes 393224 | tf_op jit(solution)/shard_map/ppermute | solution.py:352
  30.5 4.4 %copy-start = (bf16[4,64,8192]{2,1,0:T(8,128)(2,1)S(1)}, bf16[4,64,8192]{2,1,0:T(8,128)(2,1)}, u32[]{:S(2)}) copy-start(bf16[4,64,8192]{2,1,0:T(8,128)(2,1)} %param.25) | copy-start | bytes 12582916
  36.3 6.2 %collective-permute-start.9 = (bf16[4,128,128]{2,1,0:T(8,128)(2,1)S(1)}, bf16[4,128,128]{2,1,0:T(8,128)(2,1)S(1)}, u32[]{:S(2)}, u32[]{:S(2)}) collective-permute-start(bf16[4,128,128]{2,1,0:T(8,128)(2,1)S(1)} %get-tuple-element.79), channel_id=1, source_target_pairs={{2,0},{0,4},{4,8},{8,12},{12,14},{14,10},{10,6},{6,2},{3,1},{1,5},... | collective-permute-start | bytes 393224 | tf_op jit(solution)/shard_map/ppermute | solution.py:352
  38.0 6.4 %collective-permute-start.8 = (bf16[4,128,128]{2,1,0:T(8,128)(2,1)S(1)}, bf16[4,128,128]{2,1,0:T(8,128)(2,1)S(1)}, u32[]{:S(2)}, u32[]{:S(2)}) collective-permute-start(bf16[4,128,128]{2,1,0:T(8,128)(2,1)S(1)} %get-tuple-element.78), channel_id=1, source_target_pairs={{4,0},{8,4},{12,8},{14,12},{10,14},{6,10},{2,6},{0,2},{5,1},{9,5},... | collective-permute-start | bytes 393224 | tf_op jit(solution)/shard_map/ppermute | solution.py:352
  39.8 8.0 %collective-permute-start.16 = (bf16[4,128,128]{2,1,0:T(8,128)(2,1)S(1)}, bf16[4,128,128]{2,1,0:T(8,128)(2,1)S(1)}, u32[]{:S(2)}, u32[]{:S(2)}) collective-permute-start(bf16[4,128,128]{2,1,0:T(8,128)(2,1)S(1)} %convert_element_type.79), channel_id=1, source_target_pairs={{2,0},{0,4},{4,8},{8,12},{12,14},{14,10},{10,6},{6,2},{3,1},{1,5},... | collective-permute-start | bytes 393224 | tf_op jit(solution)/shard_map/ppermute | solution.py:352
  41.4 6.4 %collective-permute-start.15 = (bf16[4,128,128]{2,1,0:T(8,128)(2,1)S(1)}, bf16[4,128,128]{2,1,0:T(8,128)(2,1)S(1)}, u32[]{:S(2)}, u32[]{:S(2)}) collective-permute-start(bf16[4,128,128]{2,1,0:T(8,128)(2,1)S(1)} %convert_element_type.78), channel_id=1, source_target_pairs={{4,0},{8,4},{12,8},{14,12},{10,14},{6,10},{2,6},{0,2},{5,1},{9,5},... | collective-permute-start | bytes 393224 | tf_op jit(solution)/shard_map/ppermute | solution.py:352
  44.4 5.6 %collective-permute-start.11 = (bf16[4,128,128]{2,1,0:T(8,128)(2,1)S(1)}, bf16[4,128,128]{2,1,0:T(8,128)(2,1)S(1)}, u32[]{:S(2)}, u32[]{:S(2)}) collective-permute-start(bf16[4,128,128]{2,1,0:T(8,128)(2,1)S(1)} %add_convert_fusion.8), channel_id=1, source_target_pairs={{2,0},{0,4},{4,8},{8,12},{12,14},{14,10},{10,6},{6,2},{3,1},{1,5},... | collective-permute-start | bytes 393224 | tf_op jit(solution)/shard_map/ppermute | solution.py:352
  46.0 6.3 %collective-permute-start.10 = (bf16[4,128,128]{2,1,0:T(8,128)(2,1)S(1)}, bf16[4,128,128]{2,1,0:T(8,128)(2,1)S(1)}, u32[]{:S(2)}, u32[]{:S(2)}) collective-permute-start(bf16[4,128,128]{2,1,0:T(8,128)(2,1)S(1)} %add_convert_fusion.9), channel_id=1, source_target_pairs={{4,0},{8,4},{12,8},{14,12},{10,14},{6,10},{2,6},{0,2},{5,1},{9,5},... | collective-permute-start | bytes 393224 | tf_op jit(solution)/shard_map/ppermute | solution.py:352
  47.9 7.8 %collective-permute-start.18 = (bf16[4,128,128]{2,1,0:T(8,128)(2,1)S(1)}, bf16[4,128,128]{2,1,0:T(8,128)(2,1)S(1)}, u32[]{:S(2)}, u32[]{:S(2)}) collective-permute-start(bf16[4,128,128]{2,1,0:T(8,128)(2,1)S(1)} %add_convert_fusion.2), channel_id=1, source_target_pairs={{2,0},{0,4},{4,8},{8,12},{12,14},{14,10},{10,6},{6,2},{3,1},{1,5},... | collective-permute-start | bytes 393224 | tf_op jit(solution)/shard_map/ppermute | solution.py:352
  49.5 6.3 %collective-permute-start.17 = (bf16[4,128,128]{2,1,0:T(8,128)(2,1)S(1)}, bf16[4,128,128]{2,1,0:T(8,128)(2,1)S(1)}, u32[]{:S(2)}, u32[]{:S(2)}) collective-permute-start(bf16[4,128,128]{2,1,0:T(8,128)(2,1)S(1)} %add_convert_fusion.3), channel_id=1, source_target_pairs={{4,0},{8,4},{12,8},{14,12},{10,14},{6,10},{2,6},{0,2},{5,1},{9,5},... | collective-permute-start | bytes 393224 | tf_op jit(solution)/shard_map/ppermute | solution.py:352
  52.3 5.6 %collective-permute-start.13 = (bf16[4,128,128]{2,1,0:T(8,128)(2,1)S(1)}, bf16[4,128,128]{2,1,0:T(8,128)(2,1)S(1)}, u32[]{:S(2)}, u32[]{:S(2)}) collective-permute-start(bf16[4,128,128]{2,1,0:T(8,128)(2,1)S(1)} %add_convert_fusion.6), channel_id=1, source_target_pairs={{2,0},{0,4},{4,8},{8,12},{12,14},{14,10},{10,6},{6,2},{3,1},{1,5},... | collective-permute-start | bytes 393224 | tf_op jit(solution)/shard_map/ppermute | solution.py:352
  52.3 5.5 %collective-permute-start.12 = (bf16[4,128,128]{2,1,0:T(8,128)(2,1)S(1)}, bf16[4,128,128]{2,1,0:T(8,128)(2,1)S(1)}, u32[]{:S(2)}, u32[]{:S(2)}) collective-permute-start(bf16[4,128,128]{2,1,0:T(8,128)(2,1)S(1)} %add_convert_fusion.7), channel_id=1, source_target_pairs={{4,0},{8,4},{12,8},{14,12},{10,14},{6,10},{2,6},{0,2},{5,1},{9,5},... | collective-permute-start | bytes 393224 | tf_op jit(solution)/shard_map/ppermute | solution.py:352
  54.4 5.7 %copy-start.4 = (bf16[8,128,128]{2,1,0:T(8,128)(2,1)S(1)}, bf16[8,128,128]{2,1,0:T(8,128)(2,1)}, u32[]{:S(2)}) copy-start(bf16[8,128,128]{2,1,0:T(8,128)(2,1)} %attend.1.refs_0_) | copy-start | bytes 786436
  55.8 7.2 %collective-permute-start.19 = (bf16[4,128,128]{2,1,0:T(8,128)(2,1)S(1)}, bf16[4,128,128]{2,1,0:T(8,128)(2,1)S(1)}, u32[]{:S(2)}, u32[]{:S(2)}) collective-permute-start(bf16[4,128,128]{2,1,0:T(8,128)(2,1)S(1)} %add_convert_fusion.1), channel_id=1, source_target_pairs={{4,0},{8,4},{12,8},{14,12},{10,14},{6,10},{2,6},{0,2},{5,1},{9,5},... | collective-permute-start | bytes 393224 | tf_op jit(solution)/shard_map/ppermute | solution.py:352
  56.4 6.5 %collective-permute-start.20 = (bf16[4,128,128]{2,1,0:T(8,128)(2,1)S(1)}, bf16[4,128,128]{2,1,0:T(8,128)(2,1)S(1)}, u32[]{:S(2)}, u32[]{:S(2)}) collective-permute-start(bf16[4,128,128]{2,1,0:T(8,128)(2,1)S(1)} %add_convert_fusion), channel_id=1, source_target_pairs={{2,0},{0,4},{4,8},{8,12},{12,14},{14,10},{10,6},{6,2},{3,1},{1,5},... | collective-permute-start | bytes 393224 | tf_op jit(solution)/shard_map/ppermute | solution.py:352
  57.9 5.0 %collective-permute-start.14 = (bf16[4,128,128]{2,1,0:T(8,128)(2,1)S(1)}, bf16[4,128,128]{2,1,0:T(8,128)(2,1)S(1)}, u32[]{:S(2)}, u32[]{:S(2)}) collective-permute-start(bf16[4,128,128]{2,1,0:T(8,128)(2,1)S(1)} %add_convert_fusion.5), channel_id=1, source_target_pairs={{4,0},{8,4},{12,8},{14,12},{10,14},{6,10},{2,6},{0,2},{5,1},{9,5},... | collective-permute-start | bytes 393224 | tf_op jit(solution)/shard_map/ppermute | solution.py:352
  59.4 5.0 %collective-permute-start.21 = (bf16[4,128,128]{2,1,0:T(8,128)(2,1)S(1)}, bf16[4,128,128]{2,1,0:T(8,128)(2,1)S(1)}, u32[]{:S(2)}, u32[]{:S(2)}) collective-permute-start(bf16[4,128,128]{2,1,0:T(8,128)(2,1)S(1)} %add_convert_fusion.4), channel_id=1, source_target_pairs={{2,0},{0,4},{4,8},{8,12},{12,14},{14,10},{10,6},{6,2},{3,1},{1,5},... | collective-permute-start | bytes 393224 | tf_op jit(solution)/shard_map/ppermute | solution.py:352

commit v14 on v13

--- a/solution.py
+++ b/solution.py
@@ -359,11 +359,12 @@
     for step in range(2, half):
         right, left = after(chunks[step - 1], token), after(chunks[count - step + 1], token)
         chunks[step], chunks[count - step] = come(right, 1), come(left, -1)
+        if step == half - 1:
+            front, back = come(right[: heads // 2], 2), come(left[heads // 2 :], -2)
         if step == 2:
             slot, table = dense_for(wanted[3:5], after(attended, token), True)
             token = slot
     (token, *_) = dense_for(wanted[5:-1], after(attended, chunks[half - 2], chunks[half + 2]))
-    right, left = chunks[half - 1], chunks[half + 1]
 
     factor_t = jnp.swapaxes(factor_in, 1, 2).reshape(low_width, -1)
     second = second_factor.reshape(low_width, complete)
@@ -384,8 +385,6 @@
         flops=rows * low_width * complete,
         moved=4 * MIB,
     )
-    right, left = after(right, low, token), after(left, low, token)
-    front, back = come(right[: heads // 2], 1), come(left[heads // 2 :], -1)
     low, blocks = call(
         functools.partial(fold_kernel, late, count, False),
         "fold_late",
@@ -396,6 +395,7 @@
         flops=rows * low_width * width * 4,
         moved=MIB,
     )
+    low = after(low, token)
     extras = shape((slots * CAP, rows, side), F32)
     first = wanted[:1]
     part_half = shape((heads // 2, rows, side), F32)

time: 65.4 us -> 65.2 us (level)
  waiting for transfers between devices: 12.7 us -> 10.3 us
  starting transfers between devices: 23.8 us -> 26.1 us
    ppermute x22, waiting for transfers between devices: 12.7 us -> 10.3 us  [come(): lax.ppermute(value, 'tp', [(ring[(i + distance) % count], ring[i]) for i...]
    ppermute x22, starting transfers between devices: 23.8 us -> 26.1 us  [come(): lax.ppermute(value, 'tp', [(ring[(i + distance) % count], ring[i]) for i...]
  transfers between devices with their start and end apart: 22 -> 22, of which waited for: 8 -> 10; matrix products, arithmetic and copies ran while one was open for 1% -> 1% of each run, Pallas kernels for 31% -> 31%
where the time goes in v14:
time: 65.2 us; the launch traced here: 65 us
  Pallas kernels  26.9 us (41%)
  starting transfers between devices  26.1 us (40%)
  waiting for transfers between devices  10.3 us (16%)
  local copies, waits for them, and re-layouts  1.07 us (2%)
    pallas_call x13, Pallas kernels, call(): pl.pallas_call(kernel, out_shape=outs, in_specs=specs, out_specs=out_spec...  26.9 us
    ppermute x22, starting transfers between devices, come(): lax.ppermute(value, 'tp', [(ring[(i + distance) % count], ring[i]) for i...  26.1 us
    ppermute x22, waiting for transfers between devices, come(): lax.ppermute(value, 'tp', [(ring[(i + distance) % count], ring[i]) for i...  10.3 us
  transfers between devices with their start and end apart: 22, of which 10 were waited for; matrix products, arithmetic and copies ran while one was open for 1% of the time, Pallas kernels for 31%

profile of v14, /device:TPU:0, one launch (start us, length us, event | category | flops | bytes accessed | tf_op | source)
XLA Modules:
  0.0 65.0 jit_solution(15236108708874854236)
XLA Ops:
  0.0 4.6 %attend.1.refs_0_ = bf16[8,128,128]{2,1,0:T(8,128)(2,1)} custom-call(bf16[128,1024]{1,0:T(8,128)(2,1)} %query_hbm.1, bf16[4096,128]{1,0:T(8,128)(2,1)} %bitcast.21, bf16[4096,128]{1,0:T(8,128)(2,1)} %bitcast.22, bf16[128,128]{1,0:T(8,128)(2,1)} %bitcast.23, bf16[128,128]{1,0:T(8,128)(2,1)} %bitcast.24, s32[1,128]{1,0:T(1,128)} %bitcast.25), custom_call_target="tpu_custom_call" | custom-call | tf_op jit(solution)/shard_map/attend/pallas_call | solution.py:39
  4.6 3.1 %collective-permute-start.3 = (bf16[8,128,128]{2,1,0:T(8,128)(2,1)}, bf16[8,128,128]{2,1,0:T(8,128)(2,1)S(1)}, u32[]{:S(2)}, u32[]{:S(2)}) collective-permute-start(bf16[8,128,128]{2,1,0:T(8,128)(2,1)} %attend.1.refs_0_), channel_id=1, source_target_pairs={{2,0},{0,4},{4,8},{8,12},{12,14},{14,10},{10,6},{6,2},{3,1},{1,5},... | collective-permute-start | bytes 786440 | tf_op jit(solution)/shard_map/ppermute | solution.py:352
  7.7 1.0 %copy-done.3 = bf16[8,128,128]{2,1,0:T(8,128)(2,1)S(1)} copy-done((bf16[8,128,128]{2,1,0:T(8,128)(2,1)S(1)}, bf16[8,128,128]{2,1,0:T(8,128)(2,1)}, u32[]{:S(2)}) %copy-start.3) | copy-done | bytes 262168
  8.7 3.5 %dense.4 = (f32[128,1024]{1,0:T(8,128)S(1)}, f32[128,1024]{1,0:T(8,128)S(1)}, f32[128,1024]{1,0:T(8,128)S(1)}) custom-call(bf16[8,128,128]{2,1,0:T(8,128)(2,1)S(1)} %copy-done.3, bf16[1024,8192]{1,0:T(8,128)(2,1)} %refs_1_.7), custom_call_target="tpu_custom_call" | custom-call | flops 805306368 | bytes 6291456 | tf_op jit(solution)/shard_map/dense/pallas_call | solution.py:39
  12.1 2.0 %collective-permute-done.3.refs_2_ = bf16[8,128,128]{2,1,0:T(8,128)(2,1)S(1)} collective-permute-done((bf16[8,128,128]{2,1,0:T(8,128)(2,1)}, bf16[8,128,128]{2,1,0:T(8,128)(2,1)S(1)}, u32[]{:S(2)}, u32[]{:S(2)}) %collective-permute-start.3) | collective-permute-done | bytes 262176 | tf_op jit(solution)/shard_map/ppermute | solution.py:352
  14.1 1.8 %collective-permute-start.4 = (bf16[8,128,128]{2,1,0:T(8,128)(2,1)S(1)}, bf16[8,128,128]{2,1,0:T(8,128)(2,1)S(1)}, u32[]{:S(2)}, u32[]{:S(2)}) collective-permute-start(bf16[8,128,128]{2,1,0:T(8,128)(2,1)S(1)} %collective-permute-done.3.refs_2_), channel_id=1, source_target_pairs={{2,0},{0,4},{4,8},{8,12},{12,14},{14,10},{10,6},{6,2},{3,1},{1,5},... | collective-permute-start | bytes 786440 | tf_op jit(solution)/shard_map/ppermute | solution.py:352
  16.2 3.7 %dense.5 = (f32[128,1024]{1,0:T(8,128)S(1)}, f32[128,1024]{1,0:T(8,128)S(1)}, s32[128,128]{1,0:T(8,128)S(1)}, s32[64]{0:T(128)S(1)}) custom-call(bf16[8,128,128]{2,1,0:T(8,128)(2,1)S(1)} %copy-done.3, bf16[1024,8192]{1,0:T(8,128)(2,1)} %refs_1_.7, s32[1,128]{1,0:T(1,128)S(1)} %bitcast.20, s32[32]{0:T(128)S(1)} %copy-done.9, s32[4,16]{1,0:T(4,128)S(1)} %bitcast.19), custom_call_target="tpu_custom_call" | custom-call | flops 536870912 | bytes 4194304 | tf_op jit(solution)/shard_map/dense/pallas_call | solution.py:39
  19.9 1.7 %collective-permute-done.4.refs_4_ = bf16[8,128,128]{2,1,0:T(8,128)(2,1)S(1)} collective-permute-done((bf16[8,128,128]{2,1,0:T(8,128)(2,1)S(1)}, bf16[8,128,128]{2,1,0:T(8,128)(2,1)S(1)}, u32[]{:S(2)}, u32[]{:S(2)}) %collective-permute-start.4) | collective-permute-done | bytes 262176 | tf_op jit(solution)/shard_map/ppermute | solution.py:352
  21.6 1.5 %collective-permute-start.7 = (bf16[8,128,128]{2,1,0:T(8,128)(2,1)S(1)}, bf16[8,128,128]{2,1,0:T(8,128)(2,1)S(1)}, u32[]{:S(2)}, u32[]{:S(2)}) collective-permute-start(bf16[8,128,128]{2,1,0:T(8,128)(2,1)S(1)} %collective-permute-done.4.refs_4_), channel_id=1, source_target_pairs={{2,0},{0,4},{4,8},{8,12},{12,14},{14,10},{10,6},{6,2},{3,1},{1,5},... | collective-permute-start | bytes 786440 | tf_op jit(solution)/shard_map/ppermute | solution.py:352
  23.1 0.5 collective-permute-start.6
  23.7 2.5 %collective-permute-start.5 = (bf16[4,128,128]{2,1,0:T(8,128)(2,1)S(1)}, bf16[4,128,128]{2,1,0:T(8,128)(2,1)S(1)}, u32[]{:S(2)}, u32[]{:S(2)}) collective-permute-start(bf16[4,128,128]{2,1,0:T(8,128)(2,1)S(1)} %slice.7), channel_id=1, source_target_pairs={{6,0},{2,4},{0,8},{4,12},{8,14},{12,10},{14,6},{10,2},{7,1},{3,5},... | collective-permute-start | bytes 393224 | tf_op jit(solution)/shard_map/ppermute | solution.py:352
  26.6 2.1 %fold_early.1 = (f32[128,256]{1,0:T(8,128)S(1)}, f32[64,128,128]{2,1,0:T(8,128)S(1)}) custom-call(bf16[8,128,128]{2,1,0:T(8,128)(2,1)S(1)} %copy-done.3, bf16[8,128,128]{2,1,0:T(8,128)(2,1)S(1)} %collective-permute-done.refs_1_, bf16[8,128,128]{2,1,0:T(8,128)(2,1)S(1)} %collective-permute-done.3.refs_2_, ...), custom_call_target="tpu_custom_call" | custom-call | flops 268435456 | bytes 4194304 | tf_op jit(solution)/shard_map/fold_early/pallas_call | solution.py:39
  28.8 2.6 %dense.6 = (f32[128,1024]{1,0:T(8,128)S(1)}, f32[128,1024]{1,0:T(8,128)S(1)}) custom-call(bf16[8,128,128]{2,1,0:T(8,128)(2,1)S(1)} %copy-done.3, bf16[1024,8192]{1,0:T(8,128)(2,1)} %refs_1_.7), custom_call_target="tpu_custom_call" | custom-call | flops 536870912 | bytes 4194304 | tf_op jit(solution)/shard_map/dense/pallas_call | solution.py:39
  31.9 1.4 %fold_late.1 = (f32[128,256]{1,0:T(8,128)S(1)}, f32[64,128,128]{2,1,0:T(8,128)S(1)}) custom-call(bf16[8,128,128]{2,1,0:T(8,128)(2,1)S(1)} %collective-permute-done.6.refs_0_, bf16[8,128,128]{2,1,0:T(8,128)(2,1)S(1)} %collective-permute-done.7.refs_1_, s32[128,128]{1,0:T(8,128)S(1)} %get-tuple-element.63.refs_5_.refs_2_, bf16[256,8192]{1,0:T(8,128)(2,1)S(1)} %bitcast.17, ...), custom_call_target="tpu_custom_call" | custom-call | flops 134217728 | bytes 1048576 | tf_op jit(solution)/shard_map/fold_late/pallas_call | solution.py:39
  33.3 0.7 %collective-permute-done.5.refs_1_ = bf16[4,128,128]{2,1,0:T(8,128)(2,1)S(1)} collective-permute-done((bf16[4,128,128]{2,1,0:T(8,128)(2,1)S(1)}, bf16[4,128,128]{2,1,0:T(8,128)(2,1)S(1)}, u32[]{:S(2)}, u32[]{:S(2)}) %collective-permute-start.5) | collective-permute-done | bytes 131104 | tf_op jit(solution)/shard_map/ppermute | solution.py:352
  34.4 1.4 %finish.1 = (bf16[128,256]{1,0:T(8,128)(2,1)S(1)}, f32[8,128,128]{2,1,0:T(8,128)S(1)}, bf16[4,128,128]{2,1,0:T(8,128)(2,1)S(1)}, bf16[4,128,128]{2,1,0:T(8,128)(2,1)S(1)}) custom-call(bf16[4,128,128]{2,1,0:T(8,128)(2,1)S(1)} %collective-permute-done.2.refs_0_, bf16[4,128,128]{2,1,0:T(8,128)(2,1)S(1)} %collective-permute-done.5.refs_1_, ...), custom_call_target="tpu_custom_call" | custom-call | flops 268435456 | bytes 2097152 | tf_op jit(solution)/shard_map/finish/pallas_call | solution.py:39
  35.8 2.9 %collective-permute-start.9 = (bf16[4,128,128]{2,1,0:T(8,128)(2,1)S(1)}, bf16[4,128,128]{2,1,0:T(8,128)(2,1)S(1)}, u32[]{:S(2)}, u32[]{:S(2)}) collective-permute-start(bf16[4,128,128]{2,1,0:T(8,128)(2,1)S(1)} %get-tuple-element.77), channel_id=1, source_target_pairs={{2,0},{0,4},{4,8},{8,12},{12,14},{14,10},{10,6},{6,2},{3,1},{1,5},... | collective-permute-start | bytes 393224 | tf_op jit(solution)/shard_map/ppermute | solution.py:352
  38.7 1.3 %part.4 = (f32[4,128,128]{2,1,0:T(8,128)S(1)}, f32[4,128,128]{2,1,0:T(8,128)S(1)}, f32[4,128,128]{2,1,0:T(8,128)S(1)}, f32[4,128,128]{2,1,0:T(8,128)S(1)}) custom-call(bf16[128,256]{1,0:T(8,128)(2,1)S(1)} %get-tuple-element.99.refs_0_, bf16[256,8192]{1,0:T(8,128)(2,1)S(1)} %bitcast.12, f32[64,128,128]{2,1,0:T(8,128)S(1)} %get-tuple-element.74.refs_10_.refs_2_, ...), custom_call_target="tpu_custom_call" | custom-call | flops 67108864 | bytes 1048576 | tf_op jit(solution)/shard_map/part/pallas_call | solution.py:39
  40.1 2.1 %collective-permute-start.16 = (bf16[4,128,128]{2,1,0:T(8,128)(2,1)S(1)}, bf16[4,128,128]{2,1,0:T(8,128)(2,1)S(1)}, u32[]{:S(2)}, u32[]{:S(2)}) collective-permute-start(bf16[4,128,128]{2,1,0:T(8,128)(2,1)S(1)} %convert_element_type.79), channel_id=1, source_target_pairs={{2,0},{0,4},{4,8},{8,12},{12,14},{14,10},{10,6},{6,2},{3,1},{1,5},... | collective-permute-start | bytes 393224 | tf_op jit(solution)/shard_map/ppermute | solution.py:352
  42.6 2.4 %collective-permute-done.8 = bf16[4,128,128]{2,1,0:T(8,128)(2,1)S(1)} collective-permute-done((bf16[4,128,128]{2,1,0:T(8,128)(2,1)S(1)}, bf16[4,128,128]{2,1,0:T(8,128)(2,1)S(1)}, u32[]{:S(2)}, u32[]{:S(2)}) %collective-permute-start.8) | collective-permute-done | bytes 131104 | tf_op jit(solution)/shard_map/ppermute | solution.py:352
  45.3 1.8 %collective-permute-start.10 = (bf16[4,128,128]{2,1,0:T(8,128)(2,1)S(1)}, bf16[4,128,128]{2,1,0:T(8,128)(2,1)S(1)}, u32[]{:S(2)}, u32[]{:S(2)}) collective-permute-start(bf16[4,128,128]{2,1,0:T(8,128)(2,1)S(1)} %add_convert_fusion.9), channel_id=1, source_target_pairs={{4,0},{8,4},{12,8},{14,12},{10,14},{6,10},{2,6},{0,2},{5,1},{9,5},... | collective-permute-start | bytes 393224 | tf_op jit(solution)/shard_map/ppermute | solution.py:352
  47.1 1.3 %part.5 = (f32[4,128,128]{2,1,0:T(8,128)S(1)}, f32[4,128,128]{2,1,0:T(8,128)S(1)}, f32[4,128,128]{2,1,0:T(8,128)S(1)}, f32[4,128,128]{2,1,0:T(8,128)S(1)}) custom-call(bf16[128,256]{1,0:T(8,128)(2,1)S(1)} %get-tuple-element.99.refs_0_, bf16[256,8192]{1,0:T(8,128)(2,1)S(1)} %bitcast.13, f32[64,128,128]{2,1,0:T(8,128)S(1)} %get-tuple-element.74.refs_10_.refs_2_, ...), custom_call_target="tpu_custom_call" | custom-call | flops 67108864 | bytes 1048576 | tf_op jit(solution)/shard_map/part/pallas_call | solution.py:39
  48.8 1.8 %collective-permute-start.17 = (bf16[4,128,128]{2,1,0:T(8,128)(2,1)S(1)}, bf16[4,128,128]{2,1,0:T(8,128)(2,1)S(1)}, u32[]{:S(2)}, u32[]{:S(2)}) collective-permute-start(bf16[4,128,128]{2,1,0:T(8,128)(2,1)S(1)} %add_convert_fusion.3), channel_id=1, source_target_pairs={{4,0},{8,4},{12,8},{14,12},{10,14},{6,10},{2,6},{0,2},{5,1},{9,5},... | collective-permute-start | bytes 393224 | tf_op jit(solution)/shard_map/ppermute | solution.py:352
  51.0 1.6 %collective-permute-start.13 = (bf16[4,128,128]{2,1,0:T(8,128)(2,1)S(1)}, bf16[4,128,128]{2,1,0:T(8,128)(2,1)S(1)}, u32[]{:S(2)}, u32[]{:S(2)}) collective-permute-start(bf16[4,128,128]{2,1,0:T(8,128)(2,1)S(1)} %add_convert_fusion.6), channel_id=1, source_target_pairs={{2,0},{0,4},{4,8},{8,12},{12,14},{14,10},{10,6},{6,2},{3,1},{1,5},... | collective-permute-start | bytes 393224 | tf_op jit(solution)/shard_map/ppermute | solution.py:352
  52.7 1.0 %collective-permute-start.12 = (bf16[4,128,128]{2,1,0:T(8,128)(2,1)S(1)}, bf16[4,128,128]{2,1,0:T(8,128)(2,1)S(1)}, u32[]{:S(2)}, u32[]{:S(2)}) collective-permute-start(bf16[4,128,128]{2,1,0:T(8,128)(2,1)S(1)} %add_convert_fusion.7), channel_id=1, source_target_pairs={{4,0},{8,4},{12,8},{14,12},{10,14},{6,10},{2,6},{0,2},{5,1},{9,5},... | collective-permute-start | bytes 393224 | tf_op jit(solution)/shard_map/ppermute | solution.py:352
  53.6 1.3 %part.6 = (f32[4,128,128]{2,1,0:T(8,128)S(1)}, f32[4,128,128]{2,1,0:T(8,128)S(1)}, f32[4,128,128]{2,1,0:T(8,128)S(1)}, f32[4,128,128]{2,1,0:T(8,128)S(1)}) custom-call(bf16[128,256]{1,0:T(8,128)(2,1)S(1)} %get-tuple-element.99.refs_0_, bf16[256,8192]{1,0:T(8,128)(2,1)S(1)} %bitcast.14, f32[64,128,128]{2,1,0:T(8,128)S(1)} %get-tuple-element.74.refs_10_.refs_2_, ...), custom_call_target="tpu_custom_call" | custom-call | flops 67108864 | bytes 1048576 | tf_op jit(solution)/shard_map/part/pallas_call | solution.py:39
  55.1 2.0 %collective-permute-start.19 = (bf16[4,128,128]{2,1,0:T(8,128)(2,1)S(1)}, bf16[4,128,128]{2,1,0:T(8,128)(2,1)S(1)}, u32[]{:S(2)}, u32[]{:S(2)}) collective-permute-start(bf16[4,128,128]{2,1,0:T(8,128)(2,1)S(1)} %add_convert_fusion.1), channel_id=1, source_target_pairs={{4,0},{8,4},{12,8},{14,12},{10,14},{6,10},{2,6},{0,2},{5,1},{9,5},... | collective-permute-start | bytes 393224 | tf_op jit(solution)/shard_map/ppermute | solution.py:352
  57.7 1.6 %collective-permute-start.14 = (bf16[4,128,128]{2,1,0:T(8,128)(2,1)S(1)}, bf16[4,128,128]{2,1,0:T(8,128)(2,1)S(1)}, u32[]{:S(2)}, u32[]{:S(2)}) collective-permute-start(bf16[4,128,128]{2,1,0:T(8,128)(2,1)S(1)} %add_convert_fusion.5), channel_id=1, source_target_pairs={{4,0},{8,4},{12,8},{14,12},{10,14},{6,10},{2,6},{0,2},{5,1},{9,5},... | collective-permute-start | bytes 393224 | tf_op jit(solution)/shard_map/ppermute | solution.py:352
  59.8 1.9 %dense.7.refs_7_ = f32[128,1024]{1,0:T(8,128)S(1)} custom-call(bf16[8,128,128]{2,1,0:T(8,128)(2,1)S(1)} %copy-done.4, bf16[1024,8192]{1,0:T(8,128)(2,1)} %refs_1_.7), custom_call_target="tpu_custom_call" | custom-call | flops 268435456 | bytes 2097152 | tf_op jit(solution)/shard_map/dense/pallas_call | solution.py:39
  61.7 1.0 %part.7 = (f32[4,128,128]{2,1,0:T(8,128)S(1)}, f32[4,128,128]{2,1,0:T(8,128)S(1)}) custom-call(bf16[128,256]{1,0:T(8,128)(2,1)S(1)} %get-tuple-element.99.refs_0_, bf16[256,8192]{1,0:T(8,128)(2,1)S(1)} %bitcast.15, f32[64,128,128]{2,1,0:T(8,128)S(1)} %get-tuple-element.74.refs_10_.refs_2_, f32[8,128,128]{2,1,0:T(8,128)S(1)} %get-tuple-element.79.refs_3_, ...), custom_call_target="tpu_custom_call" | custom-call | flops 67108864 | bytes 1048576 | tf_op jit(solution)/shard_map/part/pallas_call | solution.py:39
  62.7 1.5 %collective-permute-done.21.refs_5_ = bf16[4,128,128]{2,1,0:T(8,128)(2,1)S(1)} collective-permute-done((bf16[4,128,128]{2,1,0:T(8,128)(2,1)S(1)}, bf16[4,128,128]{2,1,0:T(8,128)(2,1)S(1)}, u32[]{:S(2)}, u32[]{:S(2)}) %collective-permute-start.21) | collective-permute-done | bytes 131104 | tf_op jit(solution)/shard_map/ppermute | solution.py:352
  64.2 0.8 %sum_up.1 = bf16[128,1024]{1,0:T(8,128)(2,1)} custom-call(f32[4,128,128]{2,1,0:T(8,128)S(1)} %get-tuple-element.101.refs_0_, f32[4,128,128]{2,1,0:T(8,128)S(1)} %get-tuple-element.102.refs_1_, bf16[4,128,128]{2,1,0:T(8,128)(2,1)S(1)} %collective-permute-done.14.refs_2_, bf16[4,128,128]{2,1,0:T(8,128)(2,1)S(1)} %collective-permute-done.19.refs_3_, ...), custom_call_target="tpu_custom_call" | custom-call | flops 1 | bytes 1 | tf_op jit(solution)/shard_map/sum_up/pallas_call | solution.py:39
  (59 shorter events, 4.4 us)
Async XLA Ops:
  0.0 16.1 %copy-start.7 = (s32[4,16,1]{1,2,0:T(1,128)S(1)}, s32[4,16,1]{1,2,0:T(1,128)}, u32[]{:S(2)}) copy-start(s32[4,16,1]{1,2,0:T(1,128)} %param.28) | copy-start | bytes 772
  0.0 16.1 %copy-start.8 = (s32[128]{0:T(128)S(1)}, s32[128]{0:T(128)}, u32[]{:S(2)}) copy-start(s32[128]{0:T(128)} %param.21) | copy-start | bytes 1540
  0.0 16.1 %copy-start.9 = (s32[32]{0:T(128)S(1)}, s32[32]{0:T(128)}, u32[]{:S(2)}) copy-start(s32[32]{0:T(128)} %refs_3_.1) | copy-start | bytes 388
  4.6 9.5 %collective-permute-start.3 = (bf16[8,128,128]{2,1,0:T(8,128)(2,1)}, bf16[8,128,128]{2,1,0:T(8,128)(2,1)S(1)}, u32[]{:S(2)}, u32[]{:S(2)}) collective-permute-start(bf16[8,128,128]{2,1,0:T(8,128)(2,1)} %attend.1.refs_0_), channel_id=1, source_target_pairs={{2,0},{0,4},{4,8},{8,12},{12,14},{14,10},{10,6},{6,2},{3,1},{1,5},... | collective-permute-start | bytes 786440 | tf_op jit(solution)/shard_map/ppermute | solution.py:352
  7.6 8.3 %collective-permute-start = (bf16[8,128,128]{2,1,0:T(8,128)(2,1)}, bf16[8,128,128]{2,1,0:T(8,128)(2,1)S(1)}, u32[]{:S(2)}, u32[]{:S(2)}) collective-permute-start(bf16[8,128,128]{2,1,0:T(8,128)(2,1)} %attend.1.refs_0_), channel_id=1, source_target_pairs={{4,0},{8,4},{12,8},{14,12},{10,14},{6,10},{2,6},{0,2},{5,1},{9,5},... | collective-permute-start | bytes 786440 | tf_op jit(solution)/shard_map/ppermute | solution.py:352
  7.7 1.0 %copy-start.3 = (bf16[8,128,128]{2,1,0:T(8,128)(2,1)S(1)}, bf16[8,128,128]{2,1,0:T(8,128)(2,1)}, u32[]{:S(2)}) copy-start(bf16[8,128,128]{2,1,0:T(8,128)(2,1)} %attend.1.refs_0_) | copy-start | bytes 786436
  14.1 7.5 %collective-permute-start.4 = (bf16[8,128,128]{2,1,0:T(8,128)(2,1)S(1)}, bf16[8,128,128]{2,1,0:T(8,128)(2,1)S(1)}, u32[]{:S(2)}, u32[]{:S(2)}) collective-permute-start(bf16[8,128,128]{2,1,0:T(8,128)(2,1)S(1)} %collective-permute-done.3.refs_2_), channel_id=1, source_target_pairs={{2,0},{0,4},{4,8},{8,12},{12,14},{14,10},{10,6},{6,2},{3,1},{1,5},... | collective-permute-start | bytes 786440 | tf_op jit(solution)/shard_map/ppermute | solution.py:352
  15.9 7.2 %collective-permute-start.1 = (bf16[8,128,128]{2,1,0:T(8,128)(2,1)S(1)}, bf16[8,128,128]{2,1,0:T(8,128)(2,1)S(1)}, u32[]{:S(2)}, u32[]{:S(2)}) collective-permute-start(bf16[8,128,128]{2,1,0:T(8,128)(2,1)S(1)} %collective-permute-done.refs_1_), channel_id=1, source_target_pairs={{4,0},{8,4},{12,8},{14,12},{10,14},{6,10},{2,6},{0,2},{5,1},{9,5},... | collective-permute-start | bytes 786440 | tf_op jit(solution)/shard_map/ppermute | solution.py:352
  16.1 10.5 %copy-start.1 = (bf16[4,8192,64]{1,2,0:T(8,128)(2,1)S(1)}, bf16[4,8192,64]{1,2,0:T(8,128)(2,1)}, u32[]{:S(2)}) copy-start(bf16[4,8192,64]{1,2,0:T(8,128)(2,1)} %param.24) | copy-start | bytes 12582916
  16.1 10.5 %copy-start.2 = (bf16[4,16,128,128]{3,2,1,0:T(8,128)(2,1)S(1)}, bf16[4,16,128,128]{3,2,1,0:T(8,128)(2,1)}, u32[]{:S(2)}) copy-start(bf16[4,16,128,128]{3,2,1,0:T(8,128)(2,1)} %refs_4_.7) | copy-start | bytes 6291460
  16.2 10.5 %copy-start.5 = (f32[4,16]{1,0:T(4,128)S(1)}, f32[4,16]{1,0:T(4,128)}, u32[]{:S(2)}) copy-start(f32[4,16]{1,0:T(4,128)} %refs_4_.11) | copy-start | bytes 772
  16.2 10.5 %copy-start.6 = (s32[4,16]{1,0:T(4,128)S(1)}, s32[4,16]{1,0:T(4,128)}, u32[]{:S(2)}) copy-start(s32[4,16]{1,0:T(4,128)} %refs_5_.11) | copy-start | bytes 772
  21.6 9.8 %collective-permute-start.7 = (bf16[8,128,128]{2,1,0:T(8,128)(2,1)S(1)}, bf16[8,128,128]{2,1,0:T(8,128)(2,1)S(1)}, u32[]{:S(2)}, u32[]{:S(2)}) collective-permute-start(bf16[8,128,128]{2,1,0:T(8,128)(2,1)S(1)} %collective-permute-done.4.refs_4_), channel_id=1, source_target_pairs={{2,0},{0,4},{4,8},{8,12},{12,14},{14,10},{10,6},{6,2},{3,1},{1,5},... | collective-permute-start | bytes 786440 | tf_op jit(solution)/shard_map/ppermute | solution.py:352
  23.1 8.8 %collective-permute-start.6 = (bf16[8,128,128]{2,1,0:T(8,128)(2,1)S(1)}, bf16[8,128,128]{2,1,0:T(8,128)(2,1)S(1)}, u32[]{:S(2)}, u32[]{:S(2)}) collective-permute-start(bf16[8,128,128]{2,1,0:T(8,128)(2,1)S(1)} %collective-permute-done.1.refs_3_), channel_id=1, source_target_pairs={{4,0},{8,4},{12,8},{14,12},{10,14},{6,10},{2,6},{0,2},{5,1},{9,5},... | collective-permute-start | bytes 786440 | tf_op jit(solution)/shard_map/ppermute | solution.py:352
  23.7 10.3 %collective-permute-start.5 = (bf16[4,128,128]{2,1,0:T(8,128)(2,1)S(1)}, bf16[4,128,128]{2,1,0:T(8,128)(2,1)S(1)}, u32[]{:S(2)}, u32[]{:S(2)}) collective-permute-start(bf16[4,128,128]{2,1,0:T(8,128)(2,1)S(1)} %slice.7), channel_id=1, source_target_pairs={{6,0},{2,4},{0,8},{4,12},{8,14},{12,10},{14,6},{10,2},{7,1},{3,5},... | collective-permute-start | bytes 393224 | tf_op jit(solution)/shard_map/ppermute | solution.py:352
  26.2 8.2 %collective-permute-start.2 = (bf16[4,128,128]{2,1,0:T(8,128)(2,1)S(1)}, bf16[4,128,128]{2,1,0:T(8,128)(2,1)S(1)}, u32[]{:S(2)}, u32[]{:S(2)}) collective-permute-start(bf16[4,128,128]{2,1,0:T(8,128)(2,1)S(1)} %slice.6), channel_id=1, source_target_pairs={{8,0},{12,4},{14,8},{10,12},{6,14},{2,10},{0,6},{4,2},{9,1},{13,5}... | collective-permute-start | bytes 393224 | tf_op jit(solution)/shard_map/ppermute | solution.py:352
  31.9 2.5 %copy-start = (bf16[4,64,8192]{2,1,0:T(8,128)(2,1)S(1)}, bf16[4,64,8192]{2,1,0:T(8,128)(2,1)}, u32[]{:S(2)}) copy-start(bf16[4,64,8192]{2,1,0:T(8,128)(2,1)} %param.25) | copy-start | bytes 12582916
  35.8 6.8 %collective-permute-start.9 = (bf16[4,128,128]{2,1,0:T(8,128)(2,1)S(1)}, bf16[4,128,128]{2,1,0:T(8,128)(2,1)S(1)}, u32[]{:S(2)}, u32[]{:S(2)}) collective-permute-start(bf16[4,128,128]{2,1,0:T(8,128)(2,1)S(1)} %get-tuple-element.77), channel_id=1, source_target_pairs={{2,0},{0,4},{4,8},{8,12},{12,14},{14,10},{10,6},{6,2},{3,1},{1,5},... | collective-permute-start | bytes 393224 | tf_op jit(solution)/shard_map/ppermute | solution.py:352
  38.7 6.3 %collective-permute-start.8 = (bf16[4,128,128]{2,1,0:T(8,128)(2,1)S(1)}, bf16[4,128,128]{2,1,0:T(8,128)(2,1)S(1)}, u32[]{:S(2)}, u32[]{:S(2)}) collective-permute-start(bf16[4,128,128]{2,1,0:T(8,128)(2,1)S(1)} %get-tuple-element.76), channel_id=1, source_target_pairs={{4,0},{8,4},{12,8},{14,12},{10,14},{6,10},{2,6},{0,2},{5,1},{9,5},... | collective-permute-start | bytes 393224 | tf_op jit(solution)/shard_map/ppermute | solution.py:352
  40.1 8.4 %collective-permute-start.16 = (bf16[4,128,128]{2,1,0:T(8,128)(2,1)S(1)}, bf16[4,128,128]{2,1,0:T(8,128)(2,1)S(1)}, u32[]{:S(2)}, u32[]{:S(2)}) collective-permute-start(bf16[4,128,128]{2,1,0:T(8,128)(2,1)S(1)} %convert_element_type.79), channel_id=1, source_target_pairs={{2,0},{0,4},{4,8},{8,12},{12,14},{14,10},{10,6},{6,2},{3,1},{1,5},... | collective-permute-start | bytes 393224 | tf_op jit(solution)/shard_map/ppermute | solution.py:352
  42.2 6.3 %collective-permute-start.15 = (bf16[4,128,128]{2,1,0:T(8,128)(2,1)S(1)}, bf16[4,128,128]{2,1,0:T(8,128)(2,1)S(1)}, u32[]{:S(2)}, u32[]{:S(2)}) collective-permute-start(bf16[4,128,128]{2,1,0:T(8,128)(2,1)S(1)} %convert_element_type.78), channel_id=1, source_target_pairs={{4,0},{8,4},{12,8},{14,12},{10,14},{6,10},{2,6},{0,2},{5,1},{9,5},... | collective-permute-start | bytes 393224 | tf_op jit(solution)/shard_map/ppermute | solution.py:352
  45.0 5.7 %collective-permute-start.11 = (bf16[4,128,128]{2,1,0:T(8,128)(2,1)S(1)}, bf16[4,128,128]{2,1,0:T(8,128)(2,1)S(1)}, u32[]{:S(2)}, u32[]{:S(2)}) collective-permute-start(bf16[4,128,128]{2,1,0:T(8,128)(2,1)S(1)} %add_convert_fusion.8), channel_id=1, source_target_pairs={{2,0},{0,4},{4,8},{8,12},{12,14},{14,10},{10,6},{6,2},{3,1},{1,5},... | collective-permute-start | bytes 393224 | tf_op jit(solution)/shard_map/ppermute | solution.py:352
  45.3 5.7 %collective-permute-start.10 = (bf16[4,128,128]{2,1,0:T(8,128)(2,1)S(1)}, bf16[4,128,128]{2,1,0:T(8,128)(2,1)S(1)}, u32[]{:S(2)}, u32[]{:S(2)}) collective-permute-start(bf16[4,128,128]{2,1,0:T(8,128)(2,1)S(1)} %add_convert_fusion.9), channel_id=1, source_target_pairs={{4,0},{8,4},{12,8},{14,12},{10,14},{6,10},{2,6},{0,2},{5,1},{9,5},... | collective-permute-start | bytes 393224 | tf_op jit(solution)/shard_map/ppermute | solution.py:352
  48.6 6.4 %collective-permute-start.18 = (bf16[4,128,128]{2,1,0:T(8,128)(2,1)S(1)}, bf16[4,128,128]{2,1,0:T(8,128)(2,1)S(1)}, u32[]{:S(2)}, u32[]{:S(2)}) collective-permute-start(bf16[4,128,128]{2,1,0:T(8,128)(2,1)S(1)} %add_convert_fusion.2), channel_id=1, source_target_pairs={{2,0},{0,4},{4,8},{8,12},{12,14},{14,10},{10,6},{6,2},{3,1},{1,5},... | collective-permute-start | bytes 393224 | tf_op jit(solution)/shard_map/ppermute | solution.py:352
  48.8 6.2 %collective-permute-start.17 = (bf16[4,128,128]{2,1,0:T(8,128)(2,1)S(1)}, bf16[4,128,128]{2,1,0:T(8,128)(2,1)S(1)}, u32[]{:S(2)}, u32[]{:S(2)}) collective-permute-start(bf16[4,128,128]{2,1,0:T(8,128)(2,1)S(1)} %add_convert_fusion.3), channel_id=1, source_target_pairs={{4,0},{8,4},{12,8},{14,12},{10,14},{6,10},{2,6},{0,2},{5,1},{9,5},... | collective-permute-start | bytes 393224 | tf_op jit(solution)/shard_map/ppermute | solution.py:352
  51.0 6.1 %collective-permute-start.13 = (bf16[4,128,128]{2,1,0:T(8,128)(2,1)S(1)}, bf16[4,128,128]{2,1,0:T(8,128)(2,1)S(1)}, u32[]{:S(2)}, u32[]{:S(2)}) collective-permute-start(bf16[4,128,128]{2,1,0:T(8,128)(2,1)S(1)} %add_convert_fusion.6), channel_id=1, source_target_pairs={{2,0},{0,4},{4,8},{8,12},{12,14},{14,10},{10,6},{6,2},{3,1},{1,5},... | collective-permute-start | bytes 393224 | tf_op jit(solution)/shard_map/ppermute | solution.py:352
  52.7 5.0 %collective-permute-start.12 = (bf16[4,128,128]{2,1,0:T(8,128)(2,1)S(1)}, bf16[4,128,128]{2,1,0:T(8,128)(2,1)S(1)}, u32[]{:S(2)}, u32[]{:S(2)}) collective-permute-start(bf16[4,128,128]{2,1,0:T(8,128)(2,1)S(1)} %add_convert_fusion.7), channel_id=1, source_target_pairs={{4,0},{8,4},{12,8},{14,12},{10,14},{6,10},{2,6},{0,2},{5,1},{9,5},... | collective-permute-start | bytes 393224 | tf_op jit(solution)/shard_map/ppermute | solution.py:352
  53.6 6.1 %copy-start.4 = (bf16[8,128,128]{2,1,0:T(8,128)(2,1)S(1)}, bf16[8,128,128]{2,1,0:T(8,128)(2,1)}, u32[]{:S(2)}) copy-start(bf16[8,128,128]{2,1,0:T(8,128)(2,1)} %attend.1.refs_0_) | copy-start | bytes 786436
  55.1 7.6 %collective-permute-start.19 = (bf16[4,128,128]{2,1,0:T(8,128)(2,1)S(1)}, bf16[4,128,128]{2,1,0:T(8,128)(2,1)S(1)}, u32[]{:S(2)}, u32[]{:S(2)}) collective-permute-start(bf16[4,128,128]{2,1,0:T(8,128)(2,1)S(1)} %add_convert_fusion.1), channel_id=1, source_target_pairs={{4,0},{8,4},{12,8},{14,12},{10,14},{6,10},{2,6},{0,2},{5,1},{9,5},... | collective-permute-start | bytes 393224 | tf_op jit(solution)/shard_map/ppermute | solution.py:352
  57.1 5.6 %collective-permute-start.20 = (bf16[4,128,128]{2,1,0:T(8,128)(2,1)S(1)}, bf16[4,128,128]{2,1,0:T(8,128)(2,1)S(1)}, u32[]{:S(2)}, u32[]{:S(2)}) collective-permute-start(bf16[4,128,128]{2,1,0:T(8,128)(2,1)S(1)} %add_convert_fusion), channel_id=1, source_target_pairs={{2,0},{0,4},{4,8},{8,12},{12,14},{14,10},{10,6},{6,2},{3,1},{1,5},... | collective-permute-start | bytes 393224 | tf_op jit(solution)/shard_map/ppermute | solution.py:352
  57.7 5.0 %collective-permute-start.14 = (bf16[4,128,128]{2,1,0:T(8,128)(2,1)S(1)}, bf16[4,128,128]{2,1,0:T(8,128)(2,1)S(1)}, u32[]{:S(2)}, u32[]{:S(2)}) collective-permute-start(bf16[4,128,128]{2,1,0:T(8,128)(2,1)S(1)} %add_convert_fusion.5), channel_id=1, source_target_pairs={{4,0},{8,4},{12,8},{14,12},{10,14},{6,10},{2,6},{0,2},{5,1},{9,5},... | collective-permute-start | bytes 393224 | tf_op jit(solution)/shard_map/ppermute | solution.py:352
  59.2 5.0 %collective-permute-start.21 = (bf16[4,128,128]{2,1,0:T(8,128)(2,1)S(1)}, bf16[4,128,128]{2,1,0:T(8,128)(2,1)S(1)}, u32[]{:S(2)}, u32[]{:S(2)}) collective-permute-start(bf16[4,128,128]{2,1,0:T(8,128)(2,1)S(1)} %add_convert_fusion.4), channel_id=1, source_target_pairs={{2,0},{0,4},{4,8},{8,12},{12,14},{14,10},{10,6},{6,2},{3,1},{1,5},... | collective-permute-start | bytes 393224 | tf_op jit(solution)/shard_map/ppermute | solution.py:352

commit v15 on v14

--- a/solution.py
+++ b/solution.py
@@ -208,24 +208,30 @@
             block_ref[column] += product
 
 
-def part_for(distance, count, low_ref, second_ref, dense_ref, block_ref, extra_ref, columns, out_ref):
+def part_for(distance, count, low_ref, second_ref, dense_ref, block_ref, extra_ref, columns, halves):
     width = dense_ref.shape[1]
     side = block_ref.shape[2]
     heads = width // side
+    half = heads // 2
     owner = owner_at(distance, count)
     start = pl.multiple_of(owner * width, width)
-    blocks = jnp.concatenate([block_ref[owner * heads + i] for i in range(heads)], axis=1)
-    out_ref[...] = (
-        jnp.dot(low_ref[...], second_ref[:, pl.ds(start, width)], preferred_element_type=F32)
-        + dense_ref[...]
-        + blocks
-    )
+    delta = jnp.dot(low_ref[...], second_ref[:, pl.ds(start, width)], preferred_element_type=F32)
+    for i in range(heads):
+        tile = slice(i * side, (i + 1) * side)
+        halves[i // half][i % half] = (
+            delta[:, tile] + dense_ref[:, tile] + block_ref[owner * heads + i]
+        )
     for e, column in enumerate(columns):
-
-        @pl.when(lax.div(column, heads) == owner)
-        def _(e=e, column=column):
-            place = pl.ds(pl.multiple_of(lax.rem(column, heads) * side, side), side)
-            out_ref[:, place] += extra_ref[e]
+        here = lax.div(column, heads) == owner
+        place = lax.rem(column, heads)
+
+        @pl.when(here & (place < half))
+        def _(e=e, place=place):
+            halves[0][place] += extra_ref[e]
+
+        @pl.when(here & (place >= half))
+        def _(e=e, place=place):
+            halves[1][place - half] += extra_ref[e]
 
 
 def finish_kernel(distances, count, *refs):
@@ -233,7 +239,7 @@
     second_ref, low_in, block_ref = refs[8:11]
     dense_refs, refs = refs[11 : 11 + len(distances)], refs[11 + len(distances) :]
     low_out, extra_out, front_out, back_out = refs[:4]
-    outs, (chunk, low_sum, total) = refs[4:-3], refs[-3:]
+    chunk, low_sum, total = refs[-3:]
     half, rows, side = front_ref.shape
     chunk[:half] = front_ref[...]
     chunk[half:] = back_ref[...]
@@ -250,32 +256,21 @@
     slots_wide = jnp.concatenate([slot] * -(-low_width // side), axis=1)[:, :low_width]
     low = jnp.where(slots_wide == held, low_sum[...], 0.0).astype(BF16)
     low_out[...] = low
-    for n, (distance, dense_ref) in enumerate(zip(distances, dense_refs)):
-        part_for(distance, count, low_out, second_ref, dense_ref, block_ref, extra_out, columns,
-                 total.at[n])
-        for i in range(2 * half):
-            tile = total[n, :, i * side : (i + 1) * side]
-            if n:
-                outs[2 * n - 2 + i // half][i % half] = tile
-            elif i < half:
-                front_out[i] = tile.astype(BF16)
-            else:
-                back_out[i - half] = tile.astype(BF16)
+    part_for(distances[0], count, low_out, second_ref, dense_refs[0], block_ref, extra_out, columns,
+             (total.at[0], total.at[1]))
+    front_out[...] = total[0].astype(BF16)
+    back_out[...] = total[1].astype(BF16)
 
 
 def part_kernel(distances, count, slots, *refs):
     low_ref, second_ref, block_ref, extra_ref, scale_ref, cell_ref, table_ref = refs[:7]
     dense_refs, refs = refs[7 : 7 + len(distances)], refs[7 + len(distances) :]
-    outs, total = refs[:-1], refs[-1]
-    side = block_ref.shape[2]
-    heads = dense_refs[0].shape[1] // side
+    heads = dense_refs[0].shape[1] // block_ref.shape[2]
     listed = held_blocks(count // 2, count, slots, heads, scale_ref, cell_ref, table_ref)
     columns = [entry[-1] for entry in listed]
     for n, (distance, dense_ref) in enumerate(zip(distances, dense_refs)):
         part_for(distance, count, low_ref, second_ref, dense_ref, block_ref, extra_ref, columns,
-                 total.at[n])
-        for i in range(heads):
-            outs[2 * n + 2 * i // heads][i % (heads // 2)] = total[n, :, i * side : (i + 1) * side]
+                 refs[2 * n : 2 * n + 2])
 
 
 def sum_kernel(*refs):
@@ -409,7 +404,7 @@
         [VMEM] * 2 + table_specs + [VMEM] * (3 + len(first)),
         [VMEM] * (2 + 2 * len(first)),
         [pltpu.VMEM((heads, rows, side), BF16), pltpu.VMEM((rows, low_width), F32),
-         pltpu.VMEM((len(first), rows, width), F32)],
+         pltpu.VMEM((2, heads // 2, rows, side), F32)],
         flops=rows * low_width * width * 8,
         moved=2 * MIB,
     )
@@ -424,7 +419,6 @@
              *[dense[distance] for distance in distances]),
             [VMEM] * 4 + [SMEM] * 3 + [VMEM] * len(distances),
             [VMEM] * (2 * len(distances)),
-            [pltpu.VMEM((len(distances), rows, width), F32)],
             flops=rows * low_width * width * 2,
             moved=MIB,
         )

time: 65.2 us -> 65.2 us (level)
  transfers between devices with their start and end apart: 22 -> 22, of which waited for: 10 -> 11; matrix products, arithmetic and copies ran while one was open for 1% -> 1% of each run, Pallas kernels for 31% -> 31%
where the time goes in v15:
time: 65.2 us; the launch traced here: 65 us
  Pallas kernels  27 us (41%)
  starting transfers between devices  26 us (40%)
  waiting for transfers between devices  10.3 us (16%)
  local copies, waits for them, and re-layouts  1.07 us (2%)
    pallas_call x13, Pallas kernels, call(): pl.pallas_call(kernel, out_shape=outs, in_specs=specs, out_specs=out_spec...  27 us
    ppermute x22, starting transfers between devices, come(): lax.ppermute(value, 'tp', [(ring[(i + distance) % count], ring[i]) for i...  26 us
    ppermute x22, waiting for transfers between devices, come(): lax.ppermute(value, 'tp', [(ring[(i + distance) % count], ring[i]) for i...  10.3 us
  transfers between devices with their start and end apart: 22, of which 11 were waited for; matrix products, arithmetic and copies ran while one was open for 1% of the time, Pallas kernels for 31%

profile of v15, /device:TPU:0, one launch (start us, length us, event | category | flops | bytes accessed | tf_op | source)
XLA Modules:
  0.0 65.0 jit_solution(12259479363564817737)
XLA Ops:
  0.0 4.6 %attend.1.refs_0_ = bf16[8,128,128]{2,1,0:T(8,128)(2,1)} custom-call(bf16[128,1024]{1,0:T(8,128)(2,1)} %query_hbm.1, bf16[4096,128]{1,0:T(8,128)(2,1)} %bitcast.21, bf16[4096,128]{1,0:T(8,128)(2,1)} %bitcast.22, bf16[128,128]{1,0:T(8,128)(2,1)} %bitcast.23, bf16[128,128]{1,0:T(8,128)(2,1)} %bitcast.24, s32[1,128]{1,0:T(1,128)} %bitcast.25), custom_call_target="tpu_custom_call" | custom-call | tf_op jit(solution)/shard_map/attend/pallas_call | solution.py:39
  4.6 3.1 %collective-permute-start.3 = (bf16[8,128,128]{2,1,0:T(8,128)(2,1)}, bf16[8,128,128]{2,1,0:T(8,128)(2,1)S(1)}, u32[]{:S(2)}, u32[]{:S(2)}) collective-permute-start(bf16[8,128,128]{2,1,0:T(8,128)(2,1)} %attend.1.refs_0_), channel_id=1, source_target_pairs={{2,0},{0,4},{4,8},{8,12},{12,14},{14,10},{10,6},{6,2},{3,1},{1,5},... | collective-permute-start | bytes 786440 | tf_op jit(solution)/shard_map/ppermute | solution.py:347
  7.7 1.0 %copy-done.3 = bf16[8,128,128]{2,1,0:T(8,128)(2,1)S(1)} copy-done((bf16[8,128,128]{2,1,0:T(8,128)(2,1)S(1)}, bf16[8,128,128]{2,1,0:T(8,128)(2,1)}, u32[]{:S(2)}) %copy-start.3) | copy-done | bytes 262168
  8.7 3.5 %dense.4 = (f32[128,1024]{1,0:T(8,128)S(1)}, f32[128,1024]{1,0:T(8,128)S(1)}, f32[128,1024]{1,0:T(8,128)S(1)}) custom-call(bf16[8,128,128]{2,1,0:T(8,128)(2,1)S(1)} %copy-done.3, bf16[1024,8192]{1,0:T(8,128)(2,1)} %refs_1_.7), custom_call_target="tpu_custom_call" | custom-call | flops 805306368 | bytes 6291456 | tf_op jit(solution)/shard_map/dense/pallas_call | solution.py:39
  12.1 2.0 %collective-permute-done.3.refs_2_ = bf16[8,128,128]{2,1,0:T(8,128)(2,1)S(1)} collective-permute-done((bf16[8,128,128]{2,1,0:T(8,128)(2,1)}, bf16[8,128,128]{2,1,0:T(8,128)(2,1)S(1)}, u32[]{:S(2)}, u32[]{:S(2)}) %collective-permute-start.3) | collective-permute-done | bytes 262176 | tf_op jit(solution)/shard_map/ppermute | solution.py:347
  14.1 1.8 %collective-permute-start.4 = (bf16[8,128,128]{2,1,0:T(8,128)(2,1)S(1)}, bf16[8,128,128]{2,1,0:T(8,128)(2,1)S(1)}, u32[]{:S(2)}, u32[]{:S(2)}) collective-permute-start(bf16[8,128,128]{2,1,0:T(8,128)(2,1)S(1)} %collective-permute-done.3.refs_2_), channel_id=1, source_target_pairs={{2,0},{0,4},{4,8},{8,12},{12,14},{14,10},{10,6},{6,2},{3,1},{1,5},... | collective-permute-start | bytes 786440 | tf_op jit(solution)/shard_map/ppermute | solution.py:347
  16.2 3.7 %dense.5 = (f32[128,1024]{1,0:T(8,128)S(1)}, f32[128,1024]{1,0:T(8,128)S(1)}, s32[128,128]{1,0:T(8,128)S(1)}, s32[64]{0:T(128)S(1)}) custom-call(bf16[8,128,128]{2,1,0:T(8,128)(2,1)S(1)} %copy-done.3, bf16[1024,8192]{1,0:T(8,128)(2,1)} %refs_1_.7, s32[1,128]{1,0:T(1,128)S(1)} %bitcast.20, s32[32]{0:T(128)S(1)} %copy-done.9, s32[4,16]{1,0:T(4,128)S(1)} %bitcast.19), custom_call_target="tpu_custom_call" | custom-call | flops 536870912 | bytes 4194304 | tf_op jit(solution)/shard_map/dense/pallas_call | solution.py:39
  19.9 1.7 %collective-permute-done.4.refs_4_ = bf16[8,128,128]{2,1,0:T(8,128)(2,1)S(1)} collective-permute-done((bf16[8,128,128]{2,1,0:T(8,128)(2,1)S(1)}, bf16[8,128,128]{2,1,0:T(8,128)(2,1)S(1)}, u32[]{:S(2)}, u32[]{:S(2)}) %collective-permute-start.4) | collective-permute-done | bytes 262176 | tf_op jit(solution)/shard_map/ppermute | solution.py:347
  21.6 1.5 %collective-permute-start.7 = (bf16[8,128,128]{2,1,0:T(8,128)(2,1)S(1)}, bf16[8,128,128]{2,1,0:T(8,128)(2,1)S(1)}, u32[]{:S(2)}, u32[]{:S(2)}) collective-permute-start(bf16[8,128,128]{2,1,0:T(8,128)(2,1)S(1)} %collective-permute-done.4.refs_4_), channel_id=1, source_target_pairs={{2,0},{0,4},{4,8},{8,12},{12,14},{14,10},{10,6},{6,2},{3,1},{1,5},... | collective-permute-start | bytes 786440 | tf_op jit(solution)/shard_map/ppermute | solution.py:347
  23.1 0.5 collective-permute-start.6
  23.7 2.5 %collective-permute-start.5 = (bf16[4,128,128]{2,1,0:T(8,128)(2,1)S(1)}, bf16[4,128,128]{2,1,0:T(8,128)(2,1)S(1)}, u32[]{:S(2)}, u32[]{:S(2)}) collective-permute-start(bf16[4,128,128]{2,1,0:T(8,128)(2,1)S(1)} %slice.7), channel_id=1, source_target_pairs={{6,0},{2,4},{0,8},{4,12},{8,14},{12,10},{14,6},{10,2},{7,1},{3,5},... | collective-permute-start | bytes 393224 | tf_op jit(solution)/shard_map/ppermute | solution.py:347
  26.6 2.1 %fold_early.1 = (f32[128,256]{1,0:T(8,128)S(1)}, f32[64,128,128]{2,1,0:T(8,128)S(1)}) custom-call(bf16[8,128,128]{2,1,0:T(8,128)(2,1)S(1)} %copy-done.3, bf16[8,128,128]{2,1,0:T(8,128)(2,1)S(1)} %collective-permute-done.refs_1_, bf16[8,128,128]{2,1,0:T(8,128)(2,1)S(1)} %collective-permute-done.3.refs_2_, ...), custom_call_target="tpu_custom_call" | custom-call | flops 268435456 | bytes 4194304 | tf_op jit(solution)/shard_map/fold_early/pallas_call | solution.py:39
  28.8 2.6 %dense.6 = (f32[128,1024]{1,0:T(8,128)S(1)}, f32[128,1024]{1,0:T(8,128)S(1)}) custom-call(bf16[8,128,128]{2,1,0:T(8,128)(2,1)S(1)} %copy-done.3, bf16[1024,8192]{1,0:T(8,128)(2,1)} %refs_1_.7), custom_call_target="tpu_custom_call" | custom-call | flops 536870912 | bytes 4194304 | tf_op jit(solution)/shard_map/dense/pallas_call | solution.py:39
  31.9 1.4 %fold_late.1 = (f32[128,256]{1,0:T(8,128)S(1)}, f32[64,128,128]{2,1,0:T(8,128)S(1)}) custom-call(bf16[8,128,128]{2,1,0:T(8,128)(2,1)S(1)} %collective-permute-done.6.refs_0_, bf16[8,128,128]{2,1,0:T(8,128)(2,1)S(1)} %collective-permute-done.7.refs_1_, s32[128,128]{1,0:T(8,128)S(1)} %get-tuple-element.63.refs_5_.refs_2_, bf16[256,8192]{1,0:T(8,128)(2,1)S(1)} %bitcast.17, ...), custom_call_target="tpu_custom_call" | custom-call | flops 134217728 | bytes 1048576 | tf_op jit(solution)/shard_map/fold_late/pallas_call | solution.py:39
  33.3 0.7 %collective-permute-done.5.refs_1_ = bf16[4,128,128]{2,1,0:T(8,128)(2,1)S(1)} collective-permute-done((bf16[4,128,128]{2,1,0:T(8,128)(2,1)S(1)}, bf16[4,128,128]{2,1,0:T(8,128)(2,1)S(1)}, u32[]{:S(2)}, u32[]{:S(2)}) %collective-permute-start.5) | collective-permute-done | bytes 131104 | tf_op jit(solution)/shard_map/ppermute | solution.py:347
  34.4 1.4 %finish.1 = (bf16[128,256]{1,0:T(8,128)(2,1)S(1)}, f32[8,128,128]{2,1,0:T(8,128)S(1)}, bf16[4,128,128]{2,1,0:T(8,128)(2,1)S(1)}, bf16[4,128,128]{2,1,0:T(8,128)(2,1)S(1)}) custom-call(bf16[4,128,128]{2,1,0:T(8,128)(2,1)S(1)} %collective-permute-done.2.refs_0_, bf16[4,128,128]{2,1,0:T(8,128)(2,1)S(1)} %collective-permute-done.5.refs_1_, ...), custom_call_target="tpu_custom_call" | custom-call | flops 268435456 | bytes 2097152 | tf_op jit(solution)/shard_map/finish/pallas_call | solution.py:39
  35.8 2.9 %collective-permute-start.9 = (bf16[4,128,128]{2,1,0:T(8,128)(2,1)S(1)}, bf16[4,128,128]{2,1,0:T(8,128)(2,1)S(1)}, u32[]{:S(2)}, u32[]{:S(2)}) collective-permute-start(bf16[4,128,128]{2,1,0:T(8,128)(2,1)S(1)} %get-tuple-element.77), channel_id=1, source_target_pairs={{2,0},{0,4},{4,8},{8,12},{12,14},{14,10},{10,6},{6,2},{3,1},{1,5},... | collective-permute-start | bytes 393224 | tf_op jit(solution)/shard_map/ppermute | solution.py:347
  38.8 1.3 %part.4 = (f32[4,128,128]{2,1,0:T(8,128)S(1)}, f32[4,128,128]{2,1,0:T(8,128)S(1)}, f32[4,128,128]{2,1,0:T(8,128)S(1)}, f32[4,128,128]{2,1,0:T(8,128)S(1)}) custom-call(bf16[128,256]{1,0:T(8,128)(2,1)S(1)} %get-tuple-element.99.refs_0_, bf16[256,8192]{1,0:T(8,128)(2,1)S(1)} %bitcast.12, f32[64,128,128]{2,1,0:T(8,128)S(1)} %get-tuple-element.74.refs_10_.refs_2_, ...), custom_call_target="tpu_custom_call" | custom-call | flops 67108864 | bytes 1048576 | tf_op jit(solution)/shard_map/part/pallas_call | solution.py:39
  40.2 2.1 %collective-permute-start.16 = (bf16[4,128,128]{2,1,0:T(8,128)(2,1)S(1)}, bf16[4,128,128]{2,1,0:T(8,128)(2,1)S(1)}, u32[]{:S(2)}, u32[]{:S(2)}) collective-permute-start(bf16[4,128,128]{2,1,0:T(8,128)(2,1)S(1)} %convert_element_type.79), channel_id=1, source_target_pairs={{2,0},{0,4},{4,8},{8,12},{12,14},{14,10},{10,6},{6,2},{3,1},{1,5},... | collective-permute-start | bytes 393224 | tf_op jit(solution)/shard_map/ppermute | solution.py:347
  42.7 2.3 %collective-permute-done.8 = bf16[4,128,128]{2,1,0:T(8,128)(2,1)S(1)} collective-permute-done((bf16[4,128,128]{2,1,0:T(8,128)(2,1)S(1)}, bf16[4,128,128]{2,1,0:T(8,128)(2,1)S(1)}, u32[]{:S(2)}, u32[]{:S(2)}) %collective-permute-start.8) | collective-permute-done | bytes 131104 | tf_op jit(solution)/shard_map/ppermute | solution.py:347
  45.4 1.7 %collective-permute-start.10 = (bf16[4,128,128]{2,1,0:T(8,128)(2,1)S(1)}, bf16[4,128,128]{2,1,0:T(8,128)(2,1)S(1)}, u32[]{:S(2)}, u32[]{:S(2)}) collective-permute-start(bf16[4,128,128]{2,1,0:T(8,128)(2,1)S(1)} %add_convert_fusion.9), channel_id=1, source_target_pairs={{4,0},{8,4},{12,8},{14,12},{10,14},{6,10},{2,6},{0,2},{5,1},{9,5},... | collective-permute-start | bytes 393224 | tf_op jit(solution)/shard_map/ppermute | solution.py:347
  47.1 1.3 %part.5 = (f32[4,128,128]{2,1,0:T(8,128)S(1)}, f32[4,128,128]{2,1,0:T(8,128)S(1)}, f32[4,128,128]{2,1,0:T(8,128)S(1)}, f32[4,128,128]{2,1,0:T(8,128)S(1)}) custom-call(bf16[128,256]{1,0:T(8,128)(2,1)S(1)} %get-tuple-element.99.refs_0_, bf16[256,8192]{1,0:T(8,128)(2,1)S(1)} %bitcast.13, f32[64,128,128]{2,1,0:T(8,128)S(1)} %get-tuple-element.74.refs_10_.refs_2_, ...), custom_call_target="tpu_custom_call" | custom-call | flops 67108864 | bytes 1048576 | tf_op jit(solution)/shard_map/part/pallas_call | solution.py:39
  48.9 1.7 %collective-permute-start.17 = (bf16[4,128,128]{2,1,0:T(8,128)(2,1)S(1)}, bf16[4,128,128]{2,1,0:T(8,128)(2,1)S(1)}, u32[]{:S(2)}, u32[]{:S(2)}) collective-permute-start(bf16[4,128,128]{2,1,0:T(8,128)(2,1)S(1)} %add_convert_fusion.3), channel_id=1, source_target_pairs={{4,0},{8,4},{12,8},{14,12},{10,14},{6,10},{2,6},{0,2},{5,1},{9,5},... | collective-permute-start | bytes 393224 | tf_op jit(solution)/shard_map/ppermute | solution.py:347
  51.1 1.5 %collective-permute-start.13 = (bf16[4,128,128]{2,1,0:T(8,128)(2,1)S(1)}, bf16[4,128,128]{2,1,0:T(8,128)(2,1)S(1)}, u32[]{:S(2)}, u32[]{:S(2)}) collective-permute-start(bf16[4,128,128]{2,1,0:T(8,128)(2,1)S(1)} %add_convert_fusion.6), channel_id=1, source_target_pairs={{2,0},{0,4},{4,8},{8,12},{12,14},{14,10},{10,6},{6,2},{3,1},{1,5},... | collective-permute-start | bytes 393224 | tf_op jit(solution)/shard_map/ppermute | solution.py:347
  52.6 1.1 %collective-permute-start.12 = (bf16[4,128,128]{2,1,0:T(8,128)(2,1)S(1)}, bf16[4,128,128]{2,1,0:T(8,128)(2,1)S(1)}, u32[]{:S(2)}, u32[]{:S(2)}) collective-permute-start(bf16[4,128,128]{2,1,0:T(8,128)(2,1)S(1)} %add_convert_fusion.7), channel_id=1, source_target_pairs={{4,0},{8,4},{12,8},{14,12},{10,14},{6,10},{2,6},{0,2},{5,1},{9,5},... | collective-permute-start | bytes 393224 | tf_op jit(solution)/shard_map/ppermute | solution.py:347
  53.6 1.3 %part.6 = (f32[4,128,128]{2,1,0:T(8,128)S(1)}, f32[4,128,128]{2,1,0:T(8,128)S(1)}, f32[4,128,128]{2,1,0:T(8,128)S(1)}, f32[4,128,128]{2,1,0:T(8,128)S(1)}) custom-call(bf16[128,256]{1,0:T(8,128)(2,1)S(1)} %get-tuple-element.99.refs_0_, bf16[256,8192]{1,0:T(8,128)(2,1)S(1)} %bitcast.14, f32[64,128,128]{2,1,0:T(8,128)S(1)} %get-tuple-element.74.refs_10_.refs_2_, ...), custom_call_target="tpu_custom_call" | custom-call | flops 67108864 | bytes 1048576 | tf_op jit(solution)/shard_map/part/pallas_call | solution.py:39
  55.1 2.0 %collective-permute-start.19 = (bf16[4,128,128]{2,1,0:T(8,128)(2,1)S(1)}, bf16[4,128,128]{2,1,0:T(8,128)(2,1)S(1)}, u32[]{:S(2)}, u32[]{:S(2)}) collective-permute-start(bf16[4,128,128]{2,1,0:T(8,128)(2,1)S(1)} %add_convert_fusion.1), channel_id=1, source_target_pairs={{4,0},{8,4},{12,8},{14,12},{10,14},{6,10},{2,6},{0,2},{5,1},{9,5},... | collective-permute-start | bytes 393224 | tf_op jit(solution)/shard_map/ppermute | solution.py:347
  57.6 1.7 %collective-permute-start.14 = (bf16[4,128,128]{2,1,0:T(8,128)(2,1)S(1)}, bf16[4,128,128]{2,1,0:T(8,128)(2,1)S(1)}, u32[]{:S(2)}, u32[]{:S(2)}) collective-permute-start(bf16[4,128,128]{2,1,0:T(8,128)(2,1)S(1)} %add_convert_fusion.5), channel_id=1, source_target_pairs={{4,0},{8,4},{12,8},{14,12},{10,14},{6,10},{2,6},{0,2},{5,1},{9,5},... | collective-permute-start | bytes 393224 | tf_op jit(solution)/shard_map/ppermute | solution.py:347
  59.7 1.9 %dense.7.refs_7_ = f32[128,1024]{1,0:T(8,128)S(1)} custom-call(bf16[8,128,128]{2,1,0:T(8,128)(2,1)S(1)} %copy-done.4, bf16[1024,8192]{1,0:T(8,128)(2,1)} %refs_1_.7), custom_call_target="tpu_custom_call" | custom-call | flops 268435456 | bytes 2097152 | tf_op jit(solution)/shard_map/dense/pallas_call | solution.py:39
  61.6 1.0 %part.7 = (f32[4,128,128]{2,1,0:T(8,128)S(1)}, f32[4,128,128]{2,1,0:T(8,128)S(1)}) custom-call(bf16[128,256]{1,0:T(8,128)(2,1)S(1)} %get-tuple-element.99.refs_0_, bf16[256,8192]{1,0:T(8,128)(2,1)S(1)} %bitcast.15, f32[64,128,128]{2,1,0:T(8,128)S(1)} %get-tuple-element.74.refs_10_.refs_2_, f32[8,128,128]{2,1,0:T(8,128)S(1)} %get-tuple-element.79.refs_3_, ...), custom_call_target="tpu_custom_call" | custom-call | flops 67108864 | bytes 1048576 | tf_op jit(solution)/shard_map/part/pallas_call | solution.py:39
  62.6 1.6 %collective-permute-done.21.refs_5_ = bf16[4,128,128]{2,1,0:T(8,128)(2,1)S(1)} collective-permute-done((bf16[4,128,128]{2,1,0:T(8,128)(2,1)S(1)}, bf16[4,128,128]{2,1,0:T(8,128)(2,1)S(1)}, u32[]{:S(2)}, u32[]{:S(2)}) %collective-permute-start.21) | collective-permute-done | bytes 131104 | tf_op jit(solution)/shard_map/ppermute | solution.py:347
  64.2 0.8 %sum_up.1 = bf16[128,1024]{1,0:T(8,128)(2,1)} custom-call(f32[4,128,128]{2,1,0:T(8,128)S(1)} %get-tuple-element.101.refs_0_, f32[4,128,128]{2,1,0:T(8,128)S(1)} %get-tuple-element.102.refs_1_, bf16[4,128,128]{2,1,0:T(8,128)(2,1)S(1)} %collective-permute-done.14.refs_2_, bf16[4,128,128]{2,1,0:T(8,128)(2,1)S(1)} %collective-permute-done.19.refs_3_, ...), custom_call_target="tpu_custom_call" | custom-call | flops 1 | bytes 1 | tf_op jit(solution)/shard_map/sum_up/pallas_call | solution.py:39
  (59 shorter events, 4.3 us)
Async XLA Ops:
  0.0 16.1 %copy-start.7 = (s32[4,16,1]{1,2,0:T(1,128)S(1)}, s32[4,16,1]{1,2,0:T(1,128)}, u32[]{:S(2)}) copy-start(s32[4,16,1]{1,2,0:T(1,128)} %param.28) | copy-start | bytes 772
  0.0 16.1 %copy-start.8 = (s32[128]{0:T(128)S(1)}, s32[128]{0:T(128)}, u32[]{:S(2)}) copy-start(s32[128]{0:T(128)} %param.21) | copy-start | bytes 1540
  0.0 16.1 %copy-start.9 = (s32[32]{0:T(128)S(1)}, s32[32]{0:T(128)}, u32[]{:S(2)}) copy-start(s32[32]{0:T(128)} %refs_3_.1) | copy-start | bytes 388
  4.6 9.5 %collective-permute-start.3 = (bf16[8,128,128]{2,1,0:T(8,128)(2,1)}, bf16[8,128,128]{2,1,0:T(8,128)(2,1)S(1)}, u32[]{:S(2)}, u32[]{:S(2)}) collective-permute-start(bf16[8,128,128]{2,1,0:T(8,128)(2,1)} %attend.1.refs_0_), channel_id=1, source_target_pairs={{2,0},{0,4},{4,8},{8,12},{12,14},{14,10},{10,6},{6,2},{3,1},{1,5},... | collective-permute-start | bytes 786440 | tf_op jit(solution)/shard_map/ppermute | solution.py:347
  7.6 8.3 %collective-permute-start = (bf16[8,128,128]{2,1,0:T(8,128)(2,1)}, bf16[8,128,128]{2,1,0:T(8,128)(2,1)S(1)}, u32[]{:S(2)}, u32[]{:S(2)}) collective-permute-start(bf16[8,128,128]{2,1,0:T(8,128)(2,1)} %attend.1.refs_0_), channel_id=1, source_target_pairs={{4,0},{8,4},{12,8},{14,12},{10,14},{6,10},{2,6},{0,2},{5,1},{9,5},... | collective-permute-start | bytes 786440 | tf_op jit(solution)/shard_map/ppermute | solution.py:347
  7.7 1.0 %copy-start.3 = (bf16[8,128,128]{2,1,0:T(8,128)(2,1)S(1)}, bf16[8,128,128]{2,1,0:T(8,128)(2,1)}, u32[]{:S(2)}) copy-start(bf16[8,128,128]{2,1,0:T(8,128)(2,1)} %attend.1.refs_0_) | copy-start | bytes 786436
  14.1 7.5 %collective-permute-start.4 = (bf16[8,128,128]{2,1,0:T(8,128)(2,1)S(1)}, bf16[8,128,128]{2,1,0:T(8,128)(2,1)S(1)}, u32[]{:S(2)}, u32[]{:S(2)}) collective-permute-start(bf16[8,128,128]{2,1,0:T(8,128)(2,1)S(1)} %collective-permute-done.3.refs_2_), channel_id=1, source_target_pairs={{2,0},{0,4},{4,8},{8,12},{12,14},{14,10},{10,6},{6,2},{3,1},{1,5},... | collective-permute-start | bytes 786440 | tf_op jit(solution)/shard_map/ppermute | solution.py:347
  15.9 7.2 %collective-permute-start.1 = (bf16[8,128,128]{2,1,0:T(8,128)(2,1)S(1)}, bf16[8,128,128]{2,1,0:T(8,128)(2,1)S(1)}, u32[]{:S(2)}, u32[]{:S(2)}) collective-permute-start(bf16[8,128,128]{2,1,0:T(8,128)(2,1)S(1)} %collective-permute-done.refs_1_), channel_id=1, source_target_pairs={{4,0},{8,4},{12,8},{14,12},{10,14},{6,10},{2,6},{0,2},{5,1},{9,5},... | collective-permute-start | bytes 786440 | tf_op jit(solution)/shard_map/ppermute | solution.py:347
  16.1 10.5 %copy-start.1 = (bf16[4,8192,64]{1,2,0:T(8,128)(2,1)S(1)}, bf16[4,8192,64]{1,2,0:T(8,128)(2,1)}, u32[]{:S(2)}) copy-start(bf16[4,8192,64]{1,2,0:T(8,128)(2,1)} %param.24) | copy-start | bytes 12582916
  16.1 10.5 %copy-start.2 = (bf16[4,16,128,128]{3,2,1,0:T(8,128)(2,1)S(1)}, bf16[4,16,128,128]{3,2,1,0:T(8,128)(2,1)}, u32[]{:S(2)}) copy-start(bf16[4,16,128,128]{3,2,1,0:T(8,128)(2,1)} %refs_4_.7) | copy-start | bytes 6291460
  16.2 10.5 %copy-start.5 = (f32[4,16]{1,0:T(4,128)S(1)}, f32[4,16]{1,0:T(4,128)}, u32[]{:S(2)}) copy-start(f32[4,16]{1,0:T(4,128)} %refs_4_.11) | copy-start | bytes 772
  16.2 10.5 %copy-start.6 = (s32[4,16]{1,0:T(4,128)S(1)}, s32[4,16]{1,0:T(4,128)}, u32[]{:S(2)}) copy-start(s32[4,16]{1,0:T(4,128)} %refs_5_.11) | copy-start | bytes 772
  21.6 9.8 %collective-permute-start.7 = (bf16[8,128,128]{2,1,0:T(8,128)(2,1)S(1)}, bf16[8,128,128]{2,1,0:T(8,128)(2,1)S(1)}, u32[]{:S(2)}, u32[]{:S(2)}) collective-permute-start(bf16[8,128,128]{2,1,0:T(8,128)(2,1)S(1)} %collective-permute-done.4.refs_4_), channel_id=1, source_target_pairs={{2,0},{0,4},{4,8},{8,12},{12,14},{14,10},{10,6},{6,2},{3,1},{1,5},... | collective-permute-start | bytes 786440 | tf_op jit(solution)/shard_map/ppermute | solution.py:347
  23.1 8.8 %collective-permute-start.6 = (bf16[8,128,128]{2,1,0:T(8,128)(2,1)S(1)}, bf16[8,128,128]{2,1,0:T(8,128)(2,1)S(1)}, u32[]{:S(2)}, u32[]{:S(2)}) collective-permute-start(bf16[8,128,128]{2,1,0:T(8,128)(2,1)S(1)} %collective-permute-done.1.refs_3_), channel_id=1, source_target_pairs={{4,0},{8,4},{12,8},{14,12},{10,14},{6,10},{2,6},{0,2},{5,1},{9,5},... | collective-permute-start | bytes 786440 | tf_op jit(solution)/shard_map/ppermute | solution.py:347
  23.7 10.3 %collective-permute-start.5 = (bf16[4,128,128]{2,1,0:T(8,128)(2,1)S(1)}, bf16[4,128,128]{2,1,0:T(8,128)(2,1)S(1)}, u32[]{:S(2)}, u32[]{:S(2)}) collective-permute-start(bf16[4,128,128]{2,1,0:T(8,128)(2,1)S(1)} %slice.7), channel_id=1, source_target_pairs={{6,0},{2,4},{0,8},{4,12},{8,14},{12,10},{14,6},{10,2},{7,1},{3,5},... | collective-permute-start | bytes 393224 | tf_op jit(solution)/shard_map/ppermute | solution.py:347
  26.2 8.2 %collective-permute-start.2 = (bf16[4,128,128]{2,1,0:T(8,128)(2,1)S(1)}, bf16[4,128,128]{2,1,0:T(8,128)(2,1)S(1)}, u32[]{:S(2)}, u32[]{:S(2)}) collective-permute-start(bf16[4,128,128]{2,1,0:T(8,128)(2,1)S(1)} %slice.6), channel_id=1, source_target_pairs={{8,0},{12,4},{14,8},{10,12},{6,14},{2,10},{0,6},{4,2},{9,1},{13,5}... | collective-permute-start | bytes 393224 | tf_op jit(solution)/shard_map/ppermute | solution.py:347
  31.9 2.5 %copy-start = (bf16[4,64,8192]{2,1,0:T(8,128)(2,1)S(1)}, bf16[4,64,8192]{2,1,0:T(8,128)(2,1)}, u32[]{:S(2)}) copy-start(bf16[4,64,8192]{2,1,0:T(8,128)(2,1)} %param.25) | copy-start | bytes 12582916
  35.8 6.8 %collective-permute-start.9 = (bf16[4,128,128]{2,1,0:T(8,128)(2,1)S(1)}, bf16[4,128,128]{2,1,0:T(8,128)(2,1)S(1)}, u32[]{:S(2)}, u32[]{:S(2)}) collective-permute-start(bf16[4,128,128]{2,1,0:T(8,128)(2,1)S(1)} %get-tuple-element.77), channel_id=1, source_target_pairs={{2,0},{0,4},{4,8},{8,12},{12,14},{14,10},{10,6},{6,2},{3,1},{1,5},... | collective-permute-start | bytes 393224 | tf_op jit(solution)/shard_map/ppermute | solution.py:347
  38.8 6.2 %collective-permute-start.8 = (bf16[4,128,128]{2,1,0:T(8,128)(2,1)S(1)}, bf16[4,128,128]{2,1,0:T(8,128)(2,1)S(1)}, u32[]{:S(2)}, u32[]{:S(2)}) collective-permute-start(bf16[4,128,128]{2,1,0:T(8,128)(2,1)S(1)} %get-tuple-element.76), channel_id=1, source_target_pairs={{4,0},{8,4},{12,8},{14,12},{10,14},{6,10},{2,6},{0,2},{5,1},{9,5},... | collective-permute-start | bytes 393224 | tf_op jit(solution)/shard_map/ppermute | solution.py:347
  40.2 8.3 %collective-permute-start.16 = (bf16[4,128,128]{2,1,0:T(8,128)(2,1)S(1)}, bf16[4,128,128]{2,1,0:T(8,128)(2,1)S(1)}, u32[]{:S(2)}, u32[]{:S(2)}) collective-permute-start(bf16[4,128,128]{2,1,0:T(8,128)(2,1)S(1)} %convert_element_type.79), channel_id=1, source_target_pairs={{2,0},{0,4},{4,8},{8,12},{12,14},{14,10},{10,6},{6,2},{3,1},{1,5},... | collective-permute-start | bytes 393224 | tf_op jit(solution)/shard_map/ppermute | solution.py:347
  42.2 6.3 %collective-permute-start.15 = (bf16[4,128,128]{2,1,0:T(8,128)(2,1)S(1)}, bf16[4,128,128]{2,1,0:T(8,128)(2,1)S(1)}, u32[]{:S(2)}, u32[]{:S(2)}) collective-permute-start(bf16[4,128,128]{2,1,0:T(8,128)(2,1)S(1)} %convert_element_type.78), channel_id=1, source_target_pairs={{4,0},{8,4},{12,8},{14,12},{10,14},{6,10},{2,6},{0,2},{5,1},{9,5},... | collective-permute-start | bytes 393224 | tf_op jit(solution)/shard_map/ppermute | solution.py:347
  45.0 5.7 %collective-permute-start.11 = (bf16[4,128,128]{2,1,0:T(8,128)(2,1)S(1)}, bf16[4,128,128]{2,1,0:T(8,128)(2,1)S(1)}, u32[]{:S(2)}, u32[]{:S(2)}) collective-permute-start(bf16[4,128,128]{2,1,0:T(8,128)(2,1)S(1)} %add_convert_fusion.8), channel_id=1, source_target_pairs={{2,0},{0,4},{4,8},{8,12},{12,14},{14,10},{10,6},{6,2},{3,1},{1,5},... | collective-permute-start | bytes 393224 | tf_op jit(solution)/shard_map/ppermute | solution.py:347
  45.4 5.7 %collective-permute-start.10 = (bf16[4,128,128]{2,1,0:T(8,128)(2,1)S(1)}, bf16[4,128,128]{2,1,0:T(8,128)(2,1)S(1)}, u32[]{:S(2)}, u32[]{:S(2)}) collective-permute-start(bf16[4,128,128]{2,1,0:T(8,128)(2,1)S(1)} %add_convert_fusion.9), channel_id=1, source_target_pairs={{4,0},{8,4},{12,8},{14,12},{10,14},{6,10},{2,6},{0,2},{5,1},{9,5},... | collective-permute-start | bytes 393224 | tf_op jit(solution)/shard_map/ppermute | solution.py:347
  48.6 6.4 %collective-permute-start.18 = (bf16[4,128,128]{2,1,0:T(8,128)(2,1)S(1)}, bf16[4,128,128]{2,1,0:T(8,128)(2,1)S(1)}, u32[]{:S(2)}, u32[]{:S(2)}) collective-permute-start(bf16[4,128,128]{2,1,0:T(8,128)(2,1)S(1)} %add_convert_fusion.2), channel_id=1, source_target_pairs={{2,0},{0,4},{4,8},{8,12},{12,14},{14,10},{10,6},{6,2},{3,1},{1,5},... | collective-permute-start | bytes 393224 | tf_op jit(solution)/shard_map/ppermute | solution.py:347
  48.9 6.1 %collective-permute-start.17 = (bf16[4,128,128]{2,1,0:T(8,128)(2,1)S(1)}, bf16[4,128,128]{2,1,0:T(8,128)(2,1)S(1)}, u32[]{:S(2)}, u32[]{:S(2)}) collective-permute-start(bf16[4,128,128]{2,1,0:T(8,128)(2,1)S(1)} %add_convert_fusion.3), channel_id=1, source_target_pairs={{4,0},{8,4},{12,8},{14,12},{10,14},{6,10},{2,6},{0,2},{5,1},{9,5},... | collective-permute-start | bytes 393224 | tf_op jit(solution)/shard_map/ppermute | solution.py:347
  51.1 6.0 %collective-permute-start.13 = (bf16[4,128,128]{2,1,0:T(8,128)(2,1)S(1)}, bf16[4,128,128]{2,1,0:T(8,128)(2,1)S(1)}, u32[]{:S(2)}, u32[]{:S(2)}) collective-permute-start(bf16[4,128,128]{2,1,0:T(8,128)(2,1)S(1)} %add_convert_fusion.6), channel_id=1, source_target_pairs={{2,0},{0,4},{4,8},{8,12},{12,14},{14,10},{10,6},{6,2},{3,1},{1,5},... | collective-permute-start | bytes 393224 | tf_op jit(solution)/shard_map/ppermute | solution.py:347
  52.6 5.0 %collective-permute-start.12 = (bf16[4,128,128]{2,1,0:T(8,128)(2,1)S(1)}, bf16[4,128,128]{2,1,0:T(8,128)(2,1)S(1)}, u32[]{:S(2)}, u32[]{:S(2)}) collective-permute-start(bf16[4,128,128]{2,1,0:T(8,128)(2,1)S(1)} %add_convert_fusion.7), channel_id=1, source_target_pairs={{4,0},{8,4},{12,8},{14,12},{10,14},{6,10},{2,6},{0,2},{5,1},{9,5},... | collective-permute-start | bytes 393224 | tf_op jit(solution)/shard_map/ppermute | solution.py:347
  53.6 6.0 %copy-start.4 = (bf16[8,128,128]{2,1,0:T(8,128)(2,1)S(1)}, bf16[8,128,128]{2,1,0:T(8,128)(2,1)}, u32[]{:S(2)}) copy-start(bf16[8,128,128]{2,1,0:T(8,128)(2,1)} %attend.1.refs_0_) | copy-start | bytes 786436
  55.1 7.5 %collective-permute-start.19 = (bf16[4,128,128]{2,1,0:T(8,128)(2,1)S(1)}, bf16[4,128,128]{2,1,0:T(8,128)(2,1)S(1)}, u32[]{:S(2)}, u32[]{:S(2)}) collective-permute-start(bf16[4,128,128]{2,1,0:T(8,128)(2,1)S(1)} %add_convert_fusion.1), channel_id=1, source_target_pairs={{4,0},{8,4},{12,8},{14,12},{10,14},{6,10},{2,6},{0,2},{5,1},{9,5},... | collective-permute-start | bytes 393224 | tf_op jit(solution)/shard_map/ppermute | solution.py:347
  57.1 5.5 %collective-permute-start.20 = (bf16[4,128,128]{2,1,0:T(8,128)(2,1)S(1)}, bf16[4,128,128]{2,1,0:T(8,128)(2,1)S(1)}, u32[]{:S(2)}, u32[]{:S(2)}) collective-permute-start(bf16[4,128,128]{2,1,0:T(8,128)(2,1)S(1)} %add_convert_fusion), channel_id=1, source_target_pairs={{2,0},{0,4},{4,8},{8,12},{12,14},{14,10},{10,6},{6,2},{3,1},{1,5},... | collective-permute-start | bytes 393224 | tf_op jit(solution)/shard_map/ppermute | solution.py:347
  57.6 5.0 %collective-permute-start.14 = (bf16[4,128,128]{2,1,0:T(8,128)(2,1)S(1)}, bf16[4,128,128]{2,1,0:T(8,128)(2,1)S(1)}, u32[]{:S(2)}, u32[]{:S(2)}) collective-permute-start(bf16[4,128,128]{2,1,0:T(8,128)(2,1)S(1)} %add_convert_fusion.5), channel_id=1, source_target_pairs={{4,0},{8,4},{12,8},{14,12},{10,14},{6,10},{2,6},{0,2},{5,1},{9,5},... | collective-permute-start | bytes 393224 | tf_op jit(solution)/shard_map/ppermute | solution.py:347
  59.3 5.0 %collective-permute-start.21 = (bf16[4,128,128]{2,1,0:T(8,128)(2,1)S(1)}, bf16[4,128,128]{2,1,0:T(8,128)(2,1)S(1)}, u32[]{:S(2)}, u32[]{:S(2)}) collective-permute-start(bf16[4,128,128]{2,1,0:T(8,128)(2,1)S(1)} %add_convert_fusion.4), channel_id=1, source_target_pairs={{2,0},{0,4},{4,8},{8,12},{12,14},{14,10},{10,6},{6,2},{3,1},{1,5},... | collective-permute-start | bytes 393224 | tf_op jit(solution)/shard_map/ppermute | solution.py:347
